TPU v7x, 32 devices: a whole 2x2x4 slice. The times are simulated.
32 devices in a mesh: seq: 8 (over y, x, core), tm: 4 (over z).
Axes of the slice: x: 2, y: 2, z: 4, core: 2. Of those that a mesh axis runs over, the one named last changes fastest.
Arguments:
- phonemes: bfloat16 [32768, 512], P('seq'), may hold values from -6 to 6
- send_order: int32 [8, 4096], P('seq'), may hold values from 0 to 4095, each once within a row
- phoneme_counts: int32 [8, 4], P('seq'), may hold values from 1 to 3584, as said below
- frame_lengths: int32 [8, 4], P('seq'), may hold values from 512 to 14336, as said below
- tile_offsets: int32 [1024], P(('seq', 'tm')), may hold values from 0 to 3968, as said below
- alignment: bfloat16 [131072, 128], P(('seq', 'tm')), may hold values from 0 to 0.19921875
- style_vec: bfloat16 [32, 128], P('seq'), may hold values from -6 to 6
- first_affine_weight: bfloat16 [128, 1024], replicated, may hold values from -0.25 to 0.25
- first_affine_bias: bfloat16 [1024], replicated, may hold values from -2 to 2
- first_conv_weight: bfloat16 [1536, 512], replicated, may hold values from -0.15625 to 0.15625
- second_affine_weight: bfloat16 [128, 1024], replicated, may hold values from -0.25 to 0.25
- second_affine_bias: bfloat16 [1024], replicated, may hold values from -2 to 2
- second_conv_weight: bfloat16 [1536, 512], replicated, may hold values from -0.15625 to 0.15625
- second_conv_bias: bfloat16 [512], replicated, may hold values from -2 to 2
- cotangent: bfloat16 [131072, 512], P(('seq', 'tm')), may hold values from -6 to 6
Outputs:
- frames_out: bfloat16 [131072, 512], P(('seq', 'tm'))
- phonemes_grad: float32 [32768, 512], P('seq')
- style_grad: float32 [32, 128], P('seq')
- first_affine_weight_grad: float32 [128, 1024], replicated
- first_affine_bias_grad: float32 [1024], replicated
- first_conv_weight_grad: float32 [1536, 512], replicated
- second_affine_weight_grad: float32 [128, 1024], replicated
- second_affine_bias_grad: float32 [1024], replicated
- second_conv_weight_grad: float32 [1536, 512], replicated
- second_conv_bias_grad: float32 [512], replicated
Inputs may be any that keep to these rules, and one draw needn't show every extreme that they name: `frame_lengths`: utterances of a group in order; their sum is at most 16384, frames past it are padding; the second utterance of each group starts on the group's first 4096 frames and ends on its last 4096. `phoneme_counts`: each is a quarter of its utterance's frames, rounded down, or one less; a group's counts sum to at most 4096. `send_order`: each row is a permutation. `tile_offsets`: window start of a block within its group's 4096 slots; a block among frames t * 4096 to (t + 1) * 4096 - 1 of its group starts at slot max(0, t * 1024 - 128 / 2) or later and at slot min(3968, (t + 1) * 1024 - 128 / 2) or earlier, and both ends are taken in every group.
All inputs are finite; a program needn't handle non-finite values.
Results may differ from a plain program's by a relative error of at most 0.007.
Values may be sent and summed in bfloat16 or wider, within the bound.
No kernel may reach another device: no remote copies, remote signals or barrier semaphores. Data moves between devices by JAX's collectives and lax.ppermute only.
A program may use at most 256 MiB of HBM per device.

v0:
```python
import jax
import jax.numpy as jnp
from jax import lax
from jax.sharding import PartitionSpec as P

PRECISE = lax.Precision.HIGHEST
EPSILON = 1e-05
ROOT_HALF = 0.7071067811865476


def padded_2(shard, sides, width):
    for axis, dim in sides:
        devices, length = (lax.axis_size(axis), shard.shape[dim])
        up = [(i, (i + 1) % devices) for i in range(devices - 1)]
        down = [(j, i) for i, j in up]
        last = lax.slice_in_dim(shard, length - width, length, axis=dim)
        initial = lax.slice_in_dim(shard, 0, width, axis=dim)
        before = lax.ppermute(last, axis, up)
        after = lax.ppermute(initial, axis, down)
        shard = jnp.concatenate([before, shard, after], axis=dim)
    return shard


def smooth_act(values):
    return values * jax.nn.sigmoid(values)


def smooth_slope(values):
    logistic = jax.nn.sigmoid(values)
    return logistic * (1.0 + values * (1.0 - logistic))


def owner_of(lengths, positions):
    ends_at = jnp.cumsum(lengths)
    starts = ends_at - lengths
    inside = (positions[:, None] >= starts[None, :]) & (positions[:, None] < ends_at[None, :])
    labels = jnp.arange(1, lengths.shape[0] + 1, dtype=jnp.int32)
    return jnp.sum(jnp.where(inside, labels[None, :], 0), axis=1)


def moments(first_term, second_term):
    return lax.psum((first_term, second_term), "tm")


def edge_pad(values):
    return padded_2(values, (("tm", 0),), 1)


def tap_stack(padded, left_mask, right_mask):
    return jnp.concatenate(
        [padded[:-2] * left_mask[:, None], padded[1:-1], padded[2:] * right_mask[:, None]], axis=1
    )


def tap_gradient(padded, left_mask, right_mask, weight):
    channels = weight.shape[1]
    stacked = jnp.stack(
        [padded[2:] * right_mask[:, None], padded[1:-1], padded[:-2] * left_mask[:, None]], axis=1
    )
    return jnp.einsum(
        "fkd,kcd->fc",
        stacked,
        weight.reshape(3, channels, channels),
        preferred_element_type=jnp.float32,
    )


def norm_forward(values, member, inv_count, style_rows, affine_weight, affine_bias):
    totals, square = moments(
        jnp.dot(member.T, values, precision=PRECISE),
        jnp.dot(member.T, values * values, precision=PRECISE),
    )
    average = totals * inv_count[:, None]
    inv_std = lax.rsqrt(square * inv_count[:, None] - average * average + EPSILON)
    params = jnp.dot(
        style_rows, affine_weight, preferred_element_type=jnp.float32
    ) + affine_bias.astype(jnp.float32)
    channels = values.shape[1]
    scale_rows = jnp.dot(member, 1.0 + params[:, :channels], precision=PRECISE)
    shift_rows = jnp.dot(member, params[:, channels:], precision=PRECISE)
    inv_rows = jnp.dot(member, inv_std, precision=PRECISE)
    normed = (values - jnp.dot(member, average, precision=PRECISE)) * inv_rows
    return (scale_rows * normed + shift_rows, normed, scale_rows, inv_rows)


def norm_backward(gradient, normed, scale_rows, inv_rows, member, inv_count):
    sum_grad, sum_cross = moments(
        jnp.dot(member.T, gradient, precision=PRECISE),
        jnp.dot(member.T, gradient * normed, precision=PRECISE),
    )
    back_grad = jnp.dot(member, sum_grad * inv_count[:, None], precision=PRECISE)
    back_cross = jnp.dot(member, sum_cross * inv_count[:, None], precision=PRECISE)
    inward = inv_rows * scale_rows * (gradient - back_grad - normed * back_cross)
    return (inward, jnp.concatenate([sum_cross, sum_grad], axis=1))


def on_device(
    phonemes,
    send_order,
    phoneme_counts,
    frame_lengths,
    tile_offsets,
    alignment,
    style_vec,
    first_affine_weight,
    first_affine_bias,
    first_conv_weight,
    second_affine_weight,
    second_affine_bias,
    second_conv_weight,
    second_conv_bias,
    cotangent,
):
    frames, channels = cotangent.shape
    slot_count = phonemes.shape[0]
    groups = lax.axis_size("seq")
    copies = lax.axis_size("tm")
    tm_index = lax.axis_index("tm")
    block_rows = slot_count // groups
    piece_rows = block_rows // copies
    window = alignment.shape[1]
    send_rows = send_order[0]
    lengths = frame_lengths[0]
    counts = phoneme_counts[0]
    outgoing = jnp.take(phonemes, send_rows, axis=0).reshape(groups, copies, piece_rows, channels)
    buffer = lax.all_to_all(outgoing, "seq", split_axis=0, concat_axis=2, tiled=True).reshape(
        slot_count, channels
    )
    positions = tm_index * frames + jnp.arange(frames, dtype=jnp.int32)
    labels = jnp.arange(1, lengths.shape[0] + 1, dtype=jnp.int32)
    frame_owner = owner_of(lengths, positions)
    member = (frame_owner[:, None] == labels[None, :]).astype(jnp.float32)
    valid_rows = (frame_owner > 0).astype(jnp.float32)
    left_mask = ((owner_of(lengths, positions - 1) == frame_owner) & (frame_owner > 0)).astype(
        jnp.bfloat16
    )
    right_mask = ((owner_of(lengths, positions + 1) == frame_owner) & (frame_owner > 0)).astype(
        jnp.bfloat16
    )
    inv_count = 1.0 / lengths.astype(jnp.float32)
    buffer_rows = buffer.shape[0]
    slot_owner = owner_of(counts, jnp.arange(buffer_rows, dtype=jnp.int32))
    tile_count = tile_offsets.shape[0]
    tile_rows = frames // tile_count
    window_rows = tile_offsets[:, None] + jnp.arange(window, dtype=jnp.int32)[None, :]
    gathered = jnp.take(buffer, window_rows.reshape(-1), axis=0).reshape(
        tile_count, window, channels
    )
    tile_owner = frame_owner.reshape(tile_count, tile_rows)
    matches = (tile_owner[:, :, None] == jnp.take(slot_owner, window_rows, axis=0)[:, None, :]) & (
        tile_owner[:, :, None] > 0
    )
    masked = jnp.where(
        matches, alignment.reshape(tile_count, tile_rows, window), jnp.zeros((), jnp.bfloat16)
    )
    upsampled = jnp.einsum(
        "tfw,twc->tfc", masked, gathered, preferred_element_type=jnp.float32
    ).reshape(frames, channels)
    normed_one_out, normed_one, scale_one, inv_one = norm_forward(
        upsampled, member, inv_count, style_vec, first_affine_weight, first_affine_bias
    )
    act_one = smooth_act(normed_one_out).astype(jnp.bfloat16)
    stack_one = tap_stack(edge_pad(act_one), left_mask, right_mask)
    middle = valid_rows[:, None] * jnp.dot(
        stack_one, first_conv_weight, preferred_element_type=jnp.float32
    )
    normed_two_out, normed_two, scale_two, inv_two = norm_forward(
        middle, member, inv_count, style_vec, second_affine_weight, second_affine_bias
    )
    act_two = smooth_act(normed_two_out).astype(jnp.bfloat16)
    stack_two = tap_stack(edge_pad(act_two), left_mask, right_mask)
    branch = valid_rows[:, None] * (
        jnp.dot(stack_two, second_conv_weight, preferred_element_type=jnp.float32)
        + second_conv_bias.astype(jnp.float32)
    )
    frames_out = (valid_rows[:, None] * (upsampled + branch) * ROOT_HALF).astype(jnp.bfloat16)
    lead_mask = (tm_index == 0).astype(jnp.float32)
    style_float = style_vec.astype(jnp.float32)
    grad_out = valid_rows[:, None] * cotangent.astype(jnp.float32) * ROOT_HALF
    grad_branch = grad_out.astype(jnp.bfloat16)
    second_conv_grad = jnp.einsum(
        "fk,fc->kc", stack_two, grad_branch, preferred_element_type=jnp.float32
    )
    second_bias_grad = jnp.sum(grad_branch, axis=0, dtype=jnp.float32)
    grad_act_two = tap_gradient(edge_pad(grad_branch), left_mask, right_mask, second_conv_weight)
    grad_middle_full, params_two_grad = norm_backward(
        grad_act_two * smooth_slope(normed_two_out),
        normed_two,
        scale_two,
        inv_two,
        member,
        inv_count,
    )
    second_affine_grad = jnp.dot(style_float.T, params_two_grad, precision=PRECISE) * lead_mask
    second_shift_grad = jnp.sum(params_two_grad, axis=0) * lead_mask
    grad_middle = grad_middle_full.astype(jnp.bfloat16)
    first_conv_grad = jnp.einsum(
        "fk,fc->kc", stack_one, grad_middle, preferred_element_type=jnp.float32
    )
    grad_act_one = tap_gradient(edge_pad(grad_middle), left_mask, right_mask, first_conv_weight)
    grad_input_norm, params_one_grad = norm_backward(
        grad_act_one * smooth_slope(normed_one_out),
        normed_one,
        scale_one,
        inv_one,
        member,
        inv_count,
    )
    first_affine_grad = jnp.dot(style_float.T, params_one_grad, precision=PRECISE) * lead_mask
    first_shift_grad = jnp.sum(params_one_grad, axis=0) * lead_mask
    style_grad = jnp.dot(
        params_one_grad, first_affine_weight.astype(jnp.float32).T, precision=PRECISE
    ) + jnp.dot(params_two_grad, second_affine_weight.astype(jnp.float32).T, precision=PRECISE)
    grad_input = (grad_out + grad_input_norm).astype(jnp.bfloat16)
    grad_window = jnp.einsum(
        "tfw,tfc->twc",
        masked,
        grad_input.reshape(tile_count, tile_rows, channels),
        preferred_element_type=jnp.float32,
    )
    grad_buffer = (
        jnp.zeros((buffer_rows, channels), jnp.float32)
        .at[window_rows.reshape(-1)]
        .add(grad_window.reshape(-1, channels))
    )
    returned = lax.all_to_all(
        grad_buffer.reshape(1, copies, groups * piece_rows, channels),
        "seq",
        split_axis=2,
        concat_axis=0,
        tiled=True,
    ).reshape(slot_count, channels)
    row_grads = jnp.zeros_like(returned).at[send_rows].set(returned)
    phonemes_grad = lax.psum(row_grads, "tm")
    summed = lax.psum(
        (
            first_affine_grad,
            first_shift_grad,
            first_conv_grad,
            second_affine_grad,
            second_shift_grad,
            second_conv_grad,
            second_bias_grad,
        ),
        ("seq", "tm"),
    )
    return (
        frames_out,
        phonemes_grad,
        style_grad,
        summed[0],
        summed[1],
        summed[2],
        summed[3],
        summed[4],
        summed[5],
        summed[6],
    )


def solution(mesh):
    in_specs = (
        P("seq", None),
        P("seq", None),
        P("seq", None),
        P("seq", None),
        P(("seq", "tm")),
        P(("seq", "tm"), None),
        P("seq", None),
        P(),
        P(),
        P(),
        P(),
        P(),
        P(),
        P(),
        P(("seq", "tm"), None),
    )
    out_specs = (
        P(("seq", "tm"), None),
        P("seq", None),
        P("seq", None),
        P(),
        P(),
        P(),
        P(),
        P(),
        P(),
        P(),
    )
    return jax.shard_map(
        on_device, mesh=mesh, in_specs=in_specs, out_specs=out_specs, check_vma=False
    )
```

profile of v0, /device:TPU:0, one launch (start us, length us, event | category | flops | bytes accessed | tf_op | source)
XLA Modules:
  0.0 1014.3 jit_solution(8720104709894923069)
XLA Ops:
  8.8 20.2 %gather_fusion.1 = bf16[4096,512]{1,0:T(8,128)(2,1)} fusion(bf16[4096,512]{1,0:T(8,128)(2,1)} %param.17, s32[4096]{0:T(1024)S(1)} %fusion.130), kind=kCustom, calls=%fused_computation.clone | custom fusion | bytes 8404992 | tf_op jit(solution)/shard_map/jit(_take)/gather | solution.py:125
  53.6 23.0 %gather_fusion = s32[4096]{0:T(1024)S(1)} fusion(s32[4096]{0:T(1024)S(1)} %get-tuple-element.64, s32[4096]{0:T(1024)S(1)} %get-tuple-element.107), kind=kCustom, calls=%fused_computation.2 | custom fusion | bytes 49152 | tf_op jit(solution)/shard_map/jit(_take)/gather | solution.py:150
  92.1 20.2 %gather_fusion.2 = bf16[4096,512]{1,0:T(8,128)(2,1)} fusion(bf16[4096,512]{1,0:T(8,128)(2,1)} %bitcast.97, s32[4096]{0:T(1024)S(1)} %get-tuple-element.108), kind=kCustom, calls=%fused_computation.1.clone | custom fusion | bytes 8404992 | tf_op jit(solution)/shard_map/jit(_take)/gather | solution.py:146
  124.1 20.4 %all-reduce.5 = (f32[4,512]{1,0:T(4,128)S(1)}, f32[4,512]{1,0:T(4,128)S(1)}) all-reduce(f32[4,512]{1,0:T(4,128)S(1)} %fusion.19, f32[4,512]{1,0:T(4,128)S(1)} %fusion.78), channel_id=1, replica_groups=mesh['seq'=8,'tm'=4] {'tm'}, use_global_device_ids=true, to_apply=%region_5.7 | all-reduce | flops 4096 | bytes 32768 | tf_op jit(solution)/shard_map/psum | solution.py:42
  152.2 13.1 %multiply_convert_fusion.3 = (bf16[4096,512]{1,0:T(8,128)(2,1)S(1)}, f32[4096,512]{1,0:T(8,128)}) fusion(f32[4,1024]{1,0:T(4,128)S(1)} %convolution_add_fusion, s32[4096]{0:T(1024)S(1)} %get-tuple-element.63, s32[4]{0:T(128)S(1)} %iota_add_fusion.2, f32[4096,512]{1,0:T(8,128)} %fusion.80, f32[4096,512]{1,0:T(8,128)S(1)} %subtract_multiply_fusion.1), kind=kOutput, calls=%fused_computation.37 | convolution fusion | flops 115359744 | bytes 29385216 | tf_op jit(solution)/shard_map/dot_general | solution.py:80
  176.0 19.4 %fusion.42 = (bf16[4096,512]{1,0:T(8,128)(2,1)}, bf16[4096,512]{1,0:T(8,128)(2,1)}, bf16[4096,1,512]{2,0,1:T(8,128)(2,1)}, bf16[4096,1,512]{2,0,1:T(8,128)(2,1)}) fusion(bf16[4096,512]{1,0:T(8,128)(2,1)} %copy-done.17, bf16[1,512]{1,0:T(2,128)(2,1)S(1)} %collective-permute-done, bf16[4096]{0:T(1024)(128)(2,1)S(1)} %get-tuple-element.104, ...), kind=kLoop, calls=%fused_computation.68 | loop fusion | flops 46137344 | bytes 25186304 | tf_op jit(solution)/shard_map/mul | solution.py:51
  195.3 9.5 fusion.30
  211.4 18.8 %all-reduce.4 = (f32[4,512]{1,0:T(4,128)S(1)}, f32[4,512]{1,0:T(4,128)S(1)}) all-reduce(f32[4,512]{1,0:T(4,128)S(1)} %fusion.17, f32[4,512]{1,0:T(4,128)S(1)} %fusion.22), channel_id=1, replica_groups=mesh['seq'=8,'tm'=4] {'tm'}, use_global_device_ids=true, to_apply=%region_9.11 | all-reduce | flops 4096 | bytes 32768 | tf_op jit(solution)/shard_map/psum | solution.py:42
  237.0 8.0 subtract_multiply_fusion
  245.1 13.8 %multiply_convert_fusion.2 = (bf16[4096,512]{1,0:T(8,128)(2,1)}, f32[4096,512]{1,0:T(8,128)}) fusion(f32[4,1024]{1,0:T(4,128)S(1)} %convolution_add_fusion.1, s32[4096]{0:T(1024)S(1)} %get-tuple-element.63, s32[4]{0:T(128)S(1)} %iota_add_fusion.2, f32[4096,512]{1,0:T(8,128)} %fusion.82, f32[4096,512]{1,0:T(8,128)S(1)} %subtract_multiply_fusion), kind=kOutput, calls=%fused_computation.31 | convolution fusion | flops 115359744 | bytes 29385216 | tf_op jit(solution)/shard_map/dot_general | solution.py:80
  258.8 27.2 %bitcast_multiply_fusion.1 = f32[4096,512]{1,0:T(8,128)} fusion(f32[4096,512]{1,0:T(8,128)} %get-tuple-element.112, bf16[3,512,512]{2,1,0:T(8,128)(2,1)} %bitcast.123, bf16[4096,1,512]{2,0,1:T(8,128)(2,1)} %get-tuple-element.98, bf16[4096,1,512]{2,0,1:T(8,128)(2,1)S(1)} %bitcast.105, bf16[4096,1,512]{2,0,1:T(8,128)(2,1)} %get-tuple-element.99), kind=kOutput, calls=%fused_computation.20 | convolution fusion | flops 6471811072 | bytes 30932992 | tf_op jit(solution)/shard_map/fkd,kcd->fc/dot_general | solution.py:60
  286.0 6.7 fusion.14
  295.5 15.6 %all-reduce.3 = (f32[4,512]{1,0:T(4,128)S(1)}, f32[4,512]{1,0:T(4,128)S(1)}) all-reduce(f32[4,512]{1,0:T(4,128)S(1)} %fusion.65, f32[4,512]{1,0:T(4,128)S(1)} %fusion.14), channel_id=1, replica_groups=mesh['seq'=8,'tm'=4] {'tm'}, use_global_device_ids=true, to_apply=%region_10.12 | all-reduce | flops 4096 | bytes 32768 | tf_op jit(solution)/shard_map/psum | solution.py:42
  316.9 15.8 %multiply_convert_fusion = bf16[4096,512]{1,0:T(8,128)(2,1)S(1)} fusion(f32[4096,512]{1,0:T(8,128)} %copy-done.6, f32[4096,512]{1,0:T(8,128)} %bitcast_multiply_fusion.1, f32[4096,512]{1,0:T(8,128)} %fusion.63, f32[4096,512]{1,0:T(8,128)} %copy-done.4, f32[4096,512]{1,0:T(8,128)} %fusion.82, s32[4096]{0:T(1024)S(1)} %get-tuple-element.63, ...), kind=kOutput, calls=%fused_computation.25 | convolution fusion | flops 113264640 | bytes 46161952 | tf_op jit(solution)/shard_map/dot_general | solution.py:92
  346.7 14.1 %fusion.40 = (bf16[4096,512]{1,0:T(8,128)(2,1)}, bf16[4096,512]{1,0:T(8,128)(2,1)}, bf16[4096,1,512]{2,0,1:T(8,128)(2,1)}, bf16[4096,1,512]{2,0,1:T(8,128)(2,1)}) fusion(bf16[4096,512]{1,0:T(8,128)(2,1)} %get-tuple-element.111, bf16[1,512]{1,0:T(2,128)(2,1)S(1)} %collective-permute-done.2, bf16[4096]{0:T(1024)(128)(2,1)S(1)} %get-tuple-element.104, ...), kind=kLoop, calls=%fused_computation.64 | loop fusion | flops 46137344 | bytes 25186304 | tf_op jit(solution)/shard_map/mul | solution.py:51
  360.9 12.0 %bitcast_multiply_fusion = f32[4096,512]{1,0:T(8,128)S(1)} fusion(f32[4096,512]{1,0:T(8,128)} %get-tuple-element.110, bf16[3,512,512]{2,1,0:T(8,128)(2,1)S(1)} %bitcast.96, bf16[4096,1,512]{2,0,1:T(8,128)(2,1)} %get-tuple-element.100, bf16[4096,1,512]{2,0,1:T(8,128)(2,1)S(1)} %bitcast.104, bf16[4096,1,512]{2,0,1:T(8,128)(2,1)} %get-tuple-element.101), kind=kOutput, calls=%fused_computation.19 | convolution fusion | flops 6471811072 | bytes 30932992 | tf_op jit(solution)/shard_map/fkd,kcd->fc/dot_general | solution.py:60
  372.9 9.6 fusion.12
  385.3 15.8 %all-reduce.2 = (f32[4,512]{1,0:T(4,128)S(1)}, f32[4,512]{1,0:T(4,128)S(1)}) all-reduce(f32[4,512]{1,0:T(4,128)S(1)} %fusion.59, f32[4,512]{1,0:T(4,128)S(1)} %fusion.12), channel_id=1, replica_groups=mesh['seq'=8,'tm'=4] {'tm'}, use_global_device_ids=true, to_apply=%region_12.14 | all-reduce | flops 4096 | bytes 32768 | tf_op jit(solution)/shard_map/psum | solution.py:42
  407.0 19.8 %add_convert_fusion = bf16[4096,512]{1,0:T(8,128)(2,1)} fusion(f32[4096,512]{1,0:T(8,128)} %copy-done.10, f32[4096,512]{1,0:T(8,128)} %copy-done.9, f32[4096,512]{1,0:T(8,128)} %fusion.57, f32[4096,512]{1,0:T(8,128)} %copy-done.5, f32[4096,512]{1,0:T(8,128)} %fusion.80, bf16[4096,512]{1,0:T(8,128)(2,1)} %param.31, f32[4096]{0:T(1024)S(1)} %get-tuple-element.102, ...), kind=kOutput, calls=%fused_computation.22 | convolution fusion | flops 121653248 | bytes 50372640 | tf_op jit(solution)/shard_map/dot_general | solution.py:92
  426.8 6.2 fusion.51
  433.1 29.1 %scatter_custom_fusion = f32[4096,512]{1,0:T(8,128)} fusion(s32[4096]{0:T(1024)} %bitcast.117, f32[4096,512]{1,0:T(8,128)} %bitcast.111, f32[]{:T(128)} %constant.35.clone.1), kind=kCustom, calls=%fused_computation.71 | custom fusion | flops 2097152 | bytes 8389120 | tf_op jit(solution)/shard_map/scatter-add | solution.py:224
  462.2 12.0 %copy.52 = f32[1,4,1024,512]{3,1,0,2:T(4,128)} copy(f32[1,4,1024,512]{3,2,1,0:T(8,128)} %bitcast.102) | data formatting | bytes 16777216 | tf_op jit(solution)/shard_map/reshape | solution.py:227
  479.6 14.4 %fusion.29 = f32[1536,512]{1,0:T(8,128)} fusion(bf16[4096,512]{1,0:T(8,128)(2,1)} %copy-done.11, bf16[4096,512]{1,0:T(8,128)(2,1)} %get-tuple-element.95, bf16[4096,512]{1,0:T(8,128)(2,1)} %copy-done.17, bf16[4096,512]{1,0:T(8,128)(2,1)} %get-tuple-element.94), kind=kOutput, calls=%fused_computation.47 | convolution fusion | flops 6480199680 | bytes 19922944 | tf_op jit(solution)/shard_map/fk,fc->kc/dot_general | solution.py:197
  495.4 11.0 %fusion.28 = f32[1536,512]{1,0:T(8,128)} fusion(bf16[4096,512]{1,0:T(8,128)(2,1)S(1)} %copy-done.14, bf16[4096,512]{1,0:T(8,128)(2,1)} %get-tuple-element.91, bf16[4096,512]{1,0:T(8,128)(2,1)} %get-tuple-element.111, bf16[4096,512]{1,0:T(8,128)(2,1)} %get-tuple-element.90), kind=kOutput, calls=%fused_computation.46 | convolution fusion | flops 6480199680 | bytes 19922944 | tf_op jit(solution)/shard_map/fk,fc->kc/dot_general | solution.py:181
  507.0 86.1 %all-to-all-done.1 = f32[1,4,1024,512]{3,1,0,2:T(4,128)} async-done(((f32[1,4,1024,512]{3,1,0,2:T(4,128)}), f32[1,4,1024,512]{3,1,0,2:T(4,128)}, u32[]{:S(2)}, u32[]{:S(2)}) %all-to-all-start.1) | async-done | bytes 8388640 | tf_op jit(solution)/shard_map/all_to_all | solution.py:226
  593.0 6.2 copy.53
  603.5 21.8 %scatter_custom_fusion.1 = f32[4096,512]{1,0:T(8,128)} fusion(s32[4096]{0:T(1024)S(1)} %bitcast.118, f32[4096,512]{1,0:T(8,128)} %bitcast.112, f32[]{:T(128)} %constant.35.clone.1), kind=kCustom, calls=%fused_computation.69 | custom fusion | bytes 8389120 | tf_op jit(solution)/shard_map/scatter | solution.py:233
  625.4 37.7 %all-reduce = (f32[1024]{0:T(1024)}, f32[1024]{0:T(1024)}, f32[512]{0:T(512)}) all-reduce(f32[1024]{0:T(1024)S(1)} %broadcast_multiply_fusion.1, f32[1024]{0:T(1024)S(1)} %broadcast_multiply_fusion, f32[512]{0:T(512)S(1)} %copy-done.31), channel_id=1, replica_groups=mesh['seq'=8,'tm'=4] {'seq','tm'}, use_global_device_ids=true, to_apply=%region_19.21 | all-reduce | flops 2560 | bytes 20480 | tf_op jit(solution)/shard_map/psum | solution.py:235
  664.4 14.4 %multiply_convert_fusion.1 = bf16[4096,512]{1,0:T(8,128)(2,1)} fusion(f32[4096,512]{1,0:T(8,128)} %bitcast.100, bf16[1536,512]{1,0:T(8,128)(2,1)} %param.29, bf16[4096,512]{1,0:T(8,128)(2,1)} %get-tuple-element.91, bf16[4096,512]{1,0:T(8,128)(2,1)} %get-tuple-element.111, bf16[4096,512]{1,0:T(8,128)(2,1)} %get-tuple-element.90, ...), kind=kOutput, calls=%fused_computation.30 | convolution fusion | flops 6492782592 | bytes 26757120 | tf_op jit(solution)/shard_map/dot_general | solution.py:173
  678.7 23.8 %all-reduce.11.cloned.1.call-done = (f32[128,1024]{0,1:T(8,128)}, f32[1536,512]{1,0:T(8,128)}, f32[128,1024]{0,1:T(8,128)}, f32[1536,512]{1,0:T(8,128)}) async-done(((f32[128,1024]{0,1:T(8,128)}, f32[1536,512]{1,0:T(8,128)}, f32[128,1024]{0,1:T(8,128)}, f32[1536,512]{1,0:T(8,128)}), (f32[128,1024]{0,1:T(8,128)}, f32[1536,512]{1,0:T(8,128)}, f32[128,1024]{0,1:T(8,128)}, ...) | async-done | bytes 7340048 | tf_op jit(solution)/shard_map/psum | solution.py:235
  706.6 289.3 %all-reduce.9.cloned.1.call-done = f32[4096,512]{1,0:T(8,128)} async-done(((f32[4096,512]{1,0:T(8,128)}), f32[4096,512]{1,0:T(8,128)}) %all-reduce.9.cloned.1.call-update) | async-done | bytes 8388624 | tf_op jit(solution)/shard_map/psum | solution.py:234
  996.0 8.0 copy.65
  (161 shorter events, 136.6 us)
Async XLA Ops:
  7.2 188.2 %copy-start = (bf16[1536,512]{1,0:T(8,128)(2,1)S(1)}, bf16[1536,512]{1,0:T(8,128)(2,1)}, u32[]{:S(2)}) copy-start(bf16[1536,512]{1,0:T(8,128)(2,1)} %param.26) | copy-start | bytes 4718596
  32.9 20.5 %copy-start.33 = (bf16[1024]{0:T(1024)(128)(2,1)S(1)}, bf16[1024]{0:T(1024)(128)(2,1)}, u32[]{:S(2)}) copy-start(bf16[1024]{0:T(1024)(128)(2,1)} %param.25) | copy-start | bytes 6148
  32.9 20.5 %copy-start.34 = (bf16[1024]{0:T(1024)(128)(2,1)S(1)}, bf16[1024]{0:T(1024)(128)(2,1)}, u32[]{:S(2)}) copy-start(bf16[1024]{0:T(1024)(128)(2,1)} %param.28) | copy-start | bytes 6148
  32.9 20.5 %copy-start.32 = (s32[32]{0:T(128)S(1)}, s32[32]{0:T(128)}, u32[]{:S(2)}) copy-start(s32[32]{0:T(128)} %param.21) | copy-start | bytes 388
  32.9 54.5 %all-to-all-start = ((bf16[8,4,128,512]{3,2,1,0:T(8,128)(2,1)}), bf16[8,4,128,512]{3,2,1,0:T(8,128)(2,1)}, u32[]{:S(2)}, u32[]{:S(2)}) async-start(bf16[8,4,128,512]{3,2,1,0:T(8,128)(2,1)} %bitcast.108), calls=%async_computation | async-start | bytes 8388608 | tf_op jit(solution)/shard_map/all_to_all | solution.py:126
  44.5 131.4 %collective-permute-start.4 = (bf16[1,512]{1,0:T(2,128)(2,1)S(1)}, bf16[1,512]{1,0:T(2,128)(2,1)S(1)}, u32[]{:S(2)}, u32[]{:S(2)}) collective-permute-start(bf16[1,512]{1,0:T(2,128)(2,1)S(1)} %get-tuple-element.88), channel_id=1, source_target_pairs={{1,0},{2,1},{3,2},{5,4},{6,5},{7,6},{9,8},{10,9},{11,10},{13,12},{... | collective-permute-start | bytes 3080 | tf_op jit(solution)/shard_map/ppermute | solution.py:19
  45.8 130.1 %collective-permute-start.5 = (bf16[1,512]{1,0:T(2,128)(2,1)S(1)}, bf16[1,512]{1,0:T(2,128)(2,1)S(1)}, u32[]{:S(2)}, u32[]{:S(2)}) collective-permute-start(bf16[1,512]{1,0:T(2,128)(2,1)S(1)} %get-tuple-element.89), channel_id=1, source_target_pairs={{0,1},{1,2},{2,3},{4,5},{5,6},{6,7},{8,9},{9,10},{10,11},{12,13},{... | collective-permute-start | bytes 3080 | tf_op jit(solution)/shard_map/ppermute | solution.py:18
  53.5 23.3 %copy-start.20 = (bf16[128,1024]{1,0:T(8,128)(2,1)S(1)}, bf16[128,1024]{1,0:T(8,128)(2,1)}, u32[]{:S(2)}) copy-start(bf16[128,1024]{1,0:T(8,128)(2,1)} %param.24) | copy-start | bytes 786436
  53.5 23.3 %copy-start.29 = (bf16[4,128]{1,0:T(4,128)(2,1)S(1)}, bf16[4,128]{1,0:T(4,128)(2,1)}, u32[]{:S(2)}) copy-start(bf16[4,128]{1,0:T(4,128)(2,1)} %param.23) | copy-start | bytes 3076
  53.5 23.4 %copy-start.22 = (bf16[128,1024]{1,0:T(8,128)(2,1)S(1)}, bf16[128,1024]{1,0:T(8,128)(2,1)}, u32[]{:S(2)}) copy-start(bf16[128,1024]{1,0:T(8,128)(2,1)} %param.27) | copy-start | bytes 786436
  76.7 38.2 %copy-start.27 = (pred[32,128]{1,0:T(8,128)(4,1)}, pred[32,128]{1,0:T(8,128)(4,1)S(1)}, u32[]{:S(2)}) copy-start(pred[32,128]{1,0:T(8,128)(4,1)S(1)} %broadcast_compare_fusion) | copy-start | bytes 12292
  76.8 38.1 %copy-start.24 = (s32[32,128]{1,0:T(8,128)}, s32[32,128]{1,0:T(8,128)S(1)}, u32[]{:S(2)}) copy-start(s32[32,128]{1,0:T(8,128)S(1)} %get-tuple-element.106) | copy-start | bytes 49156
  167.3 8.6 collective-permute-start
  168.6 7.3 collective-permute-start.1
  245.0 41.0 %copy-start.6 = (f32[4096,512]{1,0:T(8,128)}, f32[4096,512]{1,0:T(8,128)S(1)}, u32[]{:S(2)}) copy-start(f32[4096,512]{1,0:T(8,128)S(1)} %subtract_multiply_fusion) | copy-start | bytes 25165828
  316.9 25.6 %copy-start.30 = (bf16[4,128]{1,0:T(4,128)(2,1)S(1)}, bf16[4,128]{1,0:T(4,128)(2,1)}, u32[]{:S(2)}) copy-start(bf16[4,128]{1,0:T(4,128)(2,1)} %param.23) | copy-start | bytes 3076
  332.7 28.1 %copy-start.11 = (bf16[4096,512]{1,0:T(8,128)(2,1)}, bf16[4096,512]{1,0:T(8,128)(2,1)S(1)}, u32[]{:S(2)}) copy-start(bf16[4096,512]{1,0:T(8,128)(2,1)S(1)} %multiply_convert_fusion) | copy-start | bytes 12582916
  332.7 11.2 %collective-permute-start.6 = (bf16[1,512]{1,0:T(2,128)(2,1)S(1)}, bf16[1,512]{1,0:T(2,128)(2,1)S(1)}, u32[]{:S(2)}, u32[]{:S(2)}) collective-permute-start(bf16[1,512]{1,0:T(2,128)(2,1)S(1)} %get-tuple-element.84), channel_id=1, source_target_pairs={{1,0},{2,1},{3,2},{5,4},{6,5},{7,6},{9,8},{10,9},{11,10},{13,12},{... | collective-permute-start | bytes 3080 | tf_op jit(solution)/shard_map/ppermute | solution.py:19
  334.0 9.9 collective-permute-start.7
  339.3 4.7 collective-permute-start.2
  341.3 5.5 collective-permute-start.3
  407.0 19.8 %copy-start.16 = (bf16[32,128,128]{1,2,0:T(8,128)(2,1)S(1)}, bf16[32,128,128]{1,2,0:T(8,128)(2,1)}, u32[]{:S(2)}) copy-start(bf16[32,128,128]{1,2,0:T(8,128)(2,1)} %copy.49) | copy-start | bytes 3145732
  407.0 19.8 %copy-start.25 = (s32[32,128]{1,0:T(8,128)S(1)}, s32[32,128]{1,0:T(8,128)}, u32[]{:S(2)}) copy-start(s32[32,128]{1,0:T(8,128)} %copy-done.24) | copy-start | bytes 49156
  407.0 19.8 %copy-start.28 = (pred[32,128]{1,0:T(8,128)(4,1)S(1)}, pred[32,128]{1,0:T(8,128)(4,1)}, u32[]{:S(2)}) copy-start(pred[32,128]{1,0:T(8,128)(4,1)} %copy-done.27) | copy-start | bytes 12292
  474.2 118.8 %all-to-all-start.1 = ((f32[1,4,1024,512]{3,1,0,2:T(4,128)}), f32[1,4,1024,512]{3,1,0,2:T(4,128)}, u32[]{:S(2)}, u32[]{:S(2)}) async-start(f32[1,4,1024,512]{3,1,0,2:T(4,128)} %copy.52), calls=%async_computation.1 | async-start | bytes 16777216 | tf_op jit(solution)/shard_map/all_to_all | solution.py:226
  479.2 223.3 %all-reduce.11.cloned.1.call-start = ((), (), s32[]{:S(2)}) async-start(), calls=%async_computation.3 | async-start | bytes 14680064 | tf_op jit(solution)/shard_map/psum | solution.py:235
  479.6 15.8 %copy-start.14 = (bf16[4096,512]{1,0:T(8,128)(2,1)S(1)}, bf16[4096,512]{1,0:T(8,128)(2,1)}, u32[]{:S(2)}) copy-start(bf16[4096,512]{1,0:T(8,128)(2,1)} %copy-done.12) | copy-start | bytes 12582916
  506.4 489.6 %all-reduce.9.cloned.1.call-start = ((), (), s32[]{:S(2)}) async-start(), calls=%async_computation.2 | async-start | bytes 16777216 | tf_op jit(solution)/shard_map/psum | solution.py:234
  603.5 21.8 %copy-start.35 = (bf16[512]{0:T(512)(128)(2,1)S(1)}, bf16[512]{0:T(512)(128)(2,1)}, u32[]{:S(2)}) copy-start(bf16[512]{0:T(512)(128)(2,1)} %param.30) | copy-start | bytes 3076
  603.5 21.9 %copy-start.31 = (f32[512]{0:T(512)S(1)}, f32[512]{0:T(512)}, u32[]{:S(2)}) copy-start(f32[512]{0:T(512)} %get-tuple-element.80) | copy-start | bytes 6148
  603.5 59.6 %copy-start.21 = (bf16[128,1024]{1,0:T(8,128)(2,1)S(1)}, bf16[128,1024]{1,0:T(8,128)(2,1)}, u32[]{:S(2)}) copy-start(bf16[128,1024]{1,0:T(8,128)(2,1)} %param.24) | copy-start | bytes 786436
  603.5 59.9 %copy-start.23 = (bf16[128,1024]{1,0:T(8,128)(2,1)S(1)}, bf16[128,1024]{1,0:T(8,128)(2,1)}, u32[]{:S(2)}) copy-start(bf16[128,1024]{1,0:T(8,128)(2,1)} %param.27) | copy-start | bytes 786436
  (18 other events, 126.7 us)
Sparse Core Ops, SparseCore 0:
  506.5 195.9 all-reduce.10
  705.0 290.8 all-reduce.8
where the time goes:
time: 1010 us
  waiting for transfers between devices  406 us (40%)
  matrix products  241 us (24%)
  local copies, waits for them, and re-layouts  139 us (14%)
  blocking collectives  108 us (11%)
  other arithmetic  76 us (8%)
  starting transfers between devices  29.6 us (3%)
  between operations  14.8 us (1%)
    psum x1, waiting for transfers between devices, on_device(): phonemes_grad = lax.psum(row_grads, 'tm')  289 us
    all_to_all x1, waiting for transfers between devices, on_device(): lax.all_to_all(grad_buffer.reshape(1, copies, groups * piece_rows, channe...  86.1 us
    psum x4, blocking collectives, moments(): return lax.psum((first_term, second_term), 'tm')  70.6 us
    dot_general x2, matrix products, tap_gradient(): jnp.einsum('fkd,kcd->fc', stacked, weight.reshape(3, channels, channels),...  39.2 us
    psum x1, blocking collectives, on_device(): lax.psum((first_affine_grad, first_shift_grad, first_conv_grad, second_af...  37.7 us
    dot_general x2, matrix products, norm_backward(): jnp.dot(member, sum_cross * inv_count[:, None], precision=PRECISE)  35.6 us
    mul x2, other arithmetic, tap_stack(): padded[:-2] * left_mask[:, None]  33.5 us
    scatter-add x1, other arithmetic, on_device(): grad_buffer = jnp.zeros((buffer_rows, channels), jnp.float32).at[window_r...  29.1 us
  transfers between devices with their start and end apart: 12, of which 5 were waited for; matrix products, arithmetic and copies ran while one was open for 18% of the time, Pallas kernels for 0%

commit v1 on v0

v1 whole, which is shorter than its diff:
```python
import functools

import jax
import jax.numpy as jnp
from jax import lax
from jax.experimental import pallas as pl
from jax.experimental.pallas import tpu as pltpu
from jax.sharding import PartitionSpec as P

EPSILON = 1e-05
ROOT_HALF = 0.7071067811865476
PRECISE = lax.Precision.HIGHEST
F32, BF16, I32 = jnp.float32, jnp.bfloat16, jnp.int32
UTTS = 4
PAD = 16
ROWS = 512
WIDE = 256
MIB = 2**20

STAT_ROWS = 24
FIRST_ROW, LAST_ROW, EXTRA_ROW = 16, 17, 18


def owner_at(ends, position):
    return sum((position >= end).astype(I32) for end in ends)


def rows_of(start, shape):
    return start + lax.broadcasted_iota(I32, shape, 0)


def fold_rows(values):
    return jnp.sum(values.reshape(values.shape[0] // 8, 8, values.shape[1]), axis=0)


def by_utterance(ends, start, count, uniform_body, mixed_body):
    low, high = owner_at(ends, start), owner_at(ends, start + count - 1)

    @pl.when(low == high)
    def _():
        uniform_body(low)

    @pl.when(low != high)
    def _():
        def step(u, carry):
            lower = jnp.int32(-1)
            upper = jnp.int32(2**30)
            for k in range(UTTS):
                lower = jnp.where(u == k + 1, ends[k], lower)
                upper = jnp.where(u == k, ends[k], upper)

            def mask(shape):
                rows = rows_of(start, shape)
                return (rows >= lower) & (rows < upper)

            mixed_body(u, mask)
            return carry

        lax.fori_loop(low, high + 1, step, 0)


def row(ref, index):
    return ref[pl.ds(index, 1), :]


def logistic(values):
    return 0.5 * jnp.tanh(0.5 * values) + 0.5


def build_taps(padded_ref, taps_ref, ends, tile_start, base, mirrored):
    rows, channels = taps_ref.shape[0], taps_ref.shape[1] // 3
    start = pl.multiple_of(tile_start, PAD)
    block = padded_ref[pl.ds(start, rows + 2 * PAD), :].astype(F32)
    before = block[PAD - 1 : PAD - 1 + rows]
    after = block[PAD + 1 : PAD + 1 + rows]
    left, right = (2, 0) if mirrored else (0, 2)
    taps_ref[:, channels : 2 * channels] = padded_ref[pl.ds(start + PAD, rows), :]
    first = base + tile_start
    same = owner_at(ends, first - 1) == owner_at(ends, first + rows)

    @pl.when(same)
    def _():
        taps_ref[:, left * channels : (left + 1) * channels] = before.astype(BF16)
        taps_ref[:, right * channels : (right + 1) * channels] = after.astype(BF16)

    @pl.when(jnp.logical_not(same))
    def _():
        positions = rows_of(first, (rows, channels))
        cut_left = positions == ends[0]
        cut_right = positions + 1 == ends[0]
        for end in ends[1:]:
            cut_left = cut_left | (positions == end)
            cut_right = cut_right | (positions + 1 == end)
        taps_ref[:, left * channels : (left + 1) * channels] = jnp.where(
            cut_left, 0.0, before
        ).astype(BF16)
        taps_ref[:, right * channels : (right + 1) * channels] = jnp.where(
            cut_right, 0.0, after
        ).astype(BF16)


def sum_over_tm(own_ref, other_refs, first, count):
    one, two, three = other_refs
    part = pl.ds(first, count)
    return (own_ref[part, :] + two[part, :]) + (one[part, :] + three[part, :])


def finish_stats(acc_ref, stat_ref):
    for kind in range(2):
        for u in range(8):
            at = kind * 8 + u
            if u < UTTS:
                first = (kind * (UTTS + 1) + u) * 8
                stat_ref[at : at + 1, :] = jnp.sum(
                    acc_ref[first : first + 8, :], axis=0, keepdims=True
                )
            else:
                stat_ref[at : at + 1, :] = jnp.zeros_like(stat_ref[at : at + 1, :])
    stat_ref[16:24, :] = jnp.zeros_like(stat_ref[16:24, :])


ACC_ROWS = 2 * (UTTS + 1) * 8


def add_stats(acc_ref, u, first, second):
    for kind, term in enumerate((first, second)):
        at = pl.ds(pl.multiple_of((kind * (UTTS + 1) + u) * 8, 8), 8)
        acc_ref[at, :] += fold_rows(term)


def read_ends(info_ref):
    return [info_ref[k] for k in range(UTTS)]


def halo_owner(info_ref, ends, base, frames):
    before = jnp.where(base == 0, UTTS, owner_at(ends, base - 1))
    return before, owner_at(ends, base + frames)


def gradient_kernel(
    info_ref, cot_ref, before_ref, after_ref, weight_ref, out_ref, padded_ref, bias_ref, taps_ref
):
    frames, channels = cot_ref.shape
    ends = read_ends(info_ref)
    base = info_ref[8]
    owner_before, owner_after = halo_owner(info_ref, ends, base, frames)
    zeros = jnp.zeros((PAD, channels), BF16)
    padded_ref[0:PAD, :] = zeros
    padded_ref[PAD + frames :, :] = zeros
    tile = jnp.broadcast_to(before_ref[...].astype(F32) * ROOT_HALF, (PAD, channels))
    padded_ref[0:PAD, :] = jnp.where(owner_before < UTTS, tile, 0.0).astype(BF16)
    tile = jnp.broadcast_to(after_ref[...].astype(F32) * ROOT_HALF, (PAD, channels))
    padded_ref[PAD + frames :, :] = jnp.where(owner_after < UTTS, tile, 0.0).astype(BF16)
    bias_ref[...] = jnp.zeros_like(bias_ref)

    def scale(i, carry):
        start = pl.multiple_of(i * ROWS, ROWS)
        here = cot_ref[pl.ds(start, ROWS), :].astype(F32) * ROOT_HALF
        here = jnp.where(rows_of(base + start, (ROWS, channels)) < ends[UTTS - 1], here, 0.0)
        rounded = here.astype(BF16)
        padded_ref[pl.ds(start + PAD, ROWS), :] = rounded
        bias_ref[...] += fold_rows(rounded.astype(F32))
        return carry

    lax.fori_loop(0, frames // ROWS, scale, 0)

    def step(i, carry):
        start = pl.multiple_of(i * ROWS, ROWS)
        build_taps(padded_ref, taps_ref, ends, start, base, True)
        out_ref[pl.ds(start, ROWS), :] = jnp.dot(
            taps_ref[...], weight_ref[...], preferred_element_type=F32
        )
        return carry

    lax.fori_loop(0, frames // ROWS, step, 0)


def upsample_kernel(
    info_ref,
    offset_ref,
    before_ref,
    own_ref,
    after_ref,
    align_ref,
    bias_ref,
    out_ref,
    wide_ref,
    stat_ref,
    buffer_ref,
    acc_ref,
):
    frames, channels = out_ref.shape
    window = align_ref.shape[1]
    tiles = offset_ref.shape[0]
    rows = frames // tiles
    halo, own = before_ref.shape[0], own_ref.shape[0]
    ends = read_ends(info_ref)
    slot_ends = [info_ref[UTTS + k] for k in range(UTTS)]
    base, slot_base = info_ref[8], info_ref[9]
    buffer_ref[0:halo, :] = before_ref[...]
    buffer_ref[halo : halo + own, :] = own_ref[...]
    buffer_ref[halo + own : 2 * halo + own, :] = after_ref[...]
    buffer_ref[2 * halo + own :, :] = jnp.zeros_like(buffer_ref[2 * halo + own :, :])
    acc_ref[...] = jnp.zeros_like(acc_ref)

    def step(i, carry):
        start = pl.multiple_of(i * rows, rows)
        shift = offset_ref[i] - slot_base
        aligned = pl.multiple_of((shift // PAD) * PAD, PAD)
        block = align_ref[pl.ds(start, rows), :].astype(F32)
        block = jnp.concatenate([block, jnp.zeros((rows, WIDE - window), F32)], axis=1)
        block = pltpu.roll(block, shift - aligned, 1)
        slots = slot_base + aligned + lax.broadcasted_iota(I32, (rows, WIDE), 1)
        slot_owner = owner_at(slot_ends, slots)
        frame_owner = owner_at(ends, rows_of(base + start, (rows, WIDE)))
        match = (slot_owner == frame_owner) & (frame_owner < UTTS)
        block = jnp.where(match, block, 0.0).astype(BF16)
        wide_ref[pl.ds(start, rows), :] = block
        out_ref[pl.ds(start, rows), :] = jnp.dot(
            block, buffer_ref[pl.ds(aligned, WIDE), :], preferred_element_type=F32
        )
        return carry

    lax.fori_loop(0, tiles, step, 0)

    def sums(i, carry):
        start = pl.multiple_of(i * ROWS, ROWS)

        def uniform(u):
            here = out_ref[pl.ds(start, ROWS), :]
            add_stats(acc_ref, u, here, here * here)

        def mixed(u, mask):
            here = jnp.where(mask((ROWS, channels)), out_ref[pl.ds(start, ROWS), :], 0.0)
            add_stats(acc_ref, u, here, here * here)

        by_utterance(ends, base + start, ROWS, uniform, mixed)
        return carry

    lax.fori_loop(0, frames // ROWS, sums, 0)
    finish_stats(acc_ref, stat_ref)
    stat_ref[FIRST_ROW : FIRST_ROW + 1, :] = out_ref[0:1, :]
    stat_ref[LAST_ROW : LAST_ROW + 1, :] = out_ref[frames - 1 : frames, :]
    stat_ref[EXTRA_ROW : EXTRA_ROW + 1, :] = jnp.sum(bias_ref[...], axis=0, keepdims=True)


def write_coefficients(own_ref, other_refs, inverse_ref, params_ref, coef_ref):
    channels = inverse_ref.shape[1]
    inverse = inverse_ref[...]
    total = sum_over_tm(own_ref, other_refs, 0, 8)
    square = sum_over_tm(own_ref, other_refs, 8, 8)
    mean = total * inverse
    rstd = lax.rsqrt(square * inverse - mean * mean + EPSILON)
    real = inverse > 0.0
    scale = jnp.where(real, (1.0 + params_ref[:, 0:channels]) * rstd, 0.0)
    shift = jnp.where(real, params_ref[:, channels : 2 * channels] - mean * scale, 0.0)
    coef_ref[0:8, :] = mean
    coef_ref[8:16, :] = jnp.where(real, rstd, 0.0)
    coef_ref[16:24, :] = scale
    coef_ref[24:32, :] = shift


def activation(values, coef_ref, u):
    normed = values * row(coef_ref, 16 + u) + row(coef_ref, 24 + u)
    return normed * logistic(normed)


def first_conv_kernel(
    info_ref,
    values_ref,
    own_ref,
    one_ref,
    two_ref,
    three_ref,
    inverse_ref,
    params_ref,
    weight_ref,
    act_ref,
    out_ref,
    coef_ref,
    stat_ref,
    taps_ref,
    acc_ref,
):
    frames, channels = values_ref.shape
    ends = read_ends(info_ref)
    base = info_ref[8]
    write_coefficients(own_ref, (one_ref, two_ref, three_ref), inverse_ref, params_ref, coef_ref)
    acc_ref[...] = jnp.zeros_like(acc_ref)
    owner_before, owner_after = halo_owner(info_ref, ends, base, frames)
    edge = activation(row(one_ref, LAST_ROW), coef_ref, owner_before)
    act_ref[0:PAD, :] = jnp.broadcast_to(edge, (PAD, channels)).astype(BF16)
    edge = activation(row(three_ref, FIRST_ROW), coef_ref, owner_after)
    act_ref[PAD + frames :, :] = jnp.broadcast_to(edge, (PAD, channels)).astype(BF16)

    def act_step(i, carry):
        start = pl.multiple_of(i * ROWS, ROWS)

        def uniform(u):
            here = activation(values_ref[pl.ds(start, ROWS), :], coef_ref, u)
            act_ref[pl.ds(start + PAD, ROWS), :] = here.astype(BF16)

        def mixed(u, mask):
            here = activation(values_ref[pl.ds(start, ROWS), :], coef_ref, u)
            old = act_ref[pl.ds(start + PAD, ROWS), :].astype(F32)
            here = jnp.where(mask((ROWS, channels)), here, old)
            act_ref[pl.ds(start + PAD, ROWS), :] = here.astype(BF16)

        by_utterance(ends, base + start, ROWS, uniform, mixed)
        return carry

    lax.fori_loop(0, frames // ROWS, act_step, 0)

    def step(i, carry):
        start = pl.multiple_of(i * ROWS, ROWS)
        build_taps(act_ref, taps_ref, ends, start, base, False)
        out_ref[pl.ds(start, ROWS), :] = jnp.dot(
            taps_ref[...], weight_ref[...], preferred_element_type=F32
        )

        def uniform(u):
            here = out_ref[pl.ds(start, ROWS), :]
            add_stats(acc_ref, u, here, here * here)

        def mixed(u, mask):
            here = jnp.where(mask((ROWS, channels)), out_ref[pl.ds(start, ROWS), :], 0.0)
            add_stats(acc_ref, u, here, here * here)

        by_utterance(ends, base + start, ROWS, uniform, mixed)
        return carry

    lax.fori_loop(0, frames // ROWS, step, 0)
    finish_stats(acc_ref, stat_ref)
    stat_ref[FIRST_ROW : FIRST_ROW + 1, :] = out_ref[0:1, :]
    stat_ref[LAST_ROW : LAST_ROW + 1, :] = out_ref[frames - 1 : frames, :]


def slope_and_sums(gradient, values, coef_ref, u):
    normed = values * row(coef_ref, 16 + u) + row(coef_ref, 24 + u)
    gate = logistic(normed)
    act = normed * gate
    inner = gradient * (gate + act * (1.0 - gate))
    unit = (values - row(coef_ref, u)) * row(coef_ref, 8 + u)
    return act, inner, inner * unit


def second_norm_kernel(
    info_ref,
    gradient_ref,
    values_ref,
    own_ref,
    one_ref,
    two_ref,
    three_ref,
    inverse_ref,
    params_ref,
    act_ref,
    inner_ref,
    coef_ref,
    stat_ref,
    acc_ref,
):
    frames, channels = values_ref.shape
    ends = read_ends(info_ref)
    base = info_ref[8]
    write_coefficients(own_ref, (one_ref, two_ref, three_ref), inverse_ref, params_ref, coef_ref)
    acc_ref[...] = jnp.zeros_like(acc_ref)
    owner_before, owner_after = halo_owner(info_ref, ends, base, frames)
    edge = activation(row(one_ref, LAST_ROW), coef_ref, owner_before)
    act_ref[0:PAD, :] = jnp.broadcast_to(edge, (PAD, channels)).astype(BF16)
    edge = activation(row(three_ref, FIRST_ROW), coef_ref, owner_after)
    act_ref[PAD + frames :, :] = jnp.broadcast_to(edge, (PAD, channels)).astype(BF16)

    def step(i, carry):
        start = pl.multiple_of(i * ROWS, ROWS)
        here = pl.ds(start, ROWS)

        def uniform(u):
            act, inner, cross = slope_and_sums(
                gradient_ref[here, :], values_ref[here, :], coef_ref, u
            )
            act_ref[pl.ds(start + PAD, ROWS), :] = act.astype(BF16)
            inner_ref[here, :] = inner
            add_stats(acc_ref, u, inner, cross)

        def mixed(u, mask):
            keep = mask((ROWS, channels))
            act, inner, cross = slope_and_sums(
                gradient_ref[here, :], values_ref[here, :], coef_ref, u
            )
            old = act_ref[pl.ds(start + PAD, ROWS), :].astype(F32)
            act_ref[pl.ds(start + PAD, ROWS), :] = jnp.where(keep, act, old).astype(BF16)
            inner_ref[here, :] = jnp.where(keep, inner, inner_ref[here, :])
            add_stats(acc_ref, u, jnp.where(keep, inner, 0.0), jnp.where(keep, cross, 0.0))

        by_utterance(ends, base + start, ROWS, uniform, mixed)
        return carry

    lax.fori_loop(0, frames // ROWS, step, 0)
    finish_stats(acc_ref, stat_ref)
    stat_ref[FIRST_ROW : FIRST_ROW + 1, :] = inner_ref[0:1, :]
    stat_ref[LAST_ROW : LAST_ROW + 1, :] = inner_ref[frames - 1 : frames, :]


def second_conv_kernel(
    info_ref, act_ref, values_ref, weight_ref, bias_ref, out_ref, taps_ref
):
    frames, channels = values_ref.shape
    ends = read_ends(info_ref)
    base = info_ref[8]
    bias = bias_ref[...].astype(F32)

    def step(i, carry):
        start = pl.multiple_of(i * ROWS, ROWS)
        here = pl.ds(start, ROWS)
        build_taps(act_ref, taps_ref, ends, start, base, False)
        branch = jnp.dot(taps_ref[...], weight_ref[...], preferred_element_type=F32) + bias
        valid = rows_of(base + start, (ROWS, channels)) < ends[UTTS - 1]
        total = jnp.where(valid, (values_ref[here, :] + branch) * ROOT_HALF, 0.0)
        out_ref[here, :] = total.astype(BF16)
        return carry

    lax.fori_loop(0, frames // ROWS, step, 0)


def weight_gradient_kernel(info_ref, act_ref, gradient_ref, out_ref, taps_ref, total_ref):
    frames = act_ref.shape[0] - 2 * PAD
    channels = act_ref.shape[1]
    ends = read_ends(info_ref)
    base = info_ref[8]
    total_ref[...] = jnp.zeros_like(total_ref)

    def step(i, carry):
        start = pl.multiple_of(i * ROWS, ROWS)
        build_taps(gradient_ref, taps_ref, ends, start, base, True)
        total_ref[...] += lax.dot_general(
            act_ref[pl.ds(start + PAD, ROWS), :],
            taps_ref[...],
            (((0,), (0,)), ((), ())),
            preferred_element_type=F32,
        )
        return carry

    lax.fori_loop(0, frames // ROWS, step, 0)
    for k in range(3):
        out_ref[k * channels : (k + 1) * channels, :] = total_ref[
            :, k * channels : (k + 1) * channels
        ]


def back_coefficients(own_ref, other_refs, inverse_ref, coef_ref, back_ref):
    inverse = inverse_ref[...]
    total = sum_over_tm(own_ref, other_refs, 0, 8)
    cross = sum_over_tm(own_ref, other_refs, 8, 8)
    mean, rstd, scale = coef_ref[0:8, :], coef_ref[8:16, :], coef_ref[16:24, :]
    back_ref[0:8, :] = total
    back_ref[8:16, :] = cross
    slant = scale * rstd * cross * inverse
    back_ref[16:24, :] = scale * total * inverse - mean * slant
    back_ref[24:32, :] = slant


def inward(inner, values, coef_ref, back_ref, u):
    return (
        inner * row(coef_ref, 16 + u) - row(back_ref, 16 + u) - values * row(back_ref, 24 + u)
    )


def first_back_kernel(
    info_ref,
    inner_ref,
    middle_ref,
    own_ref,
    one_ref,
    two_ref,
    three_ref,
    middle_one_ref,
    middle_three_ref,
    inverse_ref,
    coef_two_ref,
    coef_one_ref,
    values_ref,
    weight_ref,
    gradient_ref,
    out_ref,
    back_ref,
    stat_ref,
    taps_ref,
    acc_ref,
):
    frames, channels = values_ref.shape
    ends = read_ends(info_ref)
    base = info_ref[8]
    back_coefficients(own_ref, (one_ref, two_ref, three_ref), inverse_ref, coef_two_ref, back_ref)
    acc_ref[...] = jnp.zeros_like(acc_ref)
    owner_before, owner_after = halo_owner(info_ref, ends, base, frames)
    edge = inward(
        row(one_ref, LAST_ROW), row(middle_one_ref, LAST_ROW), coef_two_ref, back_ref, owner_before
    )
    gradient_ref[0:PAD, :] = jnp.broadcast_to(edge, (PAD, channels)).astype(BF16)
    edge = inward(
        row(three_ref, FIRST_ROW),
        row(middle_three_ref, FIRST_ROW),
        coef_two_ref,
        back_ref,
        owner_after,
    )
    gradient_ref[PAD + frames :, :] = jnp.broadcast_to(edge, (PAD, channels)).astype(BF16)

    def back_step(i, carry):
        start = pl.multiple_of(i * ROWS, ROWS)
        here = pl.ds(start, ROWS)

        def uniform(u):
            now = inward(inner_ref[here, :], middle_ref[here, :], coef_two_ref, back_ref, u)
            gradient_ref[pl.ds(start + PAD, ROWS), :] = now.astype(BF16)

        def mixed(u, mask):
            now = inward(inner_ref[here, :], middle_ref[here, :], coef_two_ref, back_ref, u)
            old = gradient_ref[pl.ds(start + PAD, ROWS), :].astype(F32)
            now = jnp.where(mask((ROWS, channels)), now, old)
            gradient_ref[pl.ds(start + PAD, ROWS), :] = now.astype(BF16)

        by_utterance(ends, base + start, ROWS, uniform, mixed)
        return carry

    lax.fori_loop(0, frames // ROWS, back_step, 0)

    def step(i, carry):
        start = pl.multiple_of(i * ROWS, ROWS)
        here = pl.ds(start, ROWS)
        build_taps(gradient_ref, taps_ref, ends, start, base, True)
        out_ref[here, :] = jnp.dot(taps_ref[...], weight_ref[...], preferred_element_type=F32)

        def uniform(u):
            _, inner, cross = slope_and_sums(
                out_ref[here, :], values_ref[here, :], coef_one_ref, u
            )
            out_ref[here, :] = inner
            add_stats(acc_ref, u, inner, cross)

        def mixed(u, mask):
            keep = mask((ROWS, channels))
            before = out_ref[here, :]
            _, inner, cross = slope_and_sums(before, values_ref[here, :], coef_one_ref, u)
            out_ref[here, :] = jnp.where(keep, inner, before)
            add_stats(acc_ref, u, jnp.where(keep, inner, 0.0), jnp.where(keep, cross, 0.0))

        by_utterance(ends, base + start, ROWS, uniform, mixed)
        return carry

    lax.fori_loop(0, frames // ROWS, step, 0)
    finish_stats(acc_ref, stat_ref)


def buffer_gradient_kernel(
    info_ref,
    offset_ref,
    inner_ref,
    values_ref,
    cot_ref,
    wide_ref,
    own_ref,
    one_ref,
    two_ref,
    three_ref,
    inverse_ref,
    coef_ref,
    before_ref,
    out_ref,
    after_ref,
    back_ref,
    up_ref,
    total_ref,
):
    frames, channels = values_ref.shape
    tiles = offset_ref.shape[0]
    rows = frames // tiles
    halo, own = before_ref.shape[0], out_ref.shape[0]
    ends = read_ends(info_ref)
    base, slot_base = info_ref[8], info_ref[9]
    back_coefficients(own_ref, (one_ref, two_ref, three_ref), inverse_ref, coef_ref, back_ref)
    total_ref[...] = jnp.zeros_like(total_ref)
    span = rows + PAD

    def step(i, carry):
        start = pl.multiple_of(i * rows, rows)
        here = pl.ds(start, rows)

        def upward(u):
            lead = cot_ref[here, :].astype(F32) * ROOT_HALF
            return lead + inward(inner_ref[here, :], values_ref[here, :], coef_ref, back_ref, u)

        def uniform(u):
            up_ref[...] = upward(u).astype(BF16)

        def mixed(u, mask):
            old = up_ref[...].astype(F32)
            up_ref[...] = jnp.where(mask((rows, channels)), upward(u), old).astype(BF16)

        by_utterance(ends, base + start, rows, uniform, mixed)
        shift = offset_ref[i] - slot_base
        aligned = pl.multiple_of((shift // PAD) * PAD, PAD)
        part = lax.dot_general(
            wide_ref[here, :], up_ref[...], (((0,), (0,)), ((), ())), preferred_element_type=F32
        )
        total_ref[pl.ds(aligned, span), :] += part[0:span]
        return carry

    lax.fori_loop(0, tiles, step, 0)
    before_ref[...] = total_ref[0:halo, :]
    out_ref[...] = total_ref[halo : halo + own, :]
    after_ref[...] = total_ref[halo + own : 2 * halo + own, :]


VM = pl.BlockSpec(memory_space=pltpu.VMEM)
SM = pl.BlockSpec(memory_space=pltpu.SMEM)


def call(kernel, inputs, outputs, scratch, scalars, flops, limit):
    return pl.pallas_call(
        kernel,
        in_specs=[SM] * scalars + [VM] * (len(inputs) - scalars),
        out_specs=tuple(VM for _ in outputs),
        out_shape=tuple(jax.ShapeDtypeStruct(shape, dtype) for shape, dtype in outputs),
        scratch_shapes=[pltpu.VMEM(shape, dtype) for shape, dtype in scratch],
        compiler_params=pltpu.CompilerParams(vmem_limit_bytes=limit * MIB),
        cost_estimate=pl.CostEstimate(flops=flops, bytes_accessed=flops // 200, transcendentals=0),
    )(*inputs)


def shifted(values, axis, step):
    devices = lax.axis_size(axis)
    return lax.ppermute(values, axis, [(i, (i + step) % devices) for i in range(devices)])


def others_over_tm(values):
    return [shifted(values, "tm", d) for d in (1, 2, 3)]


def from_neighbours(first_rows, last_rows):
    devices = lax.axis_size("tm")
    up = [(i, i + 1) for i in range(devices - 1)]
    down = [(i + 1, i) for i in range(devices - 1)]
    return lax.ppermute(last_rows, "tm", up), lax.ppermute(first_rows, "tm", down)


def swapped(values, bit):
    devices = lax.axis_size("seq")
    return lax.ppermute(values, "seq", [(i, i ^ (1 << bit)) for i in range(devices)])


def bit_of(index, bit):
    return (index >> bit) & 1


def sum_everywhere(values, bits):
    copies = lax.axis_size("tm")
    seq_index, tm_index = lax.axis_index("seq"), lax.axis_index("tm")
    part = values
    for bit in bits:
        half = part.shape[0] // 2
        mine = bit_of(seq_index, bit)
        keep = lax.dynamic_slice_in_dim(part, mine * half, half)
        give = lax.dynamic_slice_in_dim(part, (1 - mine) * half, half)
        part = keep + swapped(give.astype(BF16), bit).astype(F32)
    piece = part.shape[0] // copies
    pieces = part.reshape(copies, piece, part.shape[1])
    part = lax.dynamic_index_in_dim(pieces, tm_index, 0, False)
    for step in range(1, copies):
        give = lax.dynamic_index_in_dim(pieces, (tm_index + step) % copies, 0, False)
        part = part + shifted(give.astype(BF16), "tm", step).astype(F32)
    part = part.astype(BF16)
    every = jnp.zeros((copies,) + part.shape, BF16)
    every = lax.dynamic_update_index_in_dim(every, part, tm_index, 0)
    for step in range(1, copies):
        every = lax.dynamic_update_index_in_dim(
            every, shifted(part, "tm", step), (tm_index - step) % copies, 0
        )
    part = every.reshape(copies * piece, part.shape[1])
    for bit in reversed(bits):
        other = swapped(part, bit)
        mine = bit_of(seq_index, bit)
        part = jnp.concatenate(
            [jnp.where(mine == 0, part, other), jnp.where(mine == 0, other, part)]
        )
    return part


def gathered_over_seq(values):
    seq_index = lax.axis_index("seq")
    part = values
    bit = 0
    while (1 << bit) < lax.axis_size("seq"):
        other = swapped(part, bit)
        mine = bit_of(seq_index, bit)
        part = jnp.concatenate(
            [jnp.where(mine == 0, part, other), jnp.where(mine == 0, other, part)]
        )
        bit += 1
    return part


def on_device(
    phonemes,
    send_order,
    phoneme_counts,
    frame_lengths,
    tile_offsets,
    alignment,
    style_vec,
    first_affine_weight,
    first_affine_bias,
    first_conv_weight,
    second_affine_weight,
    second_affine_bias,
    second_conv_weight,
    second_conv_bias,
    cotangent,
):
    frames, channels = cotangent.shape
    slot_count = phonemes.shape[0]
    groups = lax.axis_size("seq")
    copies = lax.axis_size("tm")
    tm_index = lax.axis_index("tm")
    piece_rows = slot_count // groups // copies
    local_rows = slot_count // copies
    tiles = tile_offsets.shape[0]
    window = alignment.shape[1]
    halo = window // 2
    lengths = frame_lengths[0]
    conv_flops = 2 * frames * 3 * channels * channels

    info = jnp.concatenate(
        [
            jnp.cumsum(lengths),
            jnp.cumsum(phoneme_counts[0]),
            (tm_index * frames)[None],
            (tm_index * local_rows - halo)[None],
            jnp.zeros((6,), I32),
        ]
    ).astype(I32)
    inverse = jnp.zeros((8, channels), F32).at[0:UTTS].set(
        jnp.broadcast_to(1.0 / lengths.astype(F32)[:, None], (UTTS, channels))
    )
    style_rows = jnp.zeros((8, style_vec.shape[1]), BF16).at[0:UTTS].set(style_vec)
    params_one = jnp.dot(style_rows, first_affine_weight, preferred_element_type=F32) + (
        first_affine_bias.astype(F32)
    )
    params_two = jnp.dot(style_rows, second_affine_weight, preferred_element_type=F32) + (
        second_affine_bias.astype(F32)
    )

    def turned(weight):
        return (
            weight.reshape(3, channels, channels).transpose(0, 2, 1).reshape(3 * channels, channels)
        )

    order = send_order[0].reshape(groups, copies, piece_rows)
    mine = lax.dynamic_index_in_dim(order, tm_index, 1, False)
    outgoing = jnp.take(phonemes, mine.reshape(-1), axis=0, mode="clip")
    received = lax.all_to_all(
        outgoing.reshape(groups, piece_rows, channels), "seq", 0, 0, tiled=True
    ).reshape(local_rows, channels)
    slots_before, slots_after = from_neighbours(received[:halo], received[-halo:])

    cot_before, cot_after = from_neighbours(cotangent[:1], cotangent[-1:])
    grad_act_two, grad_branch, bias_part = call(
        gradient_kernel,
        (info, cotangent, cot_before, cot_after, turned(second_conv_weight)),
        (
            ((frames, channels), F32),
            ((frames + 2 * PAD, channels), BF16),
            ((8, channels), F32),
        ),
        [((ROWS, 3 * channels), BF16)],
        1,
        conv_flops,
        24,
    )

    upsampled, wide, stat = call(
        upsample_kernel,
        (info, tile_offsets, slots_before, received, slots_after, alignment, bias_part),
        (
            ((frames, channels), F32),
            ((frames, WIDE), BF16),
            ((STAT_ROWS, channels), F32),
        ),
        [((local_rows + WIDE, channels), BF16), ((ACC_ROWS, channels), F32)],
        2,
        2 * frames * WIDE * channels,
        24,
    )
    others = others_over_tm(stat)
    bias_total = (stat[EXTRA_ROW] + others[1][EXTRA_ROW]) + (
        others[0][EXTRA_ROW] + others[2][EXTRA_ROW]
    )

    act_one, middle, coef_one, stat_two = call(
        first_conv_kernel,
        (info, upsampled, stat, *others, inverse, params_one, first_conv_weight),
        (
            ((frames + 2 * PAD, channels), BF16),
            ((frames, channels), F32),
            ((32, channels), F32),
            ((STAT_ROWS, channels), F32),
        ),
        [((ROWS, 3 * channels), BF16), ((ACC_ROWS, channels), F32)],
        1,
        conv_flops,
        24,
    )
    others_two = others_over_tm(stat_two)

    act_two, inner_two, coef_two, stat_three = call(
        second_norm_kernel,
        (info, grad_act_two, middle, stat_two, *others_two, inverse, params_two),
        (
            ((frames + 2 * PAD, channels), BF16),
            ((frames, channels), F32),
            ((32, channels), F32),
            ((STAT_ROWS, channels), F32),
        ),
        [((ACC_ROWS, channels), F32)],
        1,
        2 * frames * channels * 100,
        24,
    )
    others_three = others_over_tm(stat_three)

    (frames_out,) = call(
        second_conv_kernel,
        (info, act_two, upsampled, second_conv_weight, second_conv_bias[None]),
        (((frames, channels), BF16),),
        [((ROWS, 3 * channels), BF16)],
        1,
        conv_flops,
        24,
    )
    (second_grad,) = call(
        weight_gradient_kernel,
        (info, act_two, grad_branch),
        (((3 * channels, channels), F32),),
        [((ROWS, 3 * channels), BF16), ((channels, 3 * channels), F32)],
        1,
        conv_flops,
        24,
    )

    grad_middle, inner_one, back_two, stat_four = call(
        first_back_kernel,
        (
            info,
            inner_two,
            middle,
            stat_three,
            *others_three,
            others_two[0],
            others_two[2],
            inverse,
            coef_two,
            coef_one,
            upsampled,
            turned(first_conv_weight),
        ),
        (
            ((frames + 2 * PAD, channels), BF16),
            ((frames, channels), F32),
            ((32, channels), F32),
            ((STAT_ROWS, channels), F32),
        ),
        [((ROWS, 3 * channels), BF16), ((ACC_ROWS, channels), F32)],
        1,
        conv_flops,
        24,
    )
    others_four = others_over_tm(stat_four)
    (first_grad,) = call(
        weight_gradient_kernel,
        (info, act_one, grad_middle),
        (((3 * channels, channels), F32),),
        [((ROWS, 3 * channels), BF16), ((channels, 3 * channels), F32)],
        1,
        conv_flops,
        24,
    )

    grad_before, grad_own, grad_after, back_one = call(
        buffer_gradient_kernel,
        (
            info,
            tile_offsets,
            inner_one,
            upsampled,
            cotangent,
            wide,
            stat_four,
            *others_four,
            inverse,
            coef_one,
        ),
        (
            ((halo, channels), F32),
            ((local_rows, channels), F32),
            ((halo, channels), F32),
            ((32, channels), F32),
        ),
        [((frames // tiles, channels), BF16), ((local_rows + WIDE, channels), F32)],
        2,
        2 * frames * WIDE * channels,
        24,
    )

    from_before, from_after = from_neighbours(grad_before, grad_after)
    return_rows = jnp.concatenate(
        [
            grad_own[:halo] + from_before,
            grad_own[halo:-halo],
            grad_own[-halo:] + from_after,
        ]
    ).astype(BF16)
    returned = lax.all_to_all(
        return_rows.reshape(groups, piece_rows, channels), "seq", 0, 0, tiled=True
    )
    parts = [returned] + others_over_tm(returned)
    slots_back = jnp.zeros((groups, copies, piece_rows, channels), BF16)
    for step, part in enumerate(parts):
        slots_back = lax.dynamic_update_index_in_dim(
            slots_back, part, (tm_index - step) % copies, 1
        )
    place = (
        jnp.zeros((slot_count,), I32)
        .at[send_order[0]]
        .set(jnp.arange(slot_count, dtype=I32), unique_indices=True)
    )
    phonemes_grad = jnp.take(
        slots_back.reshape(slot_count, channels), place, axis=0, mode="clip"
    ).astype(F32)

    bits = [b for b in range(16) if (1 << b) < groups]
    second_conv_grad = sum_everywhere(second_grad, bits).astype(F32)
    first_conv_grad = sum_everywhere(first_grad, bits[:1] + bits[1:][::-1]).astype(F32)
    params_grad = [
        jnp.concatenate([back[8 : 8 + UTTS], back[0:UTTS]], axis=1) for back in (back_one, back_two)
    ]
    style_grad = jnp.dot(
        params_grad[0], first_affine_weight.astype(F32).T, precision=PRECISE
    ) + jnp.dot(params_grad[1], second_affine_weight.astype(F32).T, precision=PRECISE)
    small = jnp.concatenate(
        [
            params_grad[0].reshape(2 * UTTS, channels),
            params_grad[1].reshape(2 * UTTS, channels),
            style_vec.astype(F32).reshape(-1, channels),
            bias_total[None],
            jnp.zeros((6, channels), F32),
        ]
    )
    every = gathered_over_seq(small[None])
    styles = every[:, 4 * UTTS].reshape(groups * UTTS, -1)
    grads = [
        every[:, 2 * UTTS * k : 2 * UTTS * (k + 1)].reshape(groups * UTTS, 2 * channels)
        for k in range(2)
    ]
    affine_grads = [
        lax.dot_general(styles, g, (((0,), (0,)), ((), ())), precision=PRECISE) for g in grads
    ]
    shift_grads = [jnp.sum(g, axis=0) for g in grads]
    second_bias_grad = jnp.sum(every[:, 4 * UTTS + 1], axis=0)
    return (
        frames_out,
        phonemes_grad,
        style_grad,
        affine_grads[0],
        shift_grads[0],
        first_conv_grad,
        affine_grads[1],
        shift_grads[1],
        second_conv_grad,
        second_bias_grad,
    )


def solution(mesh):
    split, whole = ("seq", "tm"), P()
    in_specs = (
        P("seq", None),
        P("seq", None),
        P("seq", None),
        P("seq", None),
        P(split),
        P(split, None),
        P("seq", None),
        *([whole] * 7),
        P(split, None),
    )
    out_specs = (P(split, None), P("seq", None), P("seq", None), *([whole] * 7))
    return jax.shard_map(
        on_device, mesh=mesh, in_specs=in_specs, out_specs=out_specs, check_vma=False
    )
```

time: 1010 us -> 466 us (0.46)
  waiting for transfers between devices: 406 us -> 95.6 us
  matrix products: 241 us -> 5.29 us
  Pallas kernels: 0 us -> 116 us
  blocking collectives: 108 us -> 0 us
  starting transfers between devices: 29.6 us -> 104 us
  other arithmetic: 76 us -> 28.5 us
  local copies, waits for them, and re-layouts: 139 us -> 114 us
  between operations: 14.8 us -> 1.58 us
    psum x2 -> x0, waiting for transfers between devices: 313 us -> none  [the longest x1 289 us: on_device(): phonemes_grad = lax.psum(row_grads, 'tm')]
    dot_general x34 -> x6, matrix products: 241 us -> 5.29 us  [the longest x2 2.84 us: on_device(): lax.dot_general(styles, g, (((0,), (0,)), ((), ())), precision=PRECISE)]
    pallas_call x0 -> x9, Pallas kernels: none -> 116 us  [call(): pl.pallas_call(kernel, in_specs=[SM] * scalars + [VM] * (len(inputs) - sc...]
    psum x5 -> x0, blocking collectives: 108 us -> none  [the longest x4 70.6 us: moments(): return lax.psum((first_term, second_term), 'tm')]
    ppermute x8 -> x48, waiting for transfers between devices: 2.78 us -> 95.6 us  [the longest x27 73.7 us: shifted(): lax.ppermute(values, axis, [(i, (i + step) % devices) for i in range(devi...]
    all_to_all x2, waiting for transfers between devices: 89.9 us -> 0.01 us  [the longest x1 0.01 us: on_device(): lax.all_to_all(outgoing.reshape(groups, piece_rows, channels), 'seq', 0,...]
    ppermute x8 -> x48, starting transfers between devices: 18.4 us -> 93.6 us  [the longest x27 52.8 us: shifted(): lax.ppermute(values, axis, [(i, (i + step) % devices) for i in range(devi...]
    gather x3 -> x2, local copies, waits for them, and re-layouts: 63.4 us -> 28.1 us  [the longest x1 20.2 us: on_device(): jnp.take(slots_back.reshape(slot_count, channels), place, axis=0, mode='c...]
  transfers between devices with their start and end apart: 12 -> 50, of which waited for: 5 -> 22; matrix products, arithmetic and copies ran while one was open for 18% -> 18% of each run, Pallas kernels for 0% -> 18%
where the time goes in v1:
time: 466 us; the launch traced here: 464 us
  Pallas kernels  116 us (25%)
  local copies, waits for them, and re-layouts  114 us (24%)
  starting transfers between devices  104 us (22%)
  waiting for transfers between devices  95.6 us (21%)
  other arithmetic  28.5 us (6%)
  matrix products  5.29 us (1%)
    pallas_call x9, Pallas kernels, call(): pl.pallas_call(kernel, in_specs=[SM] * scalars + [VM] * (len(inputs) - sc...  116 us
    ppermute x27, waiting for transfers between devices, shifted(): lax.ppermute(values, axis, [(i, (i + step) % devices) for i in range(devi...  73.7 us
    ppermute x27, starting transfers between devices, shifted(): lax.ppermute(values, axis, [(i, (i + step) % devices) for i in range(devi...  52.8 us
    unnamed x114, local copies, waits for them, and re-layouts  50.1 us
    ppermute x15, starting transfers between devices, swapped(): lax.ppermute(values, 'seq', [(i, i ^ 1 << bit) for i in range(devices)])  24.8 us
    gather x1, local copies, waits for them, and re-layouts, on_device(): jnp.take(slots_back.reshape(slot_count, channels), place, axis=0, mode='c...  20.2 us
    ppermute x15, waiting for transfers between devices, swapped(): lax.ppermute(values, 'seq', [(i, i ^ 1 << bit) for i in range(devices)])  18.3 us
    scatter x1, local copies, waits for them, and re-layouts, on_device(): place = jnp.zeros((slot_count,), I32).at[send_order[0]].set(jnp.arange(sl...  15.5 us
  transfers between devices with their start and end apart: 50, of which 22 were waited for; matrix products, arithmetic and copies ran while one was open for 18% of the time, Pallas kernels for 18%

profile of v1, /device:TPU:0, one launch (start us, length us, event | category | flops | bytes accessed | tf_op | source)
XLA Modules:
  0.0 464.2 jit_solution(14291496101799294376)
XLA Ops:
  1.5 7.9 %gather_fusion = bf16[1024,512]{1,0:T(8,128)(2,1)} fusion(bf16[4096,512]{1,0:T(8,128)(2,1)} %param.19, s32[1024]{0:T(1024)S(1)} %broadcast_clamp_fusion.1), kind=kCustom, calls=%fused_computation | custom fusion | bytes 2101248 | tf_op jit(solution)/shard_map/jit(_take)/gather | solution.py:761
  9.3 5.3 %all-to-all-start = ((bf16[8,128,512]{2,1,0:T(8,128)(2,1)}), bf16[8,128,512]{2,1,0:T(8,128)(2,1)}, u32[]{:S(2)}, u32[]{:S(2)}) async-start(bf16[8,128,512]{2,1,0:T(8,128)(2,1)} %bitcast.11), calls=%async_computation | async-start | bytes 2097152 | tf_op jit(solution)/shard_map/all_to_all | solution.py:762
  15.4 4.0 collective-permute-start
  21.9 15.5 %scatter_custom_fusion = s32[4096]{0:T(1024)S(1)} fusion(s32[4096]{0:T(1024)S(1)} %bitcast.127, s32[4096]{0:T(1024)S(1)} %iota.3, s32[]{:T(128)} %constant.182.clone.1), kind=kCustom, calls=%fused_computation.94 | custom fusion | bytes 16388 | tf_op jit(solution)/shard_map/scatter | solution.py:935
  40.3 4.5 collective-permute-start.2
  48.3 13.1 %shard_map.222 = (f32[4096,512]{1,0:T(8,128)S(1)}, bf16[4128,512]{1,0:T(8,128)(2,1)S(1)}, f32[8,512]{1,0:T(8,128)S(1)}) custom-call(s32[16]{0:T(128)S(1)} %concatenate.47.info_ref, bf16[4096,512]{1,0:T(8,128)(2,1)S(1)} %copy-done.12, bf16[1,512]{1,0:T(2,128)(2,1)S(1)} %collective-permute-done.before_ref, ...), custom_call_target="tpu_custom_call" | custom-call | flops 6442450944 | bytes 32212254 | tf_op jit(solution)/shard_map/pallas_call | solution.py:621
  61.5 3.4 copy-done.8
  67.0 10.6 %shard_map.223 = (f32[4096,512]{1,0:T(8,128)S(1)}, bf16[4096,256]{1,0:T(8,128)(2,1)S(1)}, f32[24,512]{1,0:T(8,128)S(1)}) custom-call(s32[16]{0:T(128)S(1)} %concatenate.47.info_ref, s32[32]{0:T(128)S(1)} %copy-done.29, bf16[64,512]{1,0:T(8,128)(2,1)S(1)} %collective-permute-done.2.before_ref, bf16[1024,512]{1,0:T(8,128)(2,1)} %bitcast.12.own_ref, ...), custom_call_target="tpu_custom_call" | custom-call | flops 1073741824 | bytes 5368709 | tf_op jit(solution)/shard_map/pallas_call | solution.py:621
  92.1 3.4 copy-done.2
  96.9 15.2 %shard_map.224 = (bf16[4128,512]{1,0:T(8,128)(2,1)S(1)}, f32[4096,512]{1,0:T(8,128)S(1)}, f32[32,512]{1,0:T(8,128)S(1)}, f32[24,512]{1,0:T(8,128)S(1)}) custom-call(s32[16]{0:T(128)S(1)} %copy-done.25, f32[4096,512]{1,0:T(8,128)S(1)} %copy-done.2, f32[24,512]{1,0:T(8,128)S(1)} %copy-done.32, f32[24,512]{1,0:T(8,128)} %collective-permute-done.4.one_ref, ...), custom_call_target="tpu_custom_call" | custom-call | flops 6442450944 | bytes 32212254 | tf_op jit(solution)/shard_map/pallas_call | solution.py:621
  132.7 5.6 %shard_map.225 = (bf16[4128,512]{1,0:T(8,128)(2,1)S(1)}, f32[4096,512]{1,0:T(8,128)S(1)}, f32[32,512]{1,0:T(8,128)S(1)}, f32[24,512]{1,0:T(8,128)S(1)}) custom-call(s32[16]{0:T(128)S(1)} %copy-done.26, f32[4096,512]{1,0:T(8,128)S(1)} %copy-done.9, f32[4096,512]{1,0:T(8,128)S(1)} %copy-done.5, f32[24,512]{1,0:T(8,128)S(1)} %get-tuple-element.61.own_ref, ...), custom_call_target="tpu_custom_call" | custom-call | flops 419430400 | bytes 2097152 | tf_op jit(solution)/shard_map/pallas_call | solution.py:621
  138.3 3.4 copy-done.10
  147.7 12.0 %shard_map.230 = f32[1536,512]{1,0:T(8,128)S(1)} custom-call(s32[16]{0:T(128)S(1)} %copy-done.26, bf16[4128,512]{1,0:T(8,128)(2,1)S(1)} %get-tuple-element.62.act_ref, bf16[4128,512]{1,0:T(8,128)(2,1)S(1)} %copy-done.35), custom_call_target="tpu_custom_call" | custom-call | flops 6442450944 | bytes 32212254 | tf_op jit(solution)/shard_map/pallas_call | solution.py:621
  160.7 5.0 %collective-permute-start.36 = (bf16[768,512]{1,0:T(8,128)(2,1)}, bf16[768,512]{1,0:T(8,128)(2,1)}, u32[]{:S(2)}, u32[]{:S(2)}) collective-permute-start(bf16[768,512]{1,0:T(8,128)(2,1)} %dynamic-slice_convert_fusion), channel_id=1, source_target_pairs={{0,4},{4,0},{8,12},{12,8},{16,20},{20,16},{24,28},{28,24},{1,5},{5... | collective-permute-start | bytes 2359304 | tf_op jit(solution)/shard_map/ppermute | solution.py:650
  165.8 13.6 %shard_map.226 = bf16[4096,512]{1,0:T(8,128)(2,1)} custom-call(s32[16]{0:T(128)S(1)} %copy-done.26, bf16[4128,512]{1,0:T(8,128)(2,1)S(1)} %get-tuple-element.62.act_ref, f32[4096,512]{1,0:T(8,128)S(1)} %bitcast.109, bf16[1536,512]{1,0:T(8,128)(2,1)S(1)} %copy-done.22, bf16[1,512]{1,0:T(2,128)(2,1)S(1)} %copy-done.28), custom_call_target="tpu_custom_call" | custom-call | flops 6442450944 | bytes 32212254 | tf_op jit(solution)/shard_map/pallas_call | solution.py:621
  182.8 22.7 %shard_map.227 = (bf16[4128,512]{1,0:T(8,128)(2,1)S(1)}, f32[4096,512]{1,0:T(8,128)S(1)}, f32[32,512]{1,0:T(8,128)S(1)}, f32[24,512]{1,0:T(8,128)S(1)}) custom-call(s32[16]{0:T(128)S(1)} %copy-done.26, f32[4096,512]{1,0:T(8,128)S(1)} %copy-done.11, f32[4096,512]{1,0:T(8,128)} %copy-done.4, f32[24,512]{1,0:T(8,128)S(1)} %get-tuple-element.64.own_ref, ...), custom_call_target="tpu_custom_call" | custom-call | flops 6442450944 | bytes 32212254 | tf_op jit(solution)/shard_map/pallas_call | solution.py:621
  209.4 12.0 %shard_map.229 = f32[1536,512]{1,0:T(8,128)S(1)} custom-call(s32[16]{0:T(128)S(1)} %copy-done.26, bf16[4128,512]{1,0:T(8,128)(2,1)S(1)} %bitcast.115, bf16[4128,512]{1,0:T(8,128)(2,1)S(1)} %get-tuple-element.76.gradient_ref), custom_call_target="tpu_custom_call" | custom-call | flops 6442450944 | bytes 32212254 | tf_op jit(solution)/shard_map/pallas_call | solution.py:621
  223.3 4.9 %collective-permute-start.24 = (bf16[768,512]{1,0:T(8,128)(2,1)}, bf16[768,512]{1,0:T(8,128)(2,1)}, u32[]{:S(2)}, u32[]{:S(2)}) collective-permute-start(bf16[768,512]{1,0:T(8,128)(2,1)} %dynamic-slice_convert_fusion.1), channel_id=1, source_target_pairs={{0,4},{4,0},{8,12},{12,8},{16,20},{20,16},{24,28},{28,24},{1,5},{5... | collective-permute-start | bytes 2359304 | tf_op jit(solution)/shard_map/ppermute | solution.py:650
  237.3 11.4 %shard_map.228 = (f32[64,512]{1,0:T(8,128)S(1)}, f32[1024,512]{1,0:T(8,128)S(1)}, f32[64,512]{1,0:T(8,128)S(1)}, f32[32,512]{1,0:T(8,128)S(1)}) custom-call(s32[16]{0:T(128)S(1)} %copy-done.27, s32[32]{0:T(128)S(1)} %copy-done.30, f32[4096,512]{1,0:T(8,128)S(1)} %copy-done.7, f32[4096,512]{1,0:T(8,128)S(1)} %copy-done.3, bf16[4096,512]{1,0:T(8,128)(2,1)S(1)} %copy-done.13, ...), custom_call_target="tpu_custom_call" | custom-call | flops 1073741824 | bytes 5368709 | tf_op jit(solution)/shard_map/pallas_call | solution.py:621
  251.3 5.4 %collective-permute-start.22 = (f32[2,24,512]{2,1,0:T(8,128)S(1)}, f32[2,24,512]{2,1,0:T(8,128)S(1)}, u32[]{:S(2)}, u32[]{:S(2)}) collective-permute-start(f32[2,24,512]{2,1,0:T(8,128)S(1)} %pad_maximum_fusion.6), channel_id=1, source_target_pairs={{0,8},{4,12},{8,0},{12,4},{16,24},{20,28},{24,16},{28,20},{1,9},{5... | collective-permute-start | bytes 294920 | tf_op jit(solution)/shard_map/ppermute | solution.py:650
  259.3 3.7 collective-permute-start.16
  266.5 3.5 collective-permute-done.17
  272.1 4.6 all-to-all-start.1
  295.2 4.1 collective-permute-done.37
  303.0 4.1 collective-permute-done.38
  311.2 34.6 %collective-permute-done.39 = bf16[48,512]{1,0:T(8,128)(2,1)S(1)} collective-permute-done((bf16[48,512]{1,0:T(8,128)(2,1)S(1)}, bf16[48,512]{1,0:T(8,128)(2,1)S(1)}, u32[]{:S(2)}, u32[]{:S(2)}) %collective-permute-start.39) | collective-permute-done | bytes 49184 | tf_op jit(solution)/shard_map/ppermute | solution.py:634
  345.8 21.0 %collective-permute-start.27 = (bf16[48,512]{1,0:T(8,128)(2,1)S(1)}, bf16[48,512]{1,0:T(8,128)(2,1)S(1)}, u32[]{:S(2)}, u32[]{:S(2)}) collective-permute-start(bf16[48,512]{1,0:T(8,128)(2,1)S(1)} %get-tuple-element.107), channel_id=1, source_target_pairs={{0,1},{1,2},{2,3},{3,0},{4,5},{5,6},{6,7},{7,4},{8,9},{9,10},{10,1... | collective-permute-start | bytes 147464 | tf_op jit(solution)/shard_map/ppermute | solution.py:634
  366.8 3.7 collective-permute-done.40
  378.1 21.3 %collective-permute-done.42 = bf16[48,512]{1,0:T(8,128)(2,1)S(1)} collective-permute-done((bf16[48,512]{1,0:T(8,128)(2,1)S(1)}, bf16[48,512]{1,0:T(8,128)(2,1)S(1)}, u32[]{:S(2)}, u32[]{:S(2)}) %collective-permute-start.42) | collective-permute-done | bytes 49184 | tf_op jit(solution)/shard_map/ppermute | solution.py:634
  411.3 4.4 collective-permute-done.45
  430.1 20.2 %gather_fusion.1 = bf16[4096,512]{1,0:T(8,128)(2,1)} fusion(bf16[4096,512]{1,0:T(8,128)(2,1)} %bitcast.26, s32[4096]{0:T(1024)S(1)} %copy-done.43), kind=kCustom, calls=%fused_computation.1 | custom fusion | bytes 8404992 | tf_op jit(solution)/shard_map/jit(_take)/gather | solution.py:937
  450.3 6.8 %convert_element_type.131 = f32[4096,512]{1,0:T(8,128)} convert(bf16[4096,512]{1,0:T(8,128)(2,1)} %gather_fusion.1) | non-fusion elementwise | flops 2097152 | bytes 12582912 | tf_op jit(solution)/shard_map/convert_element_type | solution.py:939
  (287 shorter events, 151.9 us)
Async XLA Ops:
  9.3 30.0 %all-to-all-start = ((bf16[8,128,512]{2,1,0:T(8,128)(2,1)}), bf16[8,128,512]{2,1,0:T(8,128)(2,1)}, u32[]{:S(2)}, u32[]{:S(2)}) async-start(bf16[8,128,512]{2,1,0:T(8,128)(2,1)} %bitcast.11), calls=%async_computation | async-start | bytes 2097152 | tf_op jit(solution)/shard_map/all_to_all | solution.py:762
  15.4 30.7 %collective-permute-start = (bf16[1,512]{1,0:T(2,128)(2,1)S(1)}, bf16[1,512]{1,0:T(2,128)(2,1)S(1)}, u32[]{:S(2)}, u32[]{:S(2)}) collective-permute-start(bf16[1,512]{1,0:T(2,128)(2,1)S(1)} %get-tuple-element.83), channel_id=1, source_target_pairs={{0,1},{1,2},{2,3},{4,5},{5,6},{6,7},{8,9},{9,10},{10,11},{12,13},{... | collective-permute-start | bytes 3080 | tf_op jit(solution)/shard_map/ppermute | solution.py:645
  19.4 26.7 %collective-permute-start.1 = (bf16[1,512]{1,0:T(2,128)(2,1)S(1)}, bf16[1,512]{1,0:T(2,128)(2,1)S(1)}, u32[]{:S(2)}, u32[]{:S(2)}) collective-permute-start(bf16[1,512]{1,0:T(2,128)(2,1)S(1)} %get-tuple-element.82), channel_id=1, source_target_pairs={{1,0},{2,1},{3,2},{5,4},{6,5},{7,6},{9,8},{10,9},{11,10},{13,12},{... | collective-permute-start | bytes 3080 | tf_op jit(solution)/shard_map/ppermute | solution.py:645
  40.3 26.7 %collective-permute-start.2 = (bf16[64,512]{1,0:T(8,128)(2,1)S(1)}, bf16[64,512]{1,0:T(8,128)(2,1)S(1)}, u32[]{:S(2)}, u32[]{:S(2)}) collective-permute-start(bf16[64,512]{1,0:T(8,128)(2,1)S(1)} %get-tuple-element.91), channel_id=1, source_target_pairs={{0,1},{1,2},{2,3},{4,5},{5,6},{6,7},{8,9},{9,10},{10,11},{12,13},{... | collective-permute-start | bytes 196616 | tf_op jit(solution)/shard_map/ppermute | solution.py:645
  44.8 22.1 %collective-permute-start.3 = (bf16[64,512]{1,0:T(8,128)(2,1)S(1)}, bf16[64,512]{1,0:T(8,128)(2,1)S(1)}, u32[]{:S(2)}, u32[]{:S(2)}) collective-permute-start(bf16[64,512]{1,0:T(8,128)(2,1)S(1)} %get-tuple-element.90), channel_id=1, source_target_pairs={{1,0},{2,1},{3,2},{5,4},{6,5},{7,6},{9,8},{10,9},{11,10},{13,12},{... | collective-permute-start | bytes 196616 | tf_op jit(solution)/shard_map/ppermute | solution.py:645
  82.2 8.2 %collective-permute-start.4 = (f32[24,512]{1,0:T(8,128)S(1)}, f32[24,512]{1,0:T(8,128)}, u32[]{:S(2)}, u32[]{:S(2)}) collective-permute-start(f32[24,512]{1,0:T(8,128)S(1)} %get-tuple-element.59.own_ref), channel_id=1, source_target_pairs={{0,1},{1,2},{2,3},{3,0},{4,5},{5,6},{6,7},{7,4},{8,9},{9,10},{10,1... | collective-permute-start | bytes 147464 | tf_op jit(solution)/shard_map/ppermute | solution.py:634
  141.6 37.7 %collective-permute-start.10 = (f32[24,512]{1,0:T(8,128)S(1)}, f32[24,512]{1,0:T(8,128)S(1)}, u32[]{:S(2)}, u32[]{:S(2)}) collective-permute-start(f32[24,512]{1,0:T(8,128)S(1)} %get-tuple-element.64.own_ref), channel_id=1, source_target_pairs={{0,1},{1,2},{2,3},{3,0},{4,5},{5,6},{6,7},{7,4},{8,9},{9,10},{10,1... | collective-permute-start | bytes 147464 | tf_op jit(solution)/shard_map/ppermute | solution.py:634
  142.7 36.7 %collective-permute-start.11 = (f32[24,512]{1,0:T(8,128)S(1)}, f32[24,512]{1,0:T(8,128)S(1)}, u32[]{:S(2)}, u32[]{:S(2)}) collective-permute-start(f32[24,512]{1,0:T(8,128)S(1)} %get-tuple-element.64.own_ref), channel_id=1, source_target_pairs={{0,2},{1,3},{2,0},{3,1},{4,6},{5,7},{6,4},{7,5},{8,10},{9,11},{10,... | collective-permute-start | bytes 147464 | tf_op jit(solution)/shard_map/ppermute | solution.py:634
  144.7 34.7 %collective-permute-start.12 = (f32[24,512]{1,0:T(8,128)S(1)}, f32[24,512]{1,0:T(8,128)S(1)}, u32[]{:S(2)}, u32[]{:S(2)}) collective-permute-start(f32[24,512]{1,0:T(8,128)S(1)} %get-tuple-element.64.own_ref), channel_id=1, source_target_pairs={{0,3},{1,0},{2,1},{3,2},{4,7},{5,4},{6,5},{7,6},{8,11},{9,8},{10,9... | collective-permute-start | bytes 147464 | tf_op jit(solution)/shard_map/ppermute | solution.py:634
  160.7 124.1 %collective-permute-start.36 = (bf16[768,512]{1,0:T(8,128)(2,1)}, bf16[768,512]{1,0:T(8,128)(2,1)}, u32[]{:S(2)}, u32[]{:S(2)}) collective-permute-start(bf16[768,512]{1,0:T(8,128)(2,1)} %dynamic-slice_convert_fusion), channel_id=1, source_target_pairs={{0,4},{4,0},{8,12},{12,8},{16,20},{20,16},{24,28},{28,24},{1,5},{5... | collective-permute-start | bytes 2359304 | tf_op jit(solution)/shard_map/ppermute | solution.py:650
  205.5 22.8 %collective-permute-start.13 = (f32[24,512]{1,0:T(8,128)S(1)}, f32[24,512]{1,0:T(8,128)S(1)}, u32[]{:S(2)}, u32[]{:S(2)}) collective-permute-start(f32[24,512]{1,0:T(8,128)S(1)} %get-tuple-element.69.own_ref), channel_id=1, source_target_pairs={{0,1},{1,2},{2,3},{3,0},{4,5},{5,6},{6,7},{7,4},{8,9},{9,10},{10,1... | collective-permute-start | bytes 147464 | tf_op jit(solution)/shard_map/ppermute | solution.py:634
  206.6 21.7 %collective-permute-start.14 = (f32[24,512]{1,0:T(8,128)S(1)}, f32[24,512]{1,0:T(8,128)S(1)}, u32[]{:S(2)}, u32[]{:S(2)}) collective-permute-start(f32[24,512]{1,0:T(8,128)S(1)} %get-tuple-element.69.own_ref), channel_id=1, source_target_pairs={{0,2},{1,3},{2,0},{3,1},{4,6},{5,7},{6,4},{7,5},{8,10},{9,11},{10,... | collective-permute-start | bytes 147464 | tf_op jit(solution)/shard_map/ppermute | solution.py:634
  208.1 20.1 %collective-permute-start.15 = (f32[24,512]{1,0:T(8,128)S(1)}, f32[24,512]{1,0:T(8,128)S(1)}, u32[]{:S(2)}, u32[]{:S(2)}) collective-permute-start(f32[24,512]{1,0:T(8,128)S(1)} %get-tuple-element.69.own_ref), channel_id=1, source_target_pairs={{0,3},{1,0},{2,1},{3,2},{4,7},{5,4},{6,5},{7,6},{8,11},{9,8},{10,9... | collective-permute-start | bytes 147464 | tf_op jit(solution)/shard_map/ppermute | solution.py:634
  223.3 64.7 %collective-permute-start.24 = (bf16[768,512]{1,0:T(8,128)(2,1)}, bf16[768,512]{1,0:T(8,128)(2,1)}, u32[]{:S(2)}, u32[]{:S(2)}) collective-permute-start(bf16[768,512]{1,0:T(8,128)(2,1)} %dynamic-slice_convert_fusion.1), channel_id=1, source_target_pairs={{0,4},{4,0},{8,12},{12,8},{16,20},{20,16},{24,28},{28,24},{1,5},{5... | collective-permute-start | bytes 2359304 | tf_op jit(solution)/shard_map/ppermute | solution.py:650
  251.3 12.9 %collective-permute-start.22 = (f32[2,24,512]{2,1,0:T(8,128)S(1)}, f32[2,24,512]{2,1,0:T(8,128)S(1)}, u32[]{:S(2)}, u32[]{:S(2)}) collective-permute-start(f32[2,24,512]{2,1,0:T(8,128)S(1)} %pad_maximum_fusion.6), channel_id=1, source_target_pairs={{0,8},{4,12},{8,0},{12,4},{16,24},{20,28},{24,16},{28,20},{1,9},{5... | collective-permute-start | bytes 294920 | tf_op jit(solution)/shard_map/ppermute | solution.py:650
  265.0 11.7 %collective-permute-start.23 = (f32[4,24,512]{2,1,0:T(8,128)}, f32[4,24,512]{2,1,0:T(8,128)}, u32[]{:S(2)}, u32[]{:S(2)}) collective-permute-start(f32[4,24,512]{2,1,0:T(8,128)} %pad_maximum_fusion.5), channel_id=1, source_target_pairs={{0,16},{4,20},{8,24},{12,28},{16,0},{20,4},{24,8},{28,12},{1,17},{... | collective-permute-start | bytes 589832 | tf_op jit(solution)/shard_map/ppermute | solution.py:650
  272.1 22.3 %all-to-all-start.1 = ((bf16[8,128,512]{2,1,0:T(8,128)(2,1)}), bf16[8,128,512]{2,1,0:T(8,128)(2,1)}, u32[]{:S(2)}, u32[]{:S(2)}) async-start(bf16[8,128,512]{2,1,0:T(8,128)(2,1)} %bitcast.116), calls=%async_computation.1 | async-start | bytes 2097152 | tf_op jit(solution)/shard_map/all_to_all | solution.py:923
  286.3 13.0 %collective-permute-start.37 = (bf16[384,512]{1,0:T(8,128)(2,1)S(1)}, bf16[384,512]{1,0:T(8,128)(2,1)S(1)}, u32[]{:S(2)}, u32[]{:S(2)}) collective-permute-start(bf16[384,512]{1,0:T(8,128)(2,1)S(1)} %dynamic-slice_convert_fusion.2), channel_id=1, source_target_pairs={{0,8},{4,12},{8,0},{12,4},{16,24},{20,28},{24,16},{28,20},{1,9},{5... | collective-permute-start | bytes 1179656 | tf_op jit(solution)/shard_map/ppermute | solution.py:650
  290.3 11.9 %collective-permute-start.25 = (bf16[384,512]{1,0:T(8,128)(2,1)}, bf16[384,512]{1,0:T(8,128)(2,1)S(1)}, u32[]{:S(2)}, u32[]{:S(2)}) collective-permute-start(bf16[384,512]{1,0:T(8,128)(2,1)} %dynamic-slice_convert_fusion.3), channel_id=1, source_target_pairs={{0,16},{4,20},{8,24},{12,28},{16,0},{20,4},{24,8},{28,12},{1,17},{... | collective-permute-start | bytes 1179656 | tf_op jit(solution)/shard_map/ppermute | solution.py:650
  294.4 132.4 %collective-permute-start.18 = (bf16[8,128,512]{2,1,0:T(8,128)(2,1)}, bf16[8,128,512]{2,1,0:T(8,128)(2,1)S(1)}, u32[]{:S(2)}, u32[]{:S(2)}) collective-permute-start(bf16[8,128,512]{2,1,0:T(8,128)(2,1)} %all-to-all-done.1), channel_id=1, source_target_pairs={{0,1},{1,2},{2,3},{3,0},{4,5},{5,6},{6,7},{7,4},{8,9},{9,10},{10,1... | collective-permute-start | bytes 3145736 | tf_op jit(solution)/shard_map/ppermute | solution.py:634
  294.7 133.2 %collective-permute-start.19 = (bf16[8,128,512]{2,1,0:T(8,128)(2,1)}, bf16[8,128,512]{2,1,0:T(8,128)(2,1)S(1)}, u32[]{:S(2)}, u32[]{:S(2)}) collective-permute-start(bf16[8,128,512]{2,1,0:T(8,128)(2,1)} %all-to-all-done.1), channel_id=1, source_target_pairs={{0,2},{1,3},{2,0},{3,1},{4,6},{5,7},{6,4},{7,5},{8,10},{9,11},{10,... | collective-permute-start | bytes 3145736 | tf_op jit(solution)/shard_map/ppermute | solution.py:634
  307.2 38.5 %collective-permute-start.39 = (bf16[48,512]{1,0:T(8,128)(2,1)S(1)}, bf16[48,512]{1,0:T(8,128)(2,1)S(1)}, u32[]{:S(2)}, u32[]{:S(2)}) collective-permute-start(bf16[48,512]{1,0:T(8,128)(2,1)S(1)} %get-tuple-element.100), channel_id=1, source_target_pairs={{0,1},{1,2},{2,3},{3,0},{4,5},{5,6},{6,7},{7,4},{8,9},{9,10},{10,1... | collective-permute-start | bytes 147464 | tf_op jit(solution)/shard_map/ppermute | solution.py:634
  307.5 62.9 %collective-permute-start.40 = (bf16[48,512]{1,0:T(8,128)(2,1)S(1)}, bf16[48,512]{1,0:T(8,128)(2,1)S(1)}, u32[]{:S(2)}, u32[]{:S(2)}) collective-permute-start(bf16[48,512]{1,0:T(8,128)(2,1)S(1)} %get-tuple-element.102), channel_id=1, source_target_pairs={{0,2},{1,3},{2,0},{3,1},{4,6},{5,7},{6,4},{7,5},{8,10},{9,11},{10,... | collective-permute-start | bytes 147464 | tf_op jit(solution)/shard_map/ppermute | solution.py:634
  308.5 61.9 %collective-permute-start.41 = (bf16[48,512]{1,0:T(8,128)(2,1)S(1)}, bf16[48,512]{1,0:T(8,128)(2,1)S(1)}, u32[]{:S(2)}, u32[]{:S(2)}) collective-permute-start(bf16[48,512]{1,0:T(8,128)(2,1)S(1)} %get-tuple-element.101), channel_id=1, source_target_pairs={{0,3},{1,0},{2,1},{3,2},{4,7},{5,4},{6,5},{7,6},{8,11},{9,8},{10,9... | collective-permute-start | bytes 147464 | tf_op jit(solution)/shard_map/ppermute | solution.py:634
  345.8 25.9 %collective-permute-start.27 = (bf16[48,512]{1,0:T(8,128)(2,1)S(1)}, bf16[48,512]{1,0:T(8,128)(2,1)S(1)}, u32[]{:S(2)}, u32[]{:S(2)}) collective-permute-start(bf16[48,512]{1,0:T(8,128)(2,1)S(1)} %get-tuple-element.107), channel_id=1, source_target_pairs={{0,1},{1,2},{2,3},{3,0},{4,5},{5,6},{6,7},{7,4},{8,9},{9,10},{10,1... | collective-permute-start | bytes 147464 | tf_op jit(solution)/shard_map/ppermute | solution.py:634
  371.7 57.3 %collective-permute-start.20 = (bf16[8,128,512]{2,1,0:T(8,128)(2,1)}, bf16[8,128,512]{2,1,0:T(8,128)(2,1)S(1)}, u32[]{:S(2)}, u32[]{:S(2)}) collective-permute-start(bf16[8,128,512]{2,1,0:T(8,128)(2,1)} %all-to-all-done.1), channel_id=1, source_target_pairs={{0,3},{1,0},{2,1},{3,2},{4,7},{5,4},{6,5},{7,6},{8,11},{9,8},{10,9... | collective-permute-start | bytes 3145736 | tf_op jit(solution)/shard_map/ppermute | solution.py:634
  376.0 23.4 %collective-permute-start.42 = (bf16[48,512]{1,0:T(8,128)(2,1)S(1)}, bf16[48,512]{1,0:T(8,128)(2,1)S(1)}, u32[]{:S(2)}, u32[]{:S(2)}) collective-permute-start(bf16[48,512]{1,0:T(8,128)(2,1)S(1)} %get-tuple-element.79), channel_id=1, source_target_pairs={{0,1},{1,2},{2,3},{3,0},{4,5},{5,6},{6,7},{7,4},{8,9},{9,10},{10,1... | collective-permute-start | bytes 147464 | tf_op jit(solution)/shard_map/ppermute | solution.py:634
  376.0 24.7 %collective-permute-start.43 = (bf16[48,512]{1,0:T(8,128)(2,1)S(1)}, bf16[48,512]{1,0:T(8,128)(2,1)S(1)}, u32[]{:S(2)}, u32[]{:S(2)}) collective-permute-start(bf16[48,512]{1,0:T(8,128)(2,1)S(1)} %get-tuple-element.79), channel_id=1, source_target_pairs={{0,2},{1,3},{2,0},{3,1},{4,6},{5,7},{6,4},{7,5},{8,10},{9,11},{10,... | collective-permute-start | bytes 147464 | tf_op jit(solution)/shard_map/ppermute | solution.py:634
  415.7 8.4 %collective-permute-start.46 = (bf16[384,512]{1,0:T(8,128)(2,1)S(1)}, bf16[384,512]{1,0:T(8,128)(2,1)S(1)}, u32[]{:S(2)}, u32[]{:S(2)}) collective-permute-start(bf16[384,512]{1,0:T(8,128)(2,1)S(1)} %pad_maximum_fusion.4), channel_id=1, source_target_pairs={{0,8},{4,12},{8,0},{12,4},{16,24},{20,28},{24,16},{28,20},{1,9},{5... | collective-permute-start | bytes 1179656 | tf_op jit(solution)/shard_map/ppermute | solution.py:650
  418.7 7.8 %collective-permute-start.34 = (bf16[384,512]{1,0:T(8,128)(2,1)S(1)}, bf16[384,512]{1,0:T(8,128)(2,1)S(1)}, u32[]{:S(2)}, u32[]{:S(2)}) collective-permute-start(bf16[384,512]{1,0:T(8,128)(2,1)S(1)} %pad_maximum_fusion.3), channel_id=1, source_target_pairs={{0,16},{4,20},{8,24},{12,28},{16,0},{20,4},{24,8},{28,12},{1,17},{... | collective-permute-start | bytes 1179656 | tf_op jit(solution)/shard_map/ppermute | solution.py:650
  424.3 32.8 %collective-permute-start.47 = (bf16[768,512]{1,0:T(8,128)(2,1)S(1)}, bf16[768,512]{1,0:T(8,128)(2,1)}, u32[]{:S(2)}, u32[]{:S(2)}) collective-permute-start(bf16[768,512]{1,0:T(8,128)(2,1)S(1)} %pad_maximum_fusion.2), channel_id=1, source_target_pairs={{0,4},{4,0},{8,12},{12,8},{16,20},{20,16},{24,28},{28,24},{1,5},{5... | collective-permute-start | bytes 2359304 | tf_op jit(solution)/shard_map/ppermute | solution.py:650
  426.8 33.9 %collective-permute-start.35 = (bf16[768,512]{1,0:T(8,128)(2,1)S(1)}, bf16[768,512]{1,0:T(8,128)(2,1)}, u32[]{:S(2)}, u32[]{:S(2)}) collective-permute-start(bf16[768,512]{1,0:T(8,128)(2,1)S(1)} %pad_maximum_fusion.1), channel_id=1, source_target_pairs={{0,4},{4,0},{8,12},{12,8},{16,20},{20,16},{24,28},{28,24},{1,5},{5... | collective-permute-start | bytes 2359304 | tf_op jit(solution)/shard_map/ppermute | solution.py:650
  (75 other events, 810.4 us)

commit v2 on v1

v2 whole, which is shorter than its diff:
```python
import functools

import jax
import jax.numpy as jnp
from jax import lax
from jax.experimental import pallas as pl
from jax.experimental.pallas import tpu as pltpu
from jax.sharding import PartitionSpec as P

EPSILON = 1e-05
ROOT_HALF = 0.7071067811865476
PRECISE = lax.Precision.HIGHEST
F32, BF16, I32 = jnp.float32, jnp.bfloat16, jnp.int32
UTTS = 4
PAD = 16
ROWS = 1024
BLOCK = 128
WIDE = 256
MIB = 2**20

STAT_ROWS = 24
FIRST_ROW, LAST_ROW, EXTRA_ROW = 16, 17, 18
SMALL_ROWS = 48
BITS_AT = 12


def owner_at(ends, position):
    return sum((position >= end).astype(I32) for end in ends)


def tile_of(ref, index, offset=0):
    return ref.at[pl.ds(pl.multiple_of(offset + index * ROWS, PAD), ROWS), :]


class Stream:
    def __init__(self, source, target, sems, source_offset=0, target_offset=0):
        self.ends = (source, source_offset, target, target_offset)
        self.sems = sems
        self.tiles = sems.shape[0]

    def tile(self, index):
        source, source_offset, target, target_offset = self.ends
        return pltpu.make_async_copy(
            tile_of(source, index, source_offset),
            tile_of(target, index, target_offset),
            self.sems.at[index],
        )

    def start(self):
        for index in range(self.tiles):
            self.tile(index).start()

    def finish(self):
        for index in range(self.tiles):
            self.tile(index).wait()


def edge_copies(source, target, sems):
    last = source.shape[0] - PAD
    return [
        pltpu.make_async_copy(
            source.at[pl.ds(at, PAD), :], target.at[pl.ds(at, PAD), :], sems.at[k]
        )
        for k, at in enumerate((0, last))
    ]


def rows_of(start, shape):
    return start + lax.broadcasted_iota(I32, shape, 0)


def fold_rows(values):
    return jnp.sum(values.reshape(values.shape[0] // 8, 8, values.shape[1]), axis=0)


def by_utterance(ends, start, count, uniform_body, mixed_body):
    low, high = owner_at(ends, start), owner_at(ends, start + count - 1)

    @pl.when(low == high)
    def _():
        uniform_body(low)

    @pl.when(low != high)
    def _():
        def step(u, carry):
            lower = jnp.int32(-1)
            upper = jnp.int32(2**30)
            for k in range(UTTS):
                lower = jnp.where(u == k + 1, ends[k], lower)
                upper = jnp.where(u == k, ends[k], upper)

            def mask(shape):
                rows = rows_of(start, shape)
                return (rows >= lower) & (rows < upper)

            mixed_body(u, mask)
            return carry

        lax.fori_loop(low, high + 1, step, 0)


def row(ref, index):
    return ref[pl.ds(index, 1), :]


def logistic(values):
    return 0.5 * jnp.tanh(0.5 * values) + 0.5


def taps_of(padded_ref, ends, start, base):
    channels = padded_ref.shape[1]
    block = padded_ref[pl.ds(start, ROWS + 2 * PAD), :].astype(F32)
    positions = rows_of(base + start, (ROWS, channels))
    cut_left = positions == ends[0]
    cut_right = positions + 1 == ends[0]
    for end in ends[1:]:
        cut_left = cut_left | (positions == end)
        cut_right = cut_right | (positions + 1 == end)
    before = jnp.where(cut_left, 0.0, block[PAD - 1 : PAD - 1 + ROWS]).astype(BF16)
    after = jnp.where(cut_right, 0.0, block[PAD + 1 : PAD + 1 + ROWS]).astype(BF16)
    return before, padded_ref[pl.ds(start + PAD, ROWS), :], after


def convolved(taps, weight_ref):
    channels = weight_ref.shape[1]
    return sum(
        jnp.dot(tap, weight_ref[k * channels : (k + 1) * channels, :], preferred_element_type=F32)
        for k, tap in enumerate(taps)
    )


def for_blocks(first, count, size, body, unroll=1):
    def step(i, carry):
        body(pl.multiple_of(first + i * size, size))
        return carry

    lax.fori_loop(0, count // size, step, 0, unroll=unroll)


def for_tiles(count, body):
    def step(i, carry):
        body(i, pl.multiple_of(i * ROWS, ROWS))
        return carry

    lax.fori_loop(0, count // ROWS, step, 0)


def wait_next(streams, i, count):
    @pl.when(i + 1 < count // ROWS)
    def _():
        for stream in streams:
            stream.tile(i + 1).wait()


def sum_over_tm(own_ref, other_refs, first, count):
    one, two, three = other_refs
    part = pl.ds(first, count)
    return (own_ref[part, :] + two[part, :]) + (one[part, :] + three[part, :])


def finish_stats(acc_ref, stat_ref):
    for kind in range(2):
        for u in range(8):
            at = kind * 8 + u
            if u < UTTS:
                first = (kind * (UTTS + 1) + u) * 8
                stat_ref[at : at + 1, :] = jnp.sum(
                    acc_ref[first : first + 8, :], axis=0, keepdims=True
                )
            else:
                stat_ref[at : at + 1, :] = jnp.zeros_like(stat_ref[at : at + 1, :])
    stat_ref[16:24, :] = jnp.zeros_like(stat_ref[16:24, :])


ACC_ROWS = 2 * (UTTS + 1) * 8


def add_stats(acc_ref, u, first, second):
    for kind, term in enumerate((first, second)):
        at = pl.ds(pl.multiple_of((kind * (UTTS + 1) + u) * 8, 8), 8)
        acc_ref[at, :] += fold_rows(term)


def read_ends(info_ref):
    return [info_ref[k] for k in range(UTTS)]


def halo_owner(info_ref, ends, base, frames):
    before = jnp.where(base == 0, UTTS, owner_at(ends, base - 1))
    return before, owner_at(ends, base + frames)


def gradient_kernel(
    info_ref,
    cot_hbm,
    before_ref,
    after_ref,
    weight_ref,
    out_hbm,
    padded_hbm,
    bias_ref,
    cot_ref,
    padded_ref,
    out_ref,
    cot_sems,
    padded_sems,
    edge_sems,
    out_sems,
):
    frames, channels = cot_ref.shape
    ends = read_ends(info_ref)
    base = info_ref[8]
    cot_in = Stream(cot_hbm, cot_ref, cot_sems)
    padded_out = Stream(padded_ref, padded_hbm, padded_sems, PAD, PAD)
    outward = Stream(out_ref, out_hbm, out_sems)
    cot_in.start()
    owner_before, owner_after = halo_owner(info_ref, ends, base, frames)
    tile = jnp.broadcast_to(before_ref[...].astype(F32) * ROOT_HALF, (PAD, channels))
    padded_ref[0:PAD, :] = jnp.where(owner_before < UTTS, tile, 0.0).astype(BF16)
    tile = jnp.broadcast_to(after_ref[...].astype(F32) * ROOT_HALF, (PAD, channels))
    padded_ref[PAD + frames :, :] = jnp.where(owner_after < UTTS, tile, 0.0).astype(BF16)
    edges = edge_copies(padded_ref, padded_hbm, edge_sems)
    for edge in edges:
        edge.start()
    bias_ref[...] = jnp.zeros_like(bias_ref)

    def scale(start):
        here = cot_ref[pl.ds(start, BLOCK), :].astype(F32) * ROOT_HALF
        here = jnp.where(rows_of(base + start, (BLOCK, channels)) < ends[UTTS - 1], here, 0.0)
        rounded = here.astype(BF16)
        padded_ref[pl.ds(start + PAD, BLOCK), :] = rounded
        bias_ref[...] += fold_rows(rounded.astype(F32))

    def scale_tile(i, start):
        cot_in.tile(i).wait()
        for_blocks(start, ROWS, BLOCK, scale)
        padded_out.tile(i).start()

    for_tiles(frames, scale_tile)

    def conv(i, start):
        before, here, after = taps_of(padded_ref, ends, start, base)
        total = convolved((after, here, before), weight_ref)
        out_ref[pl.ds(start, ROWS), :] = total.astype(BF16)
        outward.tile(i).start()

    for_tiles(frames, conv)
    padded_out.finish()
    outward.finish()
    for edge in edges:
        edge.wait()


def upsample_kernel(
    info_ref,
    offset_ref,
    before_ref,
    own_ref,
    after_ref,
    align_hbm,
    bias_ref,
    out_ref,
    out_hbm,
    wide_hbm,
    stat_ref,
    buffer_ref,
    acc_ref,
    align_ref,
    wide_ref,
    align_sems,
    out_sems,
    wide_sems,
):
    frames, channels = out_ref.shape
    align_in = Stream(align_hbm, align_ref, align_sems)
    outward = Stream(out_ref, out_hbm, out_sems)
    wide_out = Stream(wide_ref, wide_hbm, wide_sems)
    align_in.start()
    window = align_ref.shape[1]
    tiles = offset_ref.shape[0]
    rows = frames // tiles
    halo, own = before_ref.shape[0], own_ref.shape[0]
    ends = read_ends(info_ref)
    slot_ends = [info_ref[UTTS + k] for k in range(UTTS)]
    base, slot_base = info_ref[8], info_ref[9]
    buffer_ref[0:halo, :] = before_ref[...]
    buffer_ref[halo : halo + own, :] = own_ref[...]
    buffer_ref[halo + own : 2 * halo + own, :] = after_ref[...]
    buffer_ref[2 * halo + own :, :] = jnp.zeros_like(buffer_ref[2 * halo + own :, :])
    acc_ref[...] = jnp.zeros_like(acc_ref)

    def step(i):
        start = pl.multiple_of(i * rows, rows)
        shift = offset_ref[i] - slot_base
        aligned = pl.multiple_of((shift // PAD) * PAD, PAD)
        block = align_ref[pl.ds(start, rows), :].astype(F32)
        block = jnp.concatenate([block, jnp.zeros((rows, WIDE - window), F32)], axis=1)
        block = pltpu.roll(block, shift - aligned, 1)
        slots = slot_base + aligned + lax.broadcasted_iota(I32, (rows, WIDE), 1)
        slot_owner = owner_at(slot_ends, slots)
        frame_owner = owner_at(ends, rows_of(base + start, (rows, WIDE)))
        match = (slot_owner == frame_owner) & (frame_owner < UTTS)
        block = jnp.where(match, block, 0.0).astype(BF16)
        wide_ref[pl.ds(start, rows), :] = block
        out_ref[pl.ds(start, rows), :] = jnp.dot(
            block, buffer_ref[pl.ds(aligned, WIDE), :], preferred_element_type=F32
        )

    def blocks(i, start):
        align_in.tile(i).wait()
        each = ROWS // rows

        def four(k, carry):
            for n in range(4):
                step(i * each + k * 4 + n)
            return carry

        lax.fori_loop(0, each // 4, four, 0)
        outward.tile(i).start()
        wide_out.tile(i).start()
        for_blocks(
            start, ROWS, BLOCK, lambda at: value_sums(out_ref, acc_ref, ends, base, at)
        )

    for_tiles(frames, blocks)
    finish_stats(acc_ref, stat_ref)
    stat_ref[FIRST_ROW : FIRST_ROW + 1, :] = out_ref[0:1, :]
    stat_ref[LAST_ROW : LAST_ROW + 1, :] = out_ref[frames - 1 : frames, :]
    stat_ref[EXTRA_ROW : EXTRA_ROW + 1, :] = jnp.sum(bias_ref[...], axis=0, keepdims=True)
    outward.finish()
    wide_out.finish()


def value_sums(out_ref, acc_ref, ends, base, start):
    channels = out_ref.shape[1]

    def uniform(u):
        here = out_ref[pl.ds(start, BLOCK), :]
        add_stats(acc_ref, u, here, here * here)

    def mixed(u, mask):
        here = jnp.where(mask((BLOCK, channels)), out_ref[pl.ds(start, BLOCK), :], 0.0)
        add_stats(acc_ref, u, here, here * here)

    by_utterance(ends, base + start, BLOCK, uniform, mixed)


def write_coefficients(own_ref, other_refs, inverse_ref, params_ref, coef_ref):
    channels = inverse_ref.shape[1]
    inverse = inverse_ref[...]
    total = sum_over_tm(own_ref, other_refs, 0, 8)
    square = sum_over_tm(own_ref, other_refs, 8, 8)
    mean = total * inverse
    real = inverse > 0.0
    rstd = jnp.where(real, lax.rsqrt(square * inverse - mean * mean + EPSILON), 0.0)
    coef_ref[0:8, :] = rstd
    coef_ref[8:16, :] = mean * rstd
    coef_ref[16:24, :] = jnp.where(real, 1.0 + params_ref[:, 0:channels], 0.0)
    coef_ref[24:32, :] = jnp.where(real, params_ref[:, channels : 2 * channels], 0.0)


def unit_of(values, coef_ref, u):
    return values * row(coef_ref, u) - row(coef_ref, 8 + u)


def normed_of(unit, coef_ref, u):
    return unit * row(coef_ref, 16 + u) + row(coef_ref, 24 + u)


def activation(values, coef_ref, u):
    normed = normed_of(unit_of(values, coef_ref, u), coef_ref, u)
    return normed * logistic(normed)


def edge_rows(padded_ref, before, after):
    channels = padded_ref.shape[1]
    padded_ref[0:PAD, :] = jnp.broadcast_to(before, (PAD, channels)).astype(BF16)
    last = padded_ref.shape[0] - PAD
    padded_ref[last:, :] = jnp.broadcast_to(after, (PAD, channels)).astype(BF16)


def first_conv_kernel(
    info_ref,
    values_ref,
    own_ref,
    one_ref,
    two_ref,
    three_ref,
    inverse_ref,
    params_ref,
    weight_ref,
    act_hbm,
    out_ref,
    unit_hbm,
    coef_ref,
    stat_ref,
    acc_ref,
    act_ref,
    unit_ref,
    act_sems,
    edge_sems,
    unit_sems,
):
    frames, channels = values_ref.shape
    act_out = Stream(act_ref, act_hbm, act_sems, PAD, PAD)
    unit_out = Stream(unit_ref, unit_hbm, unit_sems)
    ends = read_ends(info_ref)
    base = info_ref[8]
    write_coefficients(own_ref, (one_ref, two_ref, three_ref), inverse_ref, params_ref, coef_ref)
    acc_ref[...] = jnp.zeros_like(acc_ref)
    owner_before, owner_after = halo_owner(info_ref, ends, base, frames)
    edge_rows(
        act_ref,
        activation(row(one_ref, LAST_ROW), coef_ref, owner_before),
        activation(row(three_ref, FIRST_ROW), coef_ref, owner_after),
    )

    edges = edge_copies(act_ref, act_hbm, edge_sems)
    for edge in edges:
        edge.start()

    def act_step(start):
        here = pl.ds(start, BLOCK)
        there = pl.ds(start + PAD, BLOCK)

        def parts(u):
            unit = unit_of(values_ref[here, :], coef_ref, u)
            normed = normed_of(unit, coef_ref, u)
            return unit, normed * logistic(normed)

        def uniform(u):
            unit, act = parts(u)
            unit_ref[here, :] = unit.astype(BF16)
            act_ref[there, :] = act.astype(BF16)

        def mixed(u, mask):
            keep = mask((BLOCK, channels))
            unit, act = parts(u)
            unit_ref[here, :] = jnp.where(keep, unit, unit_ref[here, :].astype(F32)).astype(BF16)
            act_ref[there, :] = jnp.where(keep, act, act_ref[there, :].astype(F32)).astype(BF16)

        by_utterance(ends, base + start, BLOCK, uniform, mixed)

    def act_tile(i, start):
        for_blocks(start, ROWS, BLOCK, act_step)
        act_out.tile(i).start()
        unit_out.tile(i).start()

    for_tiles(frames, act_tile)

    def conv(start):
        out_ref[pl.ds(start, ROWS), :] = convolved(
            taps_of(act_ref, ends, start, base), weight_ref
        )

    for_blocks(0, frames, ROWS, conv)
    for_blocks(0, frames, BLOCK, lambda start: value_sums(out_ref, acc_ref, ends, base, start))
    finish_stats(acc_ref, stat_ref)
    stat_ref[FIRST_ROW : FIRST_ROW + 1, :] = out_ref[0:1, :]
    stat_ref[LAST_ROW : LAST_ROW + 1, :] = out_ref[frames - 1 : frames, :]
    act_out.finish()
    unit_out.finish()
    for edge in edges:
        edge.wait()


def slope_and_sums(gradient, unit, coef_ref, u):
    normed = normed_of(unit, coef_ref, u)
    gate = logistic(normed)
    act = normed * gate
    inner = gradient * (gate + act * (1.0 - gate))
    return act, inner, inner * unit


def second_norm_kernel(
    info_ref,
    gradient_hbm,
    values_ref,
    own_ref,
    one_ref,
    two_ref,
    three_ref,
    inverse_ref,
    params_ref,
    act_ref,
    act_hbm,
    inner_hbm,
    unit_hbm,
    coef_ref,
    stat_ref,
    acc_ref,
    gradient_ref,
    inner_ref,
    unit_ref,
    gradient_sems,
    act_sems,
    edge_sems,
    inner_sems,
    unit_sems,
):
    frames, channels = values_ref.shape
    gradient_in = Stream(gradient_hbm, gradient_ref, gradient_sems)
    outward = [
        Stream(act_ref, act_hbm, act_sems, PAD, PAD),
        Stream(inner_ref, inner_hbm, inner_sems),
        Stream(unit_ref, unit_hbm, unit_sems),
    ]
    gradient_in.start()
    ends = read_ends(info_ref)
    base = info_ref[8]
    write_coefficients(own_ref, (one_ref, two_ref, three_ref), inverse_ref, params_ref, coef_ref)
    acc_ref[...] = jnp.zeros_like(acc_ref)
    owner_before, owner_after = halo_owner(info_ref, ends, base, frames)
    edge_rows(
        act_ref,
        activation(row(one_ref, LAST_ROW), coef_ref, owner_before),
        activation(row(three_ref, FIRST_ROW), coef_ref, owner_after),
    )

    edges = edge_copies(act_ref, act_hbm, edge_sems)
    for edge in edges:
        edge.start()

    def step(start):
        here = pl.ds(start, BLOCK)
        there = pl.ds(start + PAD, BLOCK)

        def parts(u):
            unit = unit_of(values_ref[here, :], coef_ref, u)
            return unit, *slope_and_sums(gradient_ref[here, :].astype(F32), unit, coef_ref, u)

        def uniform(u):
            unit, act, inner, cross = parts(u)
            act_ref[there, :] = act.astype(BF16)
            unit_ref[here, :] = unit.astype(BF16)
            inner_ref[here, :] = inner.astype(BF16)
            add_stats(acc_ref, u, inner, cross)

        def mixed(u, mask):
            keep = mask((BLOCK, channels))
            unit, act, inner, cross = parts(u)
            act_ref[there, :] = jnp.where(keep, act, act_ref[there, :].astype(F32)).astype(BF16)
            unit_ref[here, :] = jnp.where(keep, unit, unit_ref[here, :].astype(F32)).astype(BF16)
            old = inner_ref[here, :].astype(F32)
            inner_ref[here, :] = jnp.where(keep, inner, old).astype(BF16)
            add_stats(acc_ref, u, jnp.where(keep, inner, 0.0), jnp.where(keep, cross, 0.0))

        by_utterance(ends, base + start, BLOCK, uniform, mixed)

    def tile(i, start):
        gradient_in.tile(i).wait()
        for_blocks(start, ROWS, BLOCK, step)
        for stream in outward:
            stream.tile(i).start()

    for_tiles(frames, tile)
    finish_stats(acc_ref, stat_ref)
    stat_ref[FIRST_ROW : FIRST_ROW + 1, :] = inner_ref[0:PAD, :].astype(F32)[0:1]
    stat_ref[LAST_ROW : LAST_ROW + 1, :] = inner_ref[frames - PAD :, :].astype(F32)[PAD - 1 :]
    for stream in outward:
        stream.finish()
    for edge in edges:
        edge.wait()


def second_conv_kernel(
    info_ref,
    act_hbm,
    values_hbm,
    weight_ref,
    bias_ref,
    out_hbm,
    act_ref,
    values_ref,
    out_ref,
    act_sems,
    edge_sems,
    values_sems,
    out_sems,
):
    frames, channels = values_ref.shape
    ends = read_ends(info_ref)
    base = info_ref[8]
    bias = bias_ref[...].astype(F32)
    act_in = Stream(act_hbm, act_ref, act_sems, PAD, PAD)
    values_in = Stream(values_hbm, values_ref, values_sems)
    outward = Stream(out_ref, out_hbm, out_sems)
    edges = edge_copies(act_hbm, act_ref, edge_sems)
    for edge in edges:
        edge.start()
    act_in.start()
    values_in.start()
    for edge in edges:
        edge.wait()
    act_in.tile(0).wait()

    def step(i, start):
        here = pl.ds(start, ROWS)
        wait_next([act_in], i, frames)
        values_in.tile(i).wait()
        branch = convolved(taps_of(act_ref, ends, start, base), weight_ref) + bias
        valid = rows_of(base + start, (ROWS, channels)) < ends[UTTS - 1]
        total = jnp.where(valid, (values_ref[here, :] + branch) * ROOT_HALF, 0.0)
        out_ref[here, :] = total.astype(BF16)
        outward.tile(i).start()

    for_tiles(frames, step)
    outward.finish()


def weight_gradient_kernel(
    stream_act,
    info_ref,
    act_any,
    gradient_any,
    keep_ref,
    give_ref,
    out_ref,
    held_ref,
    held_sems,
    edge_sems,
):
    frames = held_ref.shape[0] - 2 * PAD
    channels = held_ref.shape[1]
    ends = read_ends(info_ref)
    base = info_ref[8]
    source = act_any if stream_act else gradient_any
    act_ref, gradient_ref = (held_ref, gradient_any) if stream_act else (act_any, held_ref)
    inward_stream = Stream(source, held_ref, held_sems, PAD, PAD)
    edges = edge_copies(source, held_ref, edge_sems)
    for edge in edges:
        edge.start()
    inward_stream.start()
    out_ref[...] = jnp.zeros_like(out_ref)
    for edge in edges:
        edge.wait()
    inward_stream.tile(0).wait()

    def step(i, start):
        wait_next([inward_stream], i, frames)
        before, here, after = taps_of(gradient_ref, ends, start, base)
        act = act_ref[pl.ds(start + PAD, ROWS), :]
        for k, tap in enumerate((after, here, before)):
            out_ref[k * channels : (k + 1) * channels, :] += lax.dot_general(
                act, tap, (((0,), (0,)), ((), ())), preferred_element_type=F32
            )

    for_tiles(frames, step)
    write_halves(info_ref, 0, out_ref, keep_ref, give_ref)


def write_halves(info_ref, bit, total_ref, keep_ref, give_ref):
    half = keep_ref.shape[0]
    mine = info_ref[BITS_AT + bit]
    keep_ref[...] = total_ref[pl.ds(pl.multiple_of(mine * half, PAD), half), :]
    give_ref[...] = total_ref[pl.ds(pl.multiple_of((1 - mine) * half, PAD), half), :].astype(BF16)


def halves_kernel(bits, info_ref, *refs):
    count = len(bits)
    inputs, outputs, totals = refs[: 2 * count], refs[2 * count : 4 * count], refs[4 * count :]
    for k, bit in enumerate(bits):
        totals[k][...] = inputs[2 * k][...] + inputs[2 * k + 1][...].astype(F32)
        write_halves(info_ref, bit, totals[k], outputs[2 * k], outputs[2 * k + 1])


def join_kernel(bits, info_ref, *refs):
    count = len(bits)
    for k, bit in enumerate(bits):
        part_ref, other_ref, out_ref = refs[2 * k], refs[2 * k + 1], refs[2 * count + k]
        half = part_ref.shape[0]
        mine = info_ref[BITS_AT + bit]
        out_ref[pl.ds(pl.multiple_of(mine * half, PAD), half), :] = part_ref[...]
        out_ref[pl.ds(pl.multiple_of((1 - mine) * half, PAD), half), :] = other_ref[...]


def block_order(order):
    places = []
    for index in range(1 << (len(order) + 1)):
        source, joined = index & 1, 0
        for at, bit in enumerate(order):
            source = 2 * source + ((index >> bit) & 1)
            joined += ((index >> bit) & 1) << at
        places.append((index & 1, source, joined))
    return places


def final_kernel(
    orders,
    rows,
    info_ref,
    second_ref,
    second_other_ref,
    first_ref,
    first_other_ref,
    second_out_ref,
    first_out_ref,
    first_affine_ref,
    first_shift_ref,
    second_affine_ref,
    second_shift_ref,
    bias_ref,
):
    channels = second_ref.shape[1]
    mine = info_ref[BITS_AT]
    gathered = []
    pairs = (
        (second_ref, second_other_ref, second_out_ref, rows + SMALL_ROWS),
        (first_ref, first_other_ref, first_out_ref, rows),
    )
    for k, (part_ref, other_ref, out_ref, step) in enumerate(pairs):
        for core, source, joined in block_order(orders[k]):
            here = pl.ds(joined * step, step)
            block = jnp.where(
                mine == core, part_ref[here, :].astype(F32), other_ref[here, :].astype(F32)
            )
            out_ref[source * rows : (source + 1) * rows, :] = block[:rows]
            if k == 0:
                gathered.append(block[rows:])
    styles = jnp.concatenate([block[32:40, 0:128] for block in gathered], axis=0)
    for at, (affine_ref, shift_ref) in enumerate(
        ((first_affine_ref, first_shift_ref), (second_affine_ref, second_shift_ref))
    ):
        for side in range(2):
            first = 16 * at + 8 * side
            sums = jnp.concatenate([block[first : first + 8] for block in gathered], axis=0)
            lanes = slice(side * channels, (side + 1) * channels)
            affine_ref[:, lanes] = lax.dot_general(
                styles, sums, (((0,), (0,)), ((), ())), precision=PRECISE
            )
            shift_ref[:, lanes] = jnp.sum(sums, axis=0, keepdims=True)
    biases = jnp.concatenate([block[40:48] for block in gathered], axis=0)
    bias_ref[...] = jnp.sum(biases, axis=0, keepdims=True)


def back_coefficients(own_ref, other_refs, inverse_ref, coef_ref, back_ref):
    inverse = inverse_ref[...]
    total = sum_over_tm(own_ref, other_refs, 0, 8)
    cross = sum_over_tm(own_ref, other_refs, 8, 8)
    scale = coef_ref[0:8, :] * coef_ref[16:24, :]
    back_ref[0:8, :] = total
    back_ref[8:16, :] = cross
    back_ref[16:24, :] = scale * total * inverse
    back_ref[24:32, :] = scale * cross * inverse
    back_ref[32:40, :] = scale


def inward(inner, unit, back_ref, u):
    return inner * row(back_ref, 32 + u) - row(back_ref, 16 + u) - unit * row(back_ref, 24 + u)


def first_back_kernel(
    info_ref,
    inner_hbm,
    unit_two_hbm,
    own_ref,
    one_ref,
    two_ref,
    three_ref,
    middle_one_ref,
    middle_three_ref,
    inverse_ref,
    coef_two_ref,
    coef_one_ref,
    unit_one_hbm,
    weight_ref,
    gradient_ref,
    out_hbm,
    back_ref,
    stat_ref,
    acc_ref,
    full_ref,
    inner_ref,
    unit_two_ref,
    unit_one_ref,
    out_ref,
    inner_sems,
    two_sems,
    one_sems,
    out_sems,
):
    frames, channels = unit_one_ref.shape
    early = [
        Stream(inner_hbm, inner_ref, inner_sems),
        Stream(unit_two_hbm, unit_two_ref, two_sems),
    ]
    late = Stream(unit_one_hbm, unit_one_ref, one_sems)
    outward = Stream(out_ref, out_hbm, out_sems)
    for stream in (*early, late):
        stream.start()
    ends = read_ends(info_ref)
    base = info_ref[8]
    back_coefficients(own_ref, (one_ref, two_ref, three_ref), inverse_ref, coef_two_ref, back_ref)
    acc_ref[...] = jnp.zeros_like(acc_ref)
    owner_before, owner_after = halo_owner(info_ref, ends, base, frames)
    edge_rows(
        gradient_ref,
        inward(
            row(one_ref, LAST_ROW),
            unit_of(row(middle_one_ref, LAST_ROW), coef_two_ref, owner_before),
            back_ref,
            owner_before,
        ),
        inward(
            row(three_ref, FIRST_ROW),
            unit_of(row(middle_three_ref, FIRST_ROW), coef_two_ref, owner_after),
            back_ref,
            owner_after,
        ),
    )

    def back_step(start):
        here = pl.ds(start, BLOCK)
        there = pl.ds(start + PAD, BLOCK)

        def now(u):
            return inward(
                inner_ref[here, :].astype(F32), unit_two_ref[here, :].astype(F32), back_ref, u
            )

        def uniform(u):
            gradient_ref[there, :] = now(u).astype(BF16)

        def mixed(u, mask):
            old = gradient_ref[there, :].astype(F32)
            gradient_ref[there, :] = jnp.where(mask((BLOCK, channels)), now(u), old).astype(BF16)

        by_utterance(ends, base + start, BLOCK, uniform, mixed)

    def back_tile(i, start):
        for stream in early:
            stream.tile(i).wait()
        for_blocks(start, ROWS, BLOCK, back_step)

    for_tiles(frames, back_tile)

    def slope_step(start, row_start):
        here = pl.ds(start, BLOCK)

        def parts(u):
            unit = unit_one_ref[here, :].astype(F32)
            _, inner, cross = slope_and_sums(
                full_ref[pl.ds(row_start, BLOCK), :], unit, coef_one_ref, u
            )
            return inner, cross

        def uniform(u):
            inner, cross = parts(u)
            out_ref[here, :] = inner.astype(BF16)
            add_stats(acc_ref, u, inner, cross)

        def mixed(u, mask):
            keep = mask((BLOCK, channels))
            inner, cross = parts(u)
            old = out_ref[here, :].astype(F32)
            out_ref[here, :] = jnp.where(keep, inner, old).astype(BF16)
            add_stats(acc_ref, u, jnp.where(keep, inner, 0.0), jnp.where(keep, cross, 0.0))

        by_utterance(ends, base + start, BLOCK, uniform, mixed)

    def conv(i, start):
        late.tile(i).wait()
        before, here, after = taps_of(gradient_ref, ends, start, base)
        full_ref[...] = convolved((after, here, before), weight_ref)
        for_blocks(0, ROWS, BLOCK, lambda inside: slope_step(start + inside, inside))
        outward.tile(i).start()

    for_tiles(frames, conv)
    finish_stats(acc_ref, stat_ref)
    outward.finish()


def buffer_gradient_kernel(
    info_ref,
    offset_ref,
    inner_hbm,
    unit_hbm,
    cot_hbm,
    wide_hbm,
    own_ref,
    one_ref,
    two_ref,
    three_ref,
    inverse_ref,
    coef_ref,
    before_ref,
    out_ref,
    after_ref,
    back_ref,
    free_ref,
    up_ref,
    total_ref,
    inner_ref,
    unit_ref,
    cot_ref,
    wide_ref,
    inner_sems,
    unit_sems,
    cot_sems,
    wide_sems,
):
    frames, channels = unit_ref.shape
    streams = [
        Stream(inner_hbm, inner_ref, inner_sems),
        Stream(unit_hbm, unit_ref, unit_sems),
        Stream(cot_hbm, cot_ref, cot_sems),
        Stream(wide_hbm, wide_ref, wide_sems),
    ]
    for index in range(frames // ROWS):
        for stream in streams:
            stream.tile(index).start()
    tiles = offset_ref.shape[0]
    rows = frames // tiles
    halo, own = before_ref.shape[0], out_ref.shape[0]
    ends = read_ends(info_ref)
    base, slot_base = info_ref[8], info_ref[9]
    back_coefficients(own_ref, (one_ref, two_ref, three_ref), inverse_ref, coef_ref, back_ref)
    total_ref[...] = jnp.zeros_like(total_ref)
    span = rows + PAD

    def up_step(start):
        here = pl.ds(start, BLOCK)

        def upward(u):
            lead = cot_ref[here, :].astype(F32) * ROOT_HALF
            return lead + inward(
                inner_ref[here, :].astype(F32), unit_ref[here, :].astype(F32), back_ref, u
            )

        def uniform(u):
            up_ref[here, :] = upward(u).astype(BF16)

        def mixed(u, mask):
            old = up_ref[here, :].astype(F32)
            up_ref[here, :] = jnp.where(mask((BLOCK, channels)), upward(u), old).astype(BF16)

        by_utterance(ends, base + start, BLOCK, uniform, mixed)

    def step(i):
        start = pl.multiple_of(i * rows, rows)
        here = pl.ds(start, rows)
        shift = offset_ref[i] - slot_base
        aligned = pl.multiple_of((shift // PAD) * PAD, PAD)
        part = lax.dot_general(
            wide_ref[here, :], up_ref[here, :], (((0,), (0,)), ((), ())), preferred_element_type=F32
        )
        total_ref[pl.ds(aligned, span), :] += part[0:span]

    def blocks(i, start):
        for stream in streams:
            stream.tile(i).wait()
        for_blocks(start, ROWS, BLOCK, up_step)
        each = ROWS // rows

        def four(k, carry):
            for n in range(4):
                step(i * each + k * 4 + n)
            return carry

        lax.fori_loop(0, each // 4, four, 0)

    for_tiles(frames, blocks)
    before_ref[...] = total_ref[0:halo, :]
    out_ref[...] = total_ref[halo : halo + own, :]
    after_ref[...] = total_ref[halo + own : 2 * halo + own, :]
    groups, copies, half = free_ref.shape[:3]
    for s in range(groups):
        first = halo + (2 * s + (1 if s < groups // 2 else 0)) * half
        rows_out = total_ref[first : first + half, :].astype(BF16)
        for t in range(copies):
            free_ref[s, t] = rows_out


def scatter_kernel(late, info_ref, order_ref, part_ref, *refs):
    out_ref, tmp_ref = refs[-2], refs[-1]
    blocks, half, channels = part_ref.shape
    lanes = channels // 128
    offset = jnp.where(info_ref[11] == 1 - late, half, 0)
    for old_ref in refs[:-2]:

        def copy(start, old_ref=old_ref):
            out_ref[pl.ds(start, ROWS), :] = old_ref[pl.ds(start, ROWS), :]

        for_blocks(0, out_ref.shape[0], ROWS, copy)

    def body(block, carry):
        for b in range(half // 16):
            both = part_ref[block, b * 16 : b * 16 + 16, :].astype(F32)
            for h in range(2):
                for q in range(lanes):
                    tmp_ref[pl.ds(((2 * b + h) * lanes + q) * 8, 8), :] = both[
                        8 * h : 8 * h + 8, q * 128 : (q + 1) * 128
                    ]
        first = block * 2 * half + offset
        for r in range(half):
            to = order_ref[first + r]
            out_ref[pl.ds((to >> 3) * (8 * lanes) + (to & 7), lanes, stride=8), :] = tmp_ref[
                pl.ds((r // 8) * 8 * lanes + r % 8, lanes, stride=8), :
            ]
        return carry

    lax.fori_loop(0, blocks, body, 0)


VM = pl.BlockSpec(memory_space=pltpu.VMEM)
SM = pl.BlockSpec(memory_space=pltpu.SMEM)


HB = pl.BlockSpec(memory_space=pltpu.HBM)


def call(kernel, inputs, outputs, scratch, flops, limit):
    return pl.pallas_call(
        kernel,
        in_specs=[spec for _, spec in inputs],
        out_specs=tuple(spec for _, _, spec in outputs),
        out_shape=tuple(
            pltpu.HBM(shape, dtype) if spec is HB else jax.ShapeDtypeStruct(shape, dtype)
            for shape, dtype, spec in outputs
        ),
        scratch_shapes=[
            pltpu.SemaphoreType.DMA((one,)) if isinstance(one, int) else pltpu.VMEM(*one)
            for one in scratch
        ],
        compiler_params=pltpu.CompilerParams(vmem_limit_bytes=limit * MIB),
        cost_estimate=pl.CostEstimate(flops=flops, bytes_accessed=flops // 200, transcendentals=0),
    )(
        *(
            pltpu.with_memory_space_constraint(array, pltpu.HBM) if spec is HB else array
            for array, spec in inputs
        )
    )


def scattered(old, part, late, info, order):
    half, channels = part.shape[1:]
    lanes = channels // 128
    kept = [] if old is None else [old]
    return pl.pallas_call(
        functools.partial(scatter_kernel, late),
        in_specs=[SM, SM] + [VM] * (1 + len(kept)),
        out_specs=VM,
        out_shape=jax.ShapeDtypeStruct((order.shape[0] * lanes, 128), F32),
        scratch_shapes=[pltpu.VMEM((half * lanes, 128), F32)],
        input_output_aliases={3: 0} if kept else {},
        compiler_params=pltpu.CompilerParams(vmem_limit_bytes=22 * MIB),
        cost_estimate=pl.CostEstimate(flops=10**6, bytes_accessed=10**4, transcendentals=0),
    )(info, order, part, *kept)


def shifted(values, axis, step):
    devices = lax.axis_size(axis)
    return lax.ppermute(values, axis, [(i, (i + step) % devices) for i in range(devices)])


def others_over_tm(values):
    return [shifted(values, "tm", d) for d in (1, 2, 3)]


def from_neighbours(first_rows, last_rows):
    devices = lax.axis_size("tm")
    up = [(i, i + 1) for i in range(devices - 1)]
    down = [(i + 1, i) for i in range(devices - 1)]
    return lax.ppermute(last_rows, "tm", up), lax.ppermute(first_rows, "tm", down)


def swapped(values, bit):
    devices = lax.axis_size("seq")
    return lax.ppermute(values, "seq", [(i, i ^ (1 << bit)) for i in range(devices)])


def after(values, *others):
    return lax.optimization_barrier((values, others))[0]


def summed_over_tm(parts):
    copies, tm_index = lax.axis_size("tm"), lax.axis_index("tm")
    rows, channels = parts[0].shape
    pieces = jnp.stack(parts).reshape(len(parts), copies, rows // copies, channels)
    part = lax.dynamic_index_in_dim(pieces, tm_index, 1, False)
    sent = pieces.astype(BF16)
    for step in (1, 3, 2):
        give = lax.dynamic_index_in_dim(sent, (tm_index + step) % copies, 1, False)
        part = part + shifted(give, "tm", step).astype(F32)
    return part.astype(BF16)


def gathered_over_tm(part):
    copies, tm_index = lax.axis_size("tm"), lax.axis_index("tm")
    count, rows, channels = part.shape
    every = jnp.zeros((count, copies, rows, channels), BF16)
    every = lax.dynamic_update_index_in_dim(every, part, tm_index, 1)
    for step in (1, 3, 2):
        every = lax.dynamic_update_index_in_dim(
            every, shifted(part, "tm", step), (tm_index - step) % copies, 1
        )
    return every.reshape(count, copies * rows, channels)


def on_device(
    phonemes,
    send_order,
    phoneme_counts,
    frame_lengths,
    tile_offsets,
    alignment,
    style_vec,
    first_affine_weight,
    first_affine_bias,
    first_conv_weight,
    second_affine_weight,
    second_affine_bias,
    second_conv_weight,
    second_conv_bias,
    cotangent,
):
    frames, channels = cotangent.shape
    slot_count = phonemes.shape[0]
    groups = lax.axis_size("seq")
    copies = lax.axis_size("tm")
    seq_index, tm_index = lax.axis_index("seq"), lax.axis_index("tm")
    piece_rows = slot_count // groups // copies
    local_rows = slot_count // copies
    tiles = tile_offsets.shape[0]
    window = alignment.shape[1]
    halo = window // 2
    lengths = frame_lengths[0]
    conv_flops = 2 * frames * 3 * channels * channels

    info = jnp.concatenate(
        [
            jnp.cumsum(lengths),
            jnp.cumsum(phoneme_counts[0]),
            (tm_index * frames)[None],
            (tm_index * local_rows - halo)[None],
            tm_index[None],
            (seq_index < groups // 2)[None].astype(I32),
            (seq_index[None] >> jnp.arange(12, dtype=I32)) & 1,
        ]
    ).astype(I32)
    inverse = jnp.zeros((8, channels), F32).at[0:UTTS].set(
        jnp.broadcast_to(1.0 / lengths.astype(F32)[:, None], (UTTS, channels))
    )
    style_rows = jnp.zeros((8, style_vec.shape[1]), BF16).at[0:UTTS].set(style_vec)
    params_one = jnp.dot(style_rows, first_affine_weight, preferred_element_type=F32) + (
        first_affine_bias.astype(F32)
    )
    params_two = jnp.dot(style_rows, second_affine_weight, preferred_element_type=F32) + (
        second_affine_bias.astype(F32)
    )

    def turned(weight):
        return (
            weight.reshape(3, channels, channels).transpose(0, 2, 1).reshape(3 * channels, channels)
        )

    tiles_of = frames // ROWS
    full, padded = (frames, channels), (frames + 2 * PAD, channels)
    stats_shape, coef_shape = (STAT_ROWS, channels), (32, channels)
    small_acc = ((ACC_ROWS, channels), F32)

    cot_before, cot_after = from_neighbours(cotangent[:1], cotangent[-1:])
    order = send_order[0].reshape(groups, copies, piece_rows)
    mine = lax.dynamic_index_in_dim(order, tm_index, 1, False)
    outgoing = jnp.take(phonemes, mine.reshape(-1), axis=0, mode="clip")
    outgoing = after(outgoing, cot_before, cot_after)
    received = lax.all_to_all(
        outgoing.reshape(groups, piece_rows, channels), "seq", 0, 0, tiled=True
    ).reshape(local_rows, channels)

    grad_act_two, grad_branch, bias_part = call(
        gradient_kernel,
        (
            (info, SM),
            (cotangent, HB),
            (cot_before, VM),
            (cot_after, VM),
            (turned(second_conv_weight), VM),
        ),
        ((full, BF16, HB), (padded, BF16, HB), ((8, channels), F32, VM)),
        [(full, BF16), (padded, BF16), (full, BF16), tiles_of, tiles_of, 2, tiles_of],
        conv_flops,
        24,
    )

    received, bias_part = lax.optimization_barrier((received, bias_part))
    slots_before, slots_after = from_neighbours(received[:halo], received[-halo:])
    upsampled, upsampled_far, wide, stat = call(
        upsample_kernel,
        (
            (info, SM),
            (tile_offsets, SM),
            (slots_before, VM),
            (received, VM),
            (slots_after, VM),
            (alignment, HB),
            (bias_part, VM),
        ),
        (
            (full, F32, VM),
            (full, F32, HB),
            ((frames, WIDE), BF16, HB),
            (stats_shape, F32, VM),
        ),
        [
            ((local_rows + WIDE, channels), BF16),
            small_acc,
            ((frames, window), BF16),
            ((frames, WIDE), BF16),
            tiles_of,
            tiles_of,
            tiles_of,
        ],
        2 * frames * WIDE * channels,
        12,
    )
    others = others_over_tm(stat)
    bias_total = (stat[EXTRA_ROW] + others[1][EXTRA_ROW]) + (
        others[0][EXTRA_ROW] + others[2][EXTRA_ROW]
    )

    act_one, middle, unit_one, coef_one, stat_two = call(
        first_conv_kernel,
        (
            (info, SM),
            (upsampled, VM),
            *((one, VM) for one in (stat, *others)),
            (inverse, VM),
            (params_one, VM),
            (first_conv_weight, VM),
        ),
        (
            (padded, BF16, HB),
            (full, F32, VM),
            (full, BF16, HB),
            (coef_shape, F32, VM),
            (stats_shape, F32, VM),
        ),
        [small_acc, (padded, BF16), (full, BF16), tiles_of, 2, tiles_of],
        conv_flops,
        20,
    )
    others_two = others_over_tm(stat_two)

    act_two, act_two_far, inner_two, unit_two, coef_two, stat_three = call(
        second_norm_kernel,
        (
            (info, SM),
            (grad_act_two, HB),
            (middle, VM),
            *((one, VM) for one in (stat_two, *others_two)),
            (inverse, VM),
            (params_two, VM),
        ),
        (
            (padded, BF16, VM),
            (padded, BF16, HB),
            (full, BF16, HB),
            (full, BF16, HB),
            (coef_shape, F32, VM),
            (stats_shape, F32, VM),
        ),
        [
            small_acc,
            (full, BF16),
            (full, BF16),
            (full, BF16),
            tiles_of,
            tiles_of,
            2,
            tiles_of,
            tiles_of,
        ],
        2 * frames * channels * 100,
        20,
    )
    others_three = others_over_tm(stat_three)
    second_keep, second_give = call(
        functools.partial(weight_gradient_kernel, False),
        ((info, SM), (after(act_two, others_three[0]), VM), (grad_branch, HB)),
        (((3 * channels // 2, channels), F32, VM), ((3 * channels // 2, channels), BF16, VM)),
        [((3 * channels, channels), F32), (padded, BF16), tiles_of, 2],
        conv_flops,
        16,
    )

    grad_middle, inner_one, back_two, stat_four = call(
        first_back_kernel,
        (
            (info, SM),
            (inner_two, HB),
            (unit_two, HB),
            *((one, VM) for one in (stat_three, *others_three)),
            (others_two[0], VM),
            (others_two[2], VM),
            (inverse, VM),
            (coef_two, VM),
            (coef_one, VM),
            (unit_one, HB),
            (turned(first_conv_weight), VM),
        ),
        (
            (padded, BF16, VM),
            (full, BF16, HB),
            ((40, channels), F32, VM),
            (stats_shape, F32, VM),
        ),
        [
            small_acc,
            ((ROWS, channels), F32),
            *([(full, BF16)] * 4),
            *([tiles_of] * 4),
        ],
        conv_flops,
        28,
    )
    others_four = others_over_tm(stat_four)
    first_keep, first_give = call(
        functools.partial(weight_gradient_kernel, True),
        ((info, SM), (act_one, HB), (after(grad_middle, others_four[0]), VM)),
        (((3 * channels // 2, channels), F32, VM), ((3 * channels // 2, channels), BF16, VM)),
        [((3 * channels, channels), F32), (padded, BF16), tiles_of, 2],
        conv_flops,
        16,
    )

    grad_before, grad_own, grad_after, back_one, free_rows = call(
        buffer_gradient_kernel,
        (
            (info, SM),
            (tile_offsets, SM),
            (inner_one, HB),
            (unit_one, HB),
            (cotangent, HB),
            (wide, HB),
            *((one, VM) for one in (stat_four, *others_four)),
            (inverse, VM),
            (coef_one, VM),
        ),
        (
            ((halo, channels), F32, VM),
            ((local_rows, channels), F32, VM),
            ((halo, channels), F32, VM),
            ((40, channels), F32, VM),
            ((groups, copies, piece_rows // 2, channels), BF16, VM),
        ),
        [
            (full, BF16),
            ((local_rows + WIDE, channels), F32),
            *([(full, BF16)] * 3),
            ((frames, WIDE), BF16),
            *([tiles_of] * 4),
        ],
        2 * frames * WIDE * channels,
        28,
    )

    def sent_back(rows):
        rows = rows.reshape(groups * copies, half, channels)
        return lax.all_to_all(rows, ("seq", "tm"), 0, 0, tiled=True)

    half = piece_rows // 2
    from_before, from_after = from_neighbours(grad_before, grad_after)
    if half >= halo:
        split = grad_own.reshape(groups, 2, half, channels)
        late_rows = jnp.concatenate([split[: groups // 2, 0], split[groups // 2 :, 1]], axis=0)
        late_rows = (
            late_rows.at[0, :halo].add(from_before).at[groups - 1, half - halo :].add(from_after)
        ).astype(BF16)
    else:
        own = grad_own.at[:halo].add(from_before).at[local_rows - halo :].add(from_after)
        split = own.astype(BF16).reshape(groups, 2, half, channels)
        free_rows = jnp.concatenate([split[: groups // 2, 1], split[groups // 2 :, 0]], axis=0)
        free_rows = jnp.broadcast_to(free_rows[:, None], (groups, copies, half, channels))
        late_rows = jnp.concatenate([split[: groups // 2, 0], split[groups // 2 :, 1]], axis=0)
    late_rows = jnp.broadcast_to(late_rows[:, None], (groups, copies, half, channels))
    first_chunk = sent_back(free_rows)

    bits = [b for b in range(12) if (1 << b) < groups]
    orders = (bits[1:], bits[1:][::-1])
    keeps = [second_keep, first_keep]
    gives = after([second_give, first_give], back_one)
    gots = [swapped(give, bits[0]) for give in gives]
    for pair in zip(*orders):
        count = keeps[0].shape[0] // 2
        out = call(
            functools.partial(halves_kernel, pair),
            ((info, SM), *((one, VM) for both in zip(keeps, gots) for one in both)),
            (((count, channels), F32, VM), ((count, channels), BF16, VM)) * 2,
            [((2 * count, channels), F32)] * 2,
            10**6,
            8,
        )
        keeps, gives = [out[0], out[2]], [out[1], out[3]]
        gots = [swapped(give, bit) for give, bit in zip(gives, pair)]
    row_sums = [keep + got.astype(F32) for keep, got in zip(keeps, gots)]
    act_two_far, _ = lax.optimization_barrier((act_two_far, back_one))
    (frames_out,) = call(
        second_conv_kernel,
        (
            (info, SM),
            (act_two_far, HB),
            (upsampled_far, HB),
            (second_conv_weight, VM),
            (second_conv_bias[None], VM),
        ),
        ((full, BF16, HB),),
        [(padded, BF16), (full, F32), (full, BF16), tiles_of, 2, tiles_of, tiles_of],
        10**6,
        28,
    )

    row_sums, first_chunk, frames_out = lax.optimization_barrier((row_sums, first_chunk, frames_out))
    sums = gathered_over_tm(summed_over_tm(row_sums))
    late_rows, sums, first_chunk = lax.optimization_barrier((late_rows, sums, first_chunk))
    second_chunk = sent_back(late_rows)
    placed = scattered(None, first_chunk, 0, info, send_order[0])

    params_grad = [
        jnp.concatenate([back[8 : 8 + UTTS], back[0:UTTS]], axis=1) for back in (back_one, back_two)
    ]
    style_grad = jnp.dot(
        params_grad[0], first_affine_weight.astype(F32).T, precision=PRECISE
    ) + jnp.dot(params_grad[1], second_affine_weight.astype(F32).T, precision=PRECISE)
    style_block = jnp.zeros((8, channels), BF16).at[:, : style_rows.shape[1]].set(style_rows)
    small = jnp.concatenate(
        [
            back_one[8:16].astype(BF16),
            back_one[0:8].astype(BF16),
            back_two[8:16].astype(BF16),
            back_two[0:8].astype(BF16),
            style_block,
            jnp.zeros((8, channels), BF16).at[0].set(bias_total.astype(BF16)),
        ]
    )
    rows = sums.shape[1]
    held = [jnp.concatenate([sums[0], small]), sums[1]]
    for pair in zip(*orders):
        others = [swapped(one, bit) for one, bit in zip(held, pair)]
        held = call(
            functools.partial(join_kernel, pair),
            ((info, SM), *((one, VM) for both in zip(held, others) for one in both)),
            tuple(((2 * one.shape[0], channels), BF16, VM) for one in held),
            [],
            10**6,
            8,
        )
    others = [swapped(one, bits[0]) for one in held]
    (
        second_conv_grad,
        first_conv_grad,
        first_affine_grad,
        first_shift_grad,
        second_affine_grad,
        second_shift_grad,
        second_bias_grad,
    ) = call(
        functools.partial(final_kernel, orders, rows),
        (
            (info, SM),
            (held[0], VM),
            (others[0], VM),
            (held[1], VM),
            (others[1], VM),
        ),
        (
            ((3 * channels, channels), F32, VM),
            ((3 * channels, channels), F32, VM),
            *(
                (((style_vec.shape[1], 2 * channels), F32, VM), ((1, 2 * channels), F32, VM)) * 2
            ),
            ((1, channels), F32, VM),
        ),
        [],
        10**6,
        20,
    )
    placed = scattered(placed, second_chunk, 1, info, send_order[0])
    lanes = channels // 128
    phonemes_grad = (
        placed.reshape(slot_count // 8, lanes, 8, 128)
        .transpose(0, 2, 1, 3)
        .reshape(slot_count, channels)
    )
    return (
        frames_out,
        phonemes_grad,
        style_grad,
        first_affine_grad,
        first_shift_grad[0],
        first_conv_grad,
        second_affine_grad,
        second_shift_grad[0],
        second_conv_grad,
        second_bias_grad[0],
    )


def solution(mesh):
    split, whole = ("seq", "tm"), P()
    in_specs = (
        P("seq", None),
        P("seq", None),
        P("seq", None),
        P("seq", None),
        P(split),
        P(split, None),
        P("seq", None),
        *([whole] * 7),
        P(split, None),
    )
    out_specs = (P(split, None), P("seq", None), P("seq", None), *([whole] * 7))
    return jax.shard_map(
        on_device, mesh=mesh, in_specs=in_specs, out_specs=out_specs, check_vma=False
    )
```

time: 466 us -> 338 us (0.73)
  local copies, waits for them, and re-layouts: 114 us -> 31.6 us
  starting transfers between devices: 104 us -> 72.2 us
  Pallas kernels: 116 us -> 141 us
  other arithmetic: 28.5 us -> 8.36 us
  waiting for transfers between devices: 95.6 us -> 79.4 us
    ppermute x27 -> x18, waiting for transfers between devices: 73.7 us -> 22.3 us  [shifted(): lax.ppermute(values, axis, [(i, (i + step) % devices) for i in range(devi...]
    unnamed x114 -> x78, local copies, waits for them, and re-layouts: 50.1 us -> 16.7 us
    ppermute x15 -> x12, waiting for transfers between devices: 18.3 us -> 51.2 us  [swapped(): lax.ppermute(values, 'seq', [(i, i ^ 1 << bit) for i in range(devices)])]
    ppermute x27 -> x18, starting transfers between devices: 52.8 us -> 27.4 us  [shifted(): lax.ppermute(values, axis, [(i, (i + step) % devices) for i in range(devi...]
    pallas_call x9 -> x16, Pallas kernels: 116 us -> 141 us  [the longest x14 121 us: call(): pl.pallas_call(kernel, in_specs=[spec for _, spec in inputs], out_specs=t...]
    gather x1 -> x0, local copies, waits for them, and re-layouts: 20.2 us -> none  [on_device(): jnp.take(slots_back.reshape(slot_count, channels), place, axis=0, mode='c...]
    scatter x1 -> x0, local copies, waits for them, and re-layouts: 15.5 us -> none  [on_device(): place = jnp.zeros((slot_count,), I32).at[send_order[0]].set(jnp.arange(sl...]
    ppermute x15 -> x12, starting transfers between devices: 24.8 us -> 11.9 us  [swapped(): lax.ppermute(values, 'seq', [(i, i ^ 1 << bit) for i in range(devices)])]
  transfers between devices with their start and end apart: 50 -> 39, of which waited for: 22 -> 28; matrix products, arithmetic and copies ran while one was open for 18% -> 6% of each run, Pallas kernels for 18% -> 19%
where the time goes in v2:
time: 338 us; the launch traced here: 335 us
  Pallas kernels  141 us (42%)
  waiting for transfers between devices  79.4 us (23%)
  starting transfers between devices  72.2 us (21%)
  local copies, waits for them, and re-layouts  31.6 us (9%)
  other arithmetic  8.36 us (2%)
    pallas_call x14, Pallas kernels, call(): pl.pallas_call(kernel, in_specs=[spec for _, spec in inputs], out_specs=t...  121 us
    ppermute x12, waiting for transfers between devices, swapped(): lax.ppermute(values, 'seq', [(i, i ^ 1 << bit) for i in range(devices)])  51.2 us
    ppermute x18, starting transfers between devices, shifted(): lax.ppermute(values, axis, [(i, (i + step) % devices) for i in range(devi...  27.4 us
    ppermute x18, waiting for transfers between devices, shifted(): lax.ppermute(values, axis, [(i, (i + step) % devices) for i in range(devi...  22.3 us
    pallas_call x2, Pallas kernels, scattered(): pl.pallas_call(functools.partial(scatter_kernel, late), in_specs=[SM, SM]...  19.5 us
    unnamed x78, local copies, waits for them, and re-layouts  16.7 us
    ppermute x3, starting transfers between devices, from_neighbours(): lax.ppermute(last_rows, 'tm', up)  12.8 us
    all_to_all x2, starting transfers between devices, sent_back(): return lax.all_to_all(rows, ('seq', 'tm'), 0, 0, tiled=True)  12 us
  transfers between devices with their start and end apart: 39, of which 28 were waited for; matrix products, arithmetic and copies ran while one was open for 6% of the time, Pallas kernels for 19%

profile of v2, /device:TPU:0, one launch (start us, length us, event | category | flops | bytes accessed | tf_op | source)
XLA Modules:
  0.0 335.1 jit_solution(3095697939972249449)
XLA Ops:
  1.4 4.9 %collective-permute-start = (bf16[1,512]{1,0:T(2,128)(2,1)S(1)}, bf16[1,512]{1,0:T(2,128)(2,1)S(1)}, u32[]{:S(2)}, u32[]{:S(2)}) collective-permute-start(bf16[1,512]{1,0:T(2,128)(2,1)S(1)} %get-tuple-element.215), channel_id=1, source_target_pairs={{0,1},{1,2},{2,3},{4,5},{5,6},{6,7},{8,9},{9,10},{10,11},{12,13},{... | collective-permute-start | bytes 3080 | tf_op jit(solution)/shard_map/ppermute | solution.py:1064
  8.4 8.0 %gather_fusion = bf16[1024,512]{1,0:T(8,128)(2,1)} fusion(bf16[4096,512]{1,0:T(8,128)(2,1)} %param.27, s32[1024]{0:T(1024)S(1)} %broadcast_clamp_fusion), kind=kCustom, calls=%fused_computation | custom fusion | bytes 2101248 | tf_op jit(solution)/shard_map/jit(_take)/gather | solution.py:1165
  16.4 4.3 %all-to-all-start = ((bf16[8,128,512]{2,1,0:T(8,128)(2,1)}), bf16[8,128,512]{2,1,0:T(8,128)(2,1)}, u32[]{:S(2)}, u32[]{:S(2)}) async-start(bf16[8,128,512]{2,1,0:T(8,128)(2,1)} %bitcast.13), calls=%async_computation | async-start | bytes 2097152 | tf_op jit(solution)/shard_map/all_to_all | solution.py:1167
  21.9 13.0 %shard_map.222 = (bf16[4096,512]{1,0:T(8,128)(2,1)}, bf16[4128,512]{1,0:T(8,128)(2,1)}, f32[8,512]{1,0:T(8,128)S(1)}) custom-call(s32[24]{0:T(128)S(1)} %concatenate.28.info_ref, bf16[4096,512]{1,0:T(8,128)(2,1)} %cot_hbm.3, bf16[1,512]{1,0:T(2,128)(2,1)S(1)} %collective-permute-done.before_ref, bf16[1,512]{1,0:T(2,128)(2,1)S(1)} %collective-permute-done.1.after_ref, ...), custom_call_target="tpu_custom_call" | custom-call | flops 6442450944 | bytes 32212254 | tf_op jit(solution)/shard_map/pallas_call | solution.py:1013
  37.0 4.5 %collective-permute-start.2 = (bf16[64,512]{1,0:T(8,128)(2,1)S(1)}, bf16[64,512]{1,0:T(8,128)(2,1)S(1)}, u32[]{:S(2)}, u32[]{:S(2)}) collective-permute-start(bf16[64,512]{1,0:T(8,128)(2,1)S(1)} %get-tuple-element.219), channel_id=1, source_target_pairs={{0,1},{1,2},{2,3},{4,5},{5,6},{6,7},{8,9},{9,10},{10,11},{12,13},{... | collective-permute-start | bytes 196616 | tf_op jit(solution)/shard_map/ppermute | solution.py:1064
  43.4 4.3 %collective-permute-done.3.after_ref = bf16[64,512]{1,0:T(8,128)(2,1)S(1)} collective-permute-done((bf16[64,512]{1,0:T(8,128)(2,1)S(1)}, bf16[64,512]{1,0:T(8,128)(2,1)S(1)}, u32[]{:S(2)}, u32[]{:S(2)}) %collective-permute-start.3) | collective-permute-done | bytes 65568 | tf_op jit(solution)/shard_map/ppermute | solution.py:1064
  47.7 8.4 %shard_map.223 = (f32[4096,512]{1,0:T(8,128)S(1)}, f32[4096,512]{1,0:T(8,128)}, bf16[4096,256]{1,0:T(8,128)(2,1)}, f32[24,512]{1,0:T(8,128)S(1)}) custom-call(s32[24]{0:T(128)S(1)} %concatenate.28.info_ref, s32[32]{0:T(128)S(1)} %copy-done.17, bf16[64,512]{1,0:T(8,128)(2,1)S(1)} %collective-permute-done.2.before_ref, bf16[1024,512]{1,0:T(8,128)(2,1)} %bitcast.14.own_ref, ...), custom_call_target="tpu_custom_call" | custom-call | flops 1073741824 | bytes 5368709 | tf_op jit(solution)/shard_map/pallas_call | solution.py:1013
  58.8 2.8 collective-permute-start.6
  63.5 14.6 %shard_map.224 = (bf16[4128,512]{1,0:T(8,128)(2,1)}, f32[4096,512]{1,0:T(8,128)S(1)}, bf16[4096,512]{1,0:T(8,128)(2,1)}, f32[32,512]{1,0:T(8,128)S(1)}, f32[24,512]{1,0:T(8,128)S(1)}) custom-call(s32[24]{0:T(128)S(1)} %concatenate.28.info_ref, f32[4096,512]{1,0:T(8,128)S(1)} %get-tuple-element.152.values_ref, f32[24,512]{1,0:T(8,128)S(1)} %get-tuple-element.153.own_ref, ...), custom_call_target="tpu_custom_call" | custom-call | flops 6442450944 | bytes 32212254 | tf_op jit(solution)/shard_map/pallas_call | solution.py:1013
  79.6 3.3 collective-permute-start.8
  87.0 10.4 %shard_map.225 = (bf16[4128,512]{1,0:T(8,128)(2,1)S(1)}, bf16[4128,512]{1,0:T(8,128)(2,1)}, bf16[4096,512]{1,0:T(8,128)(2,1)}, bf16[4096,512]{1,0:T(8,128)(2,1)}...) custom-call(s32[24]{0:T(128)S(1)} %concatenate.28.info_ref, bf16[4096,512]{1,0:T(8,128)(2,1)} %get-tuple-element.147.gradient_hbm, ...), custom_call_target="tpu_custom_call" | custom-call | flops 419430400 | bytes 2097152 | tf_op jit(solution)/shard_map/pallas_call | solution.py:1013
  100.1 2.8 collective-permute-start.11
  108.9 20.3 %shard_map.227 = (bf16[4128,512]{1,0:T(8,128)(2,1)S(1)}, bf16[4096,512]{1,0:T(8,128)(2,1)}, f32[40,512]{1,0:T(8,128)S(1)}, f32[24,512]{1,0:T(8,128)S(1)}) custom-call(s32[24]{0:T(128)S(1)} %concatenate.28.info_ref, bf16[4096,512]{1,0:T(8,128)(2,1)} %get-tuple-element.163.inner_hbm, bf16[4096,512]{1,0:T(8,128)(2,1)} %get-tuple-element.164.unit_two_hbm, ...), custom_call_target="tpu_custom_call" | custom-call | flops 6442450944 | bytes 32212254 | tf_op jit(solution)/shard_map/pallas_call | solution.py:1013
  139.4 10.4 %shard_map.229 = (f32[64,512]{1,0:T(8,128)}, f32[1024,512]{1,0:T(8,128)S(1)}, f32[64,512]{1,0:T(8,128)}, f32[40,512]{1,0:T(8,128)S(1)}, bf16[8,4,64,512]{3,2,1,0:T(8,128)(2,1)S(1)}) custom-call(s32[24]{0:T(128)S(1)} %concatenate.28.info_ref, s32[32]{0:T(128)S(1)} %copy-done.17, bf16[4096,512]{1,0:T(8,128)(2,1)} %get-tuple-element.172.inner_hbm, ...), custom_call_target="tpu_custom_call" | custom-call | flops 1073741824 | bytes 5368709 | tf_op jit(solution)/shard_map/pallas_call | solution.py:1013
  153.2 7.3 %all-to-all-start.1 = ((bf16[32,64,512]{2,1,0:T(8,128)(2,1)}), bf16[32,64,512]{2,1,0:T(8,128)(2,1)S(1)}, u32[]{:S(2)}, u32[]{:S(2)}) async-start(bf16[32,64,512]{2,1,0:T(8,128)(2,1)} %bitcast.97), calls=%async_computation.1 | async-start | bytes 4194304 | tf_op jit(solution)/shard_map/all_to_all | solution.py:1360
  160.5 2.2 copy-done.23
  162.7 11.3 %shard_map.226 = (f32[768,512]{1,0:T(8,128)S(1)}, bf16[768,512]{1,0:T(8,128)(2,1)S(1)}) custom-call(s32[24]{0:T(128)S(1)} %concatenate.28.info_ref, bf16[4128,512]{1,0:T(8,128)(2,1)S(1)} %copy-done.23, bf16[4128,512]{1,0:T(8,128)(2,1)} %get-tuple-element.159.gradient_any), custom_call_target="tpu_custom_call" | custom-call | flops 6442450944 | bytes 32212254 | tf_op jit(solution)/shard_map/pallas_call | solution.py:1013
  174.0 2.2 copy-done.27
  176.2 11.1 %shard_map.228 = (f32[768,512]{1,0:T(8,128)S(1)}, bf16[768,512]{1,0:T(8,128)(2,1)S(1)}) custom-call(s32[24]{0:T(128)S(1)} %concatenate.28.info_ref, bf16[4128,512]{1,0:T(8,128)(2,1)} %get-tuple-element.162.act_any, bf16[4128,512]{1,0:T(8,128)(2,1)S(1)} %copy-done.27), custom_call_target="tpu_custom_call" | custom-call | flops 6442450944 | bytes 32212254 | tf_op jit(solution)/shard_map/pallas_call | solution.py:1013
  196.8 12.2 %collective-permute-done.18.refs_1_ = bf16[384,512]{1,0:T(8,128)(2,1)S(1)} collective-permute-done((bf16[384,512]{1,0:T(8,128)(2,1)}, bf16[384,512]{1,0:T(8,128)(2,1)S(1)}, u32[]{:S(2)}, u32[]{:S(2)}) %collective-permute-start.18) | collective-permute-done | bytes 393248 | tf_op jit(solution)/shard_map/ppermute | solution.py:1069
  214.5 3.4 %collective-permute-start.22 = (f32[64,512]{1,0:T(8,128)}, f32[64,512]{1,0:T(8,128)}, u32[]{:S(2)}, u32[]{:S(2)}) collective-permute-start(f32[64,512]{1,0:T(8,128)} %get-tuple-element.192), channel_id=1, source_target_pairs={{0,1},{1,2},{2,3},{4,5},{5,6},{6,7},{8,9},{9,10},{10,11},{12,13},{... | collective-permute-start | bytes 393224 | tf_op jit(solution)/shard_map/ppermute | solution.py:1064
  219.2 12.4 %shard_map.232 = bf16[4096,512]{1,0:T(8,128)(2,1)} custom-call(s32[24]{0:T(128)S(1)} %concatenate.28.info_ref, bf16[4128,512]{1,0:T(8,128)(2,1)} %get-tuple-element.188.act_hbm, f32[4096,512]{1,0:T(8,128)} %get-tuple-element.189.values_hbm, bf16[1536,512]{1,0:T(8,128)(2,1)S(1)} %copy-done.4, bf16[1,512]{1,0:T(2,128)(2,1)S(1)} %broadcast_in_dim.54.bias_ref), custom_call_target="tpu_custom_call" | custom-call | flops 1000000 | bytes 5000 | tf_op jit(solution)/shard_map/pallas_call | solution.py:1013
  234.0 4.3 %collective-permute-done.20 = bf16[192,512]{1,0:T(8,128)(2,1)S(1)} collective-permute-done((bf16[192,512]{1,0:T(8,128)(2,1)S(1)}, bf16[192,512]{1,0:T(8,128)(2,1)S(1)}, u32[]{:S(2)}, u32[]{:S(2)}) %collective-permute-start.20) | collective-permute-done | bytes 196640 | tf_op jit(solution)/shard_map/ppermute | solution.py:1069
  238.5 2.7 collective-permute-start.24
  253.2 3.4 %collective-permute-start.28 = (bf16[2,48,512]{2,1,0:T(8,128)(2,1)S(1)}, bf16[2,48,512]{2,1,0:T(8,128)(2,1)S(1)}, u32[]{:S(2)}, u32[]{:S(2)}) collective-permute-start(bf16[2,48,512]{2,1,0:T(8,128)(2,1)S(1)} %get-tuple-element.213), channel_id=1, source_target_pairs={{0,3},{1,0},{2,1},{3,2},{4,7},{5,4},{6,5},{7,6},{8,11},{9,8},{10,9... | collective-permute-start | bytes 294920 | tf_op jit(solution)/shard_map/ppermute | solution.py:1053
  258.9 4.0 %collective-permute-done.29 = bf16[2,48,512]{2,1,0:T(8,128)(2,1)S(1)} collective-permute-done((bf16[2,48,512]{2,1,0:T(8,128)(2,1)S(1)}, bf16[2,48,512]{2,1,0:T(8,128)(2,1)S(1)}, u32[]{:S(2)}, u32[]{:S(2)}) %collective-permute-start.29) | collective-permute-done | bytes 98336 | tf_op jit(solution)/shard_map/ppermute | solution.py:1053
  264.4 4.6 %all-to-all-start.2 = ((bf16[32,64,512]{2,1,0:T(8,128)(2,1)}), bf16[32,64,512]{2,1,0:T(8,128)(2,1)S(1)}, u32[]{:S(2)}, u32[]{:S(2)}) async-start(bf16[32,64,512]{2,1,0:T(8,128)(2,1)} %bitcast.107), calls=%async_computation.2 | async-start | bytes 4194304 | tf_op jit(solution)/shard_map/all_to_all | solution.py:1360
  274.5 17.3 %collective-permute-done.31.refs_3_ = bf16[192,512]{1,0:T(8,128)(2,1)S(1)} collective-permute-done((bf16[192,512]{1,0:T(8,128)(2,1)S(1)}, bf16[192,512]{1,0:T(8,128)(2,1)S(1)}, u32[]{:S(2)}, u32[]{:S(2)}) %collective-permute-start.31) | collective-permute-done | bytes 196640 | tf_op jit(solution)/shard_map/ppermute | solution.py:1069
  293.9 13.8 %collective-permute-done.33.refs_3_ = bf16[384,512]{1,0:T(8,128)(2,1)S(1)} collective-permute-done((bf16[384,512]{1,0:T(8,128)(2,1)S(1)}, bf16[384,512]{1,0:T(8,128)(2,1)S(1)}, u32[]{:S(2)}, u32[]{:S(2)}) %collective-permute-start.33) | collective-permute-done | bytes 393248 | tf_op jit(solution)/shard_map/ppermute | solution.py:1069
  310.7 8.1 %shard_map.233.refs_0_ = f32[16384,128]{1,0:T(8,128)} custom-call(s32[24]{0:T(128)S(1)} %concatenate.28.info_ref, s32[4096]{0:T(1024)S(1)} %bitcast.104, bf16[32,64,512]{2,1,0:T(8,128)(2,1)S(1)} %copy-done.2), custom_call_target="tpu_custom_call" | custom-call | flops 1000000 | bytes 10000 | tf_op jit(solution)/shard_map/pallas_call | solution.py:1039
  318.8 4.9 %shard_map.237 = (f32[1536,512]{1,0:T(8,128)}, f32[1536,512]{1,0:T(8,128)}, f32[128,1024]{1,0:T(8,128)}, f32[1,1024]{1,0:T(1,128)}, f32[128,1024]{1,0:T(8,128)}, /*index=5*/f32[1,1024]{1,0:T(1,128)}, f32[1,512]{1,0:T(1,128)}) custom-call(s32[24]{0:T(128)S(1)} %concatenate.28.info_ref, bf16[960,512]{1,0:T(8,128)(2,1)S(1)} %get-tuple-element.203.second_ref, ...), custom_call_target="tpu_custom_call" | custom-call | flops 1000000 | bytes 5000 | tf_op jit(solution)/shard_map/pallas_call | solution.py:1013
  323.8 11.3 %shard_map.234 = f32[16384,128]{1,0:T(8,128)} custom-call(s32[24]{0:T(128)S(1)} %concatenate.28.info_ref, s32[4096]{0:T(1024)S(1)} %bitcast.105, bf16[32,64,512]{2,1,0:T(8,128)(2,1)S(1)} %all-to-all-done.2.part_ref, f32[16384,128]{1,0:T(8,128)} %shard_map.233.refs_0_), custom_call_target="tpu_custom_call", output_to_operand_aliasing={{}: (3, {})} | custom-call | flops 1000000 | bytes 10000 | tf_op jit(solution)/shard_map/pallas_call | solution.py:1039
  (185 shorter events, 85.2 us)
Async XLA Ops:
  1.4 15.0 %collective-permute-start = (bf16[1,512]{1,0:T(2,128)(2,1)S(1)}, bf16[1,512]{1,0:T(2,128)(2,1)S(1)}, u32[]{:S(2)}, u32[]{:S(2)}) collective-permute-start(bf16[1,512]{1,0:T(2,128)(2,1)S(1)} %get-tuple-element.215), channel_id=1, source_target_pairs={{0,1},{1,2},{2,3},{4,5},{5,6},{6,7},{8,9},{9,10},{10,11},{12,13},{... | collective-permute-start | bytes 3080 | tf_op jit(solution)/shard_map/ppermute | solution.py:1064
  6.3 10.1 %collective-permute-start.1 = (bf16[1,512]{1,0:T(2,128)(2,1)S(1)}, bf16[1,512]{1,0:T(2,128)(2,1)S(1)}, u32[]{:S(2)}, u32[]{:S(2)}) collective-permute-start(bf16[1,512]{1,0:T(2,128)(2,1)S(1)} %get-tuple-element.214), channel_id=1, source_target_pairs={{1,0},{2,1},{3,2},{5,4},{6,5},{7,6},{9,8},{10,9},{11,10},{13,12},{... | collective-permute-start | bytes 3080 | tf_op jit(solution)/shard_map/ppermute | solution.py:1064
  16.4 19.7 %all-to-all-start = ((bf16[8,128,512]{2,1,0:T(8,128)(2,1)}), bf16[8,128,512]{2,1,0:T(8,128)(2,1)}, u32[]{:S(2)}, u32[]{:S(2)}) async-start(bf16[8,128,512]{2,1,0:T(8,128)(2,1)} %bitcast.13), calls=%async_computation | async-start | bytes 2097152 | tf_op jit(solution)/shard_map/all_to_all | solution.py:1167
  37.0 6.4 %collective-permute-start.2 = (bf16[64,512]{1,0:T(8,128)(2,1)S(1)}, bf16[64,512]{1,0:T(8,128)(2,1)S(1)}, u32[]{:S(2)}, u32[]{:S(2)}) collective-permute-start(bf16[64,512]{1,0:T(8,128)(2,1)S(1)} %get-tuple-element.219), channel_id=1, source_target_pairs={{0,1},{1,2},{2,3},{4,5},{5,6},{6,7},{8,9},{9,10},{10,11},{12,13},{... | collective-permute-start | bytes 196616 | tf_op jit(solution)/shard_map/ppermute | solution.py:1064
  41.5 6.2 %collective-permute-start.3 = (bf16[64,512]{1,0:T(8,128)(2,1)S(1)}, bf16[64,512]{1,0:T(8,128)(2,1)S(1)}, u32[]{:S(2)}, u32[]{:S(2)}) collective-permute-start(bf16[64,512]{1,0:T(8,128)(2,1)S(1)} %get-tuple-element.218), channel_id=1, source_target_pairs={{1,0},{2,1},{3,2},{5,4},{6,5},{7,6},{9,8},{10,9},{11,10},{13,12},{... | collective-permute-start | bytes 196616 | tf_op jit(solution)/shard_map/ppermute | solution.py:1064
  56.1 5.9 %collective-permute-start.4 = (f32[24,512]{1,0:T(8,128)S(1)}, f32[24,512]{1,0:T(8,128)S(1)}, u32[]{:S(2)}, u32[]{:S(2)}) collective-permute-start(f32[24,512]{1,0:T(8,128)S(1)} %get-tuple-element.153.own_ref), channel_id=1, source_target_pairs={{0,1},{1,2},{2,3},{3,0},{4,5},{5,6},{6,7},{7,4},{8,9},{9,10},{10,1... | collective-permute-start | bytes 147464 | tf_op jit(solution)/shard_map/ppermute | solution.py:1053
  78.1 6.3 %collective-permute-start.7 = (f32[24,512]{1,0:T(8,128)S(1)}, f32[24,512]{1,0:T(8,128)S(1)}, u32[]{:S(2)}, u32[]{:S(2)}) collective-permute-start(f32[24,512]{1,0:T(8,128)S(1)} %get-tuple-element.155.own_ref), channel_id=1, source_target_pairs={{0,1},{1,2},{2,3},{3,0},{4,5},{5,6},{6,7},{7,4},{8,9},{9,10},{10,1... | collective-permute-start | bytes 147464 | tf_op jit(solution)/shard_map/ppermute | solution.py:1053
  79.6 5.9 %collective-permute-start.8 = (f32[24,512]{1,0:T(8,128)S(1)}, f32[24,512]{1,0:T(8,128)S(1)}, u32[]{:S(2)}, u32[]{:S(2)}) collective-permute-start(f32[24,512]{1,0:T(8,128)S(1)} %get-tuple-element.155.own_ref), channel_id=1, source_target_pairs={{0,2},{1,3},{2,0},{3,1},{4,6},{5,7},{6,4},{7,5},{8,10},{9,11},{10,... | collective-permute-start | bytes 147464 | tf_op jit(solution)/shard_map/ppermute | solution.py:1053
  100.0 6.2 %collective-permute-start.10 = (f32[24,512]{1,0:T(8,128)}, f32[24,512]{1,0:T(8,128)}, u32[]{:S(2)}, u32[]{:S(2)}) collective-permute-start(f32[24,512]{1,0:T(8,128)} %get-tuple-element.157.own_ref), channel_id=1, source_target_pairs={{0,1},{1,2},{2,3},{3,0},{4,5},{5,6},{6,7},{7,4},{8,9},{9,10},{10,1... | collective-permute-start | bytes 147464 | tf_op jit(solution)/shard_map/ppermute | solution.py:1053
  100.1 6.1 %collective-permute-start.11 = (f32[24,512]{1,0:T(8,128)}, f32[24,512]{1,0:T(8,128)}, u32[]{:S(2)}, u32[]{:S(2)}) collective-permute-start(f32[24,512]{1,0:T(8,128)} %get-tuple-element.157.own_ref), channel_id=1, source_target_pairs={{0,2},{1,3},{2,0},{3,1},{4,6},{5,7},{6,4},{7,5},{8,10},{9,11},{10,... | collective-permute-start | bytes 147464 | tf_op jit(solution)/shard_map/ppermute | solution.py:1053
  131.9 5.9 %collective-permute-start.13 = (f32[24,512]{1,0:T(8,128)S(1)}, f32[24,512]{1,0:T(8,128)S(1)}, u32[]{:S(2)}, u32[]{:S(2)}) collective-permute-start(f32[24,512]{1,0:T(8,128)S(1)} %get-tuple-element.169.own_ref), channel_id=1, source_target_pairs={{0,1},{1,2},{2,3},{3,0},{4,5},{5,6},{6,7},{7,4},{8,9},{9,10},{10,1... | collective-permute-start | bytes 147464 | tf_op jit(solution)/shard_map/ppermute | solution.py:1053
  133.4 5.4 %collective-permute-start.14 = (f32[24,512]{1,0:T(8,128)S(1)}, f32[24,512]{1,0:T(8,128)S(1)}, u32[]{:S(2)}, u32[]{:S(2)}) collective-permute-start(f32[24,512]{1,0:T(8,128)S(1)} %get-tuple-element.169.own_ref), channel_id=1, source_target_pairs={{0,2},{1,3},{2,0},{3,1},{4,6},{5,7},{6,4},{7,5},{8,10},{9,11},{10,... | collective-permute-start | bytes 147464 | tf_op jit(solution)/shard_map/ppermute | solution.py:1053
  153.2 85.2 %all-to-all-start.1 = ((bf16[32,64,512]{2,1,0:T(8,128)(2,1)}), bf16[32,64,512]{2,1,0:T(8,128)(2,1)S(1)}, u32[]{:S(2)}, u32[]{:S(2)}) async-start(bf16[32,64,512]{2,1,0:T(8,128)(2,1)} %bitcast.97), calls=%async_computation.1 | async-start | bytes 4194304 | tf_op jit(solution)/shard_map/all_to_all | solution.py:1360
  193.6 15.5 %collective-permute-start.18 = (bf16[384,512]{1,0:T(8,128)(2,1)}, bf16[384,512]{1,0:T(8,128)(2,1)S(1)}, u32[]{:S(2)}, u32[]{:S(2)}) collective-permute-start(bf16[384,512]{1,0:T(8,128)(2,1)} %get-tuple-element.179), channel_id=1, source_target_pairs={{0,8},{4,12},{8,0},{12,4},{16,24},{20,28},{24,16},{28,20},{1,9},{5... | collective-permute-start | bytes 1179656 | tf_op jit(solution)/shard_map/ppermute | solution.py:1069
  195.3 13.9 %collective-permute-start.19 = (bf16[384,512]{1,0:T(8,128)(2,1)}, bf16[384,512]{1,0:T(8,128)(2,1)}, u32[]{:S(2)}, u32[]{:S(2)}) collective-permute-start(bf16[384,512]{1,0:T(8,128)(2,1)} %get-tuple-element.181), channel_id=1, source_target_pairs={{0,16},{4,20},{8,24},{12,28},{16,0},{20,4},{24,8},{28,12},{1,17},{... | collective-permute-start | bytes 1179656 | tf_op jit(solution)/shard_map/ppermute | solution.py:1069
  211.6 22.3 %collective-permute-start.21 = (bf16[192,512]{1,0:T(8,128)(2,1)S(1)}, bf16[192,512]{1,0:T(8,128)(2,1)S(1)}, u32[]{:S(2)}, u32[]{:S(2)}) collective-permute-start(bf16[192,512]{1,0:T(8,128)(2,1)S(1)} %get-tuple-element.185), channel_id=1, source_target_pairs={{0,8},{4,12},{8,0},{12,4},{16,24},{20,28},{24,16},{28,20},{1,9},{5... | collective-permute-start | bytes 589832 | tf_op jit(solution)/shard_map/ppermute | solution.py:1069
  214.5 29.3 %collective-permute-start.22 = (f32[64,512]{1,0:T(8,128)}, f32[64,512]{1,0:T(8,128)}, u32[]{:S(2)}, u32[]{:S(2)}) collective-permute-start(f32[64,512]{1,0:T(8,128)} %get-tuple-element.192), channel_id=1, source_target_pairs={{0,1},{1,2},{2,3},{4,5},{5,6},{6,7},{8,9},{9,10},{10,11},{12,13},{... | collective-permute-start | bytes 393224 | tf_op jit(solution)/shard_map/ppermute | solution.py:1064
  217.9 32.4 %collective-permute-start.23 = (f32[64,512]{1,0:T(8,128)}, f32[64,512]{1,0:T(8,128)}, u32[]{:S(2)}, u32[]{:S(2)}) collective-permute-start(f32[64,512]{1,0:T(8,128)} %get-tuple-element.193), channel_id=1, source_target_pairs={{1,0},{2,1},{3,2},{5,4},{6,5},{7,6},{9,8},{10,9},{11,10},{13,12},{... | collective-permute-start | bytes 393224 | tf_op jit(solution)/shard_map/ppermute | solution.py:1064
  232.6 5.7 %collective-permute-start.20 = (bf16[192,512]{1,0:T(8,128)(2,1)S(1)}, bf16[192,512]{1,0:T(8,128)(2,1)S(1)}, u32[]{:S(2)}, u32[]{:S(2)}) collective-permute-start(bf16[192,512]{1,0:T(8,128)(2,1)S(1)} %get-tuple-element.183), channel_id=1, source_target_pairs={{0,16},{4,20},{8,24},{12,28},{16,0},{20,4},{24,8},{28,12},{1,17},{... | collective-permute-start | bytes 589832 | tf_op jit(solution)/shard_map/ppermute | solution.py:1069
  238.5 7.2 %collective-permute-start.24 = (bf16[2,48,512]{2,1,0:T(8,128)(2,1)S(1)}, bf16[2,48,512]{2,1,0:T(8,128)(2,1)S(1)}, u32[]{:S(2)}, u32[]{:S(2)}) collective-permute-start(bf16[2,48,512]{2,1,0:T(8,128)(2,1)S(1)} %get-tuple-element.220), channel_id=1, source_target_pairs={{0,1},{1,2},{2,3},{3,0},{4,5},{5,6},{6,7},{7,4},{8,9},{9,10},{10,1... | collective-permute-start | bytes 294920 | tf_op jit(solution)/shard_map/ppermute | solution.py:1053
  241.2 6.4 %collective-permute-start.25 = (bf16[2,48,512]{2,1,0:T(8,128)(2,1)S(1)}, bf16[2,48,512]{2,1,0:T(8,128)(2,1)S(1)}, u32[]{:S(2)}, u32[]{:S(2)}) collective-permute-start(bf16[2,48,512]{2,1,0:T(8,128)(2,1)S(1)} %get-tuple-element.222), channel_id=1, source_target_pairs={{0,3},{1,0},{2,1},{3,2},{4,7},{5,4},{6,5},{7,6},{8,11},{9,8},{10,9... | collective-permute-start | bytes 294920 | tf_op jit(solution)/shard_map/ppermute | solution.py:1053
  243.0 6.6 %collective-permute-start.26 = (bf16[2,48,512]{2,1,0:T(8,128)(2,1)S(1)}, bf16[2,48,512]{2,1,0:T(8,128)(2,1)S(1)}, u32[]{:S(2)}, u32[]{:S(2)}) collective-permute-start(bf16[2,48,512]{2,1,0:T(8,128)(2,1)S(1)} %get-tuple-element.221), channel_id=1, source_target_pairs={{0,2},{1,3},{2,0},{3,1},{4,6},{5,7},{6,4},{7,5},{8,10},{9,11},{10,... | collective-permute-start | bytes 294920 | tf_op jit(solution)/shard_map/ppermute | solution.py:1053
  249.7 7.0 %collective-permute-start.27 = (bf16[2,48,512]{2,1,0:T(8,128)(2,1)S(1)}, bf16[2,48,512]{2,1,0:T(8,128)(2,1)S(1)}, u32[]{:S(2)}, u32[]{:S(2)}) collective-permute-start(bf16[2,48,512]{2,1,0:T(8,128)(2,1)S(1)} %get-tuple-element.213), channel_id=1, source_target_pairs={{0,1},{1,2},{2,3},{3,0},{4,5},{5,6},{6,7},{7,4},{8,9},{9,10},{10,1... | collective-permute-start | bytes 294920 | tf_op jit(solution)/shard_map/ppermute | solution.py:1053
  253.2 5.6 %collective-permute-start.28 = (bf16[2,48,512]{2,1,0:T(8,128)(2,1)S(1)}, bf16[2,48,512]{2,1,0:T(8,128)(2,1)S(1)}, u32[]{:S(2)}, u32[]{:S(2)}) collective-permute-start(bf16[2,48,512]{2,1,0:T(8,128)(2,1)S(1)} %get-tuple-element.213), channel_id=1, source_target_pairs={{0,3},{1,0},{2,1},{3,2},{4,7},{5,4},{6,5},{7,6},{8,11},{9,8},{10,9... | collective-permute-start | bytes 294920 | tf_op jit(solution)/shard_map/ppermute | solution.py:1053
  256.7 6.2 %collective-permute-start.29 = (bf16[2,48,512]{2,1,0:T(8,128)(2,1)S(1)}, bf16[2,48,512]{2,1,0:T(8,128)(2,1)S(1)}, u32[]{:S(2)}, u32[]{:S(2)}) collective-permute-start(bf16[2,48,512]{2,1,0:T(8,128)(2,1)S(1)} %get-tuple-element.213), channel_id=1, source_target_pairs={{0,2},{1,3},{2,0},{3,1},{4,6},{5,7},{6,4},{7,5},{8,10},{9,11},{10,... | collective-permute-start | bytes 294920 | tf_op jit(solution)/shard_map/ppermute | solution.py:1053
  264.4 59.3 %all-to-all-start.2 = ((bf16[32,64,512]{2,1,0:T(8,128)(2,1)}), bf16[32,64,512]{2,1,0:T(8,128)(2,1)S(1)}, u32[]{:S(2)}, u32[]{:S(2)}) async-start(bf16[32,64,512]{2,1,0:T(8,128)(2,1)} %bitcast.107), calls=%async_computation.2 | async-start | bytes 4194304 | tf_op jit(solution)/shard_map/all_to_all | solution.py:1360
  271.3 20.5 %collective-permute-start.30 = (bf16[240,512]{1,0:T(8,128)(2,1)S(1)}, bf16[240,512]{1,0:T(8,128)(2,1)S(1)}, u32[]{:S(2)}, u32[]{:S(2)}) collective-permute-start(bf16[240,512]{1,0:T(8,128)(2,1)S(1)} %constant_dynamic-update-slice_fusion.refs_0_), channel_id=1, source_target_pairs={{0,8},{4,12},{8,0},{12,4},{16,24},{20,28},{24,16},{28,20},{1,9},{5... | collective-permute-start | bytes 737288 | tf_op jit(solution)/shard_map/ppermute | solution.py:1069
  272.9 18.8 %collective-permute-start.31 = (bf16[192,512]{1,0:T(8,128)(2,1)S(1)}, bf16[192,512]{1,0:T(8,128)(2,1)S(1)}, u32[]{:S(2)}, u32[]{:S(2)}) collective-permute-start(bf16[192,512]{1,0:T(8,128)(2,1)S(1)} %slice_bitcast_fusion.2.refs_2_), channel_id=1, source_target_pairs={{0,16},{4,20},{8,24},{12,28},{16,0},{20,4},{24,8},{28,12},{1,17},{... | collective-permute-start | bytes 589832 | tf_op jit(solution)/shard_map/ppermute | solution.py:1069
  292.4 15.8 %collective-permute-start.32 = (bf16[480,512]{1,0:T(8,128)(2,1)S(1)}, bf16[480,512]{1,0:T(8,128)(2,1)S(1)}, u32[]{:S(2)}, u32[]{:S(2)}) collective-permute-start(bf16[480,512]{1,0:T(8,128)(2,1)S(1)} %get-tuple-element.201.refs_0_), channel_id=1, source_target_pairs={{0,16},{4,20},{8,24},{12,28},{16,0},{20,4},{24,8},{28,12},{1,17},{... | collective-permute-start | bytes 1474568 | tf_op jit(solution)/shard_map/ppermute | solution.py:1069
  293.9 13.8 %collective-permute-start.33 = (bf16[384,512]{1,0:T(8,128)(2,1)S(1)}, bf16[384,512]{1,0:T(8,128)(2,1)S(1)}, u32[]{:S(2)}, u32[]{:S(2)}) collective-permute-start(bf16[384,512]{1,0:T(8,128)(2,1)S(1)} %get-tuple-element.202.refs_2_), channel_id=1, source_target_pairs={{0,8},{4,12},{8,0},{12,4},{16,24},{20,28},{24,16},{28,20},{1,9},{5... | collective-permute-start | bytes 1179656 | tf_op jit(solution)/shard_map/ppermute | solution.py:1069
  308.9 10.0 %collective-permute-start.34 = (bf16[960,512]{1,0:T(8,128)(2,1)S(1)}, bf16[960,512]{1,0:T(8,128)(2,1)S(1)}, u32[]{:S(2)}, u32[]{:S(2)}) collective-permute-start(bf16[960,512]{1,0:T(8,128)(2,1)S(1)} %get-tuple-element.203.second_ref), channel_id=1, source_target_pairs={{0,4},{4,0},{8,12},{12,8},{16,20},{20,16},{24,28},{28,24},{1,5},{5... | collective-permute-start | bytes 2949128 | tf_op jit(solution)/shard_map/ppermute | solution.py:1069
  308.9 9.9 %collective-permute-start.35 = (bf16[768,512]{1,0:T(8,128)(2,1)S(1)}, bf16[768,512]{1,0:T(8,128)(2,1)S(1)}, u32[]{:S(2)}, u32[]{:S(2)}) collective-permute-start(bf16[768,512]{1,0:T(8,128)(2,1)S(1)} %get-tuple-element.204.first_ref), channel_id=1, source_target_pairs={{0,4},{4,0},{8,12},{12,8},{16,20},{20,16},{24,28},{28,24},{1,5},{5... | collective-permute-start | bytes 2359304 | tf_op jit(solution)/shard_map/ppermute | solution.py:1069
  (43 other events, 559.1 us)

commit v3 on v2

--- a/solution.py
+++ b/solution.py
@@ -19,7 +19,7 @@
 MIB = 2**20
 
 STAT_ROWS = 24
-FIRST_ROW, LAST_ROW, EXTRA_ROW = 16, 17, 18
+FIRST_ROW, LAST_ROW, EXTRA_ROW, FIRST_GRAD, LAST_GRAD = 16, 17, 18, 19, 20
 SMALL_ROWS = 48
 BITS_AT = 12
 
@@ -97,6 +97,36 @@
             return carry
 
         lax.fori_loop(low, high + 1, step, 0)
+
+
+class Blocks:
+    def __init__(self, ends, base, channels):
+        self.ends, self.base, self.channels = ends, base, channels
+
+    def plain(self, start, body):
+        for inside in range(0, ROWS, BLOCK):
+            first = self.base + start + inside
+            low = owner_at(self.ends, first)
+            alone = (low == owner_at(self.ends, first + BLOCK - 1)).astype(F32)
+            body(start + inside, low, alone)
+
+    def mixed(self, start, body):
+        def step(i, carry):
+            at = pl.multiple_of(start + i * BLOCK, BLOCK)
+            by_utterance(
+                self.ends,
+                self.base + at,
+                BLOCK,
+                lambda u: None,
+                lambda u, mask: body(at, u, mask((BLOCK, self.channels))),
+            )
+            return carry
+
+        low = owner_at(self.ends, self.base + start)
+
+        @pl.when(low != owner_at(self.ends, self.base + start + ROWS - 1))
+        def _():
+            lax.fori_loop(0, ROWS // BLOCK, step, 0)
 
 
 def row(ref, index):
@@ -175,10 +205,11 @@
 ACC_ROWS = 2 * (UTTS + 1) * 8
 
 
-def add_stats(acc_ref, u, first, second):
+def add_stats(acc_ref, u, first, second, weight=None):
     for kind, term in enumerate((first, second)):
         at = pl.ds(pl.multiple_of((kind * (UTTS + 1) + u) * 8, 8), 8)
-        acc_ref[at, :] += fold_rows(term)
+        term = fold_rows(term)
+        acc_ref[at, :] += term if weight is None else term * weight
 
 
 def read_ends(info_ref):
@@ -193,8 +224,6 @@
 def gradient_kernel(
     info_ref,
     cot_hbm,
-    before_ref,
-    after_ref,
     weight_ref,
     out_hbm,
     padded_hbm,
@@ -204,24 +233,17 @@
     out_ref,
     cot_sems,
     padded_sems,
-    edge_sems,
     out_sems,
 ):
     frames, channels = cot_ref.shape
     ends = read_ends(info_ref)
     base = info_ref[8]
     cot_in = Stream(cot_hbm, cot_ref, cot_sems)
-    padded_out = Stream(padded_ref, padded_hbm, padded_sems, PAD, PAD)
+    padded_out = Stream(padded_ref, padded_hbm, padded_sems, PAD)
     outward = Stream(out_ref, out_hbm, out_sems)
     cot_in.start()
-    owner_before, owner_after = halo_owner(info_ref, ends, base, frames)
-    tile = jnp.broadcast_to(before_ref[...].astype(F32) * ROOT_HALF, (PAD, channels))
-    padded_ref[0:PAD, :] = jnp.where(owner_before < UTTS, tile, 0.0).astype(BF16)
-    tile = jnp.broadcast_to(after_ref[...].astype(F32) * ROOT_HALF, (PAD, channels))
-    padded_ref[PAD + frames :, :] = jnp.where(owner_after < UTTS, tile, 0.0).astype(BF16)
-    edges = edge_copies(padded_ref, padded_hbm, edge_sems)
-    for edge in edges:
-        edge.start()
+    padded_ref[0:PAD, :] = jnp.zeros((PAD, channels), BF16)
+    padded_ref[PAD + frames :, :] = jnp.zeros((PAD, channels), BF16)
     bias_ref[...] = jnp.zeros_like(bias_ref)
 
     def scale(start):
@@ -229,7 +251,7 @@
         here = jnp.where(rows_of(base + start, (BLOCK, channels)) < ends[UTTS - 1], here, 0.0)
         rounded = here.astype(BF16)
         padded_ref[pl.ds(start + PAD, BLOCK), :] = rounded
-        bias_ref[...] += fold_rows(rounded.astype(F32))
+        bias_ref[0:8, :] += fold_rows(rounded.astype(F32))
 
     def scale_tile(i, start):
         cot_in.tile(i).wait()
@@ -245,10 +267,10 @@
         outward.tile(i).start()
 
     for_tiles(frames, conv)
+    bias_ref[8:9, :] = padded_ref[PAD : 2 * PAD, :].astype(F32)[0:1]
+    bias_ref[9:10, :] = padded_ref[frames : frames + PAD, :].astype(F32)[PAD - 1 :]
     padded_out.finish()
     outward.finish()
-    for edge in edges:
-        edge.wait()
 
 
 def upsample_kernel(
@@ -326,7 +348,8 @@
     finish_stats(acc_ref, stat_ref)
     stat_ref[FIRST_ROW : FIRST_ROW + 1, :] = out_ref[0:1, :]
     stat_ref[LAST_ROW : LAST_ROW + 1, :] = out_ref[frames - 1 : frames, :]
-    stat_ref[EXTRA_ROW : EXTRA_ROW + 1, :] = jnp.sum(bias_ref[...], axis=0, keepdims=True)
+    stat_ref[EXTRA_ROW : EXTRA_ROW + 1, :] = jnp.sum(bias_ref[0:8, :], axis=0, keepdims=True)
+    stat_ref[FIRST_GRAD : FIRST_GRAD + 2, :] = bias_ref[8:10, :]
     outward.finish()
     wide_out.finish()
 
@@ -353,23 +376,35 @@
     mean = total * inverse
     real = inverse > 0.0
     rstd = jnp.where(real, lax.rsqrt(square * inverse - mean * mean + EPSILON), 0.0)
+    gain = jnp.where(real, 1.0 + params_ref[:, 0:channels], 0.0)
+    shift = jnp.where(real, params_ref[:, channels : 2 * channels], 0.0)
     coef_ref[0:8, :] = rstd
     coef_ref[8:16, :] = mean * rstd
-    coef_ref[16:24, :] = jnp.where(real, 1.0 + params_ref[:, 0:channels], 0.0)
-    coef_ref[24:32, :] = jnp.where(real, params_ref[:, channels : 2 * channels], 0.0)
+    coef_ref[16:24, :] = gain * rstd
+    coef_ref[24:32, :] = 0.5 * gain
+    coef_ref[32:40, :] = 0.5 * shift
+    coef_ref[40:48, :] = 0.5 * gain * rstd
+    coef_ref[48:56, :] = 0.5 * (shift - mean * gain * rstd)
+
+
+UNIT, HALF_OF_UNIT, HALF_OF_VALUE = (0, 8), (24, 32), (40, 48)
 
 
 def unit_of(values, coef_ref, u):
     return values * row(coef_ref, u) - row(coef_ref, 8 + u)
 
 
-def normed_of(unit, coef_ref, u):
-    return unit * row(coef_ref, 16 + u) + row(coef_ref, 24 + u)
+def half_normed(values, coef_ref, u, rows):
+    return values * row(coef_ref, rows[0] + u) + row(coef_ref, rows[1] + u)
+
+
+def twice_logistic(half):
+    return jnp.tanh(half) + 1.0
 
 
 def activation(values, coef_ref, u):
-    normed = normed_of(unit_of(values, coef_ref, u), coef_ref, u)
-    return normed * logistic(normed)
+    half = half_normed(values, coef_ref, u, HALF_OF_VALUE)
+    return half * twice_logistic(half)
 
 
 def edge_rows(padded_ref, before, after):
@@ -389,23 +424,31 @@
     inverse_ref,
     params_ref,
     weight_ref,
+    turned_ref,
     act_hbm,
     out_ref,
+    out_hbm,
     unit_hbm,
     coef_ref,
     stat_ref,
+    edge_ref,
+    added_ref,
     acc_ref,
     act_ref,
     unit_ref,
     act_sems,
     edge_sems,
+    out_sems,
     unit_sems,
 ):
     frames, channels = values_ref.shape
+    tiles = frames // ROWS
     act_out = Stream(act_ref, act_hbm, act_sems, PAD, PAD)
     unit_out = Stream(unit_ref, unit_hbm, unit_sems)
+    outward = Stream(out_ref, out_hbm, out_sems)
     ends = read_ends(info_ref)
     base = info_ref[8]
+    blocks = Blocks(ends, base, channels)
     write_coefficients(own_ref, (one_ref, two_ref, three_ref), inverse_ref, params_ref, coef_ref)
     acc_ref[...] = jnp.zeros_like(acc_ref)
     owner_before, owner_after = halo_owner(info_ref, ends, base, frames)
@@ -414,62 +457,81 @@
         activation(row(one_ref, LAST_ROW), coef_ref, owner_before),
         activation(row(three_ref, FIRST_ROW), coef_ref, owner_after),
     )
-
     edges = edge_copies(act_ref, act_hbm, edge_sems)
     for edge in edges:
         edge.start()
 
-    def act_step(start):
-        here = pl.ds(start, BLOCK)
-        there = pl.ds(start + PAD, BLOCK)
-
-        def parts(u):
-            unit = unit_of(values_ref[here, :], coef_ref, u)
-            normed = normed_of(unit, coef_ref, u)
-            return unit, normed * logistic(normed)
-
-        def uniform(u):
-            unit, act = parts(u)
-            unit_ref[here, :] = unit.astype(BF16)
-            act_ref[there, :] = act.astype(BF16)
-
-        def mixed(u, mask):
-            keep = mask((BLOCK, channels))
-            unit, act = parts(u)
-            unit_ref[here, :] = jnp.where(keep, unit, unit_ref[here, :].astype(F32)).astype(BF16)
-            act_ref[there, :] = jnp.where(keep, act, act_ref[there, :].astype(F32)).astype(BF16)
-
-        by_utterance(ends, base + start, BLOCK, uniform, mixed)
-
-    def act_tile(i, start):
-        for_blocks(start, ROWS, BLOCK, act_step)
-        act_out.tile(i).start()
-        unit_out.tile(i).start()
-
-    for_tiles(frames, act_tile)
-
-    def conv(start):
-        out_ref[pl.ds(start, ROWS), :] = convolved(
-            taps_of(act_ref, ends, start, base), weight_ref
-        )
-
-    for_blocks(0, frames, ROWS, conv)
-    for_blocks(0, frames, BLOCK, lambda start: value_sums(out_ref, acc_ref, ends, base, start))
+    def act_parts(at, u):
+        unit = unit_of(values_ref[pl.ds(at, BLOCK), :], coef_ref, u)
+        half = half_normed(unit, coef_ref, u, HALF_OF_UNIT)
+        return unit, half * twice_logistic(half)
+
+    def act_plain(at, u, alone):
+        unit, act = act_parts(at, u)
+        unit_ref[pl.ds(at, BLOCK), :] = unit.astype(BF16)
+        act_ref[pl.ds(at + PAD, BLOCK), :] = act.astype(BF16)
+
+    def act_mixed(at, u, keep):
+        here, there = pl.ds(at, BLOCK), pl.ds(at + PAD, BLOCK)
+        unit, act = act_parts(at, u)
+        unit_ref[here, :] = jnp.where(keep, unit, unit_ref[here, :].astype(F32)).astype(BF16)
+        act_ref[there, :] = jnp.where(keep, act, act_ref[there, :].astype(F32)).astype(BF16)
+
+    def sums_plain(at, u, alone):
+        here = out_ref[pl.ds(at, BLOCK), :]
+        add_stats(acc_ref, u, here, here * here, alone)
+
+    def sums_mixed(at, u, keep):
+        here = jnp.where(keep, out_ref[pl.ds(at, BLOCK), :], 0.0)
+        add_stats(acc_ref, u, here, here * here)
+
+    for turn in range(-1, tiles + 1):
+        if turn + 1 < tiles:
+            blocks.plain((turn + 1) * ROWS, act_plain)
+        if 0 <= turn < tiles:
+            start = turn * ROWS
+            out_ref[start : start + ROWS, :] = convolved(
+                taps_of(act_ref, ends, start, base), weight_ref
+            )
+        if turn > 0:
+            blocks.plain((turn - 1) * ROWS, sums_plain)
+        if turn + 1 < tiles:
+            blocks.mixed((turn + 1) * ROWS, act_mixed)
+            act_out.tile(turn + 1).start()
+            unit_out.tile(turn + 1).start()
+        if 0 <= turn < tiles:
+            outward.tile(turn).start()
+        if turn > 0:
+            blocks.mixed((turn - 1) * ROWS, sums_mixed)
+    edge_ref[...] = jnp.zeros_like(edge_ref)
+    added_ref[...] = jnp.zeros_like(added_ref)
+    neighbours = (
+        (one_ref, LAST_GRAD, owner_before, owner_at(ends, base), 2 * channels),
+        (three_ref, FIRST_GRAD, owner_after, owner_at(ends, base + frames - 1), 0),
+    )
+    for k, (ref, at, theirs, ours, tap) in enumerate(neighbours):
+        valid = (theirs == ours) & (ours < UTTS)
+        edge_ref[k : k + 1, :] = jnp.where(valid, ref[at : at + 1, :], 0.0)
+        rows = jnp.broadcast_to(edge_ref[k : k + 1, :], (PAD, channels)).astype(BF16)
+        added_ref[k : k + 1, :] = jnp.dot(
+            rows, turned_ref[tap : tap + channels, :], preferred_element_type=F32
+        )[0:1]
     finish_stats(acc_ref, stat_ref)
     stat_ref[FIRST_ROW : FIRST_ROW + 1, :] = out_ref[0:1, :]
     stat_ref[LAST_ROW : LAST_ROW + 1, :] = out_ref[frames - 1 : frames, :]
     act_out.finish()
     unit_out.finish()
+    outward.finish()
     for edge in edges:
         edge.wait()
 
 
-def slope_and_sums(gradient, unit, coef_ref, u):
-    normed = normed_of(unit, coef_ref, u)
-    gate = logistic(normed)
-    act = normed * gate
-    inner = gradient * (gate + act * (1.0 - gate))
-    return act, inner, inner * unit
+def slope_and_sums(gradient, values, coef_ref, u, rows):
+    half = half_normed(values, coef_ref, u, rows)
+    gate = twice_logistic(half)
+    act = half * gate
+    inner = gradient * (gate * (half - 0.5 * act + 0.5))
+    return act, inner, inner * values
 
 
 def second_norm_kernel(
@@ -482,28 +544,25 @@
     three_ref,
     inverse_ref,
     params_ref,
-    act_ref,
+    added_ref,
     act_hbm,
     inner_hbm,
-    unit_hbm,
     coef_ref,
     stat_ref,
     acc_ref,
     gradient_ref,
+    act_ref,
     inner_ref,
-    unit_ref,
     gradient_sems,
     act_sems,
     edge_sems,
     inner_sems,
-    unit_sems,
 ):
     frames, channels = values_ref.shape
     gradient_in = Stream(gradient_hbm, gradient_ref, gradient_sems)
     outward = [
         Stream(act_ref, act_hbm, act_sems, PAD, PAD),
         Stream(inner_ref, inner_hbm, inner_sems),
-        Stream(unit_ref, unit_hbm, unit_sems),
     ]
     gradient_in.start()
     ends = read_ends(info_ref)
@@ -526,21 +585,20 @@
         there = pl.ds(start + PAD, BLOCK)
 
         def parts(u):
-            unit = unit_of(values_ref[here, :], coef_ref, u)
-            return unit, *slope_and_sums(gradient_ref[here, :].astype(F32), unit, coef_ref, u)
+            return slope_and_sums(
+                gradient_ref[here, :].astype(F32), values_ref[here, :], coef_ref, u, HALF_OF_VALUE
+            )
 
         def uniform(u):
-            unit, act, inner, cross = parts(u)
+            act, inner, cross = parts(u)
             act_ref[there, :] = act.astype(BF16)
-            unit_ref[here, :] = unit.astype(BF16)
             inner_ref[here, :] = inner.astype(BF16)
             add_stats(acc_ref, u, inner, cross)
 
         def mixed(u, mask):
             keep = mask((BLOCK, channels))
-            unit, act, inner, cross = parts(u)
+            act, inner, cross = parts(u)
             act_ref[there, :] = jnp.where(keep, act, act_ref[there, :].astype(F32)).astype(BF16)
-            unit_ref[here, :] = jnp.where(keep, unit, unit_ref[here, :].astype(F32)).astype(BF16)
             old = inner_ref[here, :].astype(F32)
             inner_ref[here, :] = jnp.where(keep, inner, old).astype(BF16)
             add_stats(acc_ref, u, jnp.where(keep, inner, 0.0), jnp.where(keep, cross, 0.0))
@@ -549,6 +607,15 @@
 
     def tile(i, start):
         gradient_in.tile(i).wait()
+        for k, at in enumerate((0, frames - PAD)):
+
+            @pl.when(i == at // ROWS)
+            def _(k=k, at=at):
+                edge = gradient_ref[at : at + PAD, :].astype(F32)
+                inside = rows_of(0, (PAD, channels)) == k * (PAD - 1)
+                edge = edge + jnp.where(inside, added_ref[k : k + 1, :], 0.0)
+                gradient_ref[at : at + PAD, :] = edge.astype(BF16)
+
         for_blocks(start, ROWS, BLOCK, step)
         for stream in outward:
             stream.tile(i).start()
@@ -609,35 +676,34 @@
 
 
 def weight_gradient_kernel(
-    stream_act,
     info_ref,
-    act_any,
-    gradient_any,
+    act_hbm,
+    gradient_hbm,
+    edge_ref,
     keep_ref,
     give_ref,
     out_ref,
-    held_ref,
-    held_sems,
-    edge_sems,
+    act_ref,
+    gradient_ref,
+    act_sems,
+    gradient_sems,
 ):
-    frames = held_ref.shape[0] - 2 * PAD
-    channels = held_ref.shape[1]
+    frames = act_ref.shape[0] - 2 * PAD
+    channels = act_ref.shape[1]
     ends = read_ends(info_ref)
     base = info_ref[8]
-    source = act_any if stream_act else gradient_any
-    act_ref, gradient_ref = (held_ref, gradient_any) if stream_act else (act_any, held_ref)
-    inward_stream = Stream(source, held_ref, held_sems, PAD, PAD)
-    edges = edge_copies(source, held_ref, edge_sems)
-    for edge in edges:
-        edge.start()
-    inward_stream.start()
+    act_in = Stream(act_hbm, act_ref, act_sems, PAD, PAD)
+    gradient_in = Stream(gradient_hbm, gradient_ref, gradient_sems, 0, PAD)
+    for index in range(frames // ROWS):
+        gradient_in.tile(index).start()
+        act_in.tile(index).start()
     out_ref[...] = jnp.zeros_like(out_ref)
-    for edge in edges:
-        edge.wait()
-    inward_stream.tile(0).wait()
+    edge_rows(gradient_ref, edge_ref[0:1, :], edge_ref[1:2, :])
+    gradient_in.tile(0).wait()
 
     def step(i, start):
-        wait_next([inward_stream], i, frames)
+        wait_next([gradient_in], i, frames)
+        act_in.tile(i).wait()
         before, here, after = taps_of(gradient_ref, ends, start, base)
         act = act_ref[pl.ds(start + PAD, ROWS), :]
         for k, tap in enumerate((after, here, before)):
@@ -733,26 +799,29 @@
     bias_ref[...] = jnp.sum(biases, axis=0, keepdims=True)
 
 
-def back_coefficients(own_ref, other_refs, inverse_ref, coef_ref, back_ref):
+def back_coefficients(own_ref, other_refs, inverse_ref, coef_ref, back_ref, of_values):
     inverse = inverse_ref[...]
+    rstd, mean_rstd, scale = coef_ref[0:8, :], coef_ref[8:16, :], coef_ref[16:24, :]
     total = sum_over_tm(own_ref, other_refs, 0, 8)
     cross = sum_over_tm(own_ref, other_refs, 8, 8)
-    scale = coef_ref[0:8, :] * coef_ref[16:24, :]
+    if of_values:
+        cross = rstd * cross - mean_rstd * total
     back_ref[0:8, :] = total
     back_ref[8:16, :] = cross
-    back_ref[16:24, :] = scale * total * inverse
-    back_ref[24:32, :] = scale * cross * inverse
+    slant = scale * cross * inverse
+    back_ref[16:24, :] = scale * total * inverse - (mean_rstd * slant if of_values else 0.0)
+    back_ref[24:32, :] = rstd * slant if of_values else slant
     back_ref[32:40, :] = scale
 
 
-def inward(inner, unit, back_ref, u):
-    return inner * row(back_ref, 32 + u) - row(back_ref, 16 + u) - unit * row(back_ref, 24 + u)
+def inward(inner, values, back_ref, u):
+    return inner * row(back_ref, 32 + u) - row(back_ref, 16 + u) - values * row(back_ref, 24 + u)
 
 
 def first_back_kernel(
     info_ref,
     inner_hbm,
-    unit_two_hbm,
+    middle_hbm,
     own_ref,
     one_ref,
     two_ref,
@@ -764,46 +833,51 @@
     coef_one_ref,
     unit_one_hbm,
     weight_ref,
-    gradient_ref,
+    gradient_hbm,
+    edge_ref,
     out_hbm,
     back_ref,
     stat_ref,
     acc_ref,
     full_ref,
     inner_ref,
-    unit_two_ref,
+    middle_ref,
     unit_one_ref,
     out_ref,
+    gradient_ref,
     inner_sems,
     two_sems,
     one_sems,
     out_sems,
+    gradient_sems,
 ):
     frames, channels = unit_one_ref.shape
     early = [
         Stream(inner_hbm, inner_ref, inner_sems),
-        Stream(unit_two_hbm, unit_two_ref, two_sems),
+        Stream(middle_hbm, middle_ref, two_sems),
     ]
     late = Stream(unit_one_hbm, unit_one_ref, one_sems)
     outward = Stream(out_ref, out_hbm, out_sems)
-    for stream in (*early, late):
-        stream.start()
+    gradient_out = Stream(gradient_ref, gradient_hbm, gradient_sems, PAD)
+    for index in range(frames // ROWS):
+        for stream in (*early, late):
+            stream.tile(index).start()
     ends = read_ends(info_ref)
     base = info_ref[8]
-    back_coefficients(own_ref, (one_ref, two_ref, three_ref), inverse_ref, coef_two_ref, back_ref)
+    back_coefficients(own_ref, (one_ref, two_ref, three_ref), inverse_ref, coef_two_ref, back_ref, True)
     acc_ref[...] = jnp.zeros_like(acc_ref)
     owner_before, owner_after = halo_owner(info_ref, ends, base, frames)
     edge_rows(
         gradient_ref,
         inward(
             row(one_ref, LAST_ROW),
-            unit_of(row(middle_one_ref, LAST_ROW), coef_two_ref, owner_before),
+            row(middle_one_ref, LAST_ROW),
             back_ref,
             owner_before,
         ),
         inward(
             row(three_ref, FIRST_ROW),
-            unit_of(row(middle_three_ref, FIRST_ROW), coef_two_ref, owner_after),
+            row(middle_three_ref, FIRST_ROW),
             back_ref,
             owner_after,
         ),
@@ -815,7 +889,7 @@
 
         def now(u):
             return inward(
-                inner_ref[here, :].astype(F32), unit_two_ref[here, :].astype(F32), back_ref, u
+                inner_ref[here, :].astype(F32), middle_ref[here, :], back_ref, u
             )
 
         def uniform(u):
@@ -827,12 +901,16 @@
 
         by_utterance(ends, base + start, BLOCK, uniform, mixed)
 
-    def back_tile(i, start):
+    edge_ref[0:8, :] = gradient_ref[0:PAD, :].astype(F32)[0:8]
+    edge_ref[1:2, :] = gradient_ref[PAD + frames :, :].astype(F32)[0:1]
+
+    def back_tile(i):
         for stream in early:
             stream.tile(i).wait()
-        for_blocks(start, ROWS, BLOCK, back_step)
-
-    for_tiles(frames, back_tile)
+        for_blocks(pl.multiple_of(i * ROWS, ROWS), ROWS, BLOCK, back_step)
+        gradient_out.tile(i).start()
+
+    back_tile(0)
 
     def slope_step(start, row_start):
         here = pl.ds(start, BLOCK)
@@ -840,7 +918,7 @@
         def parts(u):
             unit = unit_one_ref[here, :].astype(F32)
             _, inner, cross = slope_and_sums(
-                full_ref[pl.ds(row_start, BLOCK), :], unit, coef_one_ref, u
+                full_ref[pl.ds(row_start, BLOCK), :], unit, coef_one_ref, u, HALF_OF_UNIT
             )
             return inner, cross
 
@@ -859,6 +937,10 @@
         by_utterance(ends, base + start, BLOCK, uniform, mixed)
 
     def conv(i, start):
+        @pl.when(i + 1 < frames // ROWS)
+        def _():
+            back_tile(i + 1)
+
         late.tile(i).wait()
         before, here, after = taps_of(gradient_ref, ends, start, base)
         full_ref[...] = convolved((after, here, before), weight_ref)
@@ -868,6 +950,7 @@
     for_tiles(frames, conv)
     finish_stats(acc_ref, stat_ref)
     outward.finish()
+    gradient_out.finish()
 
 
 def buffer_gradient_kernel(
@@ -887,7 +970,6 @@
     out_ref,
     after_ref,
     back_ref,
-    free_ref,
     up_ref,
     total_ref,
     inner_ref,
@@ -914,7 +996,9 @@
     halo, own = before_ref.shape[0], out_ref.shape[0]
     ends = read_ends(info_ref)
     base, slot_base = info_ref[8], info_ref[9]
-    back_coefficients(own_ref, (one_ref, two_ref, three_ref), inverse_ref, coef_ref, back_ref)
+    back_coefficients(
+        own_ref, (one_ref, two_ref, three_ref), inverse_ref, coef_ref, back_ref, False
+    )
     total_ref[...] = jnp.zeros_like(total_ref)
     span = rows + PAD
 
@@ -963,43 +1047,38 @@
     before_ref[...] = total_ref[0:halo, :]
     out_ref[...] = total_ref[halo : halo + own, :]
     after_ref[...] = total_ref[halo + own : 2 * halo + own, :]
-    groups, copies, half = free_ref.shape[:3]
-    for s in range(groups):
-        first = halo + (2 * s + (1 if s < groups // 2 else 0)) * half
-        rows_out = total_ref[first : first + half, :].astype(BF16)
-        for t in range(copies):
-            free_ref[s, t] = rows_out
-
-
-def scatter_kernel(late, info_ref, order_ref, part_ref, *refs):
-    out_ref, tmp_ref = refs[-2], refs[-1]
-    blocks, half, channels = part_ref.shape
+
+
+def scatter_kernel(places, copies, info_ref, order_ref, *refs):
+    parts, out_ref, tmp_ref = refs[: len(places)], refs[-2], refs[-1]
+    groups, piece, channels = parts[0].shape
     lanes = channels // 128
-    offset = jnp.where(info_ref[11] == 1 - late, half, 0)
-    for old_ref in refs[:-2]:
+    me = info_ref[10]
+    for old_ref in refs[len(places) : -2]:
 
         def copy(start, old_ref=old_ref):
             out_ref[pl.ds(start, ROWS), :] = old_ref[pl.ds(start, ROWS), :]
 
         for_blocks(0, out_ref.shape[0], ROWS, copy)
-
-    def body(block, carry):
-        for b in range(half // 16):
-            both = part_ref[block, b * 16 : b * 16 + 16, :].astype(F32)
-            for h in range(2):
-                for q in range(lanes):
-                    tmp_ref[pl.ds(((2 * b + h) * lanes + q) * 8, 8), :] = both[
-                        8 * h : 8 * h + 8, q * 128 : (q + 1) * 128
-                    ]
-        first = block * 2 * half + offset
-        for r in range(half):
-            to = order_ref[first + r]
-            out_ref[pl.ds((to >> 3) * (8 * lanes) + (to & 7), lanes, stride=8), :] = tmp_ref[
-                pl.ds((r // 8) * 8 * lanes + r % 8, lanes, stride=8), :
-            ]
-        return carry
-
-    lax.fori_loop(0, blocks, body, 0)
+    for back, part_ref in zip(places, parts):
+        source = lax.rem(me + copies - back, copies)
+
+        def body(g, carry, part_ref=part_ref, source=source):
+            for b in range(piece // 16):
+                both = part_ref[g, b * 16 : b * 16 + 16, :].astype(F32)
+                for h in range(2):
+                    for q in range(lanes):
+                        tmp_ref[pl.ds(((2 * b + h) * lanes + q) * 8, 8), :] = both[
+                            8 * h : 8 * h + 8, q * 128 : (q + 1) * 128
+                        ]
+            first = (g * copies + source) * piece
+            for r in range(piece):
+                out_ref[pl.ds(order_ref[first + r], lanes, stride=8), :] = tmp_ref[
+                    pl.ds((r // 8) * 8 * lanes + r % 8, lanes, stride=8), :
+                ]
+            return carry
+
+        lax.fori_loop(0, groups, body, 0)
 
 
 VM = pl.BlockSpec(memory_space=pltpu.VMEM)
@@ -1032,20 +1111,20 @@
     )
 
 
-def scattered(old, part, late, info, order):
-    half, channels = part.shape[1:]
+def scattered(old, parts, places, copies, info, order):
+    piece, channels = parts[0].shape[1:]
     lanes = channels // 128
     kept = [] if old is None else [old]
     return pl.pallas_call(
-        functools.partial(scatter_kernel, late),
-        in_specs=[SM, SM] + [VM] * (1 + len(kept)),
+        functools.partial(scatter_kernel, places, copies),
+        in_specs=[SM, SM] + [VM] * (len(parts) + len(kept)),
         out_specs=VM,
         out_shape=jax.ShapeDtypeStruct((order.shape[0] * lanes, 128), F32),
-        scratch_shapes=[pltpu.VMEM((half * lanes, 128), F32)],
-        input_output_aliases={3: 0} if kept else {},
+        scratch_shapes=[pltpu.VMEM((piece * lanes, 128), F32)],
+        input_output_aliases={2 + len(parts): 0} if kept else {},
         compiler_params=pltpu.CompilerParams(vmem_limit_bytes=22 * MIB),
         cost_estimate=pl.CostEstimate(flops=10**6, bytes_accessed=10**4, transcendentals=0),
-    )(info, order, part, *kept)
+    )(info, order, *parts, *kept)
 
 
 def shifted(values, axis, step):
@@ -1156,31 +1235,28 @@
 
     tiles_of = frames // ROWS
     full, padded = (frames, channels), (frames + 2 * PAD, channels)
-    stats_shape, coef_shape = (STAT_ROWS, channels), (32, channels)
+    stats_shape, coef_shape = (STAT_ROWS, channels), (56, channels)
     small_acc = ((ACC_ROWS, channels), F32)
 
-    cot_before, cot_after = from_neighbours(cotangent[:1], cotangent[-1:])
     order = send_order[0].reshape(groups, copies, piece_rows)
     mine = lax.dynamic_index_in_dim(order, tm_index, 1, False)
     outgoing = jnp.take(phonemes, mine.reshape(-1), axis=0, mode="clip")
-    outgoing = after(outgoing, cot_before, cot_after)
     received = lax.all_to_all(
         outgoing.reshape(groups, piece_rows, channels), "seq", 0, 0, tiled=True
     ).reshape(local_rows, channels)
 
+    second_turned = turned(second_conv_weight)
     grad_act_two, grad_branch, bias_part = call(
         gradient_kernel,
         (
             (info, SM),
             (cotangent, HB),
-            (cot_before, VM),
-            (cot_after, VM),
-            (turned(second_conv_weight), VM),
-        ),
-        ((full, BF16, HB), (padded, BF16, HB), ((8, channels), F32, VM)),
-        [(full, BF16), (padded, BF16), (full, BF16), tiles_of, tiles_of, 2, tiles_of],
+            (second_turned, VM),
+        ),
+        ((full, BF16, HB), (full, BF16, HB), ((16, channels), F32, VM)),
+        [(full, BF16), (padded, BF16), (full, BF16), tiles_of, tiles_of, tiles_of],
         conv_flops,
-        24,
+        32,
     )
 
     received, bias_part = lax.optimization_barrier((received, bias_part))
@@ -1212,14 +1288,14 @@
             tiles_of,
         ],
         2 * frames * WIDE * channels,
-        12,
+        20,
     )
     others = others_over_tm(stat)
     bias_total = (stat[EXTRA_ROW] + others[1][EXTRA_ROW]) + (
         others[0][EXTRA_ROW] + others[2][EXTRA_ROW]
     )
 
-    act_one, middle, unit_one, coef_one, stat_two = call(
+    act_one, middle, middle_far, unit_one, coef_one, stat_two, grad_edges, added = call(
         first_conv_kernel,
         (
             (info, SM),
@@ -1228,21 +1304,25 @@
             (inverse, VM),
             (params_one, VM),
             (first_conv_weight, VM),
+            (second_turned, VM),
         ),
         (
             (padded, BF16, HB),
             (full, F32, VM),
+            (full, F32, HB),
             (full, BF16, HB),
             (coef_shape, F32, VM),
             (stats_shape, F32, VM),
-        ),
-        [small_acc, (padded, BF16), (full, BF16), tiles_of, 2, tiles_of],
+            ((8, channels), F32, VM),
+            ((8, channels), F32, VM),
+        ),
+        [small_acc, (padded, BF16), (full, BF16), tiles_of, 2, tiles_of, tiles_of],
         conv_flops,
-        20,
+        28,
     )
     others_two = others_over_tm(stat_two)
 
-    act_two, act_two_far, inner_two, unit_two, coef_two, stat_three = call(
+    act_two, inner_two, coef_two, stat_three = call(
         second_norm_kernel,
         (
             (info, SM),
@@ -1251,11 +1331,10 @@
             *((one, VM) for one in (stat_two, *others_two)),
             (inverse, VM),
             (params_two, VM),
+            (added, VM),
         ),
         (
-            (padded, BF16, VM),
             (padded, BF16, HB),
-            (full, BF16, HB),
             (full, BF16, HB),
             (coef_shape, F32, VM),
             (stats_shape, F32, VM),
@@ -1263,33 +1342,23 @@
         [
             small_acc,
             (full, BF16),
-            (full, BF16),
+            (padded, BF16),
             (full, BF16),
             tiles_of,
             tiles_of,
             2,
             tiles_of,
-            tiles_of,
         ],
         2 * frames * channels * 100,
-        20,
+        28,
     )
     others_three = others_over_tm(stat_three)
-    second_keep, second_give = call(
-        functools.partial(weight_gradient_kernel, False),
-        ((info, SM), (after(act_two, others_three[0]), VM), (grad_branch, HB)),
-        (((3 * channels // 2, channels), F32, VM), ((3 * channels // 2, channels), BF16, VM)),
-        [((3 * channels, channels), F32), (padded, BF16), tiles_of, 2],
-        conv_flops,
-        16,
-    )
-
-    grad_middle, inner_one, back_two, stat_four = call(
+    grad_middle, middle_edges, inner_one, back_two, stat_four = call(
         first_back_kernel,
         (
             (info, SM),
             (inner_two, HB),
-            (unit_two, HB),
+            (middle_far, HB),
             *((one, VM) for one in (stat_three, *others_three)),
             (others_two[0], VM),
             (others_two[2], VM),
@@ -1300,7 +1369,8 @@
             (turned(first_conv_weight), VM),
         ),
         (
-            (padded, BF16, VM),
+            (full, BF16, HB),
+            ((8, channels), F32, VM),
             (full, BF16, HB),
             ((40, channels), F32, VM),
             (stats_shape, F32, VM),
@@ -1308,23 +1378,18 @@
         [
             small_acc,
             ((ROWS, channels), F32),
-            *([(full, BF16)] * 4),
-            *([tiles_of] * 4),
+            (full, BF16),
+            (full, F32),
+            (full, BF16),
+            (full, BF16),
+            (padded, BF16),
+            *([tiles_of] * 5),
         ],
         conv_flops,
-        28,
+        40,
     )
     others_four = others_over_tm(stat_four)
-    first_keep, first_give = call(
-        functools.partial(weight_gradient_kernel, True),
-        ((info, SM), (act_one, HB), (after(grad_middle, others_four[0]), VM)),
-        (((3 * channels // 2, channels), F32, VM), ((3 * channels // 2, channels), BF16, VM)),
-        [((3 * channels, channels), F32), (padded, BF16), tiles_of, 2],
-        conv_flops,
-        16,
-    )
-
-    grad_before, grad_own, grad_after, back_one, free_rows = call(
+    grad_before, grad_own, grad_after, back_one = call(
         buffer_gradient_kernel,
         (
             (info, SM),
@@ -1342,7 +1407,6 @@
             ((local_rows, channels), F32, VM),
             ((halo, channels), F32, VM),
             ((40, channels), F32, VM),
-            ((groups, copies, piece_rows // 2, channels), BF16, VM),
         ),
         [
             (full, BF16),
@@ -1352,36 +1416,45 @@
             *([tiles_of] * 4),
         ],
         2 * frames * WIDE * channels,
-        28,
-    )
-
-    def sent_back(rows):
-        rows = rows.reshape(groups * copies, half, channels)
-        return lax.all_to_all(rows, ("seq", "tm"), 0, 0, tiled=True)
-
-    half = piece_rows // 2
+        36,
+    )
+
+    row_places = (send_order[0] >> 3) * (8 * (channels // 128)) + (send_order[0] & 7)
     from_before, from_after = from_neighbours(grad_before, grad_after)
-    if half >= halo:
-        split = grad_own.reshape(groups, 2, half, channels)
-        late_rows = jnp.concatenate([split[: groups // 2, 0], split[groups // 2 :, 1]], axis=0)
-        late_rows = (
-            late_rows.at[0, :halo].add(from_before).at[groups - 1, half - halo :].add(from_after)
-        ).astype(BF16)
-    else:
-        own = grad_own.at[:halo].add(from_before).at[local_rows - halo :].add(from_after)
-        split = own.astype(BF16).reshape(groups, 2, half, channels)
-        free_rows = jnp.concatenate([split[: groups // 2, 1], split[groups // 2 :, 0]], axis=0)
-        free_rows = jnp.broadcast_to(free_rows[:, None], (groups, copies, half, channels))
-        late_rows = jnp.concatenate([split[: groups // 2, 0], split[groups // 2 :, 1]], axis=0)
-    late_rows = jnp.broadcast_to(late_rows[:, None], (groups, copies, half, channels))
-    first_chunk = sent_back(free_rows)
+    return_rows = jnp.concatenate(
+        [grad_own[:halo] + from_before, grad_own[halo:-halo], grad_own[-halo:] + from_after]
+    ).astype(BF16)
+    returned = lax.all_to_all(
+        return_rows.reshape(groups, piece_rows, channels), "seq", 0, 0, tiled=True
+    )
 
     bits = [b for b in range(12) if (1 << b) < groups]
     orders = (bits[1:], bits[1:][::-1])
-    keeps = [second_keep, first_keep]
-    gives = after([second_give, first_give], back_one)
+    second_keep, second_give = call(
+        weight_gradient_kernel,
+        ((info, SM), (after(act_two, back_one), HB), (grad_branch, HB), (grad_edges, VM)),
+        (((3 * channels // 2, channels), F32, VM), ((3 * channels // 2, channels), BF16, VM)),
+        [((3 * channels, channels), F32), (padded, BF16), (padded, BF16), tiles_of, tiles_of],
+        10**6,
+        24,
+    )
+
+    returned, second_keep, second_give = lax.optimization_barrier(
+        (returned, second_keep, second_give)
+    )
+    rounds = [returned, shifted(returned, "tm", 1)]
+    first_keep, first_give = call(
+        weight_gradient_kernel,
+        ((info, SM), (act_one, HB), (after(grad_middle, returned), HB), (middle_edges, VM)),
+        (((3 * channels // 2, channels), F32, VM), ((3 * channels // 2, channels), BF16, VM)),
+        [((3 * channels, channels), F32), (padded, BF16), (padded, BF16), tiles_of, tiles_of],
+        10**6,
+        24,
+    )
+
+    keeps, gives = [second_keep, first_keep], [second_give, first_give]
     gots = [swapped(give, bits[0]) for give in gives]
-    for pair in zip(*orders):
+    for turn, pair in enumerate(zip(*orders)):
         count = keeps[0].shape[0] // 2
         out = call(
             functools.partial(halves_kernel, pair),
@@ -1389,17 +1462,26 @@
             (((count, channels), F32, VM), ((count, channels), BF16, VM)) * 2,
             [((2 * count, channels), F32)] * 2,
             10**6,
-            8,
+            16,
         )
         keeps, gives = [out[0], out[2]], [out[1], out[3]]
+        if turn == 0:
+            rounds[1], keeps, gives = lax.optimization_barrier((rounds[1], keeps, gives))
+            rounds.append(shifted(rounds[1], "tm", 1))
         gots = [swapped(give, bit) for give, bit in zip(gives, pair)]
     row_sums = [keep + got.astype(F32) for keep, got in zip(keeps, gots)]
-    act_two_far, _ = lax.optimization_barrier((act_two_far, back_one))
+    placed = scattered(None, rounds[:2], (0, 1), copies, info, row_places)
+    rounds[2], row_sums, placed = lax.optimization_barrier((rounds[2], row_sums, placed))
+    sums = gathered_over_tm(summed_over_tm(row_sums))
+    rounds[2], sums = lax.optimization_barrier((rounds[2], sums))
+    rounds.append(shifted(rounds[2], "tm", 1))
+
+    act_two, _ = lax.optimization_barrier((act_two, sums))
     (frames_out,) = call(
         second_conv_kernel,
         (
             (info, SM),
-            (act_two_far, HB),
+            (act_two, HB),
             (upsampled_far, HB),
             (second_conv_weight, VM),
             (second_conv_bias[None], VM),
@@ -1407,14 +1489,9 @@
         ((full, BF16, HB),),
         [(padded, BF16), (full, F32), (full, BF16), tiles_of, 2, tiles_of, tiles_of],
         10**6,
-        28,
-    )
-
-    row_sums, first_chunk, frames_out = lax.optimization_barrier((row_sums, first_chunk, frames_out))
-    sums = gathered_over_tm(summed_over_tm(row_sums))
-    late_rows, sums, first_chunk = lax.optimization_barrier((late_rows, sums, first_chunk))
-    second_chunk = sent_back(late_rows)
-    placed = scattered(None, first_chunk, 0, info, send_order[0])
+        36,
+    )
+
 
     params_grad = [
         jnp.concatenate([back[8 : 8 + UTTS], back[0:UTTS]], axis=1) for back in (back_one, back_two)
@@ -1443,8 +1520,9 @@
             tuple(((2 * one.shape[0], channels), BF16, VM) for one in held),
             [],
             10**6,
-            8,
+            16,
         )
+    rounds[3], held, frames_out = lax.optimization_barrier((rounds[3], list(held), frames_out))
     others = [swapped(one, bits[0]) for one in held]
     (
         second_conv_grad,
@@ -1473,9 +1551,9 @@
         ),
         [],
         10**6,
-        20,
-    )
-    placed = scattered(placed, second_chunk, 1, info, send_order[0])
+        28,
+    )
+    placed = scattered(placed, rounds[2:], (2, 3), copies, info, row_places)
     lanes = channels // 128
     phonemes_grad = (
         placed.reshape(slot_count // 8, lanes, 8, 128)

time: 338 us -> 294 us (0.87)
  waiting for transfers between devices: 79.4 us -> 66.4 us
  starting transfers between devices: 72.2 us -> 59.6 us
  local copies, waits for them, and re-layouts: 31.6 us -> 23.4 us
  Pallas kernels: 141 us -> 135 us
    ppermute x12, waiting for transfers between devices: 51.2 us -> 19.2 us  [swapped(): lax.ppermute(values, 'seq', [(i, i ^ 1 << bit) for i in range(devices)])]
    ppermute x18 -> x21, waiting for transfers between devices: 22.3 us -> 35.1 us  [shifted(): lax.ppermute(values, axis, [(i, (i + step) % devices) for i in range(devi...]
    ppermute x3 -> x2, starting transfers between devices: 12.8 us -> 6.71 us  [from_neighbours(): lax.ppermute(last_rows, 'tm', up)]
    unnamed x78 -> x84, local copies, waits for them, and re-layouts: 16.7 us -> 10.9 us
    all_to_all x2 -> x1, starting transfers between devices: 12 us -> 7.05 us  [on_device(): lax.all_to_all(return_rows.reshape(groups, piece_rows, channels), 'seq',...]
    ppermute x3 -> x2, waiting for transfers between devices: 4.28 us -> 8.64 us  [from_neighbours(): lax.ppermute(first_rows, 'tm', down)]
    ppermute x18 -> x21, starting transfers between devices: 27.4 us -> 27.2 us  [shifted(): lax.ppermute(values, axis, [(i, (i + step) % devices) for i in range(devi...]
  transfers between devices with their start and end apart: 39 -> 39, of which waited for: 28 -> 28; matrix products, arithmetic and copies ran while one was open for 6% -> 3% of each run, Pallas kernels for 19% -> 23%
where the time goes in v3:
time: 294 us; the launch traced here: 293 us
  Pallas kernels  135 us (46%)
  waiting for transfers between devices  66.4 us (23%)
  starting transfers between devices  59.6 us (20%)
  local copies, waits for them, and re-layouts  23.4 us (8%)
  other arithmetic  6.02 us (2%)
    pallas_call x14, Pallas kernels, call(): pl.pallas_call(kernel, in_specs=[spec for _, spec in inputs], out_specs=t...  118 us
    ppermute x21, waiting for transfers between devices, shifted(): lax.ppermute(values, axis, [(i, (i + step) % devices) for i in range(devi...  35.1 us
    ppermute x21, starting transfers between devices, shifted(): lax.ppermute(values, axis, [(i, (i + step) % devices) for i in range(devi...  27.2 us
    ppermute x12, waiting for transfers between devices, swapped(): lax.ppermute(values, 'seq', [(i, i ^ 1 << bit) for i in range(devices)])  19.2 us
    pallas_call x2, Pallas kernels, scattered(): pl.pallas_call(functools.partial(scatter_kernel, places, copies), in_spec...  16.4 us
    unnamed x84, local copies, waits for them, and re-layouts  10.9 us
    ppermute x12, starting transfers between devices, swapped(): lax.ppermute(values, 'seq', [(i, i ^ 1 << bit) for i in range(devices)])  10.8 us
    ppermute x2, waiting for transfers between devices, from_neighbours(): lax.ppermute(first_rows, 'tm', down)  8.64 us
  transfers between devices with their start and end apart: 39, of which 28 were waited for; matrix products, arithmetic and copies ran while one was open for 3% of the time, Pallas kernels for 23%

profile of v3, /device:TPU:0, one launch (start us, length us, event | category | flops | bytes accessed | tf_op | source)
XLA Modules:
  0.0 293.2 jit_solution(14777586773005875187)
XLA Ops:
  1.5 8.0 %gather_fusion = bf16[1024,512]{1,0:T(8,128)(2,1)} fusion(bf16[4096,512]{1,0:T(8,128)(2,1)} %param.23, s32[1024]{0:T(1024)S(1)} %broadcast_clamp_fusion), kind=kCustom, calls=%fused_computation | custom fusion | bytes 2101248 | tf_op jit(solution)/shard_map/jit(_take)/gather | solution.py:1243
  9.4 5.3 %all-to-all-start = ((bf16[8,128,512]{2,1,0:T(8,128)(2,1)}), bf16[8,128,512]{2,1,0:T(8,128)(2,1)}, u32[]{:S(2)}, u32[]{:S(2)}) async-start(bf16[8,128,512]{2,1,0:T(8,128)(2,1)} %bitcast.13), calls=%async_computation | async-start | bytes 2097152 | tf_op jit(solution)/shard_map/all_to_all | solution.py:1244
  15.9 12.9 %shard_map.222 = (bf16[4096,512]{1,0:T(8,128)(2,1)}, bf16[4096,512]{1,0:T(8,128)(2,1)}, f32[16,512]{1,0:T(8,128)S(1)}) custom-call(s32[24]{0:T(128)S(1)} %concatenate.25.info_ref, bf16[4096,512]{1,0:T(8,128)(2,1)} %cot_hbm.3, bf16[1536,512]{1,0:T(8,128)(2,1)S(1)} %bitcast.76), custom_call_target="tpu_custom_call" | custom-call | flops 6442450944 | bytes 32212254 | tf_op jit(solution)/shard_map/pallas_call | solution.py:1092
  31.3 3.9 %collective-permute-start = (bf16[64,512]{1,0:T(8,128)(2,1)S(1)}, bf16[64,512]{1,0:T(8,128)(2,1)S(1)}, u32[]{:S(2)}, u32[]{:S(2)}) collective-permute-start(bf16[64,512]{1,0:T(8,128)(2,1)S(1)} %get-tuple-element.211), channel_id=1, source_target_pairs={{0,1},{1,2},{2,3},{4,5},{5,6},{6,7},{8,9},{9,10},{10,11},{12,13},{... | collective-permute-start | bytes 196616 | tf_op jit(solution)/shard_map/ppermute | solution.py:1143
  37.1 4.3 %collective-permute-done.1.after_ref = bf16[64,512]{1,0:T(8,128)(2,1)S(1)} collective-permute-done((bf16[64,512]{1,0:T(8,128)(2,1)S(1)}, bf16[64,512]{1,0:T(8,128)(2,1)S(1)}, u32[]{:S(2)}, u32[]{:S(2)}) %collective-permute-start.1) | collective-permute-done | bytes 65568 | tf_op jit(solution)/shard_map/ppermute | solution.py:1143
  42.1 8.4 %shard_map.223 = (f32[4096,512]{1,0:T(8,128)S(1)}, f32[4096,512]{1,0:T(8,128)}, bf16[4096,256]{1,0:T(8,128)(2,1)}, f32[24,512]{1,0:T(8,128)S(1)}) custom-call(s32[24]{0:T(128)S(1)} %concatenate.25.info_ref, s32[32]{0:T(128)S(1)} %copy-done.18, bf16[64,512]{1,0:T(8,128)(2,1)S(1)} %collective-permute-done.before_ref, bf16[1024,512]{1,0:T(8,128)(2,1)} %bitcast.14.own_ref, ...), custom_call_target="tpu_custom_call" | custom-call | flops 1073741824 | bytes 5368709 | tf_op jit(solution)/shard_map/pallas_call | solution.py:1092
  53.3 2.8 collective-permute-start.4
  57.9 13.5 %shard_map.224 = (bf16[4128,512]{1,0:T(8,128)(2,1)}, f32[4096,512]{1,0:T(8,128)S(1)}, f32[4096,512]{1,0:T(8,128)}, bf16[4096,512]{1,0:T(8,128)(2,1)}, f32[56,512...) custom-call(s32[24]{0:T(128)S(1)} %concatenate.25.info_ref, ...), custom_call_target="tpu_custom_call" | custom-call | flops 6442450944 | bytes 32212254 | tf_op jit(solution)/shard_map/pallas_call | solution.py:1092
  73.0 3.5 %collective-permute-start.6 = (f32[24,512]{1,0:T(8,128)S(1)}, f32[24,512]{1,0:T(8,128)S(1)}, u32[]{:S(2)}, u32[]{:S(2)}) collective-permute-start(f32[24,512]{1,0:T(8,128)S(1)} %get-tuple-element.139.own_ref), channel_id=1, source_target_pairs={{0,2},{1,3},{2,0},{3,1},{4,6},{5,7},{6,4},{7,5},{8,10},{9,11},{10,... | collective-permute-start | bytes 147464 | tf_op jit(solution)/shard_map/ppermute | solution.py:1132
  80.5 9.1 %shard_map.225 = (bf16[4128,512]{1,0:T(8,128)(2,1)}, bf16[4096,512]{1,0:T(8,128)(2,1)}, f32[56,512]{1,0:T(8,128)S(1)}, f32[24,512]{1,0:T(8,128)}) custom-call(s32[24]{0:T(128)S(1)} %concatenate.25.info_ref, bf16[4096,512]{1,0:T(8,128)(2,1)} %get-tuple-element.132.gradient_hbm, f32[4096,512]{1,0:T(8,128)S(1)} %get-tuple-element.138.values_ref, ...), custom_call_target="tpu_custom_call" | custom-call | flops 419430400 | bytes 2097152 | tf_op jit(solution)/shard_map/pallas_call | solution.py:1092
  94.8 4.0 %collective-permute-done.8.one_ref = f32[24,512]{1,0:T(8,128)} collective-permute-done((f32[24,512]{1,0:T(8,128)}, f32[24,512]{1,0:T(8,128)}, u32[]{:S(2)}, u32[]{:S(2)}) %collective-permute-start.8) | collective-permute-done | bytes 49184 | tf_op jit(solution)/shard_map/ppermute | solution.py:1132
  102.8 20.3 %shard_map.226 = (bf16[4096,512]{1,0:T(8,128)(2,1)}, f32[8,512]{1,0:T(8,128)S(1)}, bf16[4096,512]{1,0:T(8,128)(2,1)}, f32[40,512]{1,0:T(8,128)S(1)}, f32[24,512]{1,0:T(8,128)S(1)}) custom-call(s32[24]{0:T(128)S(1)} %concatenate.25.info_ref, bf16[4096,512]{1,0:T(8,128)(2,1)} %get-tuple-element.141.inner_hbm, f32[4096,512]{1,0:T(8,128)} %get-tuple-element.142.middle_hbm, ...), custom_call_target="tpu_custom_call" | custom-call | flops 6442450944 | bytes 32212254 | tf_op jit(solution)/shard_map/pallas_call | solution.py:1092
  124.2 2.4 collective-permute-start.12
  131.6 9.8 %shard_map.227 = (f32[64,512]{1,0:T(8,128)S(1)}, f32[1024,512]{1,0:T(8,128)S(1)}, f32[64,512]{1,0:T(8,128)S(1)}, f32[40,512]{1,0:T(8,128)S(1)}) custom-call(s32[24]{0:T(128)S(1)} %concatenate.25.info_ref, s32[32]{0:T(128)S(1)} %copy-done.18, bf16[4096,512]{1,0:T(8,128)(2,1)} %get-tuple-element.147.inner_hbm, ...), custom_call_target="tpu_custom_call" | custom-call | flops 1073741824 | bytes 5368709 | tf_op jit(solution)/shard_map/pallas_call | solution.py:1092
  141.4 2.8 collective-permute-start.14
  146.7 4.4 %collective-permute-done.15 = f32[64,512]{1,0:T(8,128)S(1)} collective-permute-done((f32[64,512]{1,0:T(8,128)S(1)}, f32[64,512]{1,0:T(8,128)S(1)}, u32[]{:S(2)}, u32[]{:S(2)}) %collective-permute-start.15) | collective-permute-done | bytes 131104 | tf_op jit(solution)/shard_map/ppermute | solution.py:1143
  152.2 7.0 %all-to-all-start.1 = ((bf16[8,128,512]{2,1,0:T(8,128)(2,1)}), bf16[8,128,512]{2,1,0:T(8,128)(2,1)S(1)}, u32[]{:S(2)}, u32[]{:S(2)}) async-start(bf16[8,128,512]{2,1,0:T(8,128)(2,1)} %bitcast.82), calls=%async_computation.1 | async-start | bytes 2097152 | tf_op jit(solution)/shard_map/all_to_all | solution.py:1427
  159.2 11.6 %shard_map.228 = (f32[768,512]{1,0:T(8,128)S(1)}, bf16[768,512]{1,0:T(8,128)(2,1)S(1)}) custom-call(s32[24]{0:T(128)S(1)} %concatenate.25.info_ref, bf16[4128,512]{1,0:T(8,128)(2,1)} %get-tuple-element.192.act_hbm, bf16[4096,512]{1,0:T(8,128)(2,1)} %get-tuple-element.156.gradient_hbm, f32[8,512]{1,0:T(8,128)S(1)} %copy-done.17), custom_call_target="tpu_custom_call" | custom-call | flops 1000000 | bytes 5000 | tf_op jit(solution)/shard_map/pallas_call | solution.py:1092
  176.4 11.7 %shard_map.229 = (f32[768,512]{1,0:T(8,128)S(1)}, bf16[768,512]{1,0:T(8,128)(2,1)S(1)}) custom-call(s32[24]{0:T(128)S(1)} %concatenate.25.info_ref, bf16[4128,512]{1,0:T(8,128)(2,1)} %get-tuple-element.163.act_hbm, bf16[4096,512]{1,0:T(8,128)(2,1)} %get-tuple-element.165.gradient_hbm, f32[8,512]{1,0:T(8,128)S(1)} %get-tuple-element.166.edge_ref), custom_call_target="tpu_custom_call" | custom-call | flops 1000000 | bytes 5000 | tf_op jit(solution)/shard_map/pallas_call | solution.py:1092
  192.7 7.5 %collective-permute-done.16.refs_1_ = bf16[8,128,512]{2,1,0:T(8,128)(2,1)} collective-permute-done((bf16[8,128,512]{2,1,0:T(8,128)(2,1)S(1)}, bf16[8,128,512]{2,1,0:T(8,128)(2,1)}, u32[]{:S(2)}, u32[]{:S(2)}) %collective-permute-start.16) | collective-permute-done | bytes 1048608 | tf_op jit(solution)/shard_map/ppermute | solution.py:1132
  203.4 7.2 %collective-permute-done.20.refs_1_ = bf16[384,512]{1,0:T(8,128)(2,1)S(1)} collective-permute-done((bf16[384,512]{1,0:T(8,128)(2,1)S(1)}, bf16[384,512]{1,0:T(8,128)(2,1)S(1)}, u32[]{:S(2)}, u32[]{:S(2)}) %collective-permute-start.20) | collective-permute-done | bytes 393248 | tf_op jit(solution)/shard_map/ppermute | solution.py:1148
  216.1 6.7 %shard_map.232.refs_2_ = f32[16384,128]{1,0:T(8,128)} custom-call(s32[24]{0:T(128)S(1)} %concatenate.25.info_ref, s32[4096]{0:T(1024)S(1)} %bitcast.79, bf16[8,128,512]{2,1,0:T(8,128)(2,1)S(1)} %all-to-all-done.1.refs_0_, bf16[8,128,512]{2,1,0:T(8,128)(2,1)} %collective-permute-done.16.refs_1_), custom_call_target="tpu_custom_call" | custom-call | flops 1000000 | bytes 10000 | tf_op jit(solution)/shard_map/pallas_call | solution.py:1118
  225.1 3.3 %collective-permute-done.22 = bf16[192,512]{1,0:T(8,128)(2,1)S(1)} collective-permute-done((bf16[192,512]{1,0:T(8,128)(2,1)S(1)}, bf16[192,512]{1,0:T(8,128)(2,1)S(1)}, u32[]{:S(2)}, u32[]{:S(2)}) %collective-permute-start.22) | collective-permute-done | bytes 196640 | tf_op jit(solution)/shard_map/ppermute | solution.py:1148
  229.5 3.8 %collective-permute-start.25 = (bf16[2,48,512]{2,1,0:T(8,128)(2,1)S(1)}, bf16[2,48,512]{2,1,0:T(8,128)(2,1)S(1)}, u32[]{:S(2)}, u32[]{:S(2)}) collective-permute-start(bf16[2,48,512]{2,1,0:T(8,128)(2,1)S(1)} %get-tuple-element.214), channel_id=1, source_target_pairs={{0,3},{1,0},{2,1},{3,2},{4,7},{5,4},{6,5},{7,6},{8,11},{9,8},{10,9... | collective-permute-start | bytes 294920 | tf_op jit(solution)/shard_map/ppermute | solution.py:1132
  236.1 3.9 %collective-permute-done.26 = bf16[2,48,512]{2,1,0:T(8,128)(2,1)S(1)} collective-permute-done((bf16[2,48,512]{2,1,0:T(8,128)(2,1)S(1)}, bf16[2,48,512]{2,1,0:T(8,128)(2,1)S(1)}, u32[]{:S(2)}, u32[]{:S(2)}) %collective-permute-start.26) | collective-permute-done | bytes 98336 | tf_op jit(solution)/shard_map/ppermute | solution.py:1132
  241.0 3.9 %collective-permute-start.28 = (bf16[2,48,512]{2,1,0:T(8,128)(2,1)S(1)}, bf16[2,48,512]{2,1,0:T(8,128)(2,1)S(1)}, u32[]{:S(2)}, u32[]{:S(2)}) collective-permute-start(bf16[2,48,512]{2,1,0:T(8,128)(2,1)S(1)} %get-tuple-element.207), channel_id=1, source_target_pairs={{0,3},{1,0},{2,1},{3,2},{4,7},{5,4},{6,5},{7,6},{8,11},{9,8},{10,9... | collective-permute-start | bytes 294920 | tf_op jit(solution)/shard_map/ppermute | solution.py:1132
  244.8 2.9 %collective-permute-done.27 = bf16[2,48,512]{2,1,0:T(8,128)(2,1)S(1)} collective-permute-done((bf16[2,48,512]{2,1,0:T(8,128)(2,1)S(1)}, bf16[2,48,512]{2,1,0:T(8,128)(2,1)S(1)}, u32[]{:S(2)}, u32[]{:S(2)}) %collective-permute-start.27) | collective-permute-done | bytes 98336 | tf_op jit(solution)/shard_map/ppermute | solution.py:1132
  247.8 3.5 %collective-permute-done.29 = bf16[2,48,512]{2,1,0:T(8,128)(2,1)S(1)} collective-permute-done((bf16[2,48,512]{2,1,0:T(8,128)(2,1)S(1)}, bf16[2,48,512]{2,1,0:T(8,128)(2,1)S(1)}, u32[]{:S(2)}, u32[]{:S(2)}) %collective-permute-start.29) | collective-permute-done | bytes 98336 | tf_op jit(solution)/shard_map/ppermute | solution.py:1132
  253.8 4.1 %collective-permute-done.32.refs_3_ = bf16[192,512]{1,0:T(8,128)(2,1)S(1)} collective-permute-done((bf16[192,512]{1,0:T(8,128)(2,1)S(1)}, bf16[192,512]{1,0:T(8,128)(2,1)S(1)}, u32[]{:S(2)}, u32[]{:S(2)}) %collective-permute-start.32) | collective-permute-done | bytes 196640 | tf_op jit(solution)/shard_map/ppermute | solution.py:1148
  261.6 12.4 %shard_map.235 = bf16[4096,512]{1,0:T(8,128)(2,1)} custom-call(s32[24]{0:T(128)S(1)} %concatenate.25.info_ref, bf16[4128,512]{1,0:T(8,128)(2,1)} %get-tuple-element.192.act_hbm, f32[4096,512]{1,0:T(8,128)} %get-tuple-element.193.values_hbm, bf16[1536,512]{1,0:T(8,128)(2,1)S(1)} %copy-done.1, bf16[1,512]{1,0:T(2,128)(2,1)S(1)} %broadcast_in_dim.54.bias_ref), custom_call_target="tpu_custom_call" | custom-call | flops 1000000 | bytes 5000 | tf_op jit(solution)/shard_map/pallas_call | solution.py:1092
  278.6 9.7 %shard_map.236 = f32[16384,128]{1,0:T(8,128)} custom-call(s32[24]{0:T(128)S(1)} %concatenate.25.info_ref, s32[4096]{0:T(1024)S(1)} %bitcast.80, bf16[8,128,512]{2,1,0:T(8,128)(2,1)} %collective-permute-done.19.refs_0_, bf16[8,128,512]{2,1,0:T(8,128)(2,1)S(1)} %collective-permute-done.30.refs_1_, ...), custom_call_target="tpu_custom_call", output_to_operand_aliasing={{}: (4, {})} | custom-call | flops 1000000 | bytes 10000 | tf_op jit(solution)/shard_map/pallas_call | solution.py:1118
  288.3 4.9 %shard_map.237 = (f32[1536,512]{1,0:T(8,128)}, f32[1536,512]{1,0:T(8,128)}, f32[128,1024]{1,0:T(8,128)}, f32[1,1024]{1,0:T(1,128)}, f32[128,1024]{1,0:T(8,128)}, /*index=5*/f32[1,1024]{1,0:T(1,128)}, f32[1,512]{1,0:T(1,128)}) custom-call(s32[24]{0:T(128)S(1)} %concatenate.25.info_ref, bf16[960,512]{1,0:T(8,128)(2,1)S(1)} %get-tuple-element.197.second_ref, ...), custom_call_target="tpu_custom_call" | custom-call | flops 1000000 | bytes 5000 | tf_op jit(solution)/shard_map/pallas_call | solution.py:1092
  (188 shorter events, 72.2 us)
Async XLA Ops:
  9.4 20.8 %all-to-all-start = ((bf16[8,128,512]{2,1,0:T(8,128)(2,1)}), bf16[8,128,512]{2,1,0:T(8,128)(2,1)}, u32[]{:S(2)}, u32[]{:S(2)}) async-start(bf16[8,128,512]{2,1,0:T(8,128)(2,1)} %bitcast.13), calls=%async_computation | async-start | bytes 2097152 | tf_op jit(solution)/shard_map/all_to_all | solution.py:1244
  31.3 5.8 %collective-permute-start = (bf16[64,512]{1,0:T(8,128)(2,1)S(1)}, bf16[64,512]{1,0:T(8,128)(2,1)S(1)}, u32[]{:S(2)}, u32[]{:S(2)}) collective-permute-start(bf16[64,512]{1,0:T(8,128)(2,1)S(1)} %get-tuple-element.211), channel_id=1, source_target_pairs={{0,1},{1,2},{2,3},{4,5},{5,6},{6,7},{8,9},{9,10},{10,11},{12,13},{... | collective-permute-start | bytes 196616 | tf_op jit(solution)/shard_map/ppermute | solution.py:1143
  35.2 6.2 %collective-permute-start.1 = (bf16[64,512]{1,0:T(8,128)(2,1)S(1)}, bf16[64,512]{1,0:T(8,128)(2,1)S(1)}, u32[]{:S(2)}, u32[]{:S(2)}) collective-permute-start(bf16[64,512]{1,0:T(8,128)(2,1)S(1)} %get-tuple-element.210), channel_id=1, source_target_pairs={{1,0},{2,1},{3,2},{5,4},{6,5},{7,6},{9,8},{10,9},{11,10},{13,12},{... | collective-permute-start | bytes 196616 | tf_op jit(solution)/shard_map/ppermute | solution.py:1143
  50.5 6.9 %collective-permute-start.2 = (f32[24,512]{1,0:T(8,128)S(1)}, f32[24,512]{1,0:T(8,128)S(1)}, u32[]{:S(2)}, u32[]{:S(2)}) collective-permute-start(f32[24,512]{1,0:T(8,128)S(1)} %get-tuple-element.137.own_ref), channel_id=1, source_target_pairs={{0,1},{1,2},{2,3},{3,0},{4,5},{5,6},{6,7},{7,4},{8,9},{9,10},{10,1... | collective-permute-start | bytes 147464 | tf_op jit(solution)/shard_map/ppermute | solution.py:1132
  71.5 6.5 %collective-permute-start.5 = (f32[24,512]{1,0:T(8,128)S(1)}, f32[24,512]{1,0:T(8,128)S(1)}, u32[]{:S(2)}, u32[]{:S(2)}) collective-permute-start(f32[24,512]{1,0:T(8,128)S(1)} %get-tuple-element.139.own_ref), channel_id=1, source_target_pairs={{0,1},{1,2},{2,3},{3,0},{4,5},{5,6},{6,7},{7,4},{8,9},{9,10},{10,1... | collective-permute-start | bytes 147464 | tf_op jit(solution)/shard_map/ppermute | solution.py:1132
  73.0 6.0 %collective-permute-start.6 = (f32[24,512]{1,0:T(8,128)S(1)}, f32[24,512]{1,0:T(8,128)S(1)}, u32[]{:S(2)}, u32[]{:S(2)}) collective-permute-start(f32[24,512]{1,0:T(8,128)S(1)} %get-tuple-element.139.own_ref), channel_id=1, source_target_pairs={{0,2},{1,3},{2,0},{3,1},{4,6},{5,7},{6,4},{7,5},{8,10},{9,11},{10,... | collective-permute-start | bytes 147464 | tf_op jit(solution)/shard_map/ppermute | solution.py:1132
  92.6 6.2 %collective-permute-start.8 = (f32[24,512]{1,0:T(8,128)}, f32[24,512]{1,0:T(8,128)}, u32[]{:S(2)}, u32[]{:S(2)}) collective-permute-start(f32[24,512]{1,0:T(8,128)} %get-tuple-element.143.own_ref), channel_id=1, source_target_pairs={{0,1},{1,2},{2,3},{3,0},{4,5},{5,6},{6,7},{7,4},{8,9},{9,10},{10,1... | collective-permute-start | bytes 147464 | tf_op jit(solution)/shard_map/ppermute | solution.py:1132
  92.6 6.2 %collective-permute-start.9 = (f32[24,512]{1,0:T(8,128)}, f32[24,512]{1,0:T(8,128)}, u32[]{:S(2)}, u32[]{:S(2)}) collective-permute-start(f32[24,512]{1,0:T(8,128)} %get-tuple-element.143.own_ref), channel_id=1, source_target_pairs={{0,2},{1,3},{2,0},{3,1},{4,6},{5,7},{6,4},{7,5},{8,10},{9,11},{10,... | collective-permute-start | bytes 147464 | tf_op jit(solution)/shard_map/ppermute | solution.py:1132
  123.0 6.0 %collective-permute-start.11 = (f32[24,512]{1,0:T(8,128)S(1)}, f32[24,512]{1,0:T(8,128)S(1)}, u32[]{:S(2)}, u32[]{:S(2)}) collective-permute-start(f32[24,512]{1,0:T(8,128)S(1)} %get-tuple-element.149.own_ref), channel_id=1, source_target_pairs={{0,1},{1,2},{2,3},{3,0},{4,5},{5,6},{6,7},{7,4},{8,9},{9,10},{10,1... | collective-permute-start | bytes 147464 | tf_op jit(solution)/shard_map/ppermute | solution.py:1132
  124.2 5.9 %collective-permute-start.12 = (f32[24,512]{1,0:T(8,128)S(1)}, f32[24,512]{1,0:T(8,128)S(1)}, u32[]{:S(2)}, u32[]{:S(2)}) collective-permute-start(f32[24,512]{1,0:T(8,128)S(1)} %get-tuple-element.149.own_ref), channel_id=1, source_target_pairs={{0,2},{1,3},{2,0},{3,1},{4,6},{5,7},{6,4},{7,5},{8,10},{9,11},{10,... | collective-permute-start | bytes 147464 | tf_op jit(solution)/shard_map/ppermute | solution.py:1132
  141.4 5.3 %collective-permute-start.14 = (f32[64,512]{1,0:T(8,128)S(1)}, f32[64,512]{1,0:T(8,128)S(1)}, u32[]{:S(2)}, u32[]{:S(2)}) collective-permute-start(f32[64,512]{1,0:T(8,128)S(1)} %get-tuple-element.151), channel_id=1, source_target_pairs={{0,1},{1,2},{2,3},{4,5},{5,6},{6,7},{8,9},{9,10},{10,11},{12,13},{... | collective-permute-start | bytes 393224 | tf_op jit(solution)/shard_map/ppermute | solution.py:1143
  144.2 6.9 %collective-permute-start.15 = (f32[64,512]{1,0:T(8,128)S(1)}, f32[64,512]{1,0:T(8,128)S(1)}, u32[]{:S(2)}, u32[]{:S(2)}) collective-permute-start(f32[64,512]{1,0:T(8,128)S(1)} %get-tuple-element.152), channel_id=1, source_target_pairs={{1,0},{2,1},{3,2},{5,4},{6,5},{7,6},{9,8},{10,9},{11,10},{13,12},{... | collective-permute-start | bytes 393224 | tf_op jit(solution)/shard_map/ppermute | solution.py:1143
  152.2 22.5 %all-to-all-start.1 = ((bf16[8,128,512]{2,1,0:T(8,128)(2,1)}), bf16[8,128,512]{2,1,0:T(8,128)(2,1)S(1)}, u32[]{:S(2)}, u32[]{:S(2)}) async-start(bf16[8,128,512]{2,1,0:T(8,128)(2,1)} %bitcast.82), calls=%async_computation.1 | async-start | bytes 2097152 | tf_op jit(solution)/shard_map/all_to_all | solution.py:1427
  174.6 25.7 %collective-permute-start.16 = (bf16[8,128,512]{2,1,0:T(8,128)(2,1)S(1)}, bf16[8,128,512]{2,1,0:T(8,128)(2,1)}, u32[]{:S(2)}, u32[]{:S(2)}) collective-permute-start(bf16[8,128,512]{2,1,0:T(8,128)(2,1)S(1)} %all-to-all-done.1.refs_0_), channel_id=1, source_target_pairs={{0,1},{1,2},{2,3},{3,0},{4,5},{5,6},{6,7},{7,4},{8,9},{9,10},{10,1... | collective-permute-start | bytes 3145736 | tf_op jit(solution)/shard_map/ppermute | solution.py:1132
  200.3 10.4 %collective-permute-start.20 = (bf16[384,512]{1,0:T(8,128)(2,1)S(1)}, bf16[384,512]{1,0:T(8,128)(2,1)S(1)}, u32[]{:S(2)}, u32[]{:S(2)}) collective-permute-start(bf16[384,512]{1,0:T(8,128)(2,1)S(1)} %get-tuple-element.175), channel_id=1, source_target_pairs={{0,8},{4,12},{8,0},{12,4},{16,24},{20,28},{24,16},{28,20},{1,9},{5... | collective-permute-start | bytes 1179656 | tf_op jit(solution)/shard_map/ppermute | solution.py:1148
  202.2 10.0 %collective-permute-start.21 = (bf16[384,512]{1,0:T(8,128)(2,1)S(1)}, bf16[384,512]{1,0:T(8,128)(2,1)S(1)}, u32[]{:S(2)}, u32[]{:S(2)}) collective-permute-start(bf16[384,512]{1,0:T(8,128)(2,1)S(1)} %get-tuple-element.177), channel_id=1, source_target_pairs={{0,16},{4,20},{8,24},{12,28},{16,0},{20,4},{24,8},{28,12},{1,17},{... | collective-permute-start | bytes 1179656 | tf_op jit(solution)/shard_map/ppermute | solution.py:1148
  203.4 25.9 %collective-permute-start.19 = (bf16[8,128,512]{2,1,0:T(8,128)(2,1)}, bf16[8,128,512]{2,1,0:T(8,128)(2,1)}, u32[]{:S(2)}, u32[]{:S(2)}) collective-permute-start(bf16[8,128,512]{2,1,0:T(8,128)(2,1)} %collective-permute-done.16.refs_1_), channel_id=1, source_target_pairs={{0,1},{1,2},{2,3},{3,0},{4,5},{5,6},{6,7},{7,4},{8,9},{9,10},{10,1... | collective-permute-start | bytes 3145736 | tf_op jit(solution)/shard_map/ppermute | solution.py:1132
  215.0 9.1 %collective-permute-start.23 = (bf16[192,512]{1,0:T(8,128)(2,1)}, bf16[192,512]{1,0:T(8,128)(2,1)}, u32[]{:S(2)}, u32[]{:S(2)}) collective-permute-start(bf16[192,512]{1,0:T(8,128)(2,1)} %get-tuple-element.181), channel_id=1, source_target_pairs={{0,8},{4,12},{8,0},{12,4},{16,24},{20,28},{24,16},{28,20},{1,9},{5... | collective-permute-start | bytes 589832 | tf_op jit(solution)/shard_map/ppermute | solution.py:1148
  222.8 5.7 %collective-permute-start.22 = (bf16[192,512]{1,0:T(8,128)(2,1)S(1)}, bf16[192,512]{1,0:T(8,128)(2,1)S(1)}, u32[]{:S(2)}, u32[]{:S(2)}) collective-permute-start(bf16[192,512]{1,0:T(8,128)(2,1)S(1)} %copy-done.26), channel_id=1, source_target_pairs={{0,16},{4,20},{8,24},{12,28},{16,0},{20,4},{24,8},{28,12},{1,17},{... | collective-permute-start | bytes 589832 | tf_op jit(solution)/shard_map/ppermute | solution.py:1148
  229.5 6.6 %collective-permute-start.24 = (bf16[2,48,512]{2,1,0:T(8,128)(2,1)S(1)}, bf16[2,48,512]{2,1,0:T(8,128)(2,1)S(1)}, u32[]{:S(2)}, u32[]{:S(2)}) collective-permute-start(bf16[2,48,512]{2,1,0:T(8,128)(2,1)S(1)} %get-tuple-element.212), channel_id=1, source_target_pairs={{0,1},{1,2},{2,3},{3,0},{4,5},{5,6},{6,7},{7,4},{8,9},{9,10},{10,1... | collective-permute-start | bytes 294920 | tf_op jit(solution)/shard_map/ppermute | solution.py:1132
  229.5 6.5 %collective-permute-start.25 = (bf16[2,48,512]{2,1,0:T(8,128)(2,1)S(1)}, bf16[2,48,512]{2,1,0:T(8,128)(2,1)S(1)}, u32[]{:S(2)}, u32[]{:S(2)}) collective-permute-start(bf16[2,48,512]{2,1,0:T(8,128)(2,1)S(1)} %get-tuple-element.214), channel_id=1, source_target_pairs={{0,3},{1,0},{2,1},{3,2},{4,7},{5,4},{6,5},{7,6},{8,11},{9,8},{10,9... | collective-permute-start | bytes 294920 | tf_op jit(solution)/shard_map/ppermute | solution.py:1132
  233.3 6.7 %collective-permute-start.26 = (bf16[2,48,512]{2,1,0:T(8,128)(2,1)S(1)}, bf16[2,48,512]{2,1,0:T(8,128)(2,1)S(1)}, u32[]{:S(2)}, u32[]{:S(2)}) collective-permute-start(bf16[2,48,512]{2,1,0:T(8,128)(2,1)S(1)} %get-tuple-element.213), channel_id=1, source_target_pairs={{0,2},{1,3},{2,0},{3,1},{4,6},{5,7},{6,4},{7,5},{8,10},{9,11},{10,... | collective-permute-start | bytes 294920 | tf_op jit(solution)/shard_map/ppermute | solution.py:1132
  240.1 7.7 %collective-permute-start.27 = (bf16[2,48,512]{2,1,0:T(8,128)(2,1)S(1)}, bf16[2,48,512]{2,1,0:T(8,128)(2,1)S(1)}, u32[]{:S(2)}, u32[]{:S(2)}) collective-permute-start(bf16[2,48,512]{2,1,0:T(8,128)(2,1)S(1)} %get-tuple-element.207), channel_id=1, source_target_pairs={{0,1},{1,2},{2,3},{3,0},{4,5},{5,6},{6,7},{7,4},{8,9},{9,10},{10,1... | collective-permute-start | bytes 294920 | tf_op jit(solution)/shard_map/ppermute | solution.py:1132
  241.0 6.8 %collective-permute-start.28 = (bf16[2,48,512]{2,1,0:T(8,128)(2,1)S(1)}, bf16[2,48,512]{2,1,0:T(8,128)(2,1)S(1)}, u32[]{:S(2)}, u32[]{:S(2)}) collective-permute-start(bf16[2,48,512]{2,1,0:T(8,128)(2,1)S(1)} %get-tuple-element.207), channel_id=1, source_target_pairs={{0,3},{1,0},{2,1},{3,2},{4,7},{5,4},{6,5},{7,6},{8,11},{9,8},{10,9... | collective-permute-start | bytes 294920 | tf_op jit(solution)/shard_map/ppermute | solution.py:1132
  244.8 6.5 %collective-permute-start.29 = (bf16[2,48,512]{2,1,0:T(8,128)(2,1)S(1)}, bf16[2,48,512]{2,1,0:T(8,128)(2,1)S(1)}, u32[]{:S(2)}, u32[]{:S(2)}) collective-permute-start(bf16[2,48,512]{2,1,0:T(8,128)(2,1)S(1)} %get-tuple-element.207), channel_id=1, source_target_pairs={{0,2},{1,3},{2,0},{3,1},{4,6},{5,7},{6,4},{7,5},{8,10},{9,11},{10,... | collective-permute-start | bytes 294920 | tf_op jit(solution)/shard_map/ppermute | solution.py:1132
  251.4 25.5 %collective-permute-start.30 = (bf16[8,128,512]{2,1,0:T(8,128)(2,1)}, bf16[8,128,512]{2,1,0:T(8,128)(2,1)S(1)}, u32[]{:S(2)}, u32[]{:S(2)}) collective-permute-start(bf16[8,128,512]{2,1,0:T(8,128)(2,1)} %collective-permute-done.19.refs_0_), channel_id=1, source_target_pairs={{0,1},{1,2},{2,3},{3,0},{4,5},{5,6},{6,7},{7,4},{8,9},{9,10},{10,1... | collective-permute-start | bytes 3145736 | tf_op jit(solution)/shard_map/ppermute | solution.py:1132
  251.7 6.3 %collective-permute-start.31 = (bf16[240,512]{1,0:T(8,128)(2,1)S(1)}, bf16[240,512]{1,0:T(8,128)(2,1)S(1)}, u32[]{:S(2)}, u32[]{:S(2)}) collective-permute-start(bf16[240,512]{1,0:T(8,128)(2,1)S(1)} %constant_dynamic-update-slice_fusion.refs_0_), channel_id=1, source_target_pairs={{0,8},{4,12},{8,0},{12,4},{16,24},{20,28},{24,16},{28,20},{1,9},{5... | collective-permute-start | bytes 737288 | tf_op jit(solution)/shard_map/ppermute | solution.py:1148
  251.8 6.1 %collective-permute-start.32 = (bf16[192,512]{1,0:T(8,128)(2,1)S(1)}, bf16[192,512]{1,0:T(8,128)(2,1)S(1)}, u32[]{:S(2)}, u32[]{:S(2)}) collective-permute-start(bf16[192,512]{1,0:T(8,128)(2,1)S(1)} %slice_bitcast_fusion.refs_2_), channel_id=1, source_target_pairs={{0,16},{4,20},{8,24},{12,28},{16,0},{20,4},{24,8},{28,12},{1,17},{... | collective-permute-start | bytes 589832 | tf_op jit(solution)/shard_map/ppermute | solution.py:1148
  258.6 15.3 %collective-permute-start.33 = (bf16[480,512]{1,0:T(8,128)(2,1)S(1)}, bf16[480,512]{1,0:T(8,128)(2,1)S(1)}, u32[]{:S(2)}, u32[]{:S(2)}) collective-permute-start(bf16[480,512]{1,0:T(8,128)(2,1)S(1)} %get-tuple-element.188.refs_0_), channel_id=1, source_target_pairs={{0,16},{4,20},{8,24},{12,28},{16,0},{20,4},{24,8},{28,12},{1,17},{... | collective-permute-start | bytes 1474568 | tf_op jit(solution)/shard_map/ppermute | solution.py:1148
  260.3 13.6 %collective-permute-start.34 = (bf16[384,512]{1,0:T(8,128)(2,1)S(1)}, bf16[384,512]{1,0:T(8,128)(2,1)S(1)}, u32[]{:S(2)}, u32[]{:S(2)}) collective-permute-start(bf16[384,512]{1,0:T(8,128)(2,1)S(1)} %get-tuple-element.189.refs_2_), channel_id=1, source_target_pairs={{0,8},{4,12},{8,0},{12,4},{16,24},{20,28},{24,16},{28,20},{1,9},{5... | collective-permute-start | bytes 1179656 | tf_op jit(solution)/shard_map/ppermute | solution.py:1148
  276.8 11.4 %collective-permute-start.35 = (bf16[960,512]{1,0:T(8,128)(2,1)S(1)}, bf16[960,512]{1,0:T(8,128)(2,1)S(1)}, u32[]{:S(2)}, u32[]{:S(2)}) collective-permute-start(bf16[960,512]{1,0:T(8,128)(2,1)S(1)} %get-tuple-element.197.second_ref), channel_id=1, source_target_pairs={{0,4},{4,0},{8,12},{12,8},{16,20},{20,16},{24,28},{28,24},{1,5},{5... | collective-permute-start | bytes 2949128 | tf_op jit(solution)/shard_map/ppermute | solution.py:1148
  276.8 11.4 %collective-permute-start.36 = (bf16[768,512]{1,0:T(8,128)(2,1)S(1)}, bf16[768,512]{1,0:T(8,128)(2,1)S(1)}, u32[]{:S(2)}, u32[]{:S(2)}) collective-permute-start(bf16[768,512]{1,0:T(8,128)(2,1)S(1)} %get-tuple-element.198.first_ref), channel_id=1, source_target_pairs={{0,4},{4,0},{8,12},{12,8},{16,20},{20,16},{24,28},{28,24},{1,5},{5... | collective-permute-start | bytes 2359304 | tf_op jit(solution)/shard_map/ppermute | solution.py:1148
  (46 other events, 513.6 us)

commit v4 on v3

--- a/solution.py
+++ b/solution.py
@@ -276,9 +276,7 @@
 def upsample_kernel(
     info_ref,
     offset_ref,
-    before_ref,
-    own_ref,
-    after_ref,
+    rows_ref,
     align_hbm,
     bias_ref,
     out_ref,
@@ -301,13 +299,21 @@
     window = align_ref.shape[1]
     tiles = offset_ref.shape[0]
     rows = frames // tiles
-    halo, own = before_ref.shape[0], own_ref.shape[0]
+    groups, both = rows_ref.shape[:2]
+    halo = window // 2
+    piece = next(n for n in range(both // 2, both) if both - n == min(halo, n))
+    own, extra = groups * piece, both - piece
     ends = read_ends(info_ref)
     slot_ends = [info_ref[UTTS + k] for k in range(UTTS)]
     base, slot_base = info_ref[8], info_ref[9]
-    buffer_ref[0:halo, :] = before_ref[...]
-    buffer_ref[halo : halo + own, :] = own_ref[...]
-    buffer_ref[halo + own : 2 * halo + own, :] = after_ref[...]
+    for s in range(groups):
+        buffer_ref[halo + s * piece : halo + (s + 1) * piece, :] = rows_ref[s, 0:piece, :]
+    for n in range(halo // extra):
+        buffer_ref[n * extra : (n + 1) * extra, :] = rows_ref[
+            groups - halo // extra + n, piece:both, :
+        ]
+        at = halo + own + n * extra
+        buffer_ref[at : at + extra, :] = rows_ref[n, piece:both, :]
     buffer_ref[2 * halo + own :, :] = jnp.zeros_like(buffer_ref[2 * halo + own :, :])
     acc_ref[...] = jnp.zeros_like(acc_ref)
 
@@ -385,6 +391,8 @@
     coef_ref[32:40, :] = 0.5 * shift
     coef_ref[40:48, :] = 0.5 * gain * rstd
     coef_ref[48:56, :] = 0.5 * (shift - mean * gain * rstd)
+    coef_ref[56:57, :] = row(other_refs[0], LAST_ROW)
+    coef_ref[57:58, :] = row(other_refs[2], FIRST_ROW)
 
 
 UNIT, HALF_OF_UNIT, HALF_OF_VALUE = (0, 8), (24, 32), (40, 48)
@@ -826,8 +834,6 @@
     one_ref,
     two_ref,
     three_ref,
-    middle_one_ref,
-    middle_three_ref,
     inverse_ref,
     coef_two_ref,
     coef_one_ref,
@@ -871,13 +877,13 @@
         gradient_ref,
         inward(
             row(one_ref, LAST_ROW),
-            row(middle_one_ref, LAST_ROW),
+            row(coef_two_ref, 56),
             back_ref,
             owner_before,
         ),
         inward(
             row(three_ref, FIRST_ROW),
-            row(middle_three_ref, FIRST_ROW),
+            row(coef_two_ref, 57),
             back_ref,
             owner_after,
         ),
@@ -1119,7 +1125,9 @@
         functools.partial(scatter_kernel, places, copies),
         in_specs=[SM, SM] + [VM] * (len(parts) + len(kept)),
         out_specs=VM,
-        out_shape=jax.ShapeDtypeStruct((order.shape[0] * lanes, 128), F32),
+        out_shape=(pltpu.VMEM if old is None else jax.ShapeDtypeStruct)(
+            (order.shape[0] * lanes, 128), F32
+        ),
         scratch_shapes=[pltpu.VMEM((piece * lanes, 128), F32)],
         input_output_aliases={2 + len(parts): 0} if kept else {},
         compiler_params=pltpu.CompilerParams(vmem_limit_bytes=22 * MIB),
@@ -1235,15 +1243,21 @@
 
     tiles_of = frames // ROWS
     full, padded = (frames, channels), (frames + 2 * PAD, channels)
-    stats_shape, coef_shape = (STAT_ROWS, channels), (56, channels)
+    stats_shape, coef_shape = (STAT_ROWS, channels), (64, channels)
     small_acc = ((ACC_ROWS, channels), F32)
 
     order = send_order[0].reshape(groups, copies, piece_rows)
+    extra = min(halo, piece_rows)
+    from_first = seq_index < groups // 2
     mine = lax.dynamic_index_in_dim(order, tm_index, 1, False)
+    following = lax.dynamic_index_in_dim(order, jnp.minimum(tm_index + 1, copies - 1), 1, False)
+    leading = lax.dynamic_index_in_dim(order, jnp.maximum(tm_index - 1, 0), 1, False)
+    beside = jnp.where(from_first, following[:, :extra], leading[:, piece_rows - extra :])
+    mine = jnp.concatenate([mine, beside], axis=1)
     outgoing = jnp.take(phonemes, mine.reshape(-1), axis=0, mode="clip")
     received = lax.all_to_all(
-        outgoing.reshape(groups, piece_rows, channels), "seq", 0, 0, tiled=True
-    ).reshape(local_rows, channels)
+        outgoing.reshape(groups, piece_rows + extra, channels), "seq", 0, 0, tiled=True
+    )
 
     second_turned = turned(second_conv_weight)
     grad_act_two, grad_branch, bias_part = call(
@@ -1260,15 +1274,12 @@
     )
 
     received, bias_part = lax.optimization_barrier((received, bias_part))
-    slots_before, slots_after = from_neighbours(received[:halo], received[-halo:])
     upsampled, upsampled_far, wide, stat = call(
         upsample_kernel,
         (
             (info, SM),
             (tile_offsets, SM),
-            (slots_before, VM),
             (received, VM),
-            (slots_after, VM),
             (alignment, HB),
             (bias_part, VM),
         ),
@@ -1360,8 +1371,6 @@
             (inner_two, HB),
             (middle_far, HB),
             *((one, VM) for one in (stat_three, *others_three)),
-            (others_two[0], VM),
-            (others_two[2], VM),
             (inverse, VM),
             (coef_two, VM),
             (coef_one, VM),

time: 294 us -> 282 us (0.959)
  starting transfers between devices: 59.6 us -> 48.4 us
  Pallas kernels: 135 us -> 126 us
  waiting for transfers between devices: 66.4 us -> 74.3 us
    pallas_call x2, Pallas kernels: 16.4 us -> 7.14 us  [scattered(): pl.pallas_call(functools.partial(scatter_kernel, places, copies), in_spec...]
    ppermute x21, waiting for transfers between devices: 35.1 us -> 41.5 us  [shifted(): lax.ppermute(values, axis, [(i, (i + step) % devices) for i in range(devi...]
    ppermute x2 -> x1, starting transfers between devices: 6.71 us -> 1.3 us  [from_neighbours(): lax.ppermute(last_rows, 'tm', up)]
    all_to_all x1, waiting for transfers between devices: 0.23 us -> 5.06 us  [on_device(): lax.all_to_all(outgoing.reshape(groups, piece_rows + extra, channels), 's...]
    ppermute x2 -> x1, waiting for transfers between devices: 8.64 us -> 4.36 us  [from_neighbours(): lax.ppermute(first_rows, 'tm', down)]
    unnamed x84 -> x89, local copies, waits for them, and re-layouts: 10.9 us -> 12.4 us
  transfers between devices with their start and end apart: 39 -> 37, of which waited for: 28 -> 32; matrix products, arithmetic and copies ran while one was open for 3% -> 4% of each run, Pallas kernels for 23% -> 21%
where the time goes in v4:
time: 282 us; the launch traced here: 281 us
  Pallas kernels  126 us (45%)
  waiting for transfers between devices  74.3 us (26%)
  starting transfers between devices  48.4 us (17%)
  local copies, waits for them, and re-layouts  24.2 us (9%)
  other arithmetic  4.78 us (2%)
    pallas_call x14, Pallas kernels, call(): pl.pallas_call(kernel, in_specs=[spec for _, spec in inputs], out_specs=t...  119 us
    ppermute x21, waiting for transfers between devices, shifted(): lax.ppermute(values, axis, [(i, (i + step) % devices) for i in range(devi...  41.5 us
    ppermute x21, starting transfers between devices, shifted(): lax.ppermute(values, axis, [(i, (i + step) % devices) for i in range(devi...  27 us
    ppermute x12, waiting for transfers between devices, swapped(): lax.ppermute(values, 'seq', [(i, i ^ 1 << bit) for i in range(devices)])  20.4 us
    unnamed x89, local copies, waits for them, and re-layouts  12.4 us
    ppermute x12, starting transfers between devices, swapped(): lax.ppermute(values, 'seq', [(i, i ^ 1 << bit) for i in range(devices)])  8.92 us
    gather x1, local copies, waits for them, and re-layouts, on_device(): outgoing = jnp.take(phonemes, mine.reshape(-1), axis=0, mode='clip')  8.21 us
    pallas_call x2, Pallas kernels, scattered(): pl.pallas_call(functools.partial(scatter_kernel, places, copies), in_spec...  7.14 us
  transfers between devices with their start and end apart: 37, of which 32 were waited for; matrix products, arithmetic and copies ran while one was open for 4% of the time, Pallas kernels for 21%

profile of v4, /device:TPU:0, one launch (start us, length us, event | category | flops | bytes accessed | tf_op | source)
XLA Modules:
  0.0 281.1 jit_solution(14425051838407035193)
XLA Ops:
  1.7 8.2 %gather_fusion = bf16[1536,512]{1,0:T(8,128)(2,1)} fusion(bf16[4096,512]{1,0:T(8,128)(2,1)} %param.23, s32[2048]{0:T(1024)S(1)} %pad_clamp_fusion), kind=kCustom, calls=%fused_computation | custom fusion | bytes 3151872 | tf_op jit(solution)/shard_map/jit(_take)/gather | solution.py:1257
  9.9 5.3 %all-to-all-start = ((bf16[8,192,512]{2,1,0:T(8,128)(2,1)}), bf16[8,192,512]{2,1,0:T(8,128)(2,1)}, u32[]{:S(2)}, u32[]{:S(2)}) async-start(bf16[8,192,512]{2,1,0:T(8,128)(2,1)} %bitcast.15), calls=%async_computation | async-start | bytes 3145728 | tf_op jit(solution)/shard_map/all_to_all | solution.py:1258
  17.2 12.9 %shard_map.222 = (bf16[4096,512]{1,0:T(8,128)(2,1)}, bf16[4096,512]{1,0:T(8,128)(2,1)}, f32[16,512]{1,0:T(8,128)S(1)}) custom-call(s32[24]{0:T(128)S(1)} %concatenate.28.info_ref, bf16[4096,512]{1,0:T(8,128)(2,1)} %cot_hbm.3, bf16[1536,512]{1,0:T(8,128)(2,1)S(1)} %bitcast.78), custom_call_target="tpu_custom_call" | custom-call | flops 6442450944 | bytes 32212254 | tf_op jit(solution)/shard_map/pallas_call | solution.py:1098
  31.3 5.1 %all-to-all-done.rows_ref = bf16[8,192,512]{2,1,0:T(8,128)(2,1)} async-done(((bf16[8,192,512]{2,1,0:T(8,128)(2,1)}), bf16[8,192,512]{2,1,0:T(8,128)(2,1)}, u32[]{:S(2)}, u32[]{:S(2)}) %all-to-all-start) | async-done | bytes 1572896 | tf_op jit(solution)/shard_map/all_to_all | solution.py:1258
  36.4 8.7 %shard_map.223 = (f32[4096,512]{1,0:T(8,128)S(1)}, f32[4096,512]{1,0:T(8,128)}, bf16[4096,256]{1,0:T(8,128)(2,1)}, f32[24,512]{1,0:T(8,128)S(1)}) custom-call(s32[24]{0:T(128)S(1)} %concatenate.28.info_ref, s32[32]{0:T(128)S(1)} %copy-done.18, bf16[8,192,512]{2,1,0:T(8,128)(2,1)} %all-to-all-done.rows_ref, bf16[4096,128]{1,0:T(8,128)(2,1)} %align_hbm.1, ...), custom_call_target="tpu_custom_call" | custom-call | flops 1073741824 | bytes 5368709 | tf_op jit(solution)/shard_map/pallas_call | solution.py:1098
  47.2 2.6 collective-permute-start.1
  54.6 13.5 %shard_map.224 = (bf16[4128,512]{1,0:T(8,128)(2,1)}, f32[4096,512]{1,0:T(8,128)S(1)}, f32[4096,512]{1,0:T(8,128)}, bf16[4096,512]{1,0:T(8,128)(2,1)}, f32[64,512...) custom-call(s32[24]{0:T(128)S(1)} %copy-done.13, ...), custom_call_target="tpu_custom_call" | custom-call | flops 6442450944 | bytes 32212254 | tf_op jit(solution)/shard_map/pallas_call | solution.py:1098
  68.7 3.5 %collective-permute-start.4 = (f32[24,512]{1,0:T(8,128)S(1)}, f32[24,512]{1,0:T(8,128)S(1)}, u32[]{:S(2)}, u32[]{:S(2)}) collective-permute-start(f32[24,512]{1,0:T(8,128)S(1)} %get-tuple-element.139.own_ref), channel_id=1, source_target_pairs={{0,2},{1,3},{2,0},{3,1},{4,6},{5,7},{6,4},{7,5},{8,10},{9,11},{10,... | collective-permute-start | bytes 147464 | tf_op jit(solution)/shard_map/ppermute | solution.py:1140
  76.2 9.1 %shard_map.225 = (bf16[4128,512]{1,0:T(8,128)(2,1)}, bf16[4096,512]{1,0:T(8,128)(2,1)}, f32[64,512]{1,0:T(8,128)S(1)}, f32[24,512]{1,0:T(8,128)}) custom-call(s32[24]{0:T(128)S(1)} %copy-done.13, bf16[4096,512]{1,0:T(8,128)(2,1)} %get-tuple-element.132.gradient_hbm, f32[4096,512]{1,0:T(8,128)S(1)} %get-tuple-element.138.values_ref, ...), custom_call_target="tpu_custom_call" | custom-call | flops 419430400 | bytes 2097152 | tf_op jit(solution)/shard_map/pallas_call | solution.py:1098
  96.3 20.3 %shard_map.226 = (bf16[4096,512]{1,0:T(8,128)(2,1)}, f32[8,512]{1,0:T(8,128)S(1)}, bf16[4096,512]{1,0:T(8,128)(2,1)}, f32[40,512]{1,0:T(8,128)S(1)}, f32[24,512]{1,0:T(8,128)S(1)}) custom-call(s32[24]{0:T(128)S(1)} %copy-done.14, bf16[4096,512]{1,0:T(8,128)(2,1)} %get-tuple-element.141.inner_hbm, f32[4096,512]{1,0:T(8,128)} %get-tuple-element.142.middle_hbm, ...), custom_call_target="tpu_custom_call" | custom-call | flops 6442450944 | bytes 32212254 | tf_op jit(solution)/shard_map/pallas_call | solution.py:1098
  117.6 2.9 %collective-permute-start.11 = (f32[24,512]{1,0:T(8,128)S(1)}, f32[24,512]{1,0:T(8,128)S(1)}, u32[]{:S(2)}, u32[]{:S(2)}) collective-permute-start(f32[24,512]{1,0:T(8,128)S(1)} %get-tuple-element.149.own_ref), channel_id=1, source_target_pairs={{0,3},{1,0},{2,1},{3,2},{4,7},{5,4},{6,5},{7,6},{8,11},{9,8},{10,9... | collective-permute-start | bytes 147464 | tf_op jit(solution)/shard_map/ppermute | solution.py:1140
  122.2 4.1 %collective-permute-done.9.one_ref = f32[24,512]{1,0:T(8,128)S(1)} collective-permute-done((f32[24,512]{1,0:T(8,128)S(1)}, f32[24,512]{1,0:T(8,128)S(1)}, u32[]{:S(2)}, u32[]{:S(2)}) %collective-permute-start.9) | collective-permute-done | bytes 49184 | tf_op jit(solution)/shard_map/ppermute | solution.py:1140
  126.4 9.8 %shard_map.227 = (f32[64,512]{1,0:T(8,128)S(1)}, f32[1024,512]{1,0:T(8,128)S(1)}, f32[64,512]{1,0:T(8,128)S(1)}, f32[40,512]{1,0:T(8,128)S(1)}) custom-call(s32[24]{0:T(128)S(1)} %copy-done.14, s32[32]{0:T(128)S(1)} %copy-done.19, bf16[4096,512]{1,0:T(8,128)(2,1)} %get-tuple-element.147.inner_hbm, ...), custom_call_target="tpu_custom_call" | custom-call | flops 1073741824 | bytes 5368709 | tf_op jit(solution)/shard_map/pallas_call | solution.py:1098
  140.0 4.4 %collective-permute-done.13 = f32[64,512]{1,0:T(8,128)S(1)} collective-permute-done((f32[64,512]{1,0:T(8,128)S(1)}, f32[64,512]{1,0:T(8,128)S(1)}, u32[]{:S(2)}, u32[]{:S(2)}) %collective-permute-start.13) | collective-permute-done | bytes 131104 | tf_op jit(solution)/shard_map/ppermute | solution.py:1151
  145.5 4.6 %all-to-all-start.1 = ((bf16[8,128,512]{2,1,0:T(8,128)(2,1)}), bf16[8,128,512]{2,1,0:T(8,128)(2,1)S(1)}, u32[]{:S(2)}, u32[]{:S(2)}) async-start(bf16[8,128,512]{2,1,0:T(8,128)(2,1)} %bitcast.83), calls=%async_computation.1 | async-start | bytes 2097152 | tf_op jit(solution)/shard_map/all_to_all | solution.py:1436
  150.1 11.6 %shard_map.228 = (f32[768,512]{1,0:T(8,128)S(1)}, bf16[768,512]{1,0:T(8,128)(2,1)S(1)}) custom-call(s32[24]{0:T(128)S(1)} %copy-done.14, bf16[4128,512]{1,0:T(8,128)(2,1)} %get-tuple-element.192.act_hbm, bf16[4096,512]{1,0:T(8,128)(2,1)} %get-tuple-element.156.gradient_hbm, f32[8,512]{1,0:T(8,128)S(1)} %copy-done.17), custom_call_target="tpu_custom_call" | custom-call | flops 1000000 | bytes 5000 | tf_op jit(solution)/shard_map/pallas_call | solution.py:1098
  166.7 11.7 %shard_map.229 = (f32[768,512]{1,0:T(8,128)S(1)}, bf16[768,512]{1,0:T(8,128)(2,1)S(1)}) custom-call(s32[24]{0:T(128)S(1)} %copy-done.14, bf16[4128,512]{1,0:T(8,128)(2,1)} %get-tuple-element.163.act_hbm, bf16[4096,512]{1,0:T(8,128)(2,1)} %get-tuple-element.165.gradient_hbm, f32[8,512]{1,0:T(8,128)S(1)} %get-tuple-element.166.edge_ref), custom_call_target="tpu_custom_call" | custom-call | flops 1000000 | bytes 5000 | tf_op jit(solution)/shard_map/pallas_call | solution.py:1098
  183.0 8.2 %collective-permute-done.14.refs_1_ = bf16[8,128,512]{2,1,0:T(8,128)(2,1)} collective-permute-done((bf16[8,128,512]{2,1,0:T(8,128)(2,1)S(1)}, bf16[8,128,512]{2,1,0:T(8,128)(2,1)}, u32[]{:S(2)}, u32[]{:S(2)}) %collective-permute-start.14) | collective-permute-done | bytes 1048608 | tf_op jit(solution)/shard_map/ppermute | solution.py:1140
  194.3 7.2 %collective-permute-done.18.refs_1_ = bf16[384,512]{1,0:T(8,128)(2,1)S(1)} collective-permute-done((bf16[384,512]{1,0:T(8,128)(2,1)S(1)}, bf16[384,512]{1,0:T(8,128)(2,1)S(1)}, u32[]{:S(2)}, u32[]{:S(2)}) %collective-permute-start.18) | collective-permute-done | bytes 393248 | tf_op jit(solution)/shard_map/ppermute | solution.py:1156
  207.0 3.1 %shard_map.232.refs_2_ = f32[16384,128]{1,0:T(8,128)S(1)} custom-call(s32[24]{0:T(128)S(1)} %copy-done.14, s32[4096]{0:T(1024)S(1)} %bitcast.81, bf16[8,128,512]{2,1,0:T(8,128)(2,1)S(1)} %all-to-all-done.1.refs_0_, bf16[8,128,512]{2,1,0:T(8,128)(2,1)} %collective-permute-done.14.refs_1_), custom_call_target="tpu_custom_call" | custom-call | flops 1000000 | bytes 10000 | tf_op jit(solution)/shard_map/pallas_call | solution.py:1124
  212.9 2.9 %collective-permute-done.20 = bf16[192,512]{1,0:T(8,128)(2,1)S(1)} collective-permute-done((bf16[192,512]{1,0:T(8,128)(2,1)S(1)}, bf16[192,512]{1,0:T(8,128)(2,1)S(1)}, u32[]{:S(2)}, u32[]{:S(2)}) %collective-permute-start.20) | collective-permute-done | bytes 196640 | tf_op jit(solution)/shard_map/ppermute | solution.py:1156
  215.9 4.4 %collective-permute-done.17.refs_0_ = bf16[8,128,512]{2,1,0:T(8,128)(2,1)} collective-permute-done((bf16[8,128,512]{2,1,0:T(8,128)(2,1)}, bf16[8,128,512]{2,1,0:T(8,128)(2,1)}, u32[]{:S(2)}, u32[]{:S(2)}) %collective-permute-start.17) | collective-permute-done | bytes 1048608 | tf_op jit(solution)/shard_map/ppermute | solution.py:1140
  220.5 3.8 %collective-permute-start.23 = (bf16[2,48,512]{2,1,0:T(8,128)(2,1)S(1)}, bf16[2,48,512]{2,1,0:T(8,128)(2,1)S(1)}, u32[]{:S(2)}, u32[]{:S(2)}) collective-permute-start(bf16[2,48,512]{2,1,0:T(8,128)(2,1)S(1)} %get-tuple-element.212), channel_id=1, source_target_pairs={{0,3},{1,0},{2,1},{3,2},{4,7},{5,4},{6,5},{7,6},{8,11},{9,8},{10,9... | collective-permute-start | bytes 294920 | tf_op jit(solution)/shard_map/ppermute | solution.py:1140
  226.9 3.1 %collective-permute-done.24 = bf16[2,48,512]{2,1,0:T(8,128)(2,1)S(1)} collective-permute-done((bf16[2,48,512]{2,1,0:T(8,128)(2,1)S(1)}, bf16[2,48,512]{2,1,0:T(8,128)(2,1)S(1)}, u32[]{:S(2)}, u32[]{:S(2)}) %collective-permute-start.24) | collective-permute-done | bytes 98336 | tf_op jit(solution)/shard_map/ppermute | solution.py:1140
  231.0 3.9 %collective-permute-start.26 = (bf16[2,48,512]{2,1,0:T(8,128)(2,1)S(1)}, bf16[2,48,512]{2,1,0:T(8,128)(2,1)S(1)}, u32[]{:S(2)}, u32[]{:S(2)}) collective-permute-start(bf16[2,48,512]{2,1,0:T(8,128)(2,1)S(1)} %get-tuple-element.207), channel_id=1, source_target_pairs={{0,3},{1,0},{2,1},{3,2},{4,7},{5,4},{6,5},{7,6},{8,11},{9,8},{10,9... | collective-permute-start | bytes 294920 | tf_op jit(solution)/shard_map/ppermute | solution.py:1140
  237.1 3.6 %collective-permute-done.27 = bf16[2,48,512]{2,1,0:T(8,128)(2,1)S(1)} collective-permute-done((bf16[2,48,512]{2,1,0:T(8,128)(2,1)S(1)}, bf16[2,48,512]{2,1,0:T(8,128)(2,1)S(1)}, u32[]{:S(2)}, u32[]{:S(2)}) %collective-permute-start.27) | collective-permute-done | bytes 98336 | tf_op jit(solution)/shard_map/ppermute | solution.py:1140
  242.3 4.9 %collective-permute-done.30.refs_3_ = bf16[192,512]{1,0:T(8,128)(2,1)S(1)} collective-permute-done((bf16[192,512]{1,0:T(8,128)(2,1)S(1)}, bf16[192,512]{1,0:T(8,128)(2,1)S(1)}, u32[]{:S(2)}, u32[]{:S(2)}) %collective-permute-start.30) | collective-permute-done | bytes 196640 | tf_op jit(solution)/shard_map/ppermute | solution.py:1156
  250.4 12.4 %shard_map.235 = bf16[4096,512]{1,0:T(8,128)(2,1)} custom-call(s32[24]{0:T(128)S(1)} %copy-done.14, bf16[4128,512]{1,0:T(8,128)(2,1)} %get-tuple-element.192.act_hbm, f32[4096,512]{1,0:T(8,128)} %get-tuple-element.193.values_hbm, bf16[1536,512]{1,0:T(8,128)(2,1)S(1)} %copy-done.1, bf16[1,512]{1,0:T(2,128)(2,1)S(1)} %broadcast_in_dim.54.bias_ref), custom_call_target="tpu_custom_call" | custom-call | flops 1000000 | bytes 5000 | tf_op jit(solution)/shard_map/pallas_call | solution.py:1098
  263.4 3.5 %collective-permute-done.28.refs_1_ = bf16[8,128,512]{2,1,0:T(8,128)(2,1)S(1)} collective-permute-done((bf16[8,128,512]{2,1,0:T(8,128)(2,1)}, bf16[8,128,512]{2,1,0:T(8,128)(2,1)S(1)}, u32[]{:S(2)}, u32[]{:S(2)}) %collective-permute-start.28) | collective-permute-done | bytes 1048608 | tf_op jit(solution)/shard_map/ppermute | solution.py:1140
  268.7 4.1 %shard_map.236 = f32[16384,128]{1,0:T(8,128)S(1)} custom-call(s32[24]{0:T(128)S(1)} %copy-done.14, s32[4096]{0:T(1024)S(1)} %bitcast.82, bf16[8,128,512]{2,1,0:T(8,128)(2,1)} %collective-permute-done.17.refs_0_, bf16[8,128,512]{2,1,0:T(8,128)(2,1)S(1)} %collective-permute-done.28.refs_1_, ...), custom_call_target="tpu_custom_call", output_to_operand_aliasing={{}: (4, {})} | custom-call | flops 1000000 | bytes 10000 | tf_op jit(solution)/shard_map/pallas_call | solution.py:1124
  272.8 3.4 %copy.42 = f32[4096,512]{1,0:T(8,128)} copy(f32[4096,512]{1,0:T(8,128)S(1)} %bitcast.75) | data formatting | bytes 16777216
  276.2 4.9 %shard_map.237 = (f32[1536,512]{1,0:T(8,128)}, f32[1536,512]{1,0:T(8,128)}, f32[128,1024]{1,0:T(8,128)}, f32[1,1024]{1,0:T(1,128)}, f32[128,1024]{1,0:T(8,128)}, /*index=5*/f32[1,1024]{1,0:T(1,128)}, f32[1,512]{1,0:T(1,128)}) custom-call(s32[24]{0:T(128)S(1)} %copy-done.14, bf16[960,512]{1,0:T(8,128)(2,1)S(1)} %get-tuple-element.197.second_ref, ...), custom_call_target="tpu_custom_call" | custom-call | flops 1000000 | bytes 5000 | tf_op jit(solution)/shard_map/pallas_call | solution.py:1098
  (191 shorter events, 68.0 us)
Async XLA Ops:
  9.9 26.4 %all-to-all-start = ((bf16[8,192,512]{2,1,0:T(8,128)(2,1)}), bf16[8,192,512]{2,1,0:T(8,128)(2,1)}, u32[]{:S(2)}, u32[]{:S(2)}) async-start(bf16[8,192,512]{2,1,0:T(8,128)(2,1)} %bitcast.15), calls=%async_computation | async-start | bytes 3145728 | tf_op jit(solution)/shard_map/all_to_all | solution.py:1258
  45.1 6.2 %collective-permute-start = (f32[24,512]{1,0:T(8,128)S(1)}, f32[24,512]{1,0:T(8,128)S(1)}, u32[]{:S(2)}, u32[]{:S(2)}) collective-permute-start(f32[24,512]{1,0:T(8,128)S(1)} %get-tuple-element.137.own_ref), channel_id=1, source_target_pairs={{0,1},{1,2},{2,3},{3,0},{4,5},{5,6},{6,7},{7,4},{8,9},{9,10},{10,1... | collective-permute-start | bytes 147464 | tf_op jit(solution)/shard_map/ppermute | solution.py:1140
  47.2 5.0 %collective-permute-start.1 = (f32[24,512]{1,0:T(8,128)S(1)}, f32[24,512]{1,0:T(8,128)S(1)}, u32[]{:S(2)}, u32[]{:S(2)}) collective-permute-start(f32[24,512]{1,0:T(8,128)S(1)} %get-tuple-element.137.own_ref), channel_id=1, source_target_pairs={{0,2},{1,3},{2,0},{3,1},{4,6},{5,7},{6,4},{7,5},{8,10},{9,11},{10,... | collective-permute-start | bytes 147464 | tf_op jit(solution)/shard_map/ppermute | solution.py:1140
  68.2 6.0 %collective-permute-start.3 = (f32[24,512]{1,0:T(8,128)S(1)}, f32[24,512]{1,0:T(8,128)S(1)}, u32[]{:S(2)}, u32[]{:S(2)}) collective-permute-start(f32[24,512]{1,0:T(8,128)S(1)} %get-tuple-element.139.own_ref), channel_id=1, source_target_pairs={{0,1},{1,2},{2,3},{3,0},{4,5},{5,6},{6,7},{7,4},{8,9},{9,10},{10,1... | collective-permute-start | bytes 147464 | tf_op jit(solution)/shard_map/ppermute | solution.py:1140
  68.7 6.5 %collective-permute-start.4 = (f32[24,512]{1,0:T(8,128)S(1)}, f32[24,512]{1,0:T(8,128)S(1)}, u32[]{:S(2)}, u32[]{:S(2)}) collective-permute-start(f32[24,512]{1,0:T(8,128)S(1)} %get-tuple-element.139.own_ref), channel_id=1, source_target_pairs={{0,2},{1,3},{2,0},{3,1},{4,6},{5,7},{6,4},{7,5},{8,10},{9,11},{10,... | collective-permute-start | bytes 147464 | tf_op jit(solution)/shard_map/ppermute | solution.py:1140
  86.0 6.3 %collective-permute-start.6 = (f32[24,512]{1,0:T(8,128)}, f32[24,512]{1,0:T(8,128)}, u32[]{:S(2)}, u32[]{:S(2)}) collective-permute-start(f32[24,512]{1,0:T(8,128)} %get-tuple-element.143.own_ref), channel_id=1, source_target_pairs={{0,1},{1,2},{2,3},{3,0},{4,5},{5,6},{6,7},{7,4},{8,9},{9,10},{10,1... | collective-permute-start | bytes 147464 | tf_op jit(solution)/shard_map/ppermute | solution.py:1140
  86.5 6.5 %collective-permute-start.7 = (f32[24,512]{1,0:T(8,128)}, f32[24,512]{1,0:T(8,128)}, u32[]{:S(2)}, u32[]{:S(2)}) collective-permute-start(f32[24,512]{1,0:T(8,128)} %get-tuple-element.143.own_ref), channel_id=1, source_target_pairs={{0,2},{1,3},{2,0},{3,1},{4,6},{5,7},{6,4},{7,5},{8,10},{9,11},{10,... | collective-permute-start | bytes 147464 | tf_op jit(solution)/shard_map/ppermute | solution.py:1140
  88.9 4.5 %collective-permute-start.8 = (f32[24,512]{1,0:T(8,128)}, f32[24,512]{1,0:T(8,128)}, u32[]{:S(2)}, u32[]{:S(2)}) collective-permute-start(f32[24,512]{1,0:T(8,128)} %get-tuple-element.143.own_ref), channel_id=1, source_target_pairs={{0,3},{1,0},{2,1},{3,2},{4,7},{5,4},{6,5},{7,6},{8,11},{9,8},{10,9... | collective-permute-start | bytes 147464 | tf_op jit(solution)/shard_map/ppermute | solution.py:1140
  116.6 5.1 %collective-permute-start.10 = (f32[24,512]{1,0:T(8,128)S(1)}, f32[24,512]{1,0:T(8,128)S(1)}, u32[]{:S(2)}, u32[]{:S(2)}) collective-permute-start(f32[24,512]{1,0:T(8,128)S(1)} %get-tuple-element.149.own_ref), channel_id=1, source_target_pairs={{0,2},{1,3},{2,0},{3,1},{4,6},{5,7},{6,4},{7,5},{8,10},{9,11},{10,... | collective-permute-start | bytes 147464 | tf_op jit(solution)/shard_map/ppermute | solution.py:1140
  117.6 4.7 %collective-permute-start.11 = (f32[24,512]{1,0:T(8,128)S(1)}, f32[24,512]{1,0:T(8,128)S(1)}, u32[]{:S(2)}, u32[]{:S(2)}) collective-permute-start(f32[24,512]{1,0:T(8,128)S(1)} %get-tuple-element.149.own_ref), channel_id=1, source_target_pairs={{0,3},{1,0},{2,1},{3,2},{4,7},{5,4},{6,5},{7,6},{8,11},{9,8},{10,9... | collective-permute-start | bytes 147464 | tf_op jit(solution)/shard_map/ppermute | solution.py:1140
  120.5 5.9 %collective-permute-start.9 = (f32[24,512]{1,0:T(8,128)S(1)}, f32[24,512]{1,0:T(8,128)S(1)}, u32[]{:S(2)}, u32[]{:S(2)}) collective-permute-start(f32[24,512]{1,0:T(8,128)S(1)} %get-tuple-element.149.own_ref), channel_id=1, source_target_pairs={{0,1},{1,2},{2,3},{3,0},{4,5},{5,6},{6,7},{7,4},{8,9},{9,10},{10,1... | collective-permute-start | bytes 147464 | tf_op jit(solution)/shard_map/ppermute | solution.py:1140
  137.5 6.9 %collective-permute-start.13 = (f32[64,512]{1,0:T(8,128)S(1)}, f32[64,512]{1,0:T(8,128)S(1)}, u32[]{:S(2)}, u32[]{:S(2)}) collective-permute-start(f32[64,512]{1,0:T(8,128)S(1)} %get-tuple-element.152), channel_id=1, source_target_pairs={{1,0},{2,1},{3,2},{5,4},{6,5},{7,6},{9,8},{10,9},{11,10},{13,12},{... | collective-permute-start | bytes 393224 | tf_op jit(solution)/shard_map/ppermute | solution.py:1151
  145.5 20.0 %all-to-all-start.1 = ((bf16[8,128,512]{2,1,0:T(8,128)(2,1)}), bf16[8,128,512]{2,1,0:T(8,128)(2,1)S(1)}, u32[]{:S(2)}, u32[]{:S(2)}) async-start(bf16[8,128,512]{2,1,0:T(8,128)(2,1)} %bitcast.83), calls=%async_computation.1 | async-start | bytes 2097152 | tf_op jit(solution)/shard_map/all_to_all | solution.py:1436
  165.5 25.7 %collective-permute-start.14 = (bf16[8,128,512]{2,1,0:T(8,128)(2,1)S(1)}, bf16[8,128,512]{2,1,0:T(8,128)(2,1)}, u32[]{:S(2)}, u32[]{:S(2)}) collective-permute-start(bf16[8,128,512]{2,1,0:T(8,128)(2,1)S(1)} %all-to-all-done.1.refs_0_), channel_id=1, source_target_pairs={{0,1},{1,2},{2,3},{3,0},{4,5},{5,6},{6,7},{7,4},{8,9},{9,10},{10,1... | collective-permute-start | bytes 3145736 | tf_op jit(solution)/shard_map/ppermute | solution.py:1140
  191.1 10.4 %collective-permute-start.18 = (bf16[384,512]{1,0:T(8,128)(2,1)S(1)}, bf16[384,512]{1,0:T(8,128)(2,1)S(1)}, u32[]{:S(2)}, u32[]{:S(2)}) collective-permute-start(bf16[384,512]{1,0:T(8,128)(2,1)S(1)} %get-tuple-element.175), channel_id=1, source_target_pairs={{0,8},{4,12},{8,0},{12,4},{16,24},{20,28},{24,16},{28,20},{1,9},{5... | collective-permute-start | bytes 1179656 | tf_op jit(solution)/shard_map/ppermute | solution.py:1156
  193.0 10.0 %collective-permute-start.19 = (bf16[384,512]{1,0:T(8,128)(2,1)S(1)}, bf16[384,512]{1,0:T(8,128)(2,1)S(1)}, u32[]{:S(2)}, u32[]{:S(2)}) collective-permute-start(bf16[384,512]{1,0:T(8,128)(2,1)S(1)} %get-tuple-element.177), channel_id=1, source_target_pairs={{0,16},{4,20},{8,24},{12,28},{16,0},{20,4},{24,8},{28,12},{1,17},{... | collective-permute-start | bytes 1179656 | tf_op jit(solution)/shard_map/ppermute | solution.py:1156
  194.3 26.0 %collective-permute-start.17 = (bf16[8,128,512]{2,1,0:T(8,128)(2,1)}, bf16[8,128,512]{2,1,0:T(8,128)(2,1)}, u32[]{:S(2)}, u32[]{:S(2)}) collective-permute-start(bf16[8,128,512]{2,1,0:T(8,128)(2,1)} %collective-permute-done.14.refs_1_), channel_id=1, source_target_pairs={{0,1},{1,2},{2,3},{3,0},{4,5},{5,6},{6,7},{7,4},{8,9},{9,10},{10,1... | collective-permute-start | bytes 3145736 | tf_op jit(solution)/shard_map/ppermute | solution.py:1140
  205.9 6.0 %collective-permute-start.21 = (bf16[192,512]{1,0:T(8,128)(2,1)}, bf16[192,512]{1,0:T(8,128)(2,1)}, u32[]{:S(2)}, u32[]{:S(2)}) collective-permute-start(bf16[192,512]{1,0:T(8,128)(2,1)} %get-tuple-element.181), channel_id=1, source_target_pairs={{0,8},{4,12},{8,0},{12,4},{16,24},{20,28},{24,16},{28,20},{1,9},{5... | collective-permute-start | bytes 589832 | tf_op jit(solution)/shard_map/ppermute | solution.py:1156
  210.1 5.7 %collective-permute-start.20 = (bf16[192,512]{1,0:T(8,128)(2,1)S(1)}, bf16[192,512]{1,0:T(8,128)(2,1)S(1)}, u32[]{:S(2)}, u32[]{:S(2)}) collective-permute-start(bf16[192,512]{1,0:T(8,128)(2,1)S(1)} %copy-done.27), channel_id=1, source_target_pairs={{0,16},{4,20},{8,24},{12,28},{16,0},{20,4},{24,8},{28,12},{1,17},{... | collective-permute-start | bytes 589832 | tf_op jit(solution)/shard_map/ppermute | solution.py:1156
  220.4 6.5 %collective-permute-start.22 = (bf16[2,48,512]{2,1,0:T(8,128)(2,1)S(1)}, bf16[2,48,512]{2,1,0:T(8,128)(2,1)S(1)}, u32[]{:S(2)}, u32[]{:S(2)}) collective-permute-start(bf16[2,48,512]{2,1,0:T(8,128)(2,1)S(1)} %get-tuple-element.210), channel_id=1, source_target_pairs={{0,1},{1,2},{2,3},{3,0},{4,5},{5,6},{6,7},{7,4},{8,9},{9,10},{10,1... | collective-permute-start | bytes 294920 | tf_op jit(solution)/shard_map/ppermute | solution.py:1140
  220.5 6.5 %collective-permute-start.23 = (bf16[2,48,512]{2,1,0:T(8,128)(2,1)S(1)}, bf16[2,48,512]{2,1,0:T(8,128)(2,1)S(1)}, u32[]{:S(2)}, u32[]{:S(2)}) collective-permute-start(bf16[2,48,512]{2,1,0:T(8,128)(2,1)S(1)} %get-tuple-element.212), channel_id=1, source_target_pairs={{0,3},{1,0},{2,1},{3,2},{4,7},{5,4},{6,5},{7,6},{8,11},{9,8},{10,9... | collective-permute-start | bytes 294920 | tf_op jit(solution)/shard_map/ppermute | solution.py:1140
  224.3 5.8 %collective-permute-start.24 = (bf16[2,48,512]{2,1,0:T(8,128)(2,1)S(1)}, bf16[2,48,512]{2,1,0:T(8,128)(2,1)S(1)}, u32[]{:S(2)}, u32[]{:S(2)}) collective-permute-start(bf16[2,48,512]{2,1,0:T(8,128)(2,1)S(1)} %get-tuple-element.211), channel_id=1, source_target_pairs={{0,2},{1,3},{2,0},{3,1},{4,6},{5,7},{6,4},{7,5},{8,10},{9,11},{10,... | collective-permute-start | bytes 294920 | tf_op jit(solution)/shard_map/ppermute | solution.py:1140
  230.1 6.6 %collective-permute-start.25 = (bf16[2,48,512]{2,1,0:T(8,128)(2,1)S(1)}, bf16[2,48,512]{2,1,0:T(8,128)(2,1)S(1)}, u32[]{:S(2)}, u32[]{:S(2)}) collective-permute-start(bf16[2,48,512]{2,1,0:T(8,128)(2,1)S(1)} %get-tuple-element.207), channel_id=1, source_target_pairs={{0,1},{1,2},{2,3},{3,0},{4,5},{5,6},{6,7},{7,4},{8,9},{9,10},{10,1... | collective-permute-start | bytes 294920 | tf_op jit(solution)/shard_map/ppermute | solution.py:1140
  231.0 6.1 %collective-permute-start.26 = (bf16[2,48,512]{2,1,0:T(8,128)(2,1)S(1)}, bf16[2,48,512]{2,1,0:T(8,128)(2,1)S(1)}, u32[]{:S(2)}, u32[]{:S(2)}) collective-permute-start(bf16[2,48,512]{2,1,0:T(8,128)(2,1)S(1)} %get-tuple-element.207), channel_id=1, source_target_pairs={{0,3},{1,0},{2,1},{3,2},{4,7},{5,4},{6,5},{7,6},{8,11},{9,8},{10,9... | collective-permute-start | bytes 294920 | tf_op jit(solution)/shard_map/ppermute | solution.py:1140
  234.9 5.9 %collective-permute-start.27 = (bf16[2,48,512]{2,1,0:T(8,128)(2,1)S(1)}, bf16[2,48,512]{2,1,0:T(8,128)(2,1)S(1)}, u32[]{:S(2)}, u32[]{:S(2)}) collective-permute-start(bf16[2,48,512]{2,1,0:T(8,128)(2,1)S(1)} %get-tuple-element.207), channel_id=1, source_target_pairs={{0,2},{1,3},{2,0},{3,1},{4,6},{5,7},{6,4},{7,5},{8,10},{9,11},{10,... | collective-permute-start | bytes 294920 | tf_op jit(solution)/shard_map/ppermute | solution.py:1140
  240.8 26.1 %collective-permute-start.28 = (bf16[8,128,512]{2,1,0:T(8,128)(2,1)}, bf16[8,128,512]{2,1,0:T(8,128)(2,1)S(1)}, u32[]{:S(2)}, u32[]{:S(2)}) collective-permute-start(bf16[8,128,512]{2,1,0:T(8,128)(2,1)} %collective-permute-done.17.refs_0_), channel_id=1, source_target_pairs={{0,1},{1,2},{2,3},{3,0},{4,5},{5,6},{6,7},{7,4},{8,9},{9,10},{10,1... | collective-permute-start | bytes 3145736 | tf_op jit(solution)/shard_map/ppermute | solution.py:1140
  241.2 6.6 %collective-permute-start.29 = (bf16[240,512]{1,0:T(8,128)(2,1)S(1)}, bf16[240,512]{1,0:T(8,128)(2,1)S(1)}, u32[]{:S(2)}, u32[]{:S(2)}) collective-permute-start(bf16[240,512]{1,0:T(8,128)(2,1)S(1)} %constant_dynamic-update-slice_fusion.refs_0_), channel_id=1, source_target_pairs={{0,8},{4,12},{8,0},{12,4},{16,24},{20,28},{24,16},{28,20},{1,9},{5... | collective-permute-start | bytes 737288 | tf_op jit(solution)/shard_map/ppermute | solution.py:1156
  241.5 5.7 %collective-permute-start.30 = (bf16[192,512]{1,0:T(8,128)(2,1)S(1)}, bf16[192,512]{1,0:T(8,128)(2,1)S(1)}, u32[]{:S(2)}, u32[]{:S(2)}) collective-permute-start(bf16[192,512]{1,0:T(8,128)(2,1)S(1)} %slice_bitcast_fusion.refs_2_), channel_id=1, source_target_pairs={{0,16},{4,20},{8,24},{12,28},{16,0},{20,4},{24,8},{28,12},{1,17},{... | collective-permute-start | bytes 589832 | tf_op jit(solution)/shard_map/ppermute | solution.py:1156
  248.4 14.3 %collective-permute-start.31 = (bf16[480,512]{1,0:T(8,128)(2,1)S(1)}, bf16[480,512]{1,0:T(8,128)(2,1)S(1)}, u32[]{:S(2)}, u32[]{:S(2)}) collective-permute-start(bf16[480,512]{1,0:T(8,128)(2,1)S(1)} %get-tuple-element.188.refs_0_), channel_id=1, source_target_pairs={{0,16},{4,20},{8,24},{12,28},{16,0},{20,4},{24,8},{28,12},{1,17},{... | collective-permute-start | bytes 1474568 | tf_op jit(solution)/shard_map/ppermute | solution.py:1156
  249.0 13.7 %collective-permute-start.32 = (bf16[384,512]{1,0:T(8,128)(2,1)S(1)}, bf16[384,512]{1,0:T(8,128)(2,1)S(1)}, u32[]{:S(2)}, u32[]{:S(2)}) collective-permute-start(bf16[384,512]{1,0:T(8,128)(2,1)S(1)} %get-tuple-element.189.refs_2_), channel_id=1, source_target_pairs={{0,8},{4,12},{8,0},{12,4},{16,24},{20,28},{24,16},{28,20},{1,9},{5... | collective-permute-start | bytes 1179656 | tf_op jit(solution)/shard_map/ppermute | solution.py:1156
  266.9 9.2 %collective-permute-start.33 = (bf16[960,512]{1,0:T(8,128)(2,1)S(1)}, bf16[960,512]{1,0:T(8,128)(2,1)S(1)}, u32[]{:S(2)}, u32[]{:S(2)}) collective-permute-start(bf16[960,512]{1,0:T(8,128)(2,1)S(1)} %get-tuple-element.197.second_ref), channel_id=1, source_target_pairs={{0,4},{4,0},{8,12},{12,8},{16,20},{20,16},{24,28},{28,24},{1,5},{5... | collective-permute-start | bytes 2949128 | tf_op jit(solution)/shard_map/ppermute | solution.py:1156
  266.9 9.2 %collective-permute-start.34 = (bf16[768,512]{1,0:T(8,128)(2,1)S(1)}, bf16[768,512]{1,0:T(8,128)(2,1)S(1)}, u32[]{:S(2)}, u32[]{:S(2)}) collective-permute-start(bf16[768,512]{1,0:T(8,128)(2,1)S(1)} %get-tuple-element.198.first_ref), channel_id=1, source_target_pairs={{0,4},{4,0},{8,12},{12,8},{16,20},{20,16},{24,28},{28,24},{1,5},{5... | collective-permute-start | bytes 2359304 | tf_op jit(solution)/shard_map/ppermute | solution.py:1156
  (46 other events, 507.0 us)

commit v5 on v4

--- a/solution.py
+++ b/solution.py
@@ -155,6 +155,19 @@
     channels = weight_ref.shape[1]
     return sum(
         jnp.dot(tap, weight_ref[k * channels : (k + 1) * channels, :], preferred_element_type=F32)
+        for k, tap in enumerate(taps)
+    )
+
+
+def convolved_back(taps, weight_ref):
+    channels = weight_ref.shape[1]
+    return sum(
+        lax.dot_general(
+            tap,
+            weight_ref[k * channels : (k + 1) * channels, :],
+            (((1,), (1,)), ((), ())),
+            preferred_element_type=F32,
+        )
         for k, tap in enumerate(taps)
     )
 
@@ -949,7 +962,7 @@
 
         late.tile(i).wait()
         before, here, after = taps_of(gradient_ref, ends, start, base)
-        full_ref[...] = convolved((after, here, before), weight_ref)
+        full_ref[...] = convolved_back((after, here, before), weight_ref)
         for_blocks(0, ROWS, BLOCK, lambda inside: slope_step(start + inside, inside))
         outward.tile(i).start()
 
@@ -1050,9 +1063,9 @@
         lax.fori_loop(0, each // 4, four, 0)
 
     for_tiles(frames, blocks)
-    before_ref[...] = total_ref[0:halo, :]
+    before_ref[...] = total_ref[0:halo, :].astype(BF16)
     out_ref[...] = total_ref[halo : halo + own, :]
-    after_ref[...] = total_ref[halo + own : 2 * halo + own, :]
+    after_ref[...] = total_ref[halo + own : 2 * halo + own, :].astype(BF16)
 
 
 def scatter_kernel(places, copies, info_ref, order_ref, *refs):
@@ -1375,7 +1388,7 @@
             (coef_two, VM),
             (coef_one, VM),
             (unit_one, HB),
-            (turned(first_conv_weight), VM),
+            (first_conv_weight, VM),
         ),
         (
             (full, BF16, HB),
@@ -1412,9 +1425,9 @@
             (coef_one, VM),
         ),
         (
-            ((halo, channels), F32, VM),
+            ((halo, channels), BF16, VM),
             ((local_rows, channels), F32, VM),
-            ((halo, channels), F32, VM),
+            ((halo, channels), BF16, VM),
             ((40, channels), F32, VM),
         ),
         [

time: 282 us -> 276 us (0.979)
  local copies, waits for them, and re-layouts: 24.2 us -> 18.7 us
    unnamed x89 -> x59, local copies, waits for them, and re-layouts: 12.4 us -> 8.49 us
  transfers between devices with their start and end apart: 37 -> 37, of which waited for: 32 -> 32; matrix products, arithmetic and copies ran while one was open for 4% -> 3% of each run, Pallas kernels for 21% -> 22%
where the time goes in v5:
time: 276 us
  Pallas kernels  125 us (45%)
  waiting for transfers between devices  76.2 us (28%)
  starting transfers between devices  48.2 us (17%)
  local copies, waits for them, and re-layouts  18.7 us (7%)
  other arithmetic  4.75 us (2%)
    pallas_call x14, Pallas kernels, call(): pl.pallas_call(kernel, in_specs=[spec for _, spec in inputs], out_specs=t...  118 us
    ppermute x21, waiting for transfers between devices, shifted(): lax.ppermute(values, axis, [(i, (i + step) % devices) for i in range(devi...  43.1 us
    ppermute x21, starting transfers between devices, shifted(): lax.ppermute(values, axis, [(i, (i + step) % devices) for i in range(devi...  27 us
    ppermute x12, waiting for transfers between devices, swapped(): lax.ppermute(values, 'seq', [(i, i ^ 1 << bit) for i in range(devices)])  20.4 us
    ppermute x12, starting transfers between devices, swapped(): lax.ppermute(values, 'seq', [(i, i ^ 1 << bit) for i in range(devices)])  8.69 us
    unnamed x59, local copies, waits for them, and re-layouts  8.49 us
    gather x1, local copies, waits for them, and re-layouts, on_device(): outgoing = jnp.take(phonemes, mine.reshape(-1), axis=0, mode='clip')  8.21 us
    pallas_call x2, Pallas kernels, scattered(): pl.pallas_call(functools.partial(scatter_kernel, places, copies), in_spec...  7.14 us
  transfers between devices with their start and end apart: 37, of which 32 were waited for; matrix products, arithmetic and copies ran while one was open for 3% of the time, Pallas kernels for 22%

profile of v5, /device:TPU:0, one launch (start us, length us, event | category | flops | bytes accessed | tf_op | source)
XLA Modules:
  0.0 275.9 jit_solution(11821600774391863302)
XLA Ops:
  1.7 8.2 %gather_fusion = bf16[1536,512]{1,0:T(8,128)(2,1)} fusion(bf16[4096,512]{1,0:T(8,128)(2,1)} %param.23, s32[2048]{0:T(1024)S(1)} %pad_clamp_fusion), kind=kCustom, calls=%fused_computation | custom fusion | bytes 3151872 | tf_op jit(solution)/shard_map/jit(_take)/gather | solution.py:1270
  9.9 5.3 %all-to-all-start = ((bf16[8,192,512]{2,1,0:T(8,128)(2,1)}), bf16[8,192,512]{2,1,0:T(8,128)(2,1)}, u32[]{:S(2)}, u32[]{:S(2)}) async-start(bf16[8,192,512]{2,1,0:T(8,128)(2,1)} %bitcast.15), calls=%async_computation | async-start | bytes 3145728 | tf_op jit(solution)/shard_map/all_to_all | solution.py:1271
  16.6 12.9 %shard_map.222 = (bf16[4096,512]{1,0:T(8,128)(2,1)}, bf16[4096,512]{1,0:T(8,128)(2,1)}, f32[16,512]{1,0:T(8,128)S(1)}) custom-call(s32[24]{0:T(128)S(1)} %concatenate.28.info_ref, bf16[4096,512]{1,0:T(8,128)(2,1)} %cot_hbm.3, bf16[1536,512]{1,0:T(8,128)(2,1)S(1)} %bitcast.73), custom_call_target="tpu_custom_call" | custom-call | flops 6442450944 | bytes 32212254 | tf_op jit(solution)/shard_map/pallas_call | solution.py:1111
  30.2 6.2 %all-to-all-done.rows_ref = bf16[8,192,512]{2,1,0:T(8,128)(2,1)} async-done(((bf16[8,192,512]{2,1,0:T(8,128)(2,1)}), bf16[8,192,512]{2,1,0:T(8,128)(2,1)}, u32[]{:S(2)}, u32[]{:S(2)}) %all-to-all-start) | async-done | bytes 1572896 | tf_op jit(solution)/shard_map/all_to_all | solution.py:1271
  37.3 8.6 %shard_map.223 = (f32[4096,512]{1,0:T(8,128)S(1)}, f32[4096,512]{1,0:T(8,128)}, bf16[4096,256]{1,0:T(8,128)(2,1)}, f32[24,512]{1,0:T(8,128)S(1)}) custom-call(s32[24]{0:T(128)S(1)} %concatenate.28.info_ref, s32[32]{0:T(128)S(1)} %copy-done.6, bf16[8,192,512]{2,1,0:T(8,128)(2,1)} %all-to-all-done.rows_ref, bf16[4096,128]{1,0:T(8,128)(2,1)} %align_hbm.1, ...), custom_call_target="tpu_custom_call" | custom-call | flops 1073741824 | bytes 5368709 | tf_op jit(solution)/shard_map/pallas_call | solution.py:1111
  47.9 2.6 collective-permute-start.1
  54.7 13.6 %shard_map.224 = (bf16[4128,512]{1,0:T(8,128)(2,1)}, f32[4096,512]{1,0:T(8,128)S(1)}, f32[4096,512]{1,0:T(8,128)}, bf16[4096,512]{1,0:T(8,128)(2,1)}, f32[64,512...) custom-call(s32[24]{0:T(128)S(1)} %concatenate.28.info_ref, ...), custom_call_target="tpu_custom_call" | custom-call | flops 6442450944 | bytes 32212254 | tf_op jit(solution)/shard_map/pallas_call | solution.py:1111
  68.8 3.5 %collective-permute-start.4 = (f32[24,512]{1,0:T(8,128)S(1)}, f32[24,512]{1,0:T(8,128)S(1)}, u32[]{:S(2)}, u32[]{:S(2)}) collective-permute-start(f32[24,512]{1,0:T(8,128)S(1)} %get-tuple-element.139.own_ref), channel_id=1, source_target_pairs={{0,2},{1,3},{2,0},{3,1},{4,6},{5,7},{6,4},{7,5},{8,10},{9,11},{10,... | collective-permute-start | bytes 147464 | tf_op jit(solution)/shard_map/ppermute | solution.py:1153
  76.4 8.6 %shard_map.225 = (bf16[4128,512]{1,0:T(8,128)(2,1)}, bf16[4096,512]{1,0:T(8,128)(2,1)}, f32[64,512]{1,0:T(8,128)S(1)}, f32[24,512]{1,0:T(8,128)S(1)}) custom-call(s32[24]{0:T(128)S(1)} %concatenate.28.info_ref, bf16[4096,512]{1,0:T(8,128)(2,1)} %get-tuple-element.132.gradient_hbm, f32[4096,512]{1,0:T(8,128)S(1)} %get-tuple-element.138.values_ref, ...), custom_call_target="tpu_custom_call" | custom-call | flops 419430400 | bytes 2097152 | tf_op jit(solution)/shard_map/pallas_call | solution.py:1111
  92.1 20.1 %shard_map.226 = (bf16[4096,512]{1,0:T(8,128)(2,1)}, f32[8,512]{1,0:T(8,128)S(1)}, bf16[4096,512]{1,0:T(8,128)(2,1)}, f32[40,512]{1,0:T(8,128)S(1)}, f32[24,512]{1,0:T(8,128)S(1)}) custom-call(s32[24]{0:T(128)S(1)} %concatenate.28.info_ref, bf16[4096,512]{1,0:T(8,128)(2,1)} %get-tuple-element.141.inner_hbm, f32[4096,512]{1,0:T(8,128)} %get-tuple-element.142.middle_hbm, ...), custom_call_target="tpu_custom_call" | custom-call | flops 6442450944 | bytes 32212254 | tf_op jit(solution)/shard_map/pallas_call | solution.py:1111
  113.1 2.9 %collective-permute-start.11 = (f32[24,512]{1,0:T(8,128)S(1)}, f32[24,512]{1,0:T(8,128)S(1)}, u32[]{:S(2)}, u32[]{:S(2)}) collective-permute-start(f32[24,512]{1,0:T(8,128)S(1)} %get-tuple-element.149.own_ref), channel_id=1, source_target_pairs={{0,3},{1,0},{2,1},{3,2},{4,7},{5,4},{6,5},{7,6},{8,11},{9,8},{10,9... | collective-permute-start | bytes 147464 | tf_op jit(solution)/shard_map/ppermute | solution.py:1153
  117.8 4.1 %collective-permute-done.9.one_ref = f32[24,512]{1,0:T(8,128)S(1)} collective-permute-done((f32[24,512]{1,0:T(8,128)S(1)}, f32[24,512]{1,0:T(8,128)S(1)}, u32[]{:S(2)}, u32[]{:S(2)}) %collective-permute-start.9) | collective-permute-done | bytes 49184 | tf_op jit(solution)/shard_map/ppermute | solution.py:1153
  121.9 9.8 %shard_map.227 = (bf16[64,512]{1,0:T(8,128)(2,1)S(1)}, f32[1024,512]{1,0:T(8,128)S(1)}, bf16[64,512]{1,0:T(8,128)(2,1)S(1)}, f32[40,512]{1,0:T(8,128)S(1)}) custom-call(s32[24]{0:T(128)S(1)} %concatenate.28.info_ref, s32[32]{0:T(128)S(1)} %copy-done.6, bf16[4096,512]{1,0:T(8,128)(2,1)} %get-tuple-element.147.inner_hbm, ...), custom_call_target="tpu_custom_call" | custom-call | flops 1073741824 | bytes 5368709 | tf_op jit(solution)/shard_map/pallas_call | solution.py:1111
  134.9 4.3 %collective-permute-done.13 = bf16[64,512]{1,0:T(8,128)(2,1)S(1)} collective-permute-done((bf16[64,512]{1,0:T(8,128)(2,1)S(1)}, bf16[64,512]{1,0:T(8,128)(2,1)S(1)}, u32[]{:S(2)}, u32[]{:S(2)}) %collective-permute-start.13) | collective-permute-done | bytes 65568 | tf_op jit(solution)/shard_map/ppermute | solution.py:1164
  140.2 4.6 %all-to-all-start.1 = ((bf16[8,128,512]{2,1,0:T(8,128)(2,1)}), bf16[8,128,512]{2,1,0:T(8,128)(2,1)S(1)}, u32[]{:S(2)}, u32[]{:S(2)}) async-start(bf16[8,128,512]{2,1,0:T(8,128)(2,1)} %bitcast.77), calls=%async_computation.1 | async-start | bytes 2097152 | tf_op jit(solution)/shard_map/all_to_all | solution.py:1449
  144.8 11.6 %shard_map.228 = (f32[768,512]{1,0:T(8,128)S(1)}, bf16[768,512]{1,0:T(8,128)(2,1)S(1)}) custom-call(s32[24]{0:T(128)S(1)} %concatenate.28.info_ref, bf16[4128,512]{1,0:T(8,128)(2,1)} %get-tuple-element.192.act_hbm, bf16[4096,512]{1,0:T(8,128)(2,1)} %get-tuple-element.156.gradient_hbm, f32[8,512]{1,0:T(8,128)S(1)} %get-tuple-element.157.edge_ref), custom_call_target="tpu_custom_call" | custom-call | flops 1000000 | bytes 5000 | tf_op jit(solution)/shard_map/pallas_call | solution.py:1111
  161.5 11.7 %shard_map.229 = (f32[768,512]{1,0:T(8,128)S(1)}, bf16[768,512]{1,0:T(8,128)(2,1)S(1)}) custom-call(s32[24]{0:T(128)S(1)} %concatenate.28.info_ref, bf16[4128,512]{1,0:T(8,128)(2,1)} %get-tuple-element.163.act_hbm, bf16[4096,512]{1,0:T(8,128)(2,1)} %get-tuple-element.165.gradient_hbm, f32[8,512]{1,0:T(8,128)S(1)} %get-tuple-element.166.edge_ref), custom_call_target="tpu_custom_call" | custom-call | flops 1000000 | bytes 5000 | tf_op jit(solution)/shard_map/pallas_call | solution.py:1111
  177.8 8.2 %collective-permute-done.14.refs_1_ = bf16[8,128,512]{2,1,0:T(8,128)(2,1)} collective-permute-done((bf16[8,128,512]{2,1,0:T(8,128)(2,1)S(1)}, bf16[8,128,512]{2,1,0:T(8,128)(2,1)}, u32[]{:S(2)}, u32[]{:S(2)}) %collective-permute-start.14) | collective-permute-done | bytes 1048608 | tf_op jit(solution)/shard_map/ppermute | solution.py:1153
  189.1 7.1 %collective-permute-done.18.refs_1_ = bf16[384,512]{1,0:T(8,128)(2,1)S(1)} collective-permute-done((bf16[384,512]{1,0:T(8,128)(2,1)S(1)}, bf16[384,512]{1,0:T(8,128)(2,1)S(1)}, u32[]{:S(2)}, u32[]{:S(2)}) %collective-permute-start.18) | collective-permute-done | bytes 393248 | tf_op jit(solution)/shard_map/ppermute | solution.py:1169
  201.6 3.1 %shard_map.232.refs_2_ = f32[16384,128]{1,0:T(8,128)S(1)} custom-call(s32[24]{0:T(128)S(1)} %concatenate.28.info_ref, s32[4096]{0:T(1024)S(1)} %bitcast.75, bf16[8,128,512]{2,1,0:T(8,128)(2,1)S(1)} %all-to-all-done.1.refs_0_, bf16[8,128,512]{2,1,0:T(8,128)(2,1)} %collective-permute-done.14.refs_1_), custom_call_target="tpu_custom_call" | custom-call | flops 1000000 | bytes 10000 | tf_op jit(solution)/shard_map/pallas_call | solution.py:1137
  207.5 2.9 %collective-permute-done.20 = bf16[192,512]{1,0:T(8,128)(2,1)S(1)} collective-permute-done((bf16[192,512]{1,0:T(8,128)(2,1)S(1)}, bf16[192,512]{1,0:T(8,128)(2,1)S(1)}, u32[]{:S(2)}, u32[]{:S(2)}) %collective-permute-start.20) | collective-permute-done | bytes 196640 | tf_op jit(solution)/shard_map/ppermute | solution.py:1169
  210.5 4.6 %collective-permute-done.17.refs_0_ = bf16[8,128,512]{2,1,0:T(8,128)(2,1)} collective-permute-done((bf16[8,128,512]{2,1,0:T(8,128)(2,1)}, bf16[8,128,512]{2,1,0:T(8,128)(2,1)}, u32[]{:S(2)}, u32[]{:S(2)}) %collective-permute-start.17) | collective-permute-done | bytes 1048608 | tf_op jit(solution)/shard_map/ppermute | solution.py:1153
  215.3 3.8 %collective-permute-start.23 = (bf16[2,48,512]{2,1,0:T(8,128)(2,1)S(1)}, bf16[2,48,512]{2,1,0:T(8,128)(2,1)S(1)}, u32[]{:S(2)}, u32[]{:S(2)}) collective-permute-start(bf16[2,48,512]{2,1,0:T(8,128)(2,1)S(1)} %get-tuple-element.212), channel_id=1, source_target_pairs={{0,3},{1,0},{2,1},{3,2},{4,7},{5,4},{6,5},{7,6},{8,11},{9,8},{10,9... | collective-permute-start | bytes 294920 | tf_op jit(solution)/shard_map/ppermute | solution.py:1153
  221.8 3.1 %collective-permute-done.24 = bf16[2,48,512]{2,1,0:T(8,128)(2,1)S(1)} collective-permute-done((bf16[2,48,512]{2,1,0:T(8,128)(2,1)S(1)}, bf16[2,48,512]{2,1,0:T(8,128)(2,1)S(1)}, u32[]{:S(2)}, u32[]{:S(2)}) %collective-permute-start.24) | collective-permute-done | bytes 98336 | tf_op jit(solution)/shard_map/ppermute | solution.py:1153
  225.8 3.9 %collective-permute-start.26 = (bf16[2,48,512]{2,1,0:T(8,128)(2,1)S(1)}, bf16[2,48,512]{2,1,0:T(8,128)(2,1)S(1)}, u32[]{:S(2)}, u32[]{:S(2)}) collective-permute-start(bf16[2,48,512]{2,1,0:T(8,128)(2,1)S(1)} %get-tuple-element.207), channel_id=1, source_target_pairs={{0,3},{1,0},{2,1},{3,2},{4,7},{5,4},{6,5},{7,6},{8,11},{9,8},{10,9... | collective-permute-start | bytes 294920 | tf_op jit(solution)/shard_map/ppermute | solution.py:1153
  231.9 3.6 %collective-permute-done.27 = bf16[2,48,512]{2,1,0:T(8,128)(2,1)S(1)} collective-permute-done((bf16[2,48,512]{2,1,0:T(8,128)(2,1)S(1)}, bf16[2,48,512]{2,1,0:T(8,128)(2,1)S(1)}, u32[]{:S(2)}, u32[]{:S(2)}) %collective-permute-start.27) | collective-permute-done | bytes 98336 | tf_op jit(solution)/shard_map/ppermute | solution.py:1153
  236.9 5.1 %collective-permute-done.30.refs_3_ = bf16[192,512]{1,0:T(8,128)(2,1)S(1)} collective-permute-done((bf16[192,512]{1,0:T(8,128)(2,1)S(1)}, bf16[192,512]{1,0:T(8,128)(2,1)S(1)}, u32[]{:S(2)}, u32[]{:S(2)}) %collective-permute-start.30) | collective-permute-done | bytes 196640 | tf_op jit(solution)/shard_map/ppermute | solution.py:1169
  245.0 12.4 %shard_map.235 = bf16[4096,512]{1,0:T(8,128)(2,1)} custom-call(s32[24]{0:T(128)S(1)} %concatenate.28.info_ref, bf16[4128,512]{1,0:T(8,128)(2,1)} %get-tuple-element.192.act_hbm, f32[4096,512]{1,0:T(8,128)} %get-tuple-element.193.values_hbm, bf16[1536,512]{1,0:T(8,128)(2,1)S(1)} %copy-done.1, bf16[1,512]{1,0:T(2,128)(2,1)S(1)} %broadcast_in_dim.54.bias_ref), custom_call_target="tpu_custom_call" | custom-call | flops 1000000 | bytes 5000 | tf_op jit(solution)/shard_map/pallas_call | solution.py:1111
  258.1 3.7 %collective-permute-done.28.refs_1_ = bf16[8,128,512]{2,1,0:T(8,128)(2,1)S(1)} collective-permute-done((bf16[8,128,512]{2,1,0:T(8,128)(2,1)}, bf16[8,128,512]{2,1,0:T(8,128)(2,1)S(1)}, u32[]{:S(2)}, u32[]{:S(2)}) %collective-permute-start.28) | collective-permute-done | bytes 1048608 | tf_op jit(solution)/shard_map/ppermute | solution.py:1153
  263.5 4.1 %shard_map.236 = f32[16384,128]{1,0:T(8,128)S(1)} custom-call(s32[24]{0:T(128)S(1)} %concatenate.28.info_ref, s32[4096]{0:T(1024)S(1)} %bitcast.76, bf16[8,128,512]{2,1,0:T(8,128)(2,1)} %collective-permute-done.17.refs_0_, bf16[8,128,512]{2,1,0:T(8,128)(2,1)S(1)} %collective-permute-done.28.refs_1_, ...), custom_call_target="tpu_custom_call", output_to_operand_aliasing={{}: (4, {})} | custom-call | flops 1000000 | bytes 10000 | tf_op jit(solution)/shard_map/pallas_call | solution.py:1137
  267.5 3.4 %copy.41 = f32[4096,512]{1,0:T(8,128)} copy(f32[4096,512]{1,0:T(8,128)S(1)} %bitcast.71) | data formatting | bytes 16777216
  271.0 4.9 %shard_map.237 = (f32[1536,512]{1,0:T(8,128)}, f32[1536,512]{1,0:T(8,128)}, f32[128,1024]{1,0:T(8,128)}, f32[1,1024]{1,0:T(1,128)}, f32[128,1024]{1,0:T(8,128)}, /*index=5*/f32[1,1024]{1,0:T(1,128)}, f32[1,512]{1,0:T(1,128)}) custom-call(s32[24]{0:T(128)S(1)} %concatenate.28.info_ref, bf16[960,512]{1,0:T(8,128)(2,1)S(1)} %get-tuple-element.197.second_ref, ...), custom_call_target="tpu_custom_call" | custom-call | flops 1000000 | bytes 5000 | tf_op jit(solution)/shard_map/pallas_call | solution.py:1111
  (160 shorter events, 62.1 us)
Async XLA Ops:
  9.9 26.4 %all-to-all-start = ((bf16[8,192,512]{2,1,0:T(8,128)(2,1)}), bf16[8,192,512]{2,1,0:T(8,128)(2,1)}, u32[]{:S(2)}, u32[]{:S(2)}) async-start(bf16[8,192,512]{2,1,0:T(8,128)(2,1)} %bitcast.15), calls=%async_computation | async-start | bytes 3145728 | tf_op jit(solution)/shard_map/all_to_all | solution.py:1271
  45.8 6.2 %collective-permute-start = (f32[24,512]{1,0:T(8,128)S(1)}, f32[24,512]{1,0:T(8,128)S(1)}, u32[]{:S(2)}, u32[]{:S(2)}) collective-permute-start(f32[24,512]{1,0:T(8,128)S(1)} %get-tuple-element.137.own_ref), channel_id=1, source_target_pairs={{0,1},{1,2},{2,3},{3,0},{4,5},{5,6},{6,7},{7,4},{8,9},{9,10},{10,1... | collective-permute-start | bytes 147464 | tf_op jit(solution)/shard_map/ppermute | solution.py:1153
  47.9 5.0 %collective-permute-start.1 = (f32[24,512]{1,0:T(8,128)S(1)}, f32[24,512]{1,0:T(8,128)S(1)}, u32[]{:S(2)}, u32[]{:S(2)}) collective-permute-start(f32[24,512]{1,0:T(8,128)S(1)} %get-tuple-element.137.own_ref), channel_id=1, source_target_pairs={{0,2},{1,3},{2,0},{3,1},{4,6},{5,7},{6,4},{7,5},{8,10},{9,11},{10,... | collective-permute-start | bytes 147464 | tf_op jit(solution)/shard_map/ppermute | solution.py:1153
  68.3 6.0 %collective-permute-start.3 = (f32[24,512]{1,0:T(8,128)S(1)}, f32[24,512]{1,0:T(8,128)S(1)}, u32[]{:S(2)}, u32[]{:S(2)}) collective-permute-start(f32[24,512]{1,0:T(8,128)S(1)} %get-tuple-element.139.own_ref), channel_id=1, source_target_pairs={{0,1},{1,2},{2,3},{3,0},{4,5},{5,6},{6,7},{7,4},{8,9},{9,10},{10,1... | collective-permute-start | bytes 147464 | tf_op jit(solution)/shard_map/ppermute | solution.py:1153
  68.8 6.5 %collective-permute-start.4 = (f32[24,512]{1,0:T(8,128)S(1)}, f32[24,512]{1,0:T(8,128)S(1)}, u32[]{:S(2)}, u32[]{:S(2)}) collective-permute-start(f32[24,512]{1,0:T(8,128)S(1)} %get-tuple-element.139.own_ref), channel_id=1, source_target_pairs={{0,2},{1,3},{2,0},{3,1},{4,6},{5,7},{6,4},{7,5},{8,10},{9,11},{10,... | collective-permute-start | bytes 147464 | tf_op jit(solution)/shard_map/ppermute | solution.py:1153
  85.0 6.0 %collective-permute-start.6 = (f32[24,512]{1,0:T(8,128)S(1)}, f32[24,512]{1,0:T(8,128)S(1)}, u32[]{:S(2)}, u32[]{:S(2)}) collective-permute-start(f32[24,512]{1,0:T(8,128)S(1)} %get-tuple-element.143.own_ref), channel_id=1, source_target_pairs={{0,1},{1,2},{2,3},{3,0},{4,5},{5,6},{6,7},{7,4},{8,9},{9,10},{10,1... | collective-permute-start | bytes 147464 | tf_op jit(solution)/shard_map/ppermute | solution.py:1153
  85.5 6.1 %collective-permute-start.7 = (f32[24,512]{1,0:T(8,128)S(1)}, f32[24,512]{1,0:T(8,128)S(1)}, u32[]{:S(2)}, u32[]{:S(2)}) collective-permute-start(f32[24,512]{1,0:T(8,128)S(1)} %get-tuple-element.143.own_ref), channel_id=1, source_target_pairs={{0,2},{1,3},{2,0},{3,1},{4,6},{5,7},{6,4},{7,5},{8,10},{9,11},{10,... | collective-permute-start | bytes 147464 | tf_op jit(solution)/shard_map/ppermute | solution.py:1153
  87.9 4.1 %collective-permute-start.8 = (f32[24,512]{1,0:T(8,128)S(1)}, f32[24,512]{1,0:T(8,128)S(1)}, u32[]{:S(2)}, u32[]{:S(2)}) collective-permute-start(f32[24,512]{1,0:T(8,128)S(1)} %get-tuple-element.143.own_ref), channel_id=1, source_target_pairs={{0,3},{1,0},{2,1},{3,2},{4,7},{5,4},{6,5},{7,6},{8,11},{9,8},{10,9... | collective-permute-start | bytes 147464 | tf_op jit(solution)/shard_map/ppermute | solution.py:1153
  112.1 5.1 %collective-permute-start.10 = (f32[24,512]{1,0:T(8,128)S(1)}, f32[24,512]{1,0:T(8,128)S(1)}, u32[]{:S(2)}, u32[]{:S(2)}) collective-permute-start(f32[24,512]{1,0:T(8,128)S(1)} %get-tuple-element.149.own_ref), channel_id=1, source_target_pairs={{0,2},{1,3},{2,0},{3,1},{4,6},{5,7},{6,4},{7,5},{8,10},{9,11},{10,... | collective-permute-start | bytes 147464 | tf_op jit(solution)/shard_map/ppermute | solution.py:1153
  113.1 4.7 %collective-permute-start.11 = (f32[24,512]{1,0:T(8,128)S(1)}, f32[24,512]{1,0:T(8,128)S(1)}, u32[]{:S(2)}, u32[]{:S(2)}) collective-permute-start(f32[24,512]{1,0:T(8,128)S(1)} %get-tuple-element.149.own_ref), channel_id=1, source_target_pairs={{0,3},{1,0},{2,1},{3,2},{4,7},{5,4},{6,5},{7,6},{8,11},{9,8},{10,9... | collective-permute-start | bytes 147464 | tf_op jit(solution)/shard_map/ppermute | solution.py:1153
  116.0 5.9 %collective-permute-start.9 = (f32[24,512]{1,0:T(8,128)S(1)}, f32[24,512]{1,0:T(8,128)S(1)}, u32[]{:S(2)}, u32[]{:S(2)}) collective-permute-start(f32[24,512]{1,0:T(8,128)S(1)} %get-tuple-element.149.own_ref), channel_id=1, source_target_pairs={{0,1},{1,2},{2,3},{3,0},{4,5},{5,6},{6,7},{7,4},{8,9},{9,10},{10,1... | collective-permute-start | bytes 147464 | tf_op jit(solution)/shard_map/ppermute | solution.py:1153
  133.0 6.2 %collective-permute-start.13 = (bf16[64,512]{1,0:T(8,128)(2,1)S(1)}, bf16[64,512]{1,0:T(8,128)(2,1)S(1)}, u32[]{:S(2)}, u32[]{:S(2)}) collective-permute-start(bf16[64,512]{1,0:T(8,128)(2,1)S(1)} %get-tuple-element.152), channel_id=1, source_target_pairs={{1,0},{2,1},{3,2},{5,4},{6,5},{7,6},{9,8},{10,9},{11,10},{13,12},{... | collective-permute-start | bytes 196616 | tf_op jit(solution)/shard_map/ppermute | solution.py:1164
  140.2 20.0 %all-to-all-start.1 = ((bf16[8,128,512]{2,1,0:T(8,128)(2,1)}), bf16[8,128,512]{2,1,0:T(8,128)(2,1)S(1)}, u32[]{:S(2)}, u32[]{:S(2)}) async-start(bf16[8,128,512]{2,1,0:T(8,128)(2,1)} %bitcast.77), calls=%async_computation.1 | async-start | bytes 2097152 | tf_op jit(solution)/shard_map/all_to_all | solution.py:1449
  160.2 25.7 %collective-permute-start.14 = (bf16[8,128,512]{2,1,0:T(8,128)(2,1)S(1)}, bf16[8,128,512]{2,1,0:T(8,128)(2,1)}, u32[]{:S(2)}, u32[]{:S(2)}) collective-permute-start(bf16[8,128,512]{2,1,0:T(8,128)(2,1)S(1)} %all-to-all-done.1.refs_0_), channel_id=1, source_target_pairs={{0,1},{1,2},{2,3},{3,0},{4,5},{5,6},{6,7},{7,4},{8,9},{9,10},{10,1... | collective-permute-start | bytes 3145736 | tf_op jit(solution)/shard_map/ppermute | solution.py:1153
  186.0 10.2 %collective-permute-start.18 = (bf16[384,512]{1,0:T(8,128)(2,1)S(1)}, bf16[384,512]{1,0:T(8,128)(2,1)S(1)}, u32[]{:S(2)}, u32[]{:S(2)}) collective-permute-start(bf16[384,512]{1,0:T(8,128)(2,1)S(1)} %get-tuple-element.175), channel_id=1, source_target_pairs={{0,8},{4,12},{8,0},{12,4},{16,24},{20,28},{24,16},{28,20},{1,9},{5... | collective-permute-start | bytes 1179656 | tf_op jit(solution)/shard_map/ppermute | solution.py:1169
  187.8 9.8 %collective-permute-start.19 = (bf16[384,512]{1,0:T(8,128)(2,1)S(1)}, bf16[384,512]{1,0:T(8,128)(2,1)S(1)}, u32[]{:S(2)}, u32[]{:S(2)}) collective-permute-start(bf16[384,512]{1,0:T(8,128)(2,1)S(1)} %get-tuple-element.177), channel_id=1, source_target_pairs={{0,16},{4,20},{8,24},{12,28},{16,0},{20,4},{24,8},{28,12},{1,17},{... | collective-permute-start | bytes 1179656 | tf_op jit(solution)/shard_map/ppermute | solution.py:1169
  189.1 26.0 %collective-permute-start.17 = (bf16[8,128,512]{2,1,0:T(8,128)(2,1)}, bf16[8,128,512]{2,1,0:T(8,128)(2,1)}, u32[]{:S(2)}, u32[]{:S(2)}) collective-permute-start(bf16[8,128,512]{2,1,0:T(8,128)(2,1)} %collective-permute-done.14.refs_1_), channel_id=1, source_target_pairs={{0,1},{1,2},{2,3},{3,0},{4,5},{5,6},{6,7},{7,4},{8,9},{9,10},{10,1... | collective-permute-start | bytes 3145736 | tf_op jit(solution)/shard_map/ppermute | solution.py:1153
  200.5 6.0 %collective-permute-start.21 = (bf16[192,512]{1,0:T(8,128)(2,1)}, bf16[192,512]{1,0:T(8,128)(2,1)}, u32[]{:S(2)}, u32[]{:S(2)}) collective-permute-start(bf16[192,512]{1,0:T(8,128)(2,1)} %get-tuple-element.181), channel_id=1, source_target_pairs={{0,8},{4,12},{8,0},{12,4},{16,24},{20,28},{24,16},{28,20},{1,9},{5... | collective-permute-start | bytes 589832 | tf_op jit(solution)/shard_map/ppermute | solution.py:1169
  204.7 5.7 %collective-permute-start.20 = (bf16[192,512]{1,0:T(8,128)(2,1)S(1)}, bf16[192,512]{1,0:T(8,128)(2,1)S(1)}, u32[]{:S(2)}, u32[]{:S(2)}) collective-permute-start(bf16[192,512]{1,0:T(8,128)(2,1)S(1)} %copy-done.14), channel_id=1, source_target_pairs={{0,16},{4,20},{8,24},{12,28},{16,0},{20,4},{24,8},{28,12},{1,17},{... | collective-permute-start | bytes 589832 | tf_op jit(solution)/shard_map/ppermute | solution.py:1169
  215.2 6.5 %collective-permute-start.22 = (bf16[2,48,512]{2,1,0:T(8,128)(2,1)S(1)}, bf16[2,48,512]{2,1,0:T(8,128)(2,1)S(1)}, u32[]{:S(2)}, u32[]{:S(2)}) collective-permute-start(bf16[2,48,512]{2,1,0:T(8,128)(2,1)S(1)} %get-tuple-element.210), channel_id=1, source_target_pairs={{0,1},{1,2},{2,3},{3,0},{4,5},{5,6},{6,7},{7,4},{8,9},{9,10},{10,1... | collective-permute-start | bytes 294920 | tf_op jit(solution)/shard_map/ppermute | solution.py:1153
  215.3 6.5 %collective-permute-start.23 = (bf16[2,48,512]{2,1,0:T(8,128)(2,1)S(1)}, bf16[2,48,512]{2,1,0:T(8,128)(2,1)S(1)}, u32[]{:S(2)}, u32[]{:S(2)}) collective-permute-start(bf16[2,48,512]{2,1,0:T(8,128)(2,1)S(1)} %get-tuple-element.212), channel_id=1, source_target_pairs={{0,3},{1,0},{2,1},{3,2},{4,7},{5,4},{6,5},{7,6},{8,11},{9,8},{10,9... | collective-permute-start | bytes 294920 | tf_op jit(solution)/shard_map/ppermute | solution.py:1153
  219.1 5.8 %collective-permute-start.24 = (bf16[2,48,512]{2,1,0:T(8,128)(2,1)S(1)}, bf16[2,48,512]{2,1,0:T(8,128)(2,1)S(1)}, u32[]{:S(2)}, u32[]{:S(2)}) collective-permute-start(bf16[2,48,512]{2,1,0:T(8,128)(2,1)S(1)} %get-tuple-element.211), channel_id=1, source_target_pairs={{0,2},{1,3},{2,0},{3,1},{4,6},{5,7},{6,4},{7,5},{8,10},{9,11},{10,... | collective-permute-start | bytes 294920 | tf_op jit(solution)/shard_map/ppermute | solution.py:1153
  225.0 6.6 %collective-permute-start.25 = (bf16[2,48,512]{2,1,0:T(8,128)(2,1)S(1)}, bf16[2,48,512]{2,1,0:T(8,128)(2,1)S(1)}, u32[]{:S(2)}, u32[]{:S(2)}) collective-permute-start(bf16[2,48,512]{2,1,0:T(8,128)(2,1)S(1)} %get-tuple-element.207), channel_id=1, source_target_pairs={{0,1},{1,2},{2,3},{3,0},{4,5},{5,6},{6,7},{7,4},{8,9},{9,10},{10,1... | collective-permute-start | bytes 294920 | tf_op jit(solution)/shard_map/ppermute | solution.py:1153
  225.8 6.1 %collective-permute-start.26 = (bf16[2,48,512]{2,1,0:T(8,128)(2,1)S(1)}, bf16[2,48,512]{2,1,0:T(8,128)(2,1)S(1)}, u32[]{:S(2)}, u32[]{:S(2)}) collective-permute-start(bf16[2,48,512]{2,1,0:T(8,128)(2,1)S(1)} %get-tuple-element.207), channel_id=1, source_target_pairs={{0,3},{1,0},{2,1},{3,2},{4,7},{5,4},{6,5},{7,6},{8,11},{9,8},{10,9... | collective-permute-start | bytes 294920 | tf_op jit(solution)/shard_map/ppermute | solution.py:1153
  229.7 5.9 %collective-permute-start.27 = (bf16[2,48,512]{2,1,0:T(8,128)(2,1)S(1)}, bf16[2,48,512]{2,1,0:T(8,128)(2,1)S(1)}, u32[]{:S(2)}, u32[]{:S(2)}) collective-permute-start(bf16[2,48,512]{2,1,0:T(8,128)(2,1)S(1)} %get-tuple-element.207), channel_id=1, source_target_pairs={{0,2},{1,3},{2,0},{3,1},{4,6},{5,7},{6,4},{7,5},{8,10},{9,11},{10,... | collective-permute-start | bytes 294920 | tf_op jit(solution)/shard_map/ppermute | solution.py:1153
  235.6 26.1 %collective-permute-start.28 = (bf16[8,128,512]{2,1,0:T(8,128)(2,1)}, bf16[8,128,512]{2,1,0:T(8,128)(2,1)S(1)}, u32[]{:S(2)}, u32[]{:S(2)}) collective-permute-start(bf16[8,128,512]{2,1,0:T(8,128)(2,1)} %collective-permute-done.17.refs_0_), channel_id=1, source_target_pairs={{0,1},{1,2},{2,3},{3,0},{4,5},{5,6},{6,7},{7,4},{8,9},{9,10},{10,1... | collective-permute-start | bytes 3145736 | tf_op jit(solution)/shard_map/ppermute | solution.py:1153
  236.0 6.6 %collective-permute-start.29 = (bf16[240,512]{1,0:T(8,128)(2,1)S(1)}, bf16[240,512]{1,0:T(8,128)(2,1)S(1)}, u32[]{:S(2)}, u32[]{:S(2)}) collective-permute-start(bf16[240,512]{1,0:T(8,128)(2,1)S(1)} %constant_dynamic-update-slice_fusion.refs_0_), channel_id=1, source_target_pairs={{0,8},{4,12},{8,0},{12,4},{16,24},{20,28},{24,16},{28,20},{1,9},{5... | collective-permute-start | bytes 737288 | tf_op jit(solution)/shard_map/ppermute | solution.py:1169
  236.3 5.7 %collective-permute-start.30 = (bf16[192,512]{1,0:T(8,128)(2,1)S(1)}, bf16[192,512]{1,0:T(8,128)(2,1)S(1)}, u32[]{:S(2)}, u32[]{:S(2)}) collective-permute-start(bf16[192,512]{1,0:T(8,128)(2,1)S(1)} %slice_bitcast_fusion.refs_2_), channel_id=1, source_target_pairs={{0,16},{4,20},{8,24},{12,28},{16,0},{20,4},{24,8},{28,12},{1,17},{... | collective-permute-start | bytes 589832 | tf_op jit(solution)/shard_map/ppermute | solution.py:1169
  243.2 14.1 %collective-permute-start.31 = (bf16[480,512]{1,0:T(8,128)(2,1)S(1)}, bf16[480,512]{1,0:T(8,128)(2,1)S(1)}, u32[]{:S(2)}, u32[]{:S(2)}) collective-permute-start(bf16[480,512]{1,0:T(8,128)(2,1)S(1)} %get-tuple-element.188.refs_0_), channel_id=1, source_target_pairs={{0,16},{4,20},{8,24},{12,28},{16,0},{20,4},{24,8},{28,12},{1,17},{... | collective-permute-start | bytes 1474568 | tf_op jit(solution)/shard_map/ppermute | solution.py:1169
  243.4 14.0 %collective-permute-start.32 = (bf16[384,512]{1,0:T(8,128)(2,1)S(1)}, bf16[384,512]{1,0:T(8,128)(2,1)S(1)}, u32[]{:S(2)}, u32[]{:S(2)}) collective-permute-start(bf16[384,512]{1,0:T(8,128)(2,1)S(1)} %get-tuple-element.189.refs_2_), channel_id=1, source_target_pairs={{0,8},{4,12},{8,0},{12,4},{16,24},{20,28},{24,16},{28,20},{1,9},{5... | collective-permute-start | bytes 1179656 | tf_op jit(solution)/shard_map/ppermute | solution.py:1169
  261.7 9.2 %collective-permute-start.33 = (bf16[960,512]{1,0:T(8,128)(2,1)S(1)}, bf16[960,512]{1,0:T(8,128)(2,1)S(1)}, u32[]{:S(2)}, u32[]{:S(2)}) collective-permute-start(bf16[960,512]{1,0:T(8,128)(2,1)S(1)} %get-tuple-element.197.second_ref), channel_id=1, source_target_pairs={{0,4},{4,0},{8,12},{12,8},{16,20},{20,16},{24,28},{28,24},{1,5},{5... | collective-permute-start | bytes 2949128 | tf_op jit(solution)/shard_map/ppermute | solution.py:1169
  261.7 9.2 %collective-permute-start.34 = (bf16[768,512]{1,0:T(8,128)(2,1)S(1)}, bf16[768,512]{1,0:T(8,128)(2,1)S(1)}, u32[]{:S(2)}, u32[]{:S(2)}) collective-permute-start(bf16[768,512]{1,0:T(8,128)(2,1)S(1)} %get-tuple-element.198.first_ref), channel_id=1, source_target_pairs={{0,4},{4,0},{8,12},{12,8},{16,20},{20,16},{24,28},{28,24},{1,5},{5... | collective-permute-start | bytes 2359304 | tf_op jit(solution)/shard_map/ppermute | solution.py:1169
  (31 other events, 315.0 us)

commit v6 on v5

--- a/solution.py
+++ b/solution.py
@@ -567,23 +567,20 @@
     params_ref,
     added_ref,
     act_hbm,
-    inner_hbm,
+    inner_ref,
     coef_ref,
     stat_ref,
     acc_ref,
     gradient_ref,
     act_ref,
-    inner_ref,
     gradient_sems,
     act_sems,
     edge_sems,
-    inner_sems,
 ):
     frames, channels = values_ref.shape
     gradient_in = Stream(gradient_hbm, gradient_ref, gradient_sems)
     outward = [
         Stream(act_ref, act_hbm, act_sems, PAD, PAD),
-        Stream(inner_ref, inner_hbm, inner_sems),
     ]
     gradient_in.start()
     ends = read_ends(info_ref)
@@ -841,7 +838,7 @@
 
 def first_back_kernel(
     info_ref,
-    inner_hbm,
+    inner_ref,
     middle_hbm,
     own_ref,
     one_ref,
@@ -854,29 +851,23 @@
     weight_ref,
     gradient_hbm,
     edge_ref,
-    out_hbm,
+    out_ref,
     back_ref,
     stat_ref,
     acc_ref,
     full_ref,
-    inner_ref,
     middle_ref,
     unit_one_ref,
-    out_ref,
     gradient_ref,
-    inner_sems,
     two_sems,
     one_sems,
-    out_sems,
     gradient_sems,
 ):
     frames, channels = unit_one_ref.shape
     early = [
-        Stream(inner_hbm, inner_ref, inner_sems),
         Stream(middle_hbm, middle_ref, two_sems),
     ]
     late = Stream(unit_one_hbm, unit_one_ref, one_sems)
-    outward = Stream(out_ref, out_hbm, out_sems)
     gradient_out = Stream(gradient_ref, gradient_hbm, gradient_sems, PAD)
     for index in range(frames // ROWS):
         for stream in (*early, late):
@@ -964,18 +955,16 @@
         before, here, after = taps_of(gradient_ref, ends, start, base)
         full_ref[...] = convolved_back((after, here, before), weight_ref)
         for_blocks(0, ROWS, BLOCK, lambda inside: slope_step(start + inside, inside))
-        outward.tile(i).start()
 
     for_tiles(frames, conv)
     finish_stats(acc_ref, stat_ref)
-    outward.finish()
     gradient_out.finish()
 
 
 def buffer_gradient_kernel(
     info_ref,
     offset_ref,
-    inner_hbm,
+    inner_ref,
     unit_hbm,
     cot_hbm,
     wide_hbm,
@@ -991,18 +980,15 @@
     back_ref,
     up_ref,
     total_ref,
-    inner_ref,
     unit_ref,
     cot_ref,
     wide_ref,
-    inner_sems,
     unit_sems,
     cot_sems,
     wide_sems,
 ):
     frames, channels = unit_ref.shape
     streams = [
-        Stream(inner_hbm, inner_ref, inner_sems),
         Stream(unit_hbm, unit_ref, unit_sems),
         Stream(cot_hbm, cot_ref, cot_sems),
         Stream(wide_hbm, wide_ref, wide_sems),
@@ -1359,7 +1345,7 @@
         ),
         (
             (padded, BF16, HB),
-            (full, BF16, HB),
+            (full, BF16, VM),
             (coef_shape, F32, VM),
             (stats_shape, F32, VM),
         ),
@@ -1367,11 +1353,9 @@
             small_acc,
             (full, BF16),
             (padded, BF16),
-            (full, BF16),
             tiles_of,
             tiles_of,
             2,
-            tiles_of,
         ],
         2 * frames * channels * 100,
         28,
@@ -1381,7 +1365,7 @@
         first_back_kernel,
         (
             (info, SM),
-            (inner_two, HB),
+            (inner_two, VM),
             (middle_far, HB),
             *((one, VM) for one in (stat_three, *others_three)),
             (inverse, VM),
@@ -1393,19 +1377,17 @@
         (
             (full, BF16, HB),
             ((8, channels), F32, VM),
-            (full, BF16, HB),
+            (full, BF16, VM),
             ((40, channels), F32, VM),
             (stats_shape, F32, VM),
         ),
         [
             small_acc,
             ((ROWS, channels), F32),
-            (full, BF16),
             (full, F32),
             (full, BF16),
-            (full, BF16),
             (padded, BF16),
-            *([tiles_of] * 5),
+            *([tiles_of] * 3),
         ],
         conv_flops,
         40,
@@ -1416,7 +1398,7 @@
         (
             (info, SM),
             (tile_offsets, SM),
-            (inner_one, HB),
+            (inner_one, VM),
             (unit_one, HB),
             (cotangent, HB),
             (wide, HB),
@@ -1433,9 +1415,9 @@
         [
             (full, BF16),
             ((local_rows + WIDE, channels), F32),
-            *([(full, BF16)] * 3),
+            *([(full, BF16)] * 2),
             ((frames, WIDE), BF16),
-            *([tiles_of] * 4),
+            *([tiles_of] * 3),
         ],
         2 * frames * WIDE * channels,
         36,

time: 276 us -> 273 us (0.989)
    unnamed x59 -> x57, local copies, waits for them, and re-layouts: 8.49 us -> 7.02 us
where the time goes in v6:
time: 273 us
  Pallas kernels  123 us (45%)
  waiting for transfers between devices  76.8 us (28%)
  starting transfers between devices  48.1 us (18%)
  local copies, waits for them, and re-layouts  17.3 us (6%)
  other arithmetic  4.77 us (2%)
    pallas_call x14, Pallas kernels, call(): pl.pallas_call(kernel, in_specs=[spec for _, spec in inputs], out_specs=t...  116 us
    ppermute x21, waiting for transfers between devices, shifted(): lax.ppermute(values, axis, [(i, (i + step) % devices) for i in range(devi...  43.3 us
    ppermute x21, starting transfers between devices, shifted(): lax.ppermute(values, axis, [(i, (i + step) % devices) for i in range(devi...  27.1 us
    ppermute x12, waiting for transfers between devices, swapped(): lax.ppermute(values, 'seq', [(i, i ^ 1 << bit) for i in range(devices)])  20.3 us
    ppermute x12, starting transfers between devices, swapped(): lax.ppermute(values, 'seq', [(i, i ^ 1 << bit) for i in range(devices)])  8.65 us
    gather x1, local copies, waits for them, and re-layouts, on_device(): outgoing = jnp.take(phonemes, mine.reshape(-1), axis=0, mode='clip')  8.21 us
    pallas_call x2, Pallas kernels, scattered(): pl.pallas_call(functools.partial(scatter_kernel, places, copies), in_spec...  7.14 us
    unnamed x57, local copies, waits for them, and re-layouts  7.02 us
  transfers between devices with their start and end apart: 37, of which 32 were waited for; matrix products, arithmetic and copies ran while one was open for 3% of the time, Pallas kernels for 22%

profile of v6, /device:TPU:0, one launch (start us, length us, event | category | flops | bytes accessed | tf_op | source)
XLA Modules:
  0.0 272.6 jit_solution(7238173415132411339)
XLA Ops:
  1.7 8.2 %gather_fusion = bf16[1536,512]{1,0:T(8,128)(2,1)} fusion(bf16[4096,512]{1,0:T(8,128)(2,1)} %param.23, s32[2048]{0:T(1024)S(1)} %pad_clamp_fusion), kind=kCustom, calls=%fused_computation | custom fusion | bytes 3151872 | tf_op jit(solution)/shard_map/jit(_take)/gather | solution.py:1256
  9.9 5.3 %all-to-all-start = ((bf16[8,192,512]{2,1,0:T(8,128)(2,1)}), bf16[8,192,512]{2,1,0:T(8,128)(2,1)}, u32[]{:S(2)}, u32[]{:S(2)}) async-start(bf16[8,192,512]{2,1,0:T(8,128)(2,1)} %bitcast.15), calls=%async_computation | async-start | bytes 3145728 | tf_op jit(solution)/shard_map/all_to_all | solution.py:1257
  16.6 12.9 %shard_map.222 = (bf16[4096,512]{1,0:T(8,128)(2,1)}, bf16[4096,512]{1,0:T(8,128)(2,1)}, f32[16,512]{1,0:T(8,128)S(1)}) custom-call(s32[24]{0:T(128)S(1)} %concatenate.28.info_ref, bf16[4096,512]{1,0:T(8,128)(2,1)} %cot_hbm.3, bf16[1536,512]{1,0:T(8,128)(2,1)S(1)} %bitcast.73), custom_call_target="tpu_custom_call" | custom-call | flops 6442450944 | bytes 32212254 | tf_op jit(solution)/shard_map/pallas_call | solution.py:1097
  29.6 6.8 %all-to-all-done.rows_ref = bf16[8,192,512]{2,1,0:T(8,128)(2,1)} async-done(((bf16[8,192,512]{2,1,0:T(8,128)(2,1)}), bf16[8,192,512]{2,1,0:T(8,128)(2,1)}, u32[]{:S(2)}, u32[]{:S(2)}) %all-to-all-start) | async-done | bytes 1572896 | tf_op jit(solution)/shard_map/all_to_all | solution.py:1257
  36.4 8.7 %shard_map.223 = (f32[4096,512]{1,0:T(8,128)S(1)}, f32[4096,512]{1,0:T(8,128)}, bf16[4096,256]{1,0:T(8,128)(2,1)}, f32[24,512]{1,0:T(8,128)S(1)}) custom-call(s32[24]{0:T(128)S(1)} %concatenate.28.info_ref, s32[32]{0:T(128)S(1)} %copy-done.6, bf16[8,192,512]{2,1,0:T(8,128)(2,1)} %all-to-all-done.rows_ref, bf16[4096,128]{1,0:T(8,128)(2,1)} %align_hbm.1, ...), custom_call_target="tpu_custom_call" | custom-call | flops 1073741824 | bytes 5368709 | tf_op jit(solution)/shard_map/pallas_call | solution.py:1097
  47.2 2.6 collective-permute-start.1
  54.0 13.6 %shard_map.224 = (bf16[4128,512]{1,0:T(8,128)(2,1)}, f32[4096,512]{1,0:T(8,128)S(1)}, f32[4096,512]{1,0:T(8,128)}, bf16[4096,512]{1,0:T(8,128)(2,1)}, f32[64,512...) custom-call(s32[24]{0:T(128)S(1)} %concatenate.28.info_ref, ...), custom_call_target="tpu_custom_call" | custom-call | flops 6442450944 | bytes 32212254 | tf_op jit(solution)/shard_map/pallas_call | solution.py:1097
  68.1 3.5 %collective-permute-start.4 = (f32[24,512]{1,0:T(8,128)S(1)}, f32[24,512]{1,0:T(8,128)S(1)}, u32[]{:S(2)}, u32[]{:S(2)}) collective-permute-start(f32[24,512]{1,0:T(8,128)S(1)} %get-tuple-element.139.own_ref), channel_id=1, source_target_pairs={{0,2},{1,3},{2,0},{3,1},{4,6},{5,7},{6,4},{7,5},{8,10},{9,11},{10,... | collective-permute-start | bytes 147464 | tf_op jit(solution)/shard_map/ppermute | solution.py:1139
  75.6 8.1 %shard_map.225 = (bf16[4128,512]{1,0:T(8,128)(2,1)}, bf16[4096,512]{1,0:T(8,128)(2,1)S(1)}, f32[64,512]{1,0:T(8,128)S(1)}, f32[24,512]{1,0:T(8,128)S(1)}) custom-call(s32[24]{0:T(128)S(1)} %concatenate.28.info_ref, bf16[4096,512]{1,0:T(8,128)(2,1)} %get-tuple-element.132.gradient_hbm, f32[4096,512]{1,0:T(8,128)S(1)} %get-tuple-element.138.values_ref, ...), custom_call_target="tpu_custom_call" | custom-call | flops 419430400 | bytes 2097152 | tf_op jit(solution)/shard_map/pallas_call | solution.py:1097
  90.8 18.4 %shard_map.226 = (bf16[4096,512]{1,0:T(8,128)(2,1)}, f32[8,512]{1,0:T(8,128)S(1)}, bf16[4096,512]{1,0:T(8,128)(2,1)S(1)}, f32[40,512]{1,0:T(8,128)S(1)}, f32[24,512]{1,0:T(8,128)S(1)}) custom-call(s32[24]{0:T(128)S(1)} %concatenate.28.info_ref, bf16[4096,512]{1,0:T(8,128)(2,1)S(1)} %get-tuple-element.141.inner_ref, ...), custom_call_target="tpu_custom_call" | custom-call | flops 6442450944 | bytes 32212254 | tf_op jit(solution)/shard_map/pallas_call | solution.py:1097
  110.3 2.9 %collective-permute-start.11 = (f32[24,512]{1,0:T(8,128)S(1)}, f32[24,512]{1,0:T(8,128)S(1)}, u32[]{:S(2)}, u32[]{:S(2)}) collective-permute-start(f32[24,512]{1,0:T(8,128)S(1)} %get-tuple-element.149.own_ref), channel_id=1, source_target_pairs={{0,3},{1,0},{2,1},{3,2},{4,7},{5,4},{6,5},{7,6},{8,11},{9,8},{10,9... | collective-permute-start | bytes 147464 | tf_op jit(solution)/shard_map/ppermute | solution.py:1139
  114.9 4.1 %collective-permute-done.9.one_ref = f32[24,512]{1,0:T(8,128)S(1)} collective-permute-done((f32[24,512]{1,0:T(8,128)S(1)}, f32[24,512]{1,0:T(8,128)S(1)}, u32[]{:S(2)}, u32[]{:S(2)}) %collective-permute-start.9) | collective-permute-done | bytes 49184 | tf_op jit(solution)/shard_map/ppermute | solution.py:1139
  119.1 9.5 %shard_map.227 = (bf16[64,512]{1,0:T(8,128)(2,1)S(1)}, f32[1024,512]{1,0:T(8,128)S(1)}, bf16[64,512]{1,0:T(8,128)(2,1)S(1)}, f32[40,512]{1,0:T(8,128)S(1)}) custom-call(s32[24]{0:T(128)S(1)} %concatenate.28.info_ref, s32[32]{0:T(128)S(1)} %copy-done.6, bf16[4096,512]{1,0:T(8,128)(2,1)S(1)} %get-tuple-element.147.inner_ref, ...), custom_call_target="tpu_custom_call" | custom-call | flops 1073741824 | bytes 5368709 | tf_op jit(solution)/shard_map/pallas_call | solution.py:1097
  131.7 4.3 %collective-permute-done.13 = bf16[64,512]{1,0:T(8,128)(2,1)S(1)} collective-permute-done((bf16[64,512]{1,0:T(8,128)(2,1)S(1)}, bf16[64,512]{1,0:T(8,128)(2,1)S(1)}, u32[]{:S(2)}, u32[]{:S(2)}) %collective-permute-start.13) | collective-permute-done | bytes 65568 | tf_op jit(solution)/shard_map/ppermute | solution.py:1150
  137.1 4.5 %all-to-all-start.1 = ((bf16[8,128,512]{2,1,0:T(8,128)(2,1)}), bf16[8,128,512]{2,1,0:T(8,128)(2,1)S(1)}, u32[]{:S(2)}, u32[]{:S(2)}) async-start(bf16[8,128,512]{2,1,0:T(8,128)(2,1)} %bitcast.77), calls=%async_computation.1 | async-start | bytes 2097152 | tf_op jit(solution)/shard_map/all_to_all | solution.py:1431
  141.6 11.6 %shard_map.228 = (f32[768,512]{1,0:T(8,128)S(1)}, bf16[768,512]{1,0:T(8,128)(2,1)S(1)}) custom-call(s32[24]{0:T(128)S(1)} %concatenate.28.info_ref, bf16[4128,512]{1,0:T(8,128)(2,1)} %get-tuple-element.192.act_hbm, bf16[4096,512]{1,0:T(8,128)(2,1)} %get-tuple-element.156.gradient_hbm, f32[8,512]{1,0:T(8,128)S(1)} %get-tuple-element.157.edge_ref), custom_call_target="tpu_custom_call" | custom-call | flops 1000000 | bytes 5000 | tf_op jit(solution)/shard_map/pallas_call | solution.py:1097
  158.2 11.7 %shard_map.229 = (f32[768,512]{1,0:T(8,128)S(1)}, bf16[768,512]{1,0:T(8,128)(2,1)S(1)}) custom-call(s32[24]{0:T(128)S(1)} %concatenate.28.info_ref, bf16[4128,512]{1,0:T(8,128)(2,1)} %get-tuple-element.163.act_hbm, bf16[4096,512]{1,0:T(8,128)(2,1)} %get-tuple-element.165.gradient_hbm, f32[8,512]{1,0:T(8,128)S(1)} %get-tuple-element.166.edge_ref), custom_call_target="tpu_custom_call" | custom-call | flops 1000000 | bytes 5000 | tf_op jit(solution)/shard_map/pallas_call | solution.py:1097
  174.5 8.2 %collective-permute-done.14.refs_1_ = bf16[8,128,512]{2,1,0:T(8,128)(2,1)} collective-permute-done((bf16[8,128,512]{2,1,0:T(8,128)(2,1)S(1)}, bf16[8,128,512]{2,1,0:T(8,128)(2,1)}, u32[]{:S(2)}, u32[]{:S(2)}) %collective-permute-start.14) | collective-permute-done | bytes 1048608 | tf_op jit(solution)/shard_map/ppermute | solution.py:1139
  185.8 7.0 %collective-permute-done.18.refs_1_ = bf16[384,512]{1,0:T(8,128)(2,1)S(1)} collective-permute-done((bf16[384,512]{1,0:T(8,128)(2,1)S(1)}, bf16[384,512]{1,0:T(8,128)(2,1)S(1)}, u32[]{:S(2)}, u32[]{:S(2)}) %collective-permute-start.18) | collective-permute-done | bytes 393248 | tf_op jit(solution)/shard_map/ppermute | solution.py:1155
  198.3 3.1 %shard_map.232.refs_2_ = f32[16384,128]{1,0:T(8,128)S(1)} custom-call(s32[24]{0:T(128)S(1)} %concatenate.28.info_ref, s32[4096]{0:T(1024)S(1)} %bitcast.75, bf16[8,128,512]{2,1,0:T(8,128)(2,1)S(1)} %all-to-all-done.1.refs_0_, bf16[8,128,512]{2,1,0:T(8,128)(2,1)} %collective-permute-done.14.refs_1_), custom_call_target="tpu_custom_call" | custom-call | flops 1000000 | bytes 10000 | tf_op jit(solution)/shard_map/pallas_call | solution.py:1123
  204.2 2.9 %collective-permute-done.20 = bf16[192,512]{1,0:T(8,128)(2,1)S(1)} collective-permute-done((bf16[192,512]{1,0:T(8,128)(2,1)S(1)}, bf16[192,512]{1,0:T(8,128)(2,1)S(1)}, u32[]{:S(2)}, u32[]{:S(2)}) %collective-permute-start.20) | collective-permute-done | bytes 196640 | tf_op jit(solution)/shard_map/ppermute | solution.py:1155
  207.2 4.7 %collective-permute-done.17.refs_0_ = bf16[8,128,512]{2,1,0:T(8,128)(2,1)} collective-permute-done((bf16[8,128,512]{2,1,0:T(8,128)(2,1)}, bf16[8,128,512]{2,1,0:T(8,128)(2,1)}, u32[]{:S(2)}, u32[]{:S(2)}) %collective-permute-start.17) | collective-permute-done | bytes 1048608 | tf_op jit(solution)/shard_map/ppermute | solution.py:1139
  212.0 3.8 %collective-permute-start.23 = (bf16[2,48,512]{2,1,0:T(8,128)(2,1)S(1)}, bf16[2,48,512]{2,1,0:T(8,128)(2,1)S(1)}, u32[]{:S(2)}, u32[]{:S(2)}) collective-permute-start(bf16[2,48,512]{2,1,0:T(8,128)(2,1)S(1)} %get-tuple-element.212), channel_id=1, source_target_pairs={{0,3},{1,0},{2,1},{3,2},{4,7},{5,4},{6,5},{7,6},{8,11},{9,8},{10,9... | collective-permute-start | bytes 294920 | tf_op jit(solution)/shard_map/ppermute | solution.py:1139
  218.5 3.1 %collective-permute-done.24 = bf16[2,48,512]{2,1,0:T(8,128)(2,1)S(1)} collective-permute-done((bf16[2,48,512]{2,1,0:T(8,128)(2,1)S(1)}, bf16[2,48,512]{2,1,0:T(8,128)(2,1)S(1)}, u32[]{:S(2)}, u32[]{:S(2)}) %collective-permute-start.24) | collective-permute-done | bytes 98336 | tf_op jit(solution)/shard_map/ppermute | solution.py:1139
  222.6 3.9 %collective-permute-start.26 = (bf16[2,48,512]{2,1,0:T(8,128)(2,1)S(1)}, bf16[2,48,512]{2,1,0:T(8,128)(2,1)S(1)}, u32[]{:S(2)}, u32[]{:S(2)}) collective-permute-start(bf16[2,48,512]{2,1,0:T(8,128)(2,1)S(1)} %get-tuple-element.207), channel_id=1, source_target_pairs={{0,3},{1,0},{2,1},{3,2},{4,7},{5,4},{6,5},{7,6},{8,11},{9,8},{10,9... | collective-permute-start | bytes 294920 | tf_op jit(solution)/shard_map/ppermute | solution.py:1139
  228.7 3.6 %collective-permute-done.27 = bf16[2,48,512]{2,1,0:T(8,128)(2,1)S(1)} collective-permute-done((bf16[2,48,512]{2,1,0:T(8,128)(2,1)S(1)}, bf16[2,48,512]{2,1,0:T(8,128)(2,1)S(1)}, u32[]{:S(2)}, u32[]{:S(2)}) %collective-permute-start.27) | collective-permute-done | bytes 98336 | tf_op jit(solution)/shard_map/ppermute | solution.py:1139
  233.6 5.2 %collective-permute-done.30.refs_3_ = bf16[192,512]{1,0:T(8,128)(2,1)S(1)} collective-permute-done((bf16[192,512]{1,0:T(8,128)(2,1)S(1)}, bf16[192,512]{1,0:T(8,128)(2,1)S(1)}, u32[]{:S(2)}, u32[]{:S(2)}) %collective-permute-start.30) | collective-permute-done | bytes 196640 | tf_op jit(solution)/shard_map/ppermute | solution.py:1155
  241.7 12.4 %shard_map.235 = bf16[4096,512]{1,0:T(8,128)(2,1)} custom-call(s32[24]{0:T(128)S(1)} %concatenate.28.info_ref, bf16[4128,512]{1,0:T(8,128)(2,1)} %get-tuple-element.192.act_hbm, f32[4096,512]{1,0:T(8,128)} %get-tuple-element.193.values_hbm, bf16[1536,512]{1,0:T(8,128)(2,1)S(1)} %copy-done.1, bf16[1,512]{1,0:T(2,128)(2,1)S(1)} %broadcast_in_dim.54.bias_ref), custom_call_target="tpu_custom_call" | custom-call | flops 1000000 | bytes 5000 | tf_op jit(solution)/shard_map/pallas_call | solution.py:1097
  254.7 3.7 %collective-permute-done.28.refs_1_ = bf16[8,128,512]{2,1,0:T(8,128)(2,1)S(1)} collective-permute-done((bf16[8,128,512]{2,1,0:T(8,128)(2,1)}, bf16[8,128,512]{2,1,0:T(8,128)(2,1)S(1)}, u32[]{:S(2)}, u32[]{:S(2)}) %collective-permute-start.28) | collective-permute-done | bytes 1048608 | tf_op jit(solution)/shard_map/ppermute | solution.py:1139
  260.2 4.1 %shard_map.236 = f32[16384,128]{1,0:T(8,128)S(1)} custom-call(s32[24]{0:T(128)S(1)} %concatenate.28.info_ref, s32[4096]{0:T(1024)S(1)} %bitcast.76, bf16[8,128,512]{2,1,0:T(8,128)(2,1)} %collective-permute-done.17.refs_0_, bf16[8,128,512]{2,1,0:T(8,128)(2,1)S(1)} %collective-permute-done.28.refs_1_, ...), custom_call_target="tpu_custom_call", output_to_operand_aliasing={{}: (4, {})} | custom-call | flops 1000000 | bytes 10000 | tf_op jit(solution)/shard_map/pallas_call | solution.py:1123
  264.3 3.4 %copy.41 = f32[4096,512]{1,0:T(8,128)} copy(f32[4096,512]{1,0:T(8,128)S(1)} %bitcast.71) | data formatting | bytes 16777216
  267.7 4.9 %shard_map.237 = (f32[1536,512]{1,0:T(8,128)}, f32[1536,512]{1,0:T(8,128)}, f32[128,1024]{1,0:T(8,128)}, f32[1,1024]{1,0:T(1,128)}, f32[128,1024]{1,0:T(8,128)}, /*index=5*/f32[1,1024]{1,0:T(1,128)}, f32[1,512]{1,0:T(1,128)}) custom-call(s32[24]{0:T(128)S(1)} %concatenate.28.info_ref, bf16[960,512]{1,0:T(8,128)(2,1)S(1)} %get-tuple-element.197.second_ref, ...), custom_call_target="tpu_custom_call" | custom-call | flops 1000000 | bytes 5000 | tf_op jit(solution)/shard_map/pallas_call | solution.py:1097
  (158 shorter events, 60.6 us)
Async XLA Ops:
  9.9 26.4 %all-to-all-start = ((bf16[8,192,512]{2,1,0:T(8,128)(2,1)}), bf16[8,192,512]{2,1,0:T(8,128)(2,1)}, u32[]{:S(2)}, u32[]{:S(2)}) async-start(bf16[8,192,512]{2,1,0:T(8,128)(2,1)} %bitcast.15), calls=%async_computation | async-start | bytes 3145728 | tf_op jit(solution)/shard_map/all_to_all | solution.py:1257
  45.1 6.2 %collective-permute-start = (f32[24,512]{1,0:T(8,128)S(1)}, f32[24,512]{1,0:T(8,128)S(1)}, u32[]{:S(2)}, u32[]{:S(2)}) collective-permute-start(f32[24,512]{1,0:T(8,128)S(1)} %get-tuple-element.137.own_ref), channel_id=1, source_target_pairs={{0,1},{1,2},{2,3},{3,0},{4,5},{5,6},{6,7},{7,4},{8,9},{9,10},{10,1... | collective-permute-start | bytes 147464 | tf_op jit(solution)/shard_map/ppermute | solution.py:1139
  47.2 5.0 %collective-permute-start.1 = (f32[24,512]{1,0:T(8,128)S(1)}, f32[24,512]{1,0:T(8,128)S(1)}, u32[]{:S(2)}, u32[]{:S(2)}) collective-permute-start(f32[24,512]{1,0:T(8,128)S(1)} %get-tuple-element.137.own_ref), channel_id=1, source_target_pairs={{0,2},{1,3},{2,0},{3,1},{4,6},{5,7},{6,4},{7,5},{8,10},{9,11},{10,... | collective-permute-start | bytes 147464 | tf_op jit(solution)/shard_map/ppermute | solution.py:1139
  67.6 6.0 %collective-permute-start.3 = (f32[24,512]{1,0:T(8,128)S(1)}, f32[24,512]{1,0:T(8,128)S(1)}, u32[]{:S(2)}, u32[]{:S(2)}) collective-permute-start(f32[24,512]{1,0:T(8,128)S(1)} %get-tuple-element.139.own_ref), channel_id=1, source_target_pairs={{0,1},{1,2},{2,3},{3,0},{4,5},{5,6},{6,7},{7,4},{8,9},{9,10},{10,1... | collective-permute-start | bytes 147464 | tf_op jit(solution)/shard_map/ppermute | solution.py:1139
  68.1 6.5 %collective-permute-start.4 = (f32[24,512]{1,0:T(8,128)S(1)}, f32[24,512]{1,0:T(8,128)S(1)}, u32[]{:S(2)}, u32[]{:S(2)}) collective-permute-start(f32[24,512]{1,0:T(8,128)S(1)} %get-tuple-element.139.own_ref), channel_id=1, source_target_pairs={{0,2},{1,3},{2,0},{3,1},{4,6},{5,7},{6,4},{7,5},{8,10},{9,11},{10,... | collective-permute-start | bytes 147464 | tf_op jit(solution)/shard_map/ppermute | solution.py:1139
  83.8 6.0 %collective-permute-start.6 = (f32[24,512]{1,0:T(8,128)S(1)}, f32[24,512]{1,0:T(8,128)S(1)}, u32[]{:S(2)}, u32[]{:S(2)}) collective-permute-start(f32[24,512]{1,0:T(8,128)S(1)} %get-tuple-element.143.own_ref), channel_id=1, source_target_pairs={{0,1},{1,2},{2,3},{3,0},{4,5},{5,6},{6,7},{7,4},{8,9},{9,10},{10,1... | collective-permute-start | bytes 147464 | tf_op jit(solution)/shard_map/ppermute | solution.py:1139
  84.3 6.1 %collective-permute-start.7 = (f32[24,512]{1,0:T(8,128)S(1)}, f32[24,512]{1,0:T(8,128)S(1)}, u32[]{:S(2)}, u32[]{:S(2)}) collective-permute-start(f32[24,512]{1,0:T(8,128)S(1)} %get-tuple-element.143.own_ref), channel_id=1, source_target_pairs={{0,2},{1,3},{2,0},{3,1},{4,6},{5,7},{6,4},{7,5},{8,10},{9,11},{10,... | collective-permute-start | bytes 147464 | tf_op jit(solution)/shard_map/ppermute | solution.py:1139
  86.7 4.1 %collective-permute-start.8 = (f32[24,512]{1,0:T(8,128)S(1)}, f32[24,512]{1,0:T(8,128)S(1)}, u32[]{:S(2)}, u32[]{:S(2)}) collective-permute-start(f32[24,512]{1,0:T(8,128)S(1)} %get-tuple-element.143.own_ref), channel_id=1, source_target_pairs={{0,3},{1,0},{2,1},{3,2},{4,7},{5,4},{6,5},{7,6},{8,11},{9,8},{10,9... | collective-permute-start | bytes 147464 | tf_op jit(solution)/shard_map/ppermute | solution.py:1139
  109.3 5.1 %collective-permute-start.10 = (f32[24,512]{1,0:T(8,128)S(1)}, f32[24,512]{1,0:T(8,128)S(1)}, u32[]{:S(2)}, u32[]{:S(2)}) collective-permute-start(f32[24,512]{1,0:T(8,128)S(1)} %get-tuple-element.149.own_ref), channel_id=1, source_target_pairs={{0,2},{1,3},{2,0},{3,1},{4,6},{5,7},{6,4},{7,5},{8,10},{9,11},{10,... | collective-permute-start | bytes 147464 | tf_op jit(solution)/shard_map/ppermute | solution.py:1139
  110.3 4.7 %collective-permute-start.11 = (f32[24,512]{1,0:T(8,128)S(1)}, f32[24,512]{1,0:T(8,128)S(1)}, u32[]{:S(2)}, u32[]{:S(2)}) collective-permute-start(f32[24,512]{1,0:T(8,128)S(1)} %get-tuple-element.149.own_ref), channel_id=1, source_target_pairs={{0,3},{1,0},{2,1},{3,2},{4,7},{5,4},{6,5},{7,6},{8,11},{9,8},{10,9... | collective-permute-start | bytes 147464 | tf_op jit(solution)/shard_map/ppermute | solution.py:1139
  113.2 5.9 %collective-permute-start.9 = (f32[24,512]{1,0:T(8,128)S(1)}, f32[24,512]{1,0:T(8,128)S(1)}, u32[]{:S(2)}, u32[]{:S(2)}) collective-permute-start(f32[24,512]{1,0:T(8,128)S(1)} %get-tuple-element.149.own_ref), channel_id=1, source_target_pairs={{0,1},{1,2},{2,3},{3,0},{4,5},{5,6},{6,7},{7,4},{8,9},{9,10},{10,1... | collective-permute-start | bytes 147464 | tf_op jit(solution)/shard_map/ppermute | solution.py:1139
  129.8 6.2 %collective-permute-start.13 = (bf16[64,512]{1,0:T(8,128)(2,1)S(1)}, bf16[64,512]{1,0:T(8,128)(2,1)S(1)}, u32[]{:S(2)}, u32[]{:S(2)}) collective-permute-start(bf16[64,512]{1,0:T(8,128)(2,1)S(1)} %get-tuple-element.152), channel_id=1, source_target_pairs={{1,0},{2,1},{3,2},{5,4},{6,5},{7,6},{9,8},{10,9},{11,10},{13,12},{... | collective-permute-start | bytes 196616 | tf_op jit(solution)/shard_map/ppermute | solution.py:1150
  137.1 19.9 %all-to-all-start.1 = ((bf16[8,128,512]{2,1,0:T(8,128)(2,1)}), bf16[8,128,512]{2,1,0:T(8,128)(2,1)S(1)}, u32[]{:S(2)}, u32[]{:S(2)}) async-start(bf16[8,128,512]{2,1,0:T(8,128)(2,1)} %bitcast.77), calls=%async_computation.1 | async-start | bytes 2097152 | tf_op jit(solution)/shard_map/all_to_all | solution.py:1431
  157.0 25.7 %collective-permute-start.14 = (bf16[8,128,512]{2,1,0:T(8,128)(2,1)S(1)}, bf16[8,128,512]{2,1,0:T(8,128)(2,1)}, u32[]{:S(2)}, u32[]{:S(2)}) collective-permute-start(bf16[8,128,512]{2,1,0:T(8,128)(2,1)S(1)} %all-to-all-done.1.refs_0_), channel_id=1, source_target_pairs={{0,1},{1,2},{2,3},{3,0},{4,5},{5,6},{6,7},{7,4},{8,9},{9,10},{10,1... | collective-permute-start | bytes 3145736 | tf_op jit(solution)/shard_map/ppermute | solution.py:1139
  182.7 10.1 %collective-permute-start.18 = (bf16[384,512]{1,0:T(8,128)(2,1)S(1)}, bf16[384,512]{1,0:T(8,128)(2,1)S(1)}, u32[]{:S(2)}, u32[]{:S(2)}) collective-permute-start(bf16[384,512]{1,0:T(8,128)(2,1)S(1)} %get-tuple-element.175), channel_id=1, source_target_pairs={{0,8},{4,12},{8,0},{12,4},{16,24},{20,28},{24,16},{28,20},{1,9},{5... | collective-permute-start | bytes 1179656 | tf_op jit(solution)/shard_map/ppermute | solution.py:1155
  184.5 9.8 %collective-permute-start.19 = (bf16[384,512]{1,0:T(8,128)(2,1)S(1)}, bf16[384,512]{1,0:T(8,128)(2,1)S(1)}, u32[]{:S(2)}, u32[]{:S(2)}) collective-permute-start(bf16[384,512]{1,0:T(8,128)(2,1)S(1)} %get-tuple-element.177), channel_id=1, source_target_pairs={{0,16},{4,20},{8,24},{12,28},{16,0},{20,4},{24,8},{28,12},{1,17},{... | collective-permute-start | bytes 1179656 | tf_op jit(solution)/shard_map/ppermute | solution.py:1155
  185.8 26.0 %collective-permute-start.17 = (bf16[8,128,512]{2,1,0:T(8,128)(2,1)}, bf16[8,128,512]{2,1,0:T(8,128)(2,1)}, u32[]{:S(2)}, u32[]{:S(2)}) collective-permute-start(bf16[8,128,512]{2,1,0:T(8,128)(2,1)} %collective-permute-done.14.refs_1_), channel_id=1, source_target_pairs={{0,1},{1,2},{2,3},{3,0},{4,5},{5,6},{6,7},{7,4},{8,9},{9,10},{10,1... | collective-permute-start | bytes 3145736 | tf_op jit(solution)/shard_map/ppermute | solution.py:1139
  197.2 6.0 %collective-permute-start.21 = (bf16[192,512]{1,0:T(8,128)(2,1)}, bf16[192,512]{1,0:T(8,128)(2,1)}, u32[]{:S(2)}, u32[]{:S(2)}) collective-permute-start(bf16[192,512]{1,0:T(8,128)(2,1)} %get-tuple-element.181), channel_id=1, source_target_pairs={{0,8},{4,12},{8,0},{12,4},{16,24},{20,28},{24,16},{28,20},{1,9},{5... | collective-permute-start | bytes 589832 | tf_op jit(solution)/shard_map/ppermute | solution.py:1155
  201.4 5.7 %collective-permute-start.20 = (bf16[192,512]{1,0:T(8,128)(2,1)S(1)}, bf16[192,512]{1,0:T(8,128)(2,1)S(1)}, u32[]{:S(2)}, u32[]{:S(2)}) collective-permute-start(bf16[192,512]{1,0:T(8,128)(2,1)S(1)} %copy-done.15), channel_id=1, source_target_pairs={{0,16},{4,20},{8,24},{12,28},{16,0},{20,4},{24,8},{28,12},{1,17},{... | collective-permute-start | bytes 589832 | tf_op jit(solution)/shard_map/ppermute | solution.py:1155
  212.0 6.5 %collective-permute-start.22 = (bf16[2,48,512]{2,1,0:T(8,128)(2,1)S(1)}, bf16[2,48,512]{2,1,0:T(8,128)(2,1)S(1)}, u32[]{:S(2)}, u32[]{:S(2)}) collective-permute-start(bf16[2,48,512]{2,1,0:T(8,128)(2,1)S(1)} %get-tuple-element.210), channel_id=1, source_target_pairs={{0,1},{1,2},{2,3},{3,0},{4,5},{5,6},{6,7},{7,4},{8,9},{9,10},{10,1... | collective-permute-start | bytes 294920 | tf_op jit(solution)/shard_map/ppermute | solution.py:1139
  212.0 6.5 %collective-permute-start.23 = (bf16[2,48,512]{2,1,0:T(8,128)(2,1)S(1)}, bf16[2,48,512]{2,1,0:T(8,128)(2,1)S(1)}, u32[]{:S(2)}, u32[]{:S(2)}) collective-permute-start(bf16[2,48,512]{2,1,0:T(8,128)(2,1)S(1)} %get-tuple-element.212), channel_id=1, source_target_pairs={{0,3},{1,0},{2,1},{3,2},{4,7},{5,4},{6,5},{7,6},{8,11},{9,8},{10,9... | collective-permute-start | bytes 294920 | tf_op jit(solution)/shard_map/ppermute | solution.py:1139
  215.8 5.8 %collective-permute-start.24 = (bf16[2,48,512]{2,1,0:T(8,128)(2,1)S(1)}, bf16[2,48,512]{2,1,0:T(8,128)(2,1)S(1)}, u32[]{:S(2)}, u32[]{:S(2)}) collective-permute-start(bf16[2,48,512]{2,1,0:T(8,128)(2,1)S(1)} %get-tuple-element.211), channel_id=1, source_target_pairs={{0,2},{1,3},{2,0},{3,1},{4,6},{5,7},{6,4},{7,5},{8,10},{9,11},{10,... | collective-permute-start | bytes 294920 | tf_op jit(solution)/shard_map/ppermute | solution.py:1139
  221.7 6.6 %collective-permute-start.25 = (bf16[2,48,512]{2,1,0:T(8,128)(2,1)S(1)}, bf16[2,48,512]{2,1,0:T(8,128)(2,1)S(1)}, u32[]{:S(2)}, u32[]{:S(2)}) collective-permute-start(bf16[2,48,512]{2,1,0:T(8,128)(2,1)S(1)} %get-tuple-element.207), channel_id=1, source_target_pairs={{0,1},{1,2},{2,3},{3,0},{4,5},{5,6},{6,7},{7,4},{8,9},{9,10},{10,1... | collective-permute-start | bytes 294920 | tf_op jit(solution)/shard_map/ppermute | solution.py:1139
  222.6 6.1 %collective-permute-start.26 = (bf16[2,48,512]{2,1,0:T(8,128)(2,1)S(1)}, bf16[2,48,512]{2,1,0:T(8,128)(2,1)S(1)}, u32[]{:S(2)}, u32[]{:S(2)}) collective-permute-start(bf16[2,48,512]{2,1,0:T(8,128)(2,1)S(1)} %get-tuple-element.207), channel_id=1, source_target_pairs={{0,3},{1,0},{2,1},{3,2},{4,7},{5,4},{6,5},{7,6},{8,11},{9,8},{10,9... | collective-permute-start | bytes 294920 | tf_op jit(solution)/shard_map/ppermute | solution.py:1139
  226.4 5.9 %collective-permute-start.27 = (bf16[2,48,512]{2,1,0:T(8,128)(2,1)S(1)}, bf16[2,48,512]{2,1,0:T(8,128)(2,1)S(1)}, u32[]{:S(2)}, u32[]{:S(2)}) collective-permute-start(bf16[2,48,512]{2,1,0:T(8,128)(2,1)S(1)} %get-tuple-element.207), channel_id=1, source_target_pairs={{0,2},{1,3},{2,0},{3,1},{4,6},{5,7},{6,4},{7,5},{8,10},{9,11},{10,... | collective-permute-start | bytes 294920 | tf_op jit(solution)/shard_map/ppermute | solution.py:1139
  232.4 26.1 %collective-permute-start.28 = (bf16[8,128,512]{2,1,0:T(8,128)(2,1)}, bf16[8,128,512]{2,1,0:T(8,128)(2,1)S(1)}, u32[]{:S(2)}, u32[]{:S(2)}) collective-permute-start(bf16[8,128,512]{2,1,0:T(8,128)(2,1)} %collective-permute-done.17.refs_0_), channel_id=1, source_target_pairs={{0,1},{1,2},{2,3},{3,0},{4,5},{5,6},{6,7},{7,4},{8,9},{9,10},{10,1... | collective-permute-start | bytes 3145736 | tf_op jit(solution)/shard_map/ppermute | solution.py:1139
  232.7 6.6 %collective-permute-start.29 = (bf16[240,512]{1,0:T(8,128)(2,1)S(1)}, bf16[240,512]{1,0:T(8,128)(2,1)S(1)}, u32[]{:S(2)}, u32[]{:S(2)}) collective-permute-start(bf16[240,512]{1,0:T(8,128)(2,1)S(1)} %constant_dynamic-update-slice_fusion.refs_0_), channel_id=1, source_target_pairs={{0,8},{4,12},{8,0},{12,4},{16,24},{20,28},{24,16},{28,20},{1,9},{5... | collective-permute-start | bytes 737288 | tf_op jit(solution)/shard_map/ppermute | solution.py:1155
  233.1 5.7 %collective-permute-start.30 = (bf16[192,512]{1,0:T(8,128)(2,1)S(1)}, bf16[192,512]{1,0:T(8,128)(2,1)S(1)}, u32[]{:S(2)}, u32[]{:S(2)}) collective-permute-start(bf16[192,512]{1,0:T(8,128)(2,1)S(1)} %slice_bitcast_fusion.refs_2_), channel_id=1, source_target_pairs={{0,16},{4,20},{8,24},{12,28},{16,0},{20,4},{24,8},{28,12},{1,17},{... | collective-permute-start | bytes 589832 | tf_op jit(solution)/shard_map/ppermute | solution.py:1155
  240.0 14.1 %collective-permute-start.31 = (bf16[480,512]{1,0:T(8,128)(2,1)S(1)}, bf16[480,512]{1,0:T(8,128)(2,1)S(1)}, u32[]{:S(2)}, u32[]{:S(2)}) collective-permute-start(bf16[480,512]{1,0:T(8,128)(2,1)S(1)} %get-tuple-element.188.refs_0_), channel_id=1, source_target_pairs={{0,16},{4,20},{8,24},{12,28},{16,0},{20,4},{24,8},{28,12},{1,17},{... | collective-permute-start | bytes 1474568 | tf_op jit(solution)/shard_map/ppermute | solution.py:1155
  240.1 14.0 %collective-permute-start.32 = (bf16[384,512]{1,0:T(8,128)(2,1)S(1)}, bf16[384,512]{1,0:T(8,128)(2,1)S(1)}, u32[]{:S(2)}, u32[]{:S(2)}) collective-permute-start(bf16[384,512]{1,0:T(8,128)(2,1)S(1)} %get-tuple-element.189.refs_2_), channel_id=1, source_target_pairs={{0,8},{4,12},{8,0},{12,4},{16,24},{20,28},{24,16},{28,20},{1,9},{5... | collective-permute-start | bytes 1179656 | tf_op jit(solution)/shard_map/ppermute | solution.py:1155
  258.5 9.2 %collective-permute-start.33 = (bf16[960,512]{1,0:T(8,128)(2,1)S(1)}, bf16[960,512]{1,0:T(8,128)(2,1)S(1)}, u32[]{:S(2)}, u32[]{:S(2)}) collective-permute-start(bf16[960,512]{1,0:T(8,128)(2,1)S(1)} %get-tuple-element.197.second_ref), channel_id=1, source_target_pairs={{0,4},{4,0},{8,12},{12,8},{16,20},{20,16},{24,28},{28,24},{1,5},{5... | collective-permute-start | bytes 2949128 | tf_op jit(solution)/shard_map/ppermute | solution.py:1155
  258.5 9.2 %collective-permute-start.34 = (bf16[768,512]{1,0:T(8,128)(2,1)S(1)}, bf16[768,512]{1,0:T(8,128)(2,1)S(1)}, u32[]{:S(2)}, u32[]{:S(2)}) collective-permute-start(bf16[768,512]{1,0:T(8,128)(2,1)S(1)} %get-tuple-element.198.first_ref), channel_id=1, source_target_pairs={{0,4},{4,0},{8,12},{12,8},{16,20},{20,16},{24,28},{28,24},{1,5},{5... | collective-permute-start | bytes 2359304 | tf_op jit(solution)/shard_map/ppermute | solution.py:1155
  (30 other events, 321.7 us)
